TPU v7x, 32 devices: a whole 2x2x4 slice. The times are simulated.
32 devices in a mesh: dp: 2 (over x), expert: 16 (over z, y, core).
Axes of the slice: x: 2, y: 2, z: 4, core: 2. Of those that a mesh axis runs over, the one named last changes fastest.
Arguments:
- expert_ids: int32 [1536, 8], P(('dp', 'expert')), may hold values from 0 to 15, all different within a row; in each aligned block of 48 rows (0 to 47, 48 to 95, ...) at most 36 rows name the same one
- route_probs: float32 [1536, 8], P(('dp', 'expert')), may hold values from 0.02 to 0.5
- expert_hidden: bfloat16 [2, 16, 16, 36, 768], P('dp', 'expert'), may hold values from -6 to 6
- down_weight: bfloat16 [16, 768, 4096], P('expert', None, 'dp'), may hold values from -0.21875 to 0.21875
- out_grad: bfloat16 [1536, 4096], P(('dp', 'expert')), may hold values from -0.75 to 0.75
Outputs:
- layer_out: bfloat16 [1536, 4096], P(('dp', 'expert'))
- prob_grad: float32 [1536, 8], P(('dp', 'expert'))
- hidden_grad: bfloat16 [2, 16, 16, 36, 768], P('dp', 'expert')
- weight_grad: float32 [16, 768, 4096], P('expert', None, 'dp')
Inputs may be any that keep to these rules, and one draw needn't show every extreme that they name: `expert_ids`: each row names 8 different experts. Among the rows of one device no expert is named by more than 36 rows, and in every draw some device names some expert exactly 36 times.
All inputs are finite; a program needn't handle non-finite values.
Results may differ from a plain program's by a relative error of at most 0.0085.
Values may be sent and summed in bfloat16 or wider, within the bound.
No kernel may reach another device: no remote copies, remote signals or barrier semaphores. Data moves between devices by JAX's collectives and lax.ppermute only.
A program may use at most 128 MiB of HBM per device.

v0:
```python
import jax
import jax.numpy as jnp
from jax import lax
from jax.sharding import PartitionSpec as P


def rounded_partial(values):
    narrow = lax.optimization_barrier(values.astype(jnp.bfloat16))
    return narrow.astype(jnp.float32)


def shards(expert_ids, route_probs, expert_hidden, down_weight, out_grad):
    tok_count, top_count = expert_ids.shape
    expert_count = lax.axis_size("expert")
    capacity = expert_hidden.shape[3]
    hidden_width = down_weight.shape[1]
    model_width = out_grad.shape[1]
    slot_count = expert_count * capacity
    flat_ids = expert_ids.reshape(-1)
    onehot = (flat_ids[:, None] == jnp.arange(expert_count, dtype=jnp.int32)[None, :]).astype(
        jnp.int32
    )
    earlier = jnp.cumsum(onehot, axis=0) - onehot
    position = jnp.sum(earlier * onehot, axis=1)
    slot_index = flat_ids * capacity + position
    slot_owner = (
        jnp.full((slot_count,), -1, dtype=jnp.int32)
        .at[slot_index]
        .set(jnp.arange(tok_count * top_count, dtype=jnp.int32))
    )
    filled = slot_owner >= 0
    safe_owner = jnp.maximum(slot_owner, 0)
    hidden_rows = expert_hidden.reshape(-1, hidden_width)
    flat_probs = route_probs.reshape(-1)
    slot_prob = jnp.where(filled, flat_probs[safe_owner], jnp.float32(0.0))
    slot_out = jnp.dot(
        hidden_rows,
        lax.all_gather(down_weight, "dp", axis=2, tiled=True)[0],
        preferred_element_type=jnp.float32,
    ).astype(jnp.bfloat16)
    returned = lax.all_to_all(
        slot_out.reshape(expert_count, capacity, model_width),
        "expert",
        split_axis=0,
        concat_axis=0,
        tiled=True,
    )
    route_out = returned.reshape(slot_count, model_width)[slot_index].reshape(
        tok_count, top_count, model_width
    )
    layer_out = jnp.einsum(
        "tk,tkd->td", route_probs, route_out, preferred_element_type=jnp.float32
    ).astype(jnp.bfloat16)
    prob_grad = jnp.einsum("td,tkd->tk", out_grad, route_out, preferred_element_type=jnp.float32)
    scaled = (slot_prob[:, None] * out_grad[safe_owner // top_count]).astype(jnp.bfloat16)
    arrived = lax.all_to_all(
        scaled.reshape(expert_count, capacity, model_width),
        "expert",
        split_axis=0,
        concat_axis=0,
        tiled=True,
    )
    arrived = arrived.reshape(-1, model_width)
    partial_value = jnp.einsum(
        "rf,rd->fd", hidden_rows, arrived, preferred_element_type=jnp.float32
    )[None]
    weight_grad = lax.psum_scatter(
        rounded_partial(partial_value).astype(jnp.bfloat16), "dp", scatter_dimension=2, tiled=True
    ).astype(jnp.float32)
    hidden_total = jnp.einsum(
        "rd,fd->rf",
        arrived,
        lax.all_gather(down_weight, "dp", axis=2, tiled=True)[0],
        preferred_element_type=jnp.float32,
    )
    hidden_grad = hidden_total.astype(jnp.bfloat16).reshape(expert_hidden.shape)
    return (layer_out, prob_grad, hidden_grad, weight_grad)


def solution(mesh):
    placed = (
        P(("dp", "expert"), None),
        P(("dp", "expert"), None),
        P("dp", "expert", None, None, None),
        P("expert", None, "dp"),
        P(("dp", "expert"), None),
    )
    return jax.shard_map(
        shards,
        mesh=mesh,
        in_specs=placed,
        out_specs=(
            P(("dp", "expert"), None),
            P(("dp", "expert"), None),
            P("dp", "expert", None, None, None),
            P("expert", None, "dp"),
        ),
        check_vma=False,
    )
```

profile of v0, /device:TPU:15, one launch (start us, length us, event | category | flops | bytes accessed | tf_op | source)
XLA Modules:
  0.0 350.1 jit_solution(9981094957262527719)
XLA Ops:
  7.2 0.0 copy-start
  7.2 0.8 copy.13
  8.0 0.1 eq.29
  8.1 0.1 eq.25
  8.2 0.7 broadcast_multiply_fusion
  8.9 0.9 reduce-window.6
  9.7 0.2 slice_reduce_fusion
  10.0 0.1 copy.12
  10.1 0.1 mul.32
  10.2 0.1 fusion.18
  10.3 2.9 scatter_custom_fusion
  13.3 0.8 copy.16
  14.0 0.1 reshape.91
  14.1 4.0 %gather_fusion.1 = f32[576]{0:T(1024)S(1)} fusion(f32[384]{0:T(512)S(1)} %reshape.91, s32[1024]{0:T(1024)S(1)} %get-tuple-element.15), kind=kCustom, calls=%fused_computation.1 | custom fusion | bytes 6912 | tf_op jit(solution)/shard_map/gather | solution.py:35
  18.1 0.1 mul.34
  18.2 0.0 copy-done
  18.2 5.2 %gather_fusion.2 = bf16[576,4096]{1,0:T(8,128)(2,1)} fusion(bf16[48,4096]{1,0:T(8,128)(2,1)S(1)} %copy-done, s32[1024]{0:T(1024)S(1)} %get-tuple-element.14), kind=kCustom, calls=%fused_computation.2 | custom fusion | bytes 9439488 | tf_op jit(solution)/shard_map/gather | solution.py:55
  23.4 7.9 %reshape.94 = f32[16,36,4096]{2,1,0:T(8,128)} reshape(bf16[576,4096]{1,0:T(8,128)(2,1)} %gather_fusion.2) | data formatting | bytes 14155776 | tf_op jit(solution)/shard_map/convert_element_type | solution.py:55
  31.3 7.9 %multiply_convert_fusion = bf16[16,36,4096]{2,1,0:T(8,128)(2,1)} fusion(f32[16,36,4096]{2,1,0:T(8,128)} %reshape.94, f32[16,36]{1,0:T(8,128)S(1)} %mul.34), kind=kLoop, calls=%fused_computation.4 | loop fusion | flops 4718592 | bytes 14158080 | tf_op jit(solution)/shard_map/convert_element_type | solution.py:55
  39.2 0.0 copy-start.1
  39.2 6.7 %all-to-all-start.1 = ((bf16[16,36,4096]{2,1,0:T(8,128)(2,1)}), bf16[16,36,4096]{2,1,0:T(8,128)(2,1)}, u32[]{:S(2)}, u32[]{:S(2)}) async-start(bf16[16,36,4096]{2,1,0:T(8,128)(2,1)} %multiply_convert_fusion), calls=%async_computation.1 | async-start | bytes 10485760 | tf_op jit(solution)/shard_map/all_to_all | solution.py:56
  45.9 0.0 all-gather.2.cloned.1.call-start
  45.9 0.7 all-gather.2.cloned.1.call-update
  46.6 0.0 reduce-scatter.2.cloned.1.call-start
  46.7 0.0 copy-done.1
  46.7 0.3 copy.11
  47.0 0.2 reshape.86
  47.1 113.7 %all-to-all-done.1 = bf16[16,36,4096]{2,1,0:T(8,128)(2,1)} async-done(((bf16[16,36,4096]{2,1,0:T(8,128)(2,1)}), bf16[16,36,4096]{2,1,0:T(8,128)(2,1)}, u32[]{:S(2)}, u32[]{:S(2)}) %all-to-all-start.1) | async-done | bytes 4718624 | tf_op jit(solution)/shard_map/all_to_all | solution.py:56
  160.8 7.3 %reshape.92 = bf16[576,4096]{1,0:T(8,128)(2,1)} reshape(bf16[16,36,4096]{2,1,0:T(8,128)(2,1)} %all-to-all-done.1) | data formatting | bytes 9437184 | tf_op jit(solution)/shard_map/reshape | solution.py:63
  168.1 9.3 %fusion.7 = bf16[1,768,4096]{1,2,0:T(8,128)(2,1)} fusion(bf16[576,4096]{1,0:T(8,128)(2,1)} %reshape.92, bf16[576,768]{1,0:T(8,128)(2,1)S(1)} %reshape.86), kind=kOutput, calls=%fused_computation.11 | convolution fusion | flops 3627024384 | bytes 11894784 | tf_op jit(solution)/shard_map/rf,rd->fd/dot_general | solution.py:64
  177.4 0.0 reduce-scatter.2.cloned.1.call-update
  177.5 0.0 all-gather.2.cloned.1.call-done
  177.5 8.3 %fusion.4 = bf16[576,4096]{1,0:T(8,128)(2,1)} fusion(bf16[576,768]{1,0:T(8,128)(2,1)S(1)} %reshape.86, bf16[1,768,4096]{2,1,0:T(8,128)(2,1)} %all-gather.2.cloned.1.call-done), kind=kOutput, calls=%fused_computation.10 | convolution fusion | flops 3626237952 | bytes 11894784 | tf_op jit(solution)/shard_map/dot_general | solution.py:36
  185.8 7.3 %reshape.87 = bf16[16,36,4096]{2,1,0:T(8,128)(2,1)} reshape(bf16[576,4096]{1,0:T(8,128)(2,1)} %fusion.4) | data formatting | bytes 9437184 | tf_op jit(solution)/shard_map/reshape | solution.py:42
  193.1 0.0 copy-start.2
  193.1 5.1 %all-to-all-start = ((bf16[16,36,4096]{2,1,0:T(8,128)(2,1)}), bf16[16,36,4096]{2,1,0:T(8,128)(2,1)}, u32[]{:S(2)}, u32[]{:S(2)}) async-start(bf16[16,36,4096]{2,1,0:T(8,128)(2,1)} %reshape.87), calls=%async_computation | async-start | bytes 10485760 | tf_op jit(solution)/shard_map/all_to_all | solution.py:41
  198.2 0.0 copy-done.2
  198.2 0.7 copy.19
  198.9 8.3 %fusion.12 = bf16[576,768]{1,0:T(8,128)(2,1)S(1)} fusion(bf16[576,4096]{1,0:T(8,128)(2,1)} %reshape.92, bf16[1,768,4096]{2,1,0:T(8,128)(2,1)} %all-gather.2.cloned.1.call-done), kind=kOutput, calls=%fused_computation.16 | convolution fusion | flops 3624321024 | bytes 11894784 | tf_op jit(solution)/shard_map/rd,fd->rf/dot_general | solution.py:70
  207.3 0.2 reshape.93
  207.4 1.1 copy.17
  208.5 104.6 %all-to-all-done = bf16[16,36,4096]{2,1,0:T(8,128)(2,1)} async-done(((bf16[16,36,4096]{2,1,0:T(8,128)(2,1)}), bf16[16,36,4096]{2,1,0:T(8,128)(2,1)}, u32[]{:S(2)}, u32[]{:S(2)}) %all-to-all-start) | async-done | bytes 4718624 | tf_op jit(solution)/shard_map/all_to_all | solution.py:41
  313.1 7.3 %reshape.88 = bf16[576,4096]{1,0:T(8,128)(2,1)} reshape(bf16[16,36,4096]{2,1,0:T(8,128)(2,1)} %all-to-all-done) | data formatting | bytes 9437184 | tf_op jit(solution)/shard_map/reshape | solution.py:48
  320.4 10.5 %gather_fusion = bf16[384,4096]{1,0:T(8,128)(2,1)S(1)} fusion(bf16[576,4096]{1,0:T(8,128)(2,1)} %reshape.88, s32[1024]{0:T(1024)S(1)} %pad_clamp_fusion.2), kind=kCustom, calls=%fused_computation | custom fusion | bytes 6292992 | tf_op jit(solution)/shard_map/gather | solution.py:48
  330.9 1.7 fusion.10
  332.6 1.2 copy.28
  333.8 2.7 fusion.8
  336.5 1.4 copy.22
  337.9 0.0 reduce-scatter.2.cloned.1.call-done
  337.9 5.4 %copy.18 = f32[1,768,2048]{2,1,0:T(8,128)} copy(bf16[1,768,2048]{1,2,0:T(8,128)(2,1)} %reduce-scatter.2.cloned.1.call-done) | data formatting | bytes 9437184
  (8 shorter events, 0.1 us)
Async XLA Ops:
  7.2 11.0 %copy-start = (bf16[48,4096]{1,0:T(8,128)(2,1)S(1)}, bf16[48,4096]{1,0:T(8,128)(2,1)}, u32[]{:S(2)}) copy-start(bf16[48,4096]{1,0:T(8,128)(2,1)} %param.9) | copy-start | bytes 1179652
  39.2 7.5 %copy-start.1 = (bf16[1,1,16,36,768]{4,2,3,1,0:T(8,128)(2,1)S(1)}, bf16[1,1,16,36,768]{4,2,3,1,0:T(8,128)(2,1)}, u32[]{:S(2)}) copy-start(bf16[1,1,16,36,768]{4,2,3,1,0:T(8,128)(2,1)} %param.7) | copy-start | bytes 2654212
  39.2 121.6 %all-to-all-start.1 = ((bf16[16,36,4096]{2,1,0:T(8,128)(2,1)}), bf16[16,36,4096]{2,1,0:T(8,128)(2,1)}, u32[]{:S(2)}, u32[]{:S(2)}) async-start(bf16[16,36,4096]{2,1,0:T(8,128)(2,1)} %multiply_convert_fusion), calls=%async_computation.1 | async-start | bytes 10485760 | tf_op jit(solution)/shard_map/all_to_all | solution.py:56
  45.9 131.6 %all-gather.2.cloned.1.call-start = ((), (), s32[]{:S(2)}) async-start(), calls=%async_computation.3 | async-start | bytes 9437184 | tf_op jit(solution)/shard_map/all_gather | solution.py:38
  46.6 291.2 %reduce-scatter.2.cloned.1.call-start = ((), (), s32[]{:S(2)}) async-start(), calls=%async_computation.4 | async-start | bytes 9437184 | tf_op jit(solution)/shard_map/reduce_scatter | solution.py:67
  193.1 5.1 %copy-start.2 = (f32[48,8]{0,1:T(8,128)S(1)}, f32[48,8]{0,1:T(8,128)}, u32[]{:S(2)}) copy-start(f32[48,8]{0,1:T(8,128)} %param.6) | copy-start | bytes 4612
  193.1 120.1 %all-to-all-start = ((bf16[16,36,4096]{2,1,0:T(8,128)(2,1)}), bf16[16,36,4096]{2,1,0:T(8,128)(2,1)}, u32[]{:S(2)}, u32[]{:S(2)}) async-start(bf16[16,36,4096]{2,1,0:T(8,128)(2,1)} %reshape.87), calls=%async_computation | async-start | bytes 10485760 | tf_op jit(solution)/shard_map/all_to_all | solution.py:41
Sparse Core Ops, SparseCore 0:
  48.3 80.0 all-gather.1
  177.6 75.5 reduce-scatter.1
where the time goes:
time: 351 us; the launch traced here: 350 us
  waiting for transfers between devices  219 us (62%)
  local copies, waits for them, and re-layouts  64.9 us (18%)
  matrix products  30.4 us (9%)
  between operations  14.2 us (4%)
  starting transfers between devices  11.9 us (3%)
  other arithmetic  9.67 us (3%)
    all_to_all x1, waiting for transfers between devices, shards(): lax.all_to_all(scaled.reshape(expert_count, capacity, model_width), 'expe...  114 us
    all_to_all x1, waiting for transfers between devices, shards(): lax.all_to_all(slot_out.reshape(expert_count, capacity, model_width), 'ex...  105 us
    gather x1, local copies, waits for them, and re-layouts, shards(): returned.reshape(slot_count, model_width)[slot_index]  10.5 us
    dot_general x1, matrix products, shards(): jnp.einsum('rf,rd->fd', hidden_rows, arrived, preferred_element_type=jnp....  9.34 us
    unnamed x12, local copies, waits for them, and re-layouts  9 us
    dot_general x1, matrix products, shards(): jnp.einsum('rd,fd->rf', arrived, lax.all_gather(down_weight, 'dp', axis=2...  8.33 us
    dot_general x1, matrix products, shards(): jnp.dot(hidden_rows, lax.all_gather(down_weight, 'dp', axis=2, tiled=True...  8.3 us
    convert_element_type x1, other arithmetic, shards(): (slot_prob[:, None] * out_grad[safe_owner // top_count]).astype(jnp.bfloa...  7.93 us
  transfers between devices with their start and end apart: 4, of which 2 were waited for; matrix products, arithmetic and copies ran while one was open for 19% of the time, Pallas kernels for 0%

commit v1 on v0

v1 whole, which is shorter than its diff:
```python
import jax
import jax.numpy as jnp
from jax import lax
from jax.sharding import PartitionSpec as P


def dot(a, b, ca, cb):
    return lax.dot_general(a, b, (((ca,), (cb,)), ((), ())), preferred_element_type=jnp.float32)


def shards(expert_ids, route_probs, expert_hidden, down_weight, out_grad):
    tok, _ = expert_ids.shape
    n_dp = lax.axis_size("dp")
    n_ex = lax.axis_size("expert")
    cap = expert_hidden.shape[3]
    ff = down_weight.shape[1]
    width = down_weight.shape[2]
    weight = down_weight[0]
    me_dp = lax.axis_index("dp")

    names = expert_ids[:, :, None] == jnp.arange(n_ex, dtype=jnp.int32)[None, None, :]
    table = jnp.sum(jnp.where(names, route_probs[:, :, None], 0.0), axis=1)
    mine = lax.all_to_all(table.T, "expert", 0, 0, tiled=True)
    mine = lax.all_gather(mine, "dp", axis=0)
    taken = (mine > 0.0).astype(jnp.float32)
    earlier = jnp.tril(jnp.ones((tok, tok), jnp.float32), -1)
    place = jnp.einsum("nst,ut->nsu", taken, earlier).astype(jnp.int32)
    place = jnp.where(mine > 0.0, place, -1)

    grads = out_grad.reshape(tok, n_dp, width).transpose(1, 0, 2)
    grads = lax.all_to_all(grads, "dp", 0, 0, tiled=True)
    grads = lax.all_gather(grads, "expert", axis=0)
    rows = grads.reshape(n_ex * n_dp * tok, width)

    hidden = expert_hidden[0, 0].transpose(1, 0, 2).reshape(cap * n_ex, ff)
    hidden = lax.all_gather(hidden, "dp", axis=0)

    slot_c = jnp.arange(cap * n_ex, dtype=jnp.int32) // n_ex
    slot_s = jnp.arange(cap * n_ex, dtype=jnp.int32) % n_ex
    source = jnp.arange(n_ex, dtype=jnp.int32)
    pick = (place.reshape(n_dp, n_ex, tok, 1) == slot_c) & (source[None, :, None, None] == slot_s)
    pick = pick.reshape(n_dp, n_ex * tok, cap * n_ex).astype(jnp.bfloat16)
    held = jnp.einsum("ntr,nrf->ntf", pick, hidden)
    held = held.reshape(n_dp, n_ex, tok, ff).transpose(1, 0, 2, 3)
    prob_rows = mine.transpose(1, 0, 2)[..., None]
    scaled = (held * prob_rows).astype(jnp.bfloat16).reshape(-1, ff)

    part = dot(scaled, weight, 1, 0).astype(jnp.bfloat16)
    part = part.reshape(n_ex, n_dp, tok, width)
    layer = lax.psum_scatter(part, "expert", scatter_dimension=0, tiled=True)[0]
    layer = lax.all_to_all(layer, "dp", 0, 0, tiled=True)
    layer_out = layer.transpose(1, 0, 2).reshape(tok, n_dp * width)

    layer, rows = lax.optimization_barrier((layer, rows))
    back = dot(rows, weight, 1, 1).astype(jnp.bfloat16).reshape(n_ex, n_dp, tok, ff)
    inner = jnp.sum(back.astype(jnp.float32) * held, axis=3)
    inner = lax.psum_scatter(inner.transpose(1, 0, 2), "dp", scatter_dimension=0, tiled=True)[0]
    inner = lax.all_to_all(inner, "expert", 0, 0, tiled=True).T
    prob_grad = jnp.sum(jnp.where(names, inner[:, None, :], 0.0), axis=2)

    spread = (back * prob_rows).astype(jnp.bfloat16).transpose(1, 0, 2, 3)
    spread = spread.reshape(n_dp, n_ex * tok, ff)
    spread = jnp.einsum("ntr,ntf->nrf", pick, spread, preferred_element_type=jnp.float32)
    spread = lax.all_to_all(spread.astype(jnp.bfloat16), "dp", 0, 0, tiled=True)
    hidden_grad = jnp.sum(spread.astype(jnp.float32), axis=0).astype(jnp.bfloat16)
    hidden_grad = hidden_grad.reshape(cap, n_ex, ff).transpose(1, 0, 2)[None, None]

    weight_grad = dot(scaled, rows, 0, 0)[None]
    return (layer_out, prob_grad, hidden_grad, weight_grad)


def solution(mesh):
    placed = (
        P(("dp", "expert"), None),
        P(("dp", "expert"), None),
        P("dp", "expert", None, None, None),
        P("expert", None, "dp"),
        P(("dp", "expert"), None),
    )
    return jax.shard_map(
        shards,
        mesh=mesh,
        in_specs=placed,
        out_specs=(
            P(("dp", "expert"), None),
            P(("dp", "expert"), None),
            P("dp", "expert", None, None, None),
            P("expert", None, "dp"),
        ),
        check_vma=False,
    )
```

time: 351 us -> 271 us (0.77)
  the two profiles are of different devices: /device:TPU:15 before, /device:TPU:0 now
where the time goes in v1:
time: 271 us
  waiting for transfers between devices  163 us (60%)
  matrix products  32.7 us (12%)
  blocking collectives  24.1 us (9%)
  starting transfers between devices  17.9 us (7%)
  between operations  14 us (5%)
  local copies, waits for them, and re-layouts  11 us (4%)
  other arithmetic  8.2 us (3%)
    reduce_scatter x1, waiting for transfers between devices, shards(): layer = lax.psum_scatter(part, 'expert', scatter_dimension=0, tiled=True)[0]  73.9 us
    all_gather x1, waiting for transfers between devices, shards(): grads = lax.all_gather(grads, 'expert', axis=0)  54 us
    dot_general x3, matrix products, dot(): lax.dot_general(a, b, (((ca,), (cb,)), ((), ())), preferred_element_type=...  24 us
    all_gather x1, waiting for transfers between devices, shards(): hidden = lax.all_gather(hidden, 'dp', axis=0)  13.9 us
    all_to_all x1, waiting for transfers between devices, shards(): spread = lax.all_to_all(spread.astype(jnp.bfloat16), 'dp', 0, 0, tiled=True)  11.4 us
    all_to_all x1, blocking collectives, shards(): grads = lax.all_to_all(grads, 'dp', 0, 0, tiled=True)  9.95 us
    all_to_all x1, blocking collectives, shards(): layer = lax.all_to_all(layer, 'dp', 0, 0, tiled=True)  9.62 us
    all_to_all x1, starting transfers between devices, shards(): mine = lax.all_to_all(table.T, 'expert', 0, 0, tiled=True)  7.39 us
  transfers between devices with their start and end apart: 7, of which 7 were waited for; matrix products, arithmetic and copies ran while one was open for 9% of the time, Pallas kernels for 0%

profile of v1, /device:TPU:0, one launch (start us, length us, event | category | flops | bytes accessed | tf_op | source)
XLA Modules:
  0.0 270.9 jit_solution(5161782539893964343)
XLA Ops:
  7.2 0.0 copy-start
  7.2 0.0 all-gather.5.cloned.1.call-start
  7.2 0.7 all-gather.5.cloned.1.call-update
  7.9 1.5 select_reduce_fusion.1
  9.4 7.4 %all-to-all-start = ((f32[16,1,48]{2,1,0:T(1,128)}), f32[16,1,48]{2,1,0:T(1,128)S(1)}, u32[]{:S(2)}, u32[]{:S(2)}) async-start(f32[16,1,48]{2,1,0:T(1,128)} %bitcast.2), calls=%async_computation | async-start | bytes 16384 | tf_op jit(solution)/shard_map/all_to_all | solution.py:23
  16.8 0.0 reduce-scatter.3.cloned.1.call-start
  16.9 0.0 copy-start.7
  16.9 0.9 and.40
  17.8 2.3 copy.50
  20.2 3.0 %all-to-all-done = f32[16,1,48]{2,1,0:T(1,128)S(1)} async-done(((f32[16,1,48]{2,1,0:T(1,128)}), f32[16,1,48]{2,1,0:T(1,128)S(1)}, u32[]{:S(2)}, u32[]{:S(2)}) %all-to-all-start) | async-done | bytes 3104 | tf_op jit(solution)/shard_map/all_to_all | solution.py:23
  23.2 4.5 %all-gather = f32[32,1,48]{2,1,0:T(1,128)S(1)} all-gather(f32[16,1,48]{2,1,0:T(1,128)S(1)} %all-to-all-done), channel_id=2, replica_groups=mesh['dp'=2,'expert'=16] {'dp'}, dimensions={0}, use_global_device_ids=true | all-gather | bytes 9216 | tf_op jit(solution)/shard_map/all_gather | solution.py:24
  27.7 0.2 fusion.15
  27.9 0.1 eq.52
  28.0 0.0 copy-start.5
  28.0 13.9 %all-gather.5.cloned.1.call-done = bf16[2,576,768]{2,1,0:T(8,128)(2,1)} async-done(((bf16[1,576,768]{2,1,0:T(8,128)(2,1)}), bf16[2,576,768]{2,1,0:T(8,128)(2,1)}) %all-gather.5.cloned.1.call-update) | async-done | bytes 1769488 | tf_op jit(solution)/shard_map/all_gather | solution.py:36
  41.9 3.8 %fusion.4 = bf16[2,768,768]{2,1,0:T(8,128)(2,1)S(1)} fusion(bf16[2,576,768]{2,1,0:T(8,128)(2,1)} %all-gather.5.cloned.1.call-done, s32[2,768]{1,0:T(2,128)S(1)} %eq.52, s32[576]{0:T(1024)S(1)} %add_select_fusion, pred[768,576]{0,1:T(8,128)(4,1)} %copy.50), kind=kOutput, calls=%fused_computation.10 | convolution fusion | flops 1360723968 | bytes 4579584 | tf_op jit(solution)/shard_map/ntr,nrf->ntf/dot_general | solution.py:43
  45.7 0.0 copy-done.7
  45.8 0.0 copy-done.5
  45.8 0.0 copy-start.1
  45.8 1.5 copy-done.1
  47.3 0.5 fusion.2
  47.7 0.0 copy-start.3
  47.7 0.0 copy-done
  47.7 7.0 %convolution_convert_fusion = bf16[1536,2048]{1,0:T(8,128)(2,1)} fusion(bf16[1536,768]{1,0:T(8,128)(2,1)S(1)} %bitcast.69, bf16[1,768,2048]{2,1,0:T(8,128)(2,1)S(1)} %copy-done), kind=kOutput, calls=%fused_computation | convolution fusion | flops 4834983936 | bytes 11796480 | tf_op jit(solution)/shard_map/dot_general | solution.py:8
  54.8 0.0 copy-done.3
  54.8 0.0 reduce-scatter.3.cloned.1.call-update
  54.8 0.0 all-gather.7.cloned.1.call-start
  54.8 1.3 reshape.101
  56.1 0.1 copy.54
  56.3 9.9 %all_to_all.36 = bf16[2,48,2048]{2,1,0:T(8,128)(2,1)} all-to-all(bf16[2,48,2048]{2,1,0:T(8,128)(2,1)S(1)} %copy.54), channel_id=1, replica_groups=mesh['dp'=2,'expert'=16] {'dp'}, dimensions={0} | all-to-all | bytes 786432 | tf_op jit(solution)/shard_map/all_to_all | solution.py:31
  66.2 0.0 all-gather.7.cloned.1.call-update
  66.2 0.0 reduce-scatter.5.cloned.1.call-start
  66.3 73.9 %reduce-scatter.3.cloned.1.call-done = bf16[1,2,48,2048]{3,2,1,0:T(8,128)(2,1)} async-done(((bf16[16,2,48,2048]{3,2,1,0:T(8,128)(2,1)}), bf16[1,2,48,2048]{3,2,1,0:T(8,128)(2,1)}) %reduce-scatter.3.cloned.1.call-update) | async-done | bytes 393232 | tf_op jit(solution)/shard_map/reduce_scatter | solution.py:50
  140.2 9.6 %all_to_all.37 = bf16[2,48,2048]{2,1,0:T(8,128)(2,1)S(1)} all-to-all(bf16[2,48,2048]{2,1,0:T(8,128)(2,1)} %bitcast.78), channel_id=1, replica_groups=mesh['dp'=2,'expert'=16] {'dp'}, dimensions={0} | all-to-all | bytes 786432 | tf_op jit(solution)/shard_map/all_to_all | solution.py:51
  149.8 54.0 %all-gather.7.cloned.1.call-done = bf16[32,48,2048]{2,1,0:T(8,128)(2,1)} async-done(((bf16[2,48,2048]{2,1,0:T(8,128)(2,1)}), bf16[32,48,2048]{2,1,0:T(8,128)(2,1)}) %all-gather.7.cloned.1.call-update) | async-done | bytes 6291472 | tf_op jit(solution)/shard_map/all_gather | solution.py:32
  203.8 0.0 copy-start.2
  203.8 7.3 %convolution_convert_fusion.1 = bf16[1536,768]{1,0:T(8,128)(2,1)S(1)} fusion(bf16[1536,2048]{1,0:T(8,128)(2,1)} %bitcast.84, bf16[1,768,2048]{2,1,0:T(8,128)(2,1)S(1)} %copy-done), kind=kOutput, calls=%fused_computation.11 | convolution fusion | flops 4833017856 | bytes 11796480 | tf_op jit(solution)/shard_map/dot_general | solution.py:8
  211.2 0.0 copy-done.2
  211.2 2.6 fusion.7
  213.8 0.0 copy-start.6
  213.8 0.0 copy-start.8
  213.8 0.6 copy.55
  214.4 0.0 reduce-scatter.5.cloned.1.call-update
  214.5 0.8 copy.58
  215.2 3.3 %copy.57 = bf16[2,16,48,768]{3,2,1,0:T(8,128)(2,1)} copy(bf16[2,16,48,768]{3,2,0,1:T(8,128)(2,1)} %get-tuple-element.6) | data formatting | bytes 4718592 | tf_op jit(solution)/shard_map/transpose | solution.py:61
  218.5 4.4 %reduce-scatter.5.cloned.1.call-done = f32[1,16,48]{2,1,0:T(8,128)} async-done(((f32[2,16,48]{2,1,0:T(8,128)}), f32[1,16,48]{2,1,0:T(8,128)}) %reduce-scatter.5.cloned.1.call-update) | async-done | bytes 3088 | tf_op jit(solution)/shard_map/reduce_scatter | solution.py:57
  223.0 5.6 %all-to-all-start.3 = ((f32[16,1,48]{2,1,0:T(1,128)}), f32[16,1,48]{2,1,0:T(1,128)S(1)}, u32[]{:S(2)}, u32[]{:S(2)}) async-start(f32[16,1,48]{2,1,0:T(1,128)} %bitcast.83), calls=%async_computation.5 | async-start | bytes 16384 | tf_op jit(solution)/shard_map/all_to_all | solution.py:58
  228.6 0.0 copy-done.6
  228.6 0.0 copy-done.8
  228.6 4.6 %fusion.14 = bf16[2,576,768]{2,1,0:T(8,128)(2,1)} fusion(bf16[2,768,768]{2,1,0:T(8,128)(2,1)} %bitcast.71, s32[2,768]{1,0:T(2,128)S(1)} %copy-done.6, s32[576]{0:T(1024)S(1)} %copy-done.8, pred[768,576]{0,1:T(8,128)(4,1)} %copy.50), kind=kOutput, calls=%fused_computation.21 | convolution fusion | flops 1361608704 | bytes 4579584 | tf_op jit(solution)/shard_map/ntr,ntf->nrf/dot_general | solution.py:63
  233.2 1.7 all-to-all-done.3
  235.0 4.8 %all-to-all-start.4 = ((bf16[2,576,768]{2,1,0:T(8,128)(2,1)}), bf16[2,576,768]{2,1,0:T(8,128)(2,1)}, u32[]{:S(2)}, u32[]{:S(2)}) async-start(bf16[2,576,768]{2,1,0:T(8,128)(2,1)} %fusion.14), calls=%async_computation.6 | async-start | bytes 3538944 | tf_op jit(solution)/shard_map/all_to_all | solution.py:64
  239.8 0.0 copy-start.4
  239.8 9.6 %convolution_bitcast_fusion = f32[1,768,2048]{2,1,0:T(8,128)} fusion(bf16[1536,768]{1,0:T(8,128)(2,1)} %bitcast.70, bf16[1536,2048]{1,0:T(8,128)(2,1)} %bitcast.85), kind=kOutput, calls=%fused_computation.7 | convolution fusion | flops 4831838208 | bytes 14942208 | tf_op jit(solution)/shard_map/dot_general | solution.py:8
  249.4 0.0 copy-done.4
  249.4 0.6 select_reduce_fusion
  250.0 11.4 %all-to-all-done.4 = bf16[2,576,768]{2,1,0:T(8,128)(2,1)} async-done(((bf16[2,576,768]{2,1,0:T(8,128)(2,1)}), bf16[2,576,768]{2,1,0:T(8,128)(2,1)}, u32[]{:S(2)}, u32[]{:S(2)}) %all-to-all-start.4) | async-done | bytes 1769504 | tf_op jit(solution)/shard_map/all_to_all | solution.py:64
  261.4 2.9 %reduce_sum.42 = bf16[576,768]{1,0:T(8,128)(2,1)} reduce(bf16[2,576,768]{2,1,0:T(8,128)(2,1)} %all-to-all-done.4, bf16[]{:T(256)} %constant.42.clone.1), dimensions={0}, to_apply=%region_5.6 | reduce | flops 442368 | bytes 2654210 | tf_op jit(solution)/shard_map/reduce_sum | solution.py:65
  (6 shorter events, 0.0 us)
Async XLA Ops:
  7.2 40.6 %copy-start = (bf16[1,768,2048]{2,1,0:T(8,128)(2,1)S(1)}, bf16[1,768,2048]{2,1,0:T(8,128)(2,1)}, u32[]{:S(2)}) copy-start(bf16[1,768,2048]{2,1,0:T(8,128)(2,1)} %param.8) | copy-start | bytes 9437188
  7.2 34.7 %all-gather.5.cloned.1.call-start = ((), (), s32[]{:S(2)}) async-start(), calls=%async_computation.7 | async-start | bytes 2654208 | tf_op jit(solution)/shard_map/all_gather | solution.py:36
  9.4 13.7 %all-to-all-start = ((f32[16,1,48]{2,1,0:T(1,128)}), f32[16,1,48]{2,1,0:T(1,128)S(1)}, u32[]{:S(2)}, u32[]{:S(2)}) async-start(f32[16,1,48]{2,1,0:T(1,128)} %bitcast.2), calls=%async_computation | async-start | bytes 16384 | tf_op jit(solution)/shard_map/all_to_all | solution.py:23
  16.8 123.3 %reduce-scatter.3.cloned.1.call-start = ((), (), s32[]{:S(2)}) async-start(), calls=%async_computation.8 | async-start | bytes 6684672 | tf_op jit(solution)/shard_map/reduce_scatter | solution.py:50
  16.9 28.8 %copy-start.7 = (s32[576]{0:T(1024)}, s32[576]{0:T(1024)S(1)}, u32[]{:S(2)}) copy-start(s32[576]{0:T(1024)S(1)} %add_select_fusion) | copy-start | bytes 6916
  28.0 17.8 %copy-start.5 = (s32[2,768]{1,0:T(2,128)}, s32[2,768]{1,0:T(2,128)S(1)}, u32[]{:S(2)}) copy-start(s32[2,768]{1,0:T(2,128)S(1)} %eq.52) | copy-start | bytes 18436
  45.8 1.5 copy-start.1
  47.7 7.0 %copy-start.3 = (bf16[16,2,48,768]{3,2,1,0:T(8,128)(2,1)}, bf16[16,2,48,768]{3,2,1,0:T(8,128)(2,1)S(1)}, u32[]{:S(2)}) copy-start(bf16[16,2,48,768]{3,2,1,0:T(8,128)(2,1)S(1)} %fusion.2) | copy-start | bytes 7077892
  54.8 149.0 %all-gather.7.cloned.1.call-start = ((), (), s32[]{:S(2)}) async-start(), calls=%async_computation.10 | async-start | bytes 6684672 | tf_op jit(solution)/shard_map/all_gather | solution.py:32
  66.2 156.7 %reduce-scatter.5.cloned.1.call-start = ((), (), s32[]{:S(2)}) async-start(), calls=%async_computation.9 | async-start | bytes 24576 | tf_op jit(solution)/shard_map/reduce_scatter | solution.py:57
  203.8 7.4 %copy-start.2 = (bf16[2,768,768]{2,1,0:T(8,128)(2,1)S(1)}, bf16[2,768,768]{2,1,0:T(8,128)(2,1)}, u32[]{:S(2)}) copy-start(bf16[2,768,768]{2,1,0:T(8,128)(2,1)} %copy-done.1) | copy-start | bytes 7077892
  213.8 14.8 %copy-start.6 = (s32[2,768]{1,0:T(2,128)S(1)}, s32[2,768]{1,0:T(2,128)}, u32[]{:S(2)}) copy-start(s32[2,768]{1,0:T(2,128)} %copy-done.5) | copy-start | bytes 18436
  213.8 14.8 %copy-start.8 = (s32[576]{0:T(1024)S(1)}, s32[576]{0:T(1024)}, u32[]{:S(2)}) copy-start(s32[576]{0:T(1024)} %copy-done.7) | copy-start | bytes 6916
  223.0 12.0 %all-to-all-start.3 = ((f32[16,1,48]{2,1,0:T(1,128)}), f32[16,1,48]{2,1,0:T(1,128)S(1)}, u32[]{:S(2)}, u32[]{:S(2)}) async-start(f32[16,1,48]{2,1,0:T(1,128)} %bitcast.83), calls=%async_computation.5 | async-start | bytes 16384 | tf_op jit(solution)/shard_map/all_to_all | solution.py:58
  235.0 26.4 %all-to-all-start.4 = ((bf16[2,576,768]{2,1,0:T(8,128)(2,1)}), bf16[2,576,768]{2,1,0:T(8,128)(2,1)}, u32[]{:S(2)}, u32[]{:S(2)}) async-start(bf16[2,576,768]{2,1,0:T(8,128)(2,1)} %fusion.14), calls=%async_computation.6 | async-start | bytes 3538944 | tf_op jit(solution)/shard_map/all_to_all | solution.py:64
  239.8 9.6 %copy-start.4 = (s32[48,8]{0,1:T(8,128)S(1)}, s32[48,8]{0,1:T(8,128)}, u32[]{:S(2)}) copy-start(s32[48,8]{0,1:T(8,128)} %param.5) | copy-start | bytes 4612
Sparse Core Ops, SparseCore 0:
  9.6 32.2 all-gather.4
  54.9 85.2 reduce-scatter.2
  142.7 61.0 all-gather.6
  214.6 8.3 reduce-scatter.4

commit v2 on v1

v2 whole, which is shorter than its diff:
```python
import jax
import jax.numpy as jnp
import numpy as np
from jax import lax
from jax.sharding import PartitionSpec as P


def dot(a, b, ca, cb):
    return lax.dot_general(a, b, (((ca,), (cb,)), ((), ())), preferred_element_type=jnp.float32)


def chip_ring(mesh):
    chips = mesh.shape["expert"] // 2
    devices = mesh.devices.reshape(mesh.shape["dp"], -1)
    if not hasattr(devices[0, 0], "coords"):
        return list(range(chips))
    at = [tuple(devices[0, 2 * chip].coords)[1:] for chip in range(chips)]
    rows = max(z for _, z in at) + 1
    cols = max(y for y, _ in at) + 1
    if rows * cols != chips or rows % 2:
        return list(range(chips))
    walk = [(0, z) for z in range(rows)]
    for step, z in enumerate(reversed(range(rows))):
        span = range(1, cols)
        walk += [(y, z) for y in (span if step % 2 == 0 else reversed(span))]
    return [at.index(place) for place in walk]


def body(ring):
    chips = len(ring)
    half = chips // 2
    offsets = [0]
    for step in range(1, half):
        offsets += [-step, step]
    offsets.append(half)
    lookup = np.zeros((chips,), np.int32)
    lookup[np.asarray(ring)] = np.arange(chips)

    def along(step):
        pairs = []
        for at in range(chips):
            for core in range(2):
                pairs.append((2 * ring[at] + core, 2 * ring[(at + step) % chips] + core))
        return pairs

    forward, backward = along(1), along(-1)
    sibling = [(e, e ^ 1) for e in range(2 * chips)]

    def shards(expert_ids, route_probs, expert_hidden, down_weight, out_grad):
        tok, top = expert_ids.shape
        n_dp = lax.axis_size("dp")
        n_ex = lax.axis_size("expert")
        cap = expert_hidden.shape[3]
        slots = cap * n_ex
        ff = down_weight.shape[1]
        width = down_weight.shape[2]
        weight = down_weight[0]
        replica = lax.axis_index("dp")
        expert = lax.axis_index("expert")
        core = expert % 2
        place = jnp.asarray(lookup)[expert // 2]
        groups = [list(range(n_dp // 2)), list(range(n_dp // 2, n_dp))]
        per = n_dp // 2

        def shift(value, step):
            return lax.ppermute(value, "dp", [(i, (i + step) % n_dp) for i in range(n_dp)])

        def ring_send(value, step):
            return lax.ppermute(value, "expert", forward if step > 0 else backward)

        def swap(value):
            return lax.ppermute(value, "expert", sibling)

        table = jnp.asarray(np.asarray(ring, np.int32))
        order = []
        for off in offsets:
            for other in range(2):
                order.append(2 * table[(place + off) % chips] + (core ^ other))
        order = jnp.stack(order)

        facts = jnp.concatenate([expert_ids.astype(jnp.float32), route_probs], axis=1).T
        facts = lax.all_gather(facts, ("dp", "expert"), axis=0)
        names = facts[:, :top] == expert.astype(jnp.float32)
        probs = jnp.sum(jnp.where(names, facts[:, top:], 0.0), axis=1).reshape(n_dp, n_ex, tok)
        taken = (probs > 0.0).astype(jnp.float32)
        earlier = jnp.tril(jnp.ones((tok, tok), jnp.float32), -1)
        position = jnp.einsum("nst,ut->nsu", taken, earlier).astype(jnp.int32)
        position = jnp.where(probs > 0.0, position, -1)

        shard_of = lambda d: lax.dynamic_slice_in_dim(
            out_grad, ((replica + d) % n_dp) * width, width, axis=1
        )
        exchanged = [shard_of(0)] + [shift(shard_of(d), d) for d in range(1, n_dp)]
        seed = [jnp.stack([exchanged[d] for d in group]) for group in groups]
        blocks = {0: list(seed)}
        for step in range(1, half):
            blocks[-step] = [ring_send(blocks[1 - step][g], 1) for g in range(2)]
            blocks[step] = [ring_send(blocks[step - 1][g], -1) for g in range(2)]
        blocks[half] = [ring_send(blocks[1 - half][0], 1), ring_send(blocks[half - 1][1], -1)]

        hidden = expert_hidden[0, 0].transpose(1, 0, 2).reshape(slots, ff)
        hiddens = [hidden] + [shift(hidden, d) for d in range(1, n_dp)]

        slot_c = jnp.arange(slots, dtype=jnp.int32) // n_ex
        slot_s = jnp.arange(slots, dtype=jnp.int32) % n_ex
        picks, helds, scaleds, prob_rows, parts = [], [], [], [], []
        for d in range(n_dp):
            at = (replica - d) % n_dp
            position_d = lax.dynamic_index_in_dim(position, at, 0, keepdims=False)[order]
            prob_d = lax.dynamic_index_in_dim(probs, at, 0, keepdims=False)[order]
            pick = (position_d[:, :, None] == slot_c) & (order[:, None, None] == slot_s)
            pick = pick.reshape(n_ex * tok, slots).astype(jnp.bfloat16)
            held = dot(pick, hiddens[d], 1, 0)
            prob_row = prob_d.reshape(n_ex * tok, 1)
            scaled = (held * prob_row).astype(jnp.bfloat16)
            part = dot(scaled, weight, 1, 0).astype(jnp.bfloat16)
            picks.append(pick)
            helds.append(held.astype(jnp.bfloat16))
            scaleds.append(scaled)
            prob_rows.append(prob_row)
            parts.append(part.reshape(chips, 2, tok, width))

        own = [jnp.stack([parts[d][:, 0] for d in group], axis=1) for group in groups]
        other = [swap(jnp.stack([parts[d][:, 1] for d in group], axis=1)) for group in groups]

        def term(off, g):
            index = offsets.index(off)
            return own[g][index].astype(jnp.float32) + other[g][index].astype(jnp.float32)

        arrived = {}
        for g in range(2):
            for direction in (1, -1):
                first = half if (direction == 1) == (g == 0) else half - 1
                carry = None
                for hop in range(first, 0, -1):
                    off = half if hop == half else hop * direction
                    value = term(off, g)
                    if carry is not None:
                        value = value + carry.astype(jnp.float32)
                    carry = ring_send(value.astype(jnp.bfloat16), direction)
                arrived[g, direction] = carry
        layer_out = jnp.zeros((tok, n_dp * width), jnp.bfloat16)
        for g, group in enumerate(groups):
            total = term(0, g) + arrived[g, 1].astype(jnp.float32)
            total = (total + arrived[g, -1].astype(jnp.float32)).astype(jnp.bfloat16)
            for i, d in enumerate(group):
                piece = total[i] if d == 0 else shift(total[i], -d)
                layer_out = lax.dynamic_update_slice_in_dim(
                    layer_out, piece, ((replica + d) % n_dp) * width, axis=1
                )

        others = {off: [swap(value) for value in blocks[off]] for off in offsets}
        weight_sum = None
        spreads, inners = [], []
        for d in range(n_dp):
            g, i = divmod(d, per)
            rows = jnp.concatenate(
                [x for off in offsets for x in (blocks[off][g][i], others[off][g][i])], axis=0
            )
            back = dot(rows, weight, 1, 1)
            inners.append(jnp.sum(back * helds[d].astype(jnp.float32), axis=1))
            spread = (back * prob_rows[d]).astype(jnp.bfloat16)
            spreads.append(dot(picks[d], spread, 0, 0).astype(jnp.bfloat16))
            more = dot(scaleds[d], rows, 0, 0)
            weight_sum = more if weight_sum is None else weight_sum + more
        hidden_sum = spreads[0].astype(jnp.float32)
        for d in range(1, n_dp):
            hidden_sum = hidden_sum + shift(spreads[d], -d).astype(jnp.float32)
        hidden_grad = hidden_sum.astype(jnp.bfloat16).reshape(cap, n_ex, ff).transpose(1, 0, 2)

        inverse = jnp.argsort(order)
        inner = jnp.stack(inners)[(replica - jnp.arange(n_dp)) % n_dp].reshape(n_dp, n_ex, tok)
        inner = inner[:, inverse].reshape(n_dp * n_ex, tok)
        inner = lax.all_to_all(inner, ("dp", "expert"), 0, 0, tiled=True)
        inner = jnp.sum(inner.reshape(n_dp, n_ex, tok), axis=0)
        mine = expert_ids[:, :, None] == jnp.arange(n_ex, dtype=jnp.int32)
        prob_grad = jnp.sum(jnp.where(mine, inner.T[:, None, :], 0.0), axis=2)
        return (layer_out, prob_grad, hidden_grad[None, None], weight_sum[None])

    return shards


def solution(mesh):
    placed = (
        P(("dp", "expert"), None),
        P(("dp", "expert"), None),
        P("dp", "expert", None, None, None),
        P("expert", None, "dp"),
        P(("dp", "expert"), None),
    )
    return jax.shard_map(
        body(chip_ring(mesh)),
        mesh=mesh,
        in_specs=placed,
        out_specs=(
            P(("dp", "expert"), None),
            P(("dp", "expert"), None),
            P("dp", "expert", None, None, None),
            P("expert", None, "dp"),
        ),
        check_vma=False,
    )
```

time: 271 us -> 231 us (0.85)
  waiting for transfers between devices: 163 us -> 42.5 us
  starting transfers between devices: 17.9 us -> 42.2 us
  blocking collectives: 24.1 us -> 43 us
  local copies, waits for them, and re-layouts: 11 us -> 29 us
  other arithmetic: 8.2 us -> 19.8 us
  matrix products: 32.7 us -> 40.5 us
    reduce_scatter x2 -> x0, waiting for transfers between devices: 78.3 us -> none  [the longest x1 73.9 us: shards(): layer = lax.psum_scatter(part, 'expert', scatter_dimension=0, tiled=True)[0]]
    all_gather x2 -> x0, waiting for transfers between devices: 67.9 us -> none  [the longest x1 54 us: shards(): grads = lax.all_gather(grads, 'expert', axis=0)]
    ppermute x0 -> x50, waiting for transfers between devices: none -> 42.5 us  [the longest x28 38.2 us: ring_send(): return lax.ppermute(value, 'expert', forward if step > 0 else backward)]
    ppermute x0 -> x50, starting transfers between devices: none -> 39.6 us  [the longest x28 31.1 us: ring_send(): return lax.ppermute(value, 'expert', forward if step > 0 else backward)]
    all_gather x1, blocking collectives: 4.5 us -> 43 us  [shards(): facts = lax.all_gather(facts, ('dp', 'expert'), axis=0)]
    all_to_all x2 -> x0, blocking collectives: 19.6 us -> none  [the longest x1 9.95 us: shards(): grads = lax.all_to_all(grads, 'dp', 0, 0, tiled=True)]
    dot_general x3 -> x10, matrix products: 24 us -> 40.4 us  [dot(): lax.dot_general(a, b, (((ca,), (cb,)), ((), ())), preferred_element_type=...]
    all_to_all x3 -> x1, waiting for transfers between devices: 16.1 us -> 0.01 us  [shards(): inner = lax.all_to_all(inner, ('dp', 'expert'), 0, 0, tiled=True)]
  transfers between devices with their start and end apart: 7 -> 51, of which waited for: 7 -> 21; matrix products, arithmetic and copies ran while one was open for 9% -> 36% of each run, Pallas kernels for 0% -> 0%
where the time goes in v2:
time: 231 us; the launch traced here: 230 us
  blocking collectives  43 us (19%)
  waiting for transfers between devices  42.5 us (18%)
  starting transfers between devices  42.2 us (18%)
  matrix products  40.5 us (18%)
  local copies, waits for them, and re-layouts  29 us (13%)
  other arithmetic  19.8 us (9%)
  between operations  12.9 us (6%)
    all_gather x1, blocking collectives, shards(): facts = lax.all_gather(facts, ('dp', 'expert'), axis=0)  43 us
    dot_general x10, matrix products, dot(): lax.dot_general(a, b, (((ca,), (cb,)), ((), ())), preferred_element_type=...  40.4 us
    ppermute x28, waiting for transfers between devices, ring_send(): return lax.ppermute(value, 'expert', forward if step > 0 else backward)  38.2 us
    ppermute x28, starting transfers between devices, ring_send(): return lax.ppermute(value, 'expert', forward if step > 0 else backward)  31.1 us
    unnamed x53, local copies, waits for them, and re-layouts  16.8 us
    convert_element_type x10, other arithmetic, shards(): carry = ring_send(value.astype(jnp.bfloat16), direction)  12.1 us
  transfers between devices with their start and end apart: 51, of which 21 were waited for; matrix products, arithmetic and copies ran while one was open for 36% of the time, Pallas kernels for 0%

profile of v2, /device:TPU:0, one launch (start us, length us, event | category | flops | bytes accessed | tf_op | source)
XLA Modules:
  0.0 229.8 jit_solution(17548578107747334766)
XLA Ops:
  0.7 2.0 dynamic-slice_bitcast_fusion
  3.2 2.6 %collective-permute-start.19 = (bf16[1,48,2048]{2,1,0:T(8,128)(2,1)}, bf16[1,48,2048]{2,1,0:T(8,128)(2,1)}, u32[]{:S(2)}, u32[]{:S(2)}) collective-permute-start(bf16[1,48,2048]{2,1,0:T(8,128)(2,1)} %get-tuple-element.14), channel_id=1, source_target_pairs={{0,4},{1,5},{4,8},{5,9},{8,12},{9,13},{12,14},{13,15},{14,10},{15,... | collective-permute-start | bytes 589832 | tf_op jit(solution)/shard_map/ppermute | solution.py:69
  5.7 1.9 collective-permute-start.8
  7.8 1.2 dynamic_slice.56
  15.6 1.7 fusion.53
  23.8 43.0 %all-gather = f32[512,48]{1,0:T(8,128)S(1)} all-gather(f32[16,48]{1,0:T(8,128)S(1)} %maximum_bitcast_fusion), channel_id=2, replica_groups=mesh['dp'=2,'expert'=16] {'dp','expert'}, dimensions={0}, use_global_device_ids=true | all-gather | bytes 101376 | tf_op jit(solution)/shard_map/all_gather | solution.py:82
  68.4 3.7 %fusion.54 = f32[768,768]{0,1:T(8,128)} fusion(pred[768,576]{1,0:T(8,128)(4,1)S(1)} %bitcast.261, bf16[576,768]{1,0:T(8,128)(2,1)} %bitcast.268), kind=kOutput, calls=%fused_computation.154 | convolution fusion | flops 679477248 | bytes 3686400 | tf_op jit(solution)/shard_map/dot_general | solution.py:9
  72.8 4.5 %convolution_convert_fusion.1 = bf16[768,2048]{1,0:T(8,128)(2,1)S(1)} fusion(bf16[1,768,2048]{2,1,0:T(8,128)(2,1)S(1)} %copy-done, f32[768,768]{0,1:T(8,128)} %fusion.54, f32[768]{0:T(1024)S(1)} %mul.118), kind=kOutput, calls=%fused_computation.8 | convolution fusion | flops 2418671616 | bytes 8653824 | tf_op jit(solution)/shard_map/dot_general | solution.py:9
  77.3 1.6 copy-done.6
  79.0 1.3 slice.177
  81.5 1.3 sort.17
  82.8 1.6 fusion.6
  85.3 1.6 bitcast_dynamic-update-slice_fusion.29
  86.9 1.6 bitcast_dynamic-update-slice_fusion.28
  90.2 2.0 collective-permute-start.37
  93.0 3.8 %collective-permute-done.35 = bf16[1,48,2048]{2,1,0:T(8,128)(2,1)S(1)} collective-permute-done((bf16[1,48,2048]{2,1,0:T(8,128)(2,1)}, bf16[1,48,2048]{2,1,0:T(8,128)(2,1)S(1)}, u32[]{:S(2)}, u32[]{:S(2)}) %collective-permute-start.35) | collective-permute-done | bytes 196640 | tf_op jit(solution)/shard_map/ppermute | solution.py:69
  97.0 1.8 collective-permute-start.25
  99.5 3.6 %collective-permute-done.23 = bf16[1,48,2048]{2,1,0:T(8,128)(2,1)S(1)} collective-permute-done((bf16[1,48,2048]{2,1,0:T(8,128)(2,1)}, bf16[1,48,2048]{2,1,0:T(8,128)(2,1)S(1)}, u32[]{:S(2)}, u32[]{:S(2)}) %collective-permute-start.23) | collective-permute-done | bytes 196640 | tf_op jit(solution)/shard_map/ppermute | solution.py:69
  106.7 1.4 collective-permute-start.41
  108.8 3.7 %collective-permute-done.39 = bf16[1,48,2048]{2,1,0:T(8,128)(2,1)S(1)} collective-permute-done((bf16[1,48,2048]{2,1,0:T(8,128)(2,1)S(1)}, bf16[1,48,2048]{2,1,0:T(8,128)(2,1)S(1)}, u32[]{:S(2)}, u32[]{:S(2)}) %collective-permute-start.39) | collective-permute-done | bytes 196640 | tf_op jit(solution)/shard_map/ppermute | solution.py:69
  113.2 1.5 collective-permute-start.29
  115.3 3.6 %collective-permute-done.27 = bf16[1,48,2048]{2,1,0:T(8,128)(2,1)S(1)} collective-permute-done((bf16[1,48,2048]{2,1,0:T(8,128)(2,1)S(1)}, bf16[1,48,2048]{2,1,0:T(8,128)(2,1)S(1)}, u32[]{:S(2)}, u32[]{:S(2)}) %collective-permute-start.27) | collective-permute-done | bytes 196640 | tf_op jit(solution)/shard_map/ppermute | solution.py:69
  122.5 1.4 collective-permute-start.45
  124.6 3.7 %collective-permute-done.43 = bf16[1,48,2048]{2,1,0:T(8,128)(2,1)S(1)} collective-permute-done((bf16[1,48,2048]{2,1,0:T(8,128)(2,1)S(1)}, bf16[1,48,2048]{2,1,0:T(8,128)(2,1)S(1)}, u32[]{:S(2)}, u32[]{:S(2)}) %collective-permute-start.43) | collective-permute-done | bytes 196640 | tf_op jit(solution)/shard_map/ppermute | solution.py:69
  130.6 4.1 %collective-permute-done.31 = bf16[1,48,2048]{2,1,0:T(8,128)(2,1)S(1)} collective-permute-done((bf16[1,48,2048]{2,1,0:T(8,128)(2,1)S(1)}, bf16[1,48,2048]{2,1,0:T(8,128)(2,1)S(1)}, u32[]{:S(2)}, u32[]{:S(2)}) %collective-permute-start.31) | collective-permute-done | bytes 196640 | tf_op jit(solution)/shard_map/ppermute | solution.py:69
  135.4 2.3 %fusion.55 = f32[768,768]{0,1:T(8,128)S(1)} fusion(pred[768,576]{1,0:T(32,128)(4,1)S(1)} %get-tuple-element.22, bf16[576,768]{1,0:T(8,128)(2,1)} %collective-permute-done.8), kind=kOutput, calls=%fused_computation.155 | convolution fusion | flops 679477248 | bytes 3686400 | tf_op jit(solution)/shard_map/dot_general | solution.py:9
  137.7 2.9 %convolution_convert_fusion = bf16[768,2048]{1,0:T(8,128)(2,1)S(1)} fusion(bf16[1,768,2048]{2,1,0:T(8,128)(2,1)S(1)} %copy-done, f32[768,768]{0,1:T(8,128)S(1)} %fusion.55, f32[768]{0:T(1024)S(1)} %mul.122), kind=kOutput, calls=%fused_computation.7 | convolution fusion | flops 2418671616 | bytes 8653824 | tf_op jit(solution)/shard_map/dot_general | solution.py:9
  140.7 1.3 slice.194
  142.5 1.8 copy-done.2
  144.3 4.1 %multiply_reduce_fusion.1 = (f32[768]{0:T(1024)S(1)}, f32[768,768]{0,1:T(8,128)}) fusion(f32[768,768]{0,1:T(8,128)S(1)} %copy-done.8, bf16[768,2048]{1,0:T(8,128)(2,1)S(1)} %bitcast_dynamic-update-slice_fusion.15, bf16[1,768,2048]{2,1,0:T(8,128)(2,1)S(1)} %copy-done), kind=kOutput, calls=%fused_computation.20 | convolution fusion | flops 2418277632 | bytes 11013120 | tf_op jit(solution)/shard_map/dot_general | solution.py:9
  150.1 4.0 %multiply_reduce_fusion = (f32[768]{0:T(1024)S(1)}, f32[768,768]{0,1:T(8,128)}) fusion(f32[768,768]{0,1:T(8,128)S(1)} %fusion.55, bf16[768,2048]{1,0:T(8,128)(2,1)S(1)} %bitcast_dynamic-update-slice_fusion, bf16[1,768,2048]{2,1,0:T(8,128)(2,1)S(1)} %copy-done), kind=kOutput, calls=%fused_computation.19 | convolution fusion | flops 2418277632 | bytes 11013120 | tf_op jit(solution)/shard_map/dot_general | solution.py:9
  154.1 4.4 %fusion.11 = f32[768,2048]{1,0:T(8,128)} fusion(bf16[768,2048]{1,0:T(8,128)(2,1)S(1)} %bitcast_dynamic-update-slice_fusion, f32[768,768]{0,1:T(8,128)S(1)} %fusion.55, f32[768]{0:T(1024)S(1)} %mul.122), kind=kOutput, calls=%fused_computation.33 | convolution fusion | flops 2417098752 | bytes 11799552 | tf_op jit(solution)/shard_map/dot_general | solution.py:9
  160.5 2.5 %all-to-all-start = ((f32[32,1,48]{2,1,0:T(1,128)}), f32[32,1,48]{2,1,0:T(1,128)S(1)}, u32[]{:S(2)}, u32[]{:S(2)}) async-start(f32[32,1,48]{2,1,0:T(1,128)} %bitcast.113), calls=%async_computation | async-start | bytes 32768 | tf_op jit(solution)/shard_map/all_to_all | solution.py:174
  163.0 4.0 %convolution_convert_fusion.2 = bf16[576,768]{1,0:T(8,128)(2,1)} fusion(f32[768,768]{0,1:T(8,128)} %get-tuple-element.32, f32[768]{0:T(1024)S(1)} %mul.122, pred[768,576]{1,0:T(32,128)(4,1)} %copy-done.9), kind=kOutput, calls=%fused_computation.26 | convolution fusion | flops 681541632 | bytes 3689472 | tf_op jit(solution)/shard_map/dot_general | solution.py:9
  167.0 1.7 collective-permute-start.49
  168.7 7.2 %add_bitcast_fusion = f32[1,768,2048]{2,1,0:T(8,128)} fusion(f32[768,2048]{1,0:T(8,128)} %fusion.11, bf16[768,2048]{1,0:T(8,128)(2,1)S(1)} %copy-done.4, f32[768,768]{0,1:T(8,128)} %fusion.54, f32[768]{0:T(1024)S(1)} %mul.118), kind=kOutput, calls=%fused_computation.6 | convolution fusion | flops 2418671616 | bytes 18091008 | tf_op jit(solution)/shard_map/dot_general | solution.py:9
  176.5 1.5 fusion.26
  178.0 1.6 collective-permute-start.1
  180.1 1.3 fusion.28
  181.4 1.6 collective-permute-start.10
  182.9 2.9 %collective-permute-done.1 = bf16[1,48,2048]{2,1,0:T(8,128)(2,1)S(1)} collective-permute-done((bf16[1,48,2048]{2,1,0:T(8,128)(2,1)S(1)}, bf16[1,48,2048]{2,1,0:T(8,128)(2,1)S(1)}, u32[]{:S(2)}, u32[]{:S(2)}) %collective-permute-start.1) | collective-permute-done | bytes 196640 | tf_op jit(solution)/shard_map/ppermute | solution.py:69
  185.8 1.1 fusion.21
  186.9 1.6 collective-permute-start.2
  191.1 1.6 collective-permute-start.11
  192.7 1.8 collective-permute-done.2
  194.5 1.1 fusion.22
  195.6 1.8 collective-permute-start.3
  197.4 1.7 collective-permute-done.11
  199.0 1.4 fusion.16
  200.4 1.5 collective-permute-start.14
  201.9 3.1 %add_convert_fusion = bf16[576,768]{1,0:T(8,128)(2,1)} fusion(bf16[576,768]{1,0:T(8,128)(2,1)} %collective-permute-done.49, bf16[768,576]{1,0:T(8,128)(2,1)S(1)} %copy-done.1, f32[768,768]{0,1:T(8,128)S(1)} %copy-done.7, f32[768]{0:T(1024)S(1)} %mul.118), kind=kOutput, calls=%fused_computation.25 | convolution fusion | flops 682868736 | bytes 5016576 | tf_op jit(solution)/shard_map/dot_general | solution.py:9
  205.1 1.7 collective-permute-done.14
  207.8 1.5 collective-permute-start.15
  209.3 1.4 fusion.23
  210.7 1.6 collective-permute-start.6
  213.4 2.0 collective-permute-done.15
  216.5 1.5 collective-permute-start.16
  217.9 1.7 collective-permute-done.6
  219.6 1.1 fusion.20
  220.7 1.5 collective-permute-start.7
  222.2 1.1 fusion.32
  223.9 2.5 %collective-permute-done.7 = bf16[1,48,2048]{2,1,0:T(8,128)(2,1)S(1)} collective-permute-done((bf16[1,48,2048]{2,1,0:T(8,128)(2,1)S(1)}, bf16[1,48,2048]{2,1,0:T(8,128)(2,1)S(1)}, u32[]{:S(2)}, u32[]{:S(2)}) %collective-permute-start.7) | collective-permute-done | bytes 196640 | tf_op jit(solution)/shard_map/ppermute | solution.py:69
  226.5 1.1 fusion.31
  227.6 1.5 collective-permute-done.17
  (162 shorter events, 35.2 us)
Async XLA Ops:
  0.6 72.2 %copy-start = (bf16[1,768,2048]{2,1,0:T(8,128)(2,1)S(1)}, bf16[1,768,2048]{2,1,0:T(8,128)(2,1)}, u32[]{:S(2)}) copy-start(bf16[1,768,2048]{2,1,0:T(8,128)(2,1)} %param.10) | copy-start | bytes 9437188
  2.7 82.1 %collective-permute-start.18 = (bf16[1,48,2048]{2,1,0:T(8,128)(2,1)}, bf16[1,48,2048]{2,1,0:T(8,128)(2,1)}, u32[]{:S(2)}, u32[]{:S(2)}) collective-permute-start(bf16[1,48,2048]{2,1,0:T(8,128)(2,1)} %get-tuple-element.14), channel_id=1, source_target_pairs={{0,1},{1,0},{2,3},{3,2},{4,5},{5,4},{6,7},{7,6},{8,9},{9,8},{10,11... | collective-permute-start | bytes 589832 | tf_op jit(solution)/shard_map/ppermute | solution.py:72
  3.2 81.8 %collective-permute-start.19 = (bf16[1,48,2048]{2,1,0:T(8,128)(2,1)}, bf16[1,48,2048]{2,1,0:T(8,128)(2,1)}, u32[]{:S(2)}, u32[]{:S(2)}) collective-permute-start(bf16[1,48,2048]{2,1,0:T(8,128)(2,1)} %get-tuple-element.14), channel_id=1, source_target_pairs={{0,4},{1,5},{4,8},{5,9},{8,12},{9,13},{12,14},{13,15},{14,10},{15,... | collective-permute-start | bytes 589832 | tf_op jit(solution)/shard_map/ppermute | solution.py:69
  5.7 84.5 %collective-permute-start.21 = (bf16[1,48,2048]{2,1,0:T(8,128)(2,1)}, bf16[1,48,2048]{2,1,0:T(8,128)(2,1)S(1)}, u32[]{:S(2)}, u32[]{:S(2)}) collective-permute-start(bf16[1,48,2048]{2,1,0:T(8,128)(2,1)} %get-tuple-element.14), channel_id=1, source_target_pairs={{0,2},{1,3},{4,0},{5,1},{8,4},{9,5},{12,8},{13,9},{14,12},{15,13},... | collective-permute-start | bytes 589832 | tf_op jit(solution)/shard_map/ppermute | solution.py:69
  5.7 129.7 %collective-permute-start.8 = (bf16[576,768]{1,0:T(8,128)(2,1)}, bf16[576,768]{1,0:T(8,128)(2,1)}, u32[]{:S(2)}, u32[]{:S(2)}) collective-permute-start(bf16[576,768]{1,0:T(8,128)(2,1)} %bitcast.267), channel_id=1, source_target_pairs={{0,16},{16,0},{1,17},{17,1},{2,18},{18,2},{3,19},{19,3},{4,20},{20... | collective-permute-start | bytes 2654216 | tf_op jit(solution)/shard_map/ppermute | solution.py:66
  7.7 76.7 %collective-permute-start.33 = (bf16[48,2048]{1,0:T(8,128)(2,1)}, bf16[48,2048]{1,0:T(8,128)(2,1)}, u32[]{:S(2)}, u32[]{:S(2)}) collective-permute-start(bf16[48,2048]{1,0:T(8,128)(2,1)} %get-tuple-element.16), channel_id=1, source_target_pairs={{0,16},{16,0},{1,17},{17,1},{2,18},{18,2},{3,19},{19,3},{4,20},{20... | collective-permute-start | bytes 589832 | tf_op jit(solution)/shard_map/ppermute | solution.py:66
  77.3 1.6 copy-start.6
  84.3 51.1 %copy-start.9 = (pred[768,576]{1,0:T(32,128)(4,1)}, pred[768,576]{1,0:T(32,128)(4,1)S(1)}, u32[]{:S(2)}) copy-start(pred[768,576]{1,0:T(32,128)(4,1)S(1)} %get-tuple-element.22) | copy-start | bytes 1327108
  84.4 92.2 %collective-permute-start = (bf16[8,1,48,2048]{3,2,1,0:T(8,128)(2,1)}, bf16[8,1,48,2048]{3,2,1,0:T(8,128)(2,1)}, u32[]{:S(2)}, u32[]{:S(2)}) collective-permute-start(bf16[8,1,48,2048]{3,2,1,0:T(8,128)(2,1)} %slice.177), channel_id=1, source_target_pairs={{0,1},{1,0},{2,3},{3,2},{4,5},{5,4},{6,7},{7,6},{8,9},{9,8},{10,11... | collective-permute-start | bytes 4718600 | tf_op jit(solution)/shard_map/ppermute | solution.py:72
  84.8 8.2 %collective-permute-start.34 = (bf16[1,48,2048]{2,1,0:T(8,128)(2,1)}, bf16[1,48,2048]{2,1,0:T(8,128)(2,1)S(1)}, u32[]{:S(2)}, u32[]{:S(2)}) collective-permute-start(bf16[1,48,2048]{2,1,0:T(8,128)(2,1)} %bitcast.94), channel_id=1, source_target_pairs={{0,1},{1,0},{2,3},{3,2},{4,5},{5,4},{6,7},{7,6},{8,9},{9,8},{10,11... | collective-permute-start | bytes 589832 | tf_op jit(solution)/shard_map/ppermute | solution.py:72
  85.0 4.5 %collective-permute-start.20 = (bf16[1,48,2048]{2,1,0:T(8,128)(2,1)}, bf16[1,48,2048]{2,1,0:T(8,128)(2,1)S(1)}, u32[]{:S(2)}, u32[]{:S(2)}) collective-permute-start(bf16[1,48,2048]{2,1,0:T(8,128)(2,1)} %collective-permute-done.19), channel_id=1, source_target_pairs={{0,1},{1,0},{2,3},{3,2},{4,5},{5,4},{6,7},{7,6},{8,9},{9,8},{10,11... | collective-permute-start | bytes 589832 | tf_op jit(solution)/shard_map/ppermute | solution.py:72
  89.5 7.2 %collective-permute-start.35 = (bf16[1,48,2048]{2,1,0:T(8,128)(2,1)}, bf16[1,48,2048]{2,1,0:T(8,128)(2,1)S(1)}, u32[]{:S(2)}, u32[]{:S(2)}) collective-permute-start(bf16[1,48,2048]{2,1,0:T(8,128)(2,1)} %bitcast.94), channel_id=1, source_target_pairs={{0,4},{1,5},{4,8},{5,9},{8,12},{9,13},{12,14},{13,15},{14,10},{15,... | collective-permute-start | bytes 589832 | tf_op jit(solution)/shard_map/ppermute | solution.py:69
  90.2 13.5 %collective-permute-start.37 = (bf16[1,48,2048]{2,1,0:T(8,128)(2,1)}, bf16[1,48,2048]{2,1,0:T(8,128)(2,1)S(1)}, u32[]{:S(2)}, u32[]{:S(2)}) collective-permute-start(bf16[1,48,2048]{2,1,0:T(8,128)(2,1)} %bitcast.94), channel_id=1, source_target_pairs={{0,2},{1,3},{4,0},{5,1},{8,4},{9,5},{12,8},{13,9},{14,12},{15,13},... | collective-permute-start | bytes 589832 | tf_op jit(solution)/shard_map/ppermute | solution.py:69
  93.0 4.1 %collective-permute-start.22 = (bf16[1,48,2048]{2,1,0:T(8,128)(2,1)S(1)}, bf16[1,48,2048]{2,1,0:T(8,128)(2,1)S(1)}, u32[]{:S(2)}, u32[]{:S(2)}) collective-permute-start(bf16[1,48,2048]{2,1,0:T(8,128)(2,1)S(1)} %collective-permute-done.21), channel_id=1, source_target_pairs={{0,1},{1,0},{2,3},{3,2},{4,5},{5,4},{6,7},{7,6},{8,9},{9,8},{10,11... | collective-permute-start | bytes 589832 | tf_op jit(solution)/shard_map/ppermute | solution.py:72
  96.7 6.4 %collective-permute-start.23 = (bf16[1,48,2048]{2,1,0:T(8,128)(2,1)}, bf16[1,48,2048]{2,1,0:T(8,128)(2,1)S(1)}, u32[]{:S(2)}, u32[]{:S(2)}) collective-permute-start(bf16[1,48,2048]{2,1,0:T(8,128)(2,1)} %collective-permute-done.19), channel_id=1, source_target_pairs={{0,4},{1,5},{4,8},{5,9},{8,12},{9,13},{12,14},{13,15},{14,10},{15,... | collective-permute-start | bytes 589832 | tf_op jit(solution)/shard_map/ppermute | solution.py:69
  97.0 9.6 %collective-permute-start.25 = (bf16[1,48,2048]{2,1,0:T(8,128)(2,1)S(1)}, bf16[1,48,2048]{2,1,0:T(8,128)(2,1)S(1)}, u32[]{:S(2)}, u32[]{:S(2)}) collective-permute-start(bf16[1,48,2048]{2,1,0:T(8,128)(2,1)S(1)} %collective-permute-done.21), channel_id=1, source_target_pairs={{0,2},{1,3},{4,0},{5,1},{8,4},{9,5},{12,8},{13,9},{14,12},{15,13},... | collective-permute-start | bytes 589832 | tf_op jit(solution)/shard_map/ppermute | solution.py:69
  103.1 1.4 collective-permute-start.36
  103.8 1.6 collective-permute-start.24
  104.5 4.3 %collective-permute-start.38 = (bf16[1,48,2048]{2,1,0:T(8,128)(2,1)S(1)}, bf16[1,48,2048]{2,1,0:T(8,128)(2,1)S(1)}, u32[]{:S(2)}, u32[]{:S(2)}) collective-permute-start(bf16[1,48,2048]{2,1,0:T(8,128)(2,1)S(1)} %collective-permute-done.37), channel_id=1, source_target_pairs={{0,1},{1,0},{2,3},{3,2},{4,5},{5,4},{6,7},{7,6},{8,9},{9,8},{10,11... | collective-permute-start | bytes 589832 | tf_op jit(solution)/shard_map/ppermute | solution.py:72
  105.4 7.2 %collective-permute-start.39 = (bf16[1,48,2048]{2,1,0:T(8,128)(2,1)S(1)}, bf16[1,48,2048]{2,1,0:T(8,128)(2,1)S(1)}, u32[]{:S(2)}, u32[]{:S(2)}) collective-permute-start(bf16[1,48,2048]{2,1,0:T(8,128)(2,1)S(1)} %collective-permute-done.35), channel_id=1, source_target_pairs={{0,4},{1,5},{4,8},{5,9},{8,12},{9,13},{12,14},{13,15},{14,10},{15,... | collective-permute-start | bytes 589832 | tf_op jit(solution)/shard_map/ppermute | solution.py:69
  106.7 12.9 %collective-permute-start.41 = (bf16[1,48,2048]{2,1,0:T(8,128)(2,1)S(1)}, bf16[1,48,2048]{2,1,0:T(8,128)(2,1)S(1)}, u32[]{:S(2)}, u32[]{:S(2)}) collective-permute-start(bf16[1,48,2048]{2,1,0:T(8,128)(2,1)S(1)} %collective-permute-done.37), channel_id=1, source_target_pairs={{0,2},{1,3},{4,0},{5,1},{8,4},{9,5},{12,8},{13,9},{14,12},{15,13},... | collective-permute-start | bytes 589832 | tf_op jit(solution)/shard_map/ppermute | solution.py:69
  108.8 4.4 %collective-permute-start.26 = (bf16[1,48,2048]{2,1,0:T(8,128)(2,1)S(1)}, bf16[1,48,2048]{2,1,0:T(8,128)(2,1)S(1)}, u32[]{:S(2)}, u32[]{:S(2)}) collective-permute-start(bf16[1,48,2048]{2,1,0:T(8,128)(2,1)S(1)} %collective-permute-done.25), channel_id=1, source_target_pairs={{0,1},{1,0},{2,3},{3,2},{4,5},{5,4},{6,7},{7,6},{8,9},{9,8},{10,11... | collective-permute-start | bytes 589832 | tf_op jit(solution)/shard_map/ppermute | solution.py:72
  112.5 6.4 %collective-permute-start.27 = (bf16[1,48,2048]{2,1,0:T(8,128)(2,1)S(1)}, bf16[1,48,2048]{2,1,0:T(8,128)(2,1)S(1)}, u32[]{:S(2)}, u32[]{:S(2)}) collective-permute-start(bf16[1,48,2048]{2,1,0:T(8,128)(2,1)S(1)} %collective-permute-done.23), channel_id=1, source_target_pairs={{0,4},{1,5},{4,8},{5,9},{8,12},{9,13},{12,14},{13,15},{14,10},{15,... | collective-permute-start | bytes 589832 | tf_op jit(solution)/shard_map/ppermute | solution.py:69
  113.2 9.3 %collective-permute-start.29 = (bf16[1,48,2048]{2,1,0:T(8,128)(2,1)S(1)}, bf16[1,48,2048]{2,1,0:T(8,128)(2,1)S(1)}, u32[]{:S(2)}, u32[]{:S(2)}) collective-permute-start(bf16[1,48,2048]{2,1,0:T(8,128)(2,1)S(1)} %collective-permute-done.25), channel_id=1, source_target_pairs={{0,2},{1,3},{4,0},{5,1},{8,4},{9,5},{12,8},{13,9},{14,12},{15,13},... | collective-permute-start | bytes 589832 | tf_op jit(solution)/shard_map/ppermute | solution.py:69
  118.9 1.4 collective-permute-start.40
  119.6 1.6 collective-permute-start.28
  120.3 4.3 %collective-permute-start.42 = (bf16[1,48,2048]{2,1,0:T(8,128)(2,1)S(1)}, bf16[1,48,2048]{2,1,0:T(8,128)(2,1)S(1)}, u32[]{:S(2)}, u32[]{:S(2)}) collective-permute-start(bf16[1,48,2048]{2,1,0:T(8,128)(2,1)S(1)} %collective-permute-done.41), channel_id=1, source_target_pairs={{0,1},{1,0},{2,3},{3,2},{4,5},{5,4},{6,7},{7,6},{8,9},{9,8},{10,11... | collective-permute-start | bytes 589832 | tf_op jit(solution)/shard_map/ppermute | solution.py:72
  121.2 7.2 %collective-permute-start.43 = (bf16[1,48,2048]{2,1,0:T(8,128)(2,1)S(1)}, bf16[1,48,2048]{2,1,0:T(8,128)(2,1)S(1)}, u32[]{:S(2)}, u32[]{:S(2)}) collective-permute-start(bf16[1,48,2048]{2,1,0:T(8,128)(2,1)S(1)} %collective-permute-done.39), channel_id=1, source_target_pairs={{0,4},{1,5},{4,8},{5,9},{8,12},{9,13},{12,14},{13,15},{14,10},{15,... | collective-permute-start | bytes 589832 | tf_op jit(solution)/shard_map/ppermute | solution.py:69
  122.5 6.9 %collective-permute-start.45 = (bf16[1,48,2048]{2,1,0:T(8,128)(2,1)S(1)}, bf16[1,48,2048]{2,1,0:T(8,128)(2,1)S(1)}, u32[]{:S(2)}, u32[]{:S(2)}) collective-permute-start(bf16[1,48,2048]{2,1,0:T(8,128)(2,1)S(1)} %collective-permute-done.41), channel_id=1, source_target_pairs={{0,2},{1,3},{4,0},{5,1},{8,4},{9,5},{12,8},{13,9},{14,12},{15,13},... | collective-permute-start | bytes 589832 | tf_op jit(solution)/shard_map/ppermute | solution.py:69
  124.6 4.8 %collective-permute-start.30 = (bf16[1,48,2048]{2,1,0:T(8,128)(2,1)S(1)}, bf16[1,48,2048]{2,1,0:T(8,128)(2,1)S(1)}, u32[]{:S(2)}, u32[]{:S(2)}) collective-permute-start(bf16[1,48,2048]{2,1,0:T(8,128)(2,1)S(1)} %collective-permute-done.29), channel_id=1, source_target_pairs={{0,1},{1,0},{2,3},{3,2},{4,5},{5,4},{6,7},{7,6},{8,9},{9,8},{10,11... | collective-permute-start | bytes 589832 | tf_op jit(solution)/shard_map/ppermute | solution.py:72
  128.3 6.4 %collective-permute-start.31 = (bf16[1,48,2048]{2,1,0:T(8,128)(2,1)S(1)}, bf16[1,48,2048]{2,1,0:T(8,128)(2,1)S(1)}, u32[]{:S(2)}, u32[]{:S(2)}) collective-permute-start(bf16[1,48,2048]{2,1,0:T(8,128)(2,1)S(1)} %collective-permute-done.27), channel_id=1, source_target_pairs={{0,4},{1,5},{4,8},{5,9},{8,12},{9,13},{12,14},{13,15},{14,10},{15,... | collective-permute-start | bytes 589832 | tf_op jit(solution)/shard_map/ppermute | solution.py:69
  129.4 19.0 %collective-permute-start.44 = (bf16[1,48,2048]{2,1,0:T(8,128)(2,1)S(1)}, bf16[1,48,2048]{2,1,0:T(8,128)(2,1)S(1)}, u32[]{:S(2)}, u32[]{:S(2)}) collective-permute-start(bf16[1,48,2048]{2,1,0:T(8,128)(2,1)S(1)} %collective-permute-done.43), channel_id=1, source_target_pairs={{0,1},{1,0},{2,3},{3,2},{4,5},{5,4},{6,7},{7,6},{8,9},{9,8},{10,11... | collective-permute-start | bytes 589832 | tf_op jit(solution)/shard_map/ppermute | solution.py:72
  129.4 19.7 %collective-permute-start.46 = (bf16[1,48,2048]{2,1,0:T(8,128)(2,1)S(1)}, bf16[1,48,2048]{2,1,0:T(8,128)(2,1)S(1)}, u32[]{:S(2)}, u32[]{:S(2)}) collective-permute-start(bf16[1,48,2048]{2,1,0:T(8,128)(2,1)S(1)} %collective-permute-done.45), channel_id=1, source_target_pairs={{0,1},{1,0},{2,3},{3,2},{4,5},{5,4},{6,7},{7,6},{8,9},{9,8},{10,11... | collective-permute-start | bytes 589832 | tf_op jit(solution)/shard_map/ppermute | solution.py:72
  134.7 13.7 %collective-permute-start.47 = (bf16[1,48,2048]{2,1,0:T(8,128)(2,1)S(1)}, bf16[1,48,2048]{2,1,0:T(8,128)(2,1)S(1)}, u32[]{:S(2)}, u32[]{:S(2)}) collective-permute-start(bf16[1,48,2048]{2,1,0:T(8,128)(2,1)S(1)} %collective-permute-done.45), channel_id=1, source_target_pairs={{0,2},{1,3},{4,0},{5,1},{8,4},{9,5},{12,8},{13,9},{14,12},{15,13},... | collective-permute-start | bytes 589832 | tf_op jit(solution)/shard_map/ppermute | solution.py:69
  135.4 6.6 %collective-permute-start.32 = (bf16[1,48,2048]{2,1,0:T(8,128)(2,1)S(1)}, bf16[1,48,2048]{2,1,0:T(8,128)(2,1)S(1)}, u32[]{:S(2)}, u32[]{:S(2)}) collective-permute-start(bf16[1,48,2048]{2,1,0:T(8,128)(2,1)S(1)} %collective-permute-done.31), channel_id=1, source_target_pairs={{0,1},{1,0},{2,3},{3,2},{4,5},{5,4},{6,7},{7,6},{8,9},{9,8},{10,11... | collective-permute-start | bytes 589832 | tf_op jit(solution)/shard_map/ppermute | solution.py:72
  137.7 6.6 %copy-start.8 = (f32[768,768]{0,1:T(8,128)S(1)}, f32[768,768]{0,1:T(8,128)}, u32[]{:S(2)}) copy-start(f32[768,768]{0,1:T(8,128)} %fusion.54) | copy-start | bytes 7077892
  140.7 7.7 %copy-start.5 = (bf16[768,2048]{1,0:T(8,128)(2,1)}, bf16[768,2048]{1,0:T(8,128)(2,1)S(1)}, u32[]{:S(2)}) copy-start(bf16[768,2048]{1,0:T(8,128)(2,1)S(1)} %convolution_convert_fusion) | copy-start | bytes 9437188
  140.7 3.6 %copy-start.2 = (bf16[768,2048]{1,0:T(8,128)(2,1)S(1)}, bf16[768,2048]{1,0:T(8,128)(2,1)}, u32[]{:S(2)}) copy-start(bf16[768,2048]{1,0:T(8,128)(2,1)} %bitcast_dynamic-update-slice_fusion.16) | copy-start | bytes 9437188
  142.0 38.1 %collective-permute-start.9 = (bf16[8,1,48,2048]{3,2,1,0:T(8,128)(2,1)}, bf16[8,1,48,2048]{3,2,1,0:T(8,128)(2,1)}, u32[]{:S(2)}, u32[]{:S(2)}) collective-permute-start(bf16[8,1,48,2048]{3,2,1,0:T(8,128)(2,1)} %slice.194), channel_id=1, source_target_pairs={{0,1},{1,0},{2,3},{3,2},{4,5},{5,4},{6,7},{7,6},{8,9},{9,8},{10,11... | collective-permute-start | bytes 4718600 | tf_op jit(solution)/shard_map/ppermute | solution.py:72
  144.3 4.1 %copy-start.3 = (bf16[768,2048]{1,0:T(8,128)(2,1)}, bf16[768,2048]{1,0:T(8,128)(2,1)S(1)}, u32[]{:S(2)}) copy-start(bf16[768,2048]{1,0:T(8,128)(2,1)S(1)} %bitcast_dynamic-update-slice_fusion.15) | copy-start | bytes 9437188
  148.5 1.6 collective-permute-start.48
  160.5 15.4 %all-to-all-start = ((f32[32,1,48]{2,1,0:T(1,128)}), f32[32,1,48]{2,1,0:T(1,128)S(1)}, u32[]{:S(2)}, u32[]{:S(2)}) async-start(f32[32,1,48]{2,1,0:T(1,128)} %bitcast.113), calls=%async_computation | async-start | bytes 32768 | tf_op jit(solution)/shard_map/all_to_all | solution.py:174
  163.0 5.7 %copy-start.4 = (bf16[768,2048]{1,0:T(8,128)(2,1)S(1)}, bf16[768,2048]{1,0:T(8,128)(2,1)}, u32[]{:S(2)}) copy-start(bf16[768,2048]{1,0:T(8,128)(2,1)} %copy-done.3) | copy-start | bytes 9437188
  167.0 8.9 %copy-start.11 = (s32[48,8]{0,1:T(8,128)S(1)}, s32[48,8]{0,1:T(8,128)}, u32[]{:S(2)}) copy-start(s32[48,8]{0,1:T(8,128)} %param.7) | copy-start | bytes 4612
  167.0 34.9 %collective-permute-start.49 = (bf16[576,768]{1,0:T(8,128)(2,1)}, bf16[576,768]{1,0:T(8,128)(2,1)}, u32[]{:S(2)}, u32[]{:S(2)}) collective-permute-start(bf16[576,768]{1,0:T(8,128)(2,1)} %convolution_convert_fusion.2), channel_id=1, source_target_pairs={{0,16},{16,0},{1,17},{17,1},{2,18},{18,2},{3,19},{19,3},{4,20},{20... | collective-permute-start | bytes 2654216 | tf_op jit(solution)/shard_map/ppermute | solution.py:66
  176.5 25.4 %copy-start.1 = (bf16[768,576]{1,0:T(8,128)(2,1)S(1)}, bf16[768,576]{1,0:T(8,128)(2,1)}, u32[]{:S(2)}) copy-start(bf16[768,576]{1,0:T(8,128)(2,1)} %get-tuple-element.21) | copy-start | bytes 2654212
  176.5 25.4 %copy-start.7 = (f32[768,768]{0,1:T(8,128)S(1)}, f32[768,768]{0,1:T(8,128)}, u32[]{:S(2)}) copy-start(f32[768,768]{0,1:T(8,128)} %get-tuple-element.34) | copy-start | bytes 7077892
  178.0 7.8 %collective-permute-start.1 = (bf16[1,48,2048]{2,1,0:T(8,128)(2,1)S(1)}, bf16[1,48,2048]{2,1,0:T(8,128)(2,1)S(1)}, u32[]{:S(2)}, u32[]{:S(2)}) collective-permute-start(bf16[1,48,2048]{2,1,0:T(8,128)(2,1)S(1)} %get-tuple-element.12), channel_id=1, source_target_pairs={{0,4},{1,5},{4,8},{5,9},{8,12},{9,13},{12,14},{13,15},{14,10},{15,... | collective-permute-start | bytes 589832 | tf_op jit(solution)/shard_map/ppermute | solution.py:69
  179.6 29.8 %collective-permute-start.5 = (bf16[1,48,2048]{2,1,0:T(8,128)(2,1)S(1)}, bf16[1,48,2048]{2,1,0:T(8,128)(2,1)S(1)}, u32[]{:S(2)}, u32[]{:S(2)}) collective-permute-start(bf16[1,48,2048]{2,1,0:T(8,128)(2,1)S(1)} %get-tuple-element.13), channel_id=1, source_target_pairs={{0,2},{1,3},{4,0},{5,1},{8,4},{9,5},{12,8},{13,9},{14,12},{15,13},... | collective-permute-start | bytes 589832 | tf_op jit(solution)/shard_map/ppermute | solution.py:69
  181.4 8.7 %collective-permute-start.10 = (bf16[1,48,2048]{2,1,0:T(8,128)(2,1)S(1)}, bf16[1,48,2048]{2,1,0:T(8,128)(2,1)S(1)}, u32[]{:S(2)}, u32[]{:S(2)}) collective-permute-start(bf16[1,48,2048]{2,1,0:T(8,128)(2,1)S(1)} %get-tuple-element.8), channel_id=1, source_target_pairs={{0,4},{1,5},{4,8},{5,9},{8,12},{9,13},{12,14},{13,15},{14,10},{15,... | collective-permute-start | bytes 589832 | tf_op jit(solution)/shard_map/ppermute | solution.py:69
  186.9 7.5 %collective-permute-start.2 = (bf16[1,48,2048]{2,1,0:T(8,128)(2,1)S(1)}, bf16[1,48,2048]{2,1,0:T(8,128)(2,1)S(1)}, u32[]{:S(2)}, u32[]{:S(2)}) collective-permute-start(bf16[1,48,2048]{2,1,0:T(8,128)(2,1)S(1)} %fusion.21), channel_id=1, source_target_pairs={{0,4},{1,5},{4,8},{5,9},{8,12},{9,13},{12,14},{13,15},{14,10},{15,... | collective-permute-start | bytes 589832 | tf_op jit(solution)/shard_map/ppermute | solution.py:69
  188.5 8.9 %collective-permute-start.13 = (bf16[1,48,2048]{2,1,0:T(8,128)(2,1)S(1)}, bf16[1,48,2048]{2,1,0:T(8,128)(2,1)S(1)}, u32[]{:S(2)}, u32[]{:S(2)}) collective-permute-start(bf16[1,48,2048]{2,1,0:T(8,128)(2,1)S(1)} %get-tuple-element.9), channel_id=1, source_target_pairs={{0,2},{1,3},{4,0},{5,1},{8,4},{9,5},{12,8},{13,9},{14,12},{15,13},... | collective-permute-start | bytes 589832 | tf_op jit(solution)/shard_map/ppermute | solution.py:69
  191.1 7.9 %collective-permute-start.11 = (bf16[1,48,2048]{2,1,0:T(8,128)(2,1)S(1)}, bf16[1,48,2048]{2,1,0:T(8,128)(2,1)S(1)}, u32[]{:S(2)}, u32[]{:S(2)}) collective-permute-start(bf16[1,48,2048]{2,1,0:T(8,128)(2,1)S(1)} %fusion.15), channel_id=1, source_target_pairs={{0,4},{1,5},{4,8},{5,9},{8,12},{9,13},{12,14},{13,15},{14,10},{15,... | collective-permute-start | bytes 589832 | tf_op jit(solution)/shard_map/ppermute | solution.py:69
  195.6 13.7 %collective-permute-start.3 = (bf16[1,48,2048]{2,1,0:T(8,128)(2,1)S(1)}, bf16[1,48,2048]{2,1,0:T(8,128)(2,1)S(1)}, u32[]{:S(2)}, u32[]{:S(2)}) collective-permute-start(bf16[1,48,2048]{2,1,0:T(8,128)(2,1)S(1)} %fusion.22), channel_id=1, source_target_pairs={{0,4},{1,5},{4,8},{5,9},{8,12},{9,13},{12,14},{13,15},{14,10},{15,... | collective-permute-start | bytes 589832 | tf_op jit(solution)/shard_map/ppermute | solution.py:69
  200.4 6.3 %collective-permute-start.14 = (bf16[1,48,2048]{2,1,0:T(8,128)(2,1)S(1)}, bf16[1,48,2048]{2,1,0:T(8,128)(2,1)S(1)}, u32[]{:S(2)}, u32[]{:S(2)}) collective-permute-start(bf16[1,48,2048]{2,1,0:T(8,128)(2,1)S(1)} %get-tuple-element.7), channel_id=1, source_target_pairs={{0,2},{1,3},{4,0},{5,1},{8,4},{9,5},{12,8},{13,9},{14,12},{15,13},... | collective-permute-start | bytes 589832 | tf_op jit(solution)/shard_map/ppermute | solution.py:69
  207.8 7.6 %collective-permute-start.15 = (bf16[1,48,2048]{2,1,0:T(8,128)(2,1)S(1)}, bf16[1,48,2048]{2,1,0:T(8,128)(2,1)S(1)}, u32[]{:S(2)}, u32[]{:S(2)}) collective-permute-start(bf16[1,48,2048]{2,1,0:T(8,128)(2,1)S(1)} %fusion.13), channel_id=1, source_target_pairs={{0,2},{1,3},{4,0},{5,1},{8,4},{9,5},{12,8},{13,9},{14,12},{15,13},... | collective-permute-start | bytes 589832 | tf_op jit(solution)/shard_map/ppermute | solution.py:69
  210.7 8.9 %collective-permute-start.6 = (bf16[1,48,2048]{2,1,0:T(8,128)(2,1)S(1)}, bf16[1,48,2048]{2,1,0:T(8,128)(2,1)S(1)}, u32[]{:S(2)}, u32[]{:S(2)}) collective-permute-start(bf16[1,48,2048]{2,1,0:T(8,128)(2,1)S(1)} %get-tuple-element.11), channel_id=1, source_target_pairs={{0,2},{1,3},{4,0},{5,1},{8,4},{9,5},{12,8},{13,9},{14,12},{15,13},... | collective-permute-start | bytes 589832 | tf_op jit(solution)/shard_map/ppermute | solution.py:69
  212.3 11.6 %collective-permute-start.4 = (bf16[1,48,2048]{2,1,0:T(8,128)(2,1)S(1)}, bf16[1,48,2048]{2,1,0:T(8,128)(2,1)S(1)}, u32[]{:S(2)}, u32[]{:S(2)}) collective-permute-start(bf16[1,48,2048]{2,1,0:T(8,128)(2,1)S(1)} %get-tuple-element.10), channel_id=1, source_target_pairs={{0,4},{1,5},{4,8},{5,9},{8,12},{9,13},{12,14},{13,15},{14,10},{15,... | collective-permute-start | bytes 589832 | tf_op jit(solution)/shard_map/ppermute | solution.py:69
  212.8 9.4 %collective-permute-start.12 = (bf16[1,48,2048]{2,1,0:T(8,128)(2,1)S(1)}, bf16[1,48,2048]{2,1,0:T(8,128)(2,1)S(1)}, u32[]{:S(2)}, u32[]{:S(2)}) collective-permute-start(bf16[1,48,2048]{2,1,0:T(8,128)(2,1)S(1)} %get-tuple-element.6), channel_id=1, source_target_pairs={{0,4},{1,5},{4,8},{5,9},{8,12},{9,13},{12,14},{13,15},{14,10},{15,... | collective-permute-start | bytes 589832 | tf_op jit(solution)/shard_map/ppermute | solution.py:69
  216.5 5.7 %collective-permute-start.16 = (bf16[1,48,2048]{2,1,0:T(8,128)(2,1)S(1)}, bf16[1,48,2048]{2,1,0:T(8,128)(2,1)S(1)}, u32[]{:S(2)}, u32[]{:S(2)}) collective-permute-start(bf16[1,48,2048]{2,1,0:T(8,128)(2,1)S(1)} %fusion.14), channel_id=1, source_target_pairs={{0,2},{1,3},{4,0},{5,1},{8,4},{9,5},{12,8},{13,9},{14,12},{15,13},... | collective-permute-start | bytes 589832 | tf_op jit(solution)/shard_map/ppermute | solution.py:69
  220.7 5.7 %collective-permute-start.7 = (bf16[1,48,2048]{2,1,0:T(8,128)(2,1)S(1)}, bf16[1,48,2048]{2,1,0:T(8,128)(2,1)S(1)}, u32[]{:S(2)}, u32[]{:S(2)}) collective-permute-start(bf16[1,48,2048]{2,1,0:T(8,128)(2,1)S(1)} %fusion.20), channel_id=1, source_target_pairs={{0,2},{1,3},{4,0},{5,1},{8,4},{9,5},{12,8},{13,9},{14,12},{15,13},... | collective-permute-start | bytes 589832 | tf_op jit(solution)/shard_map/ppermute | solution.py:69
  223.3 5.7 %collective-permute-start.17 = (bf16[48,2048]{1,0:T(8,128)(2,1)S(1)}, bf16[48,2048]{1,0:T(8,128)(2,1)S(1)}, u32[]{:S(2)}, u32[]{:S(2)}) collective-permute-start(bf16[48,2048]{1,0:T(8,128)(2,1)S(1)} %fusion.32), channel_id=1, source_target_pairs={{0,16},{16,0},{1,17},{17,1},{2,18},{18,2},{3,19},{19,3},{4,20},{20... | collective-permute-start | bytes 589832 | tf_op jit(solution)/shard_map/ppermute | solution.py:66
  229.1 0.7 copy-start.10

commit v3 on v1

v3 whole, which is shorter than its diff:
```python
import jax
import jax.numpy as jnp
from jax import lax
from jax.sharding import PartitionSpec as P


def dot(a, b, ca, cb):
    return lax.dot_general(a, b, (((ca,), (cb,)), ((), ())), preferred_element_type=jnp.float32)


def shards(expert_ids, route_probs, expert_hidden, down_weight, out_grad):
    tok, top = expert_ids.shape
    n_dp = lax.axis_size("dp")
    n_ex = lax.axis_size("expert")
    chips = n_ex // 2
    cap = expert_hidden.shape[3]
    slots = cap * n_ex
    ff = down_weight.shape[1]
    width = down_weight.shape[2]
    weight = down_weight[0]
    replica = lax.axis_index("dp")
    expert = lax.axis_index("expert")
    core = expert % 2
    rows = chips * tok
    same_core = [[2 * chip + c for chip in range(chips)] for c in range(2)]
    sibling = [(e, e ^ 1) for e in range(n_ex)]

    def shift(value, step):
        return lax.ppermute(value, "dp", [(i, (i + step) % n_dp) for i in range(n_dp)])

    def swap(value):
        return lax.ppermute(value, "expert", sibling)

    def width_shard(d):
        at = ((replica + d) % n_dp) * width
        return lax.dynamic_slice_in_dim(out_grad, at, width, axis=1)

    grads = []
    for d in range(n_dp):
        piece = width_shard(0) if d == 0 else shift(width_shard(d), d)
        piece = lax.all_gather(piece, "expert", axis=0, axis_index_groups=same_core)
        grads.append(piece.reshape(rows, width))

    weights = jnp.concatenate([weight, swap(weight)], axis=0)
    hidden = expert_hidden[0, 0].transpose(1, 0, 2).reshape(slots, ff)
    hiddens = [hidden, swap(hidden)]

    names = expert_ids.T[None] == jnp.arange(n_ex, dtype=jnp.int32)[:, None, None]
    table = jnp.sum(jnp.where(names, route_probs.T[None], 0.0), axis=1)
    table = lax.all_to_all(
        table.reshape(chips, 2, tok), "expert", 0, 0, tiled=True, axis_index_groups=same_core
    )
    table = jnp.where(core == 0, table, table[:, ::-1])
    taken = (table > 0.0).astype(jnp.float32)
    earlier = jnp.tril(jnp.ones((tok, tok), jnp.float32), -1)
    position = jnp.einsum("set,ut->seu", taken, earlier).astype(jnp.int32)
    position = jnp.where(table > 0.0, position, -1)

    slot_c = jnp.arange(slots, dtype=jnp.int32) // n_ex
    slot_s = jnp.arange(slots, dtype=jnp.int32) % n_ex
    source = 2 * jnp.arange(chips, dtype=jnp.int32) + core
    here = source[:, None, None] == slot_s
    picks, helds, prob_rows = [], [], []
    for x in range(2):
        pick = (position[:, x, :, None] == slot_c) & here
        pick = pick.reshape(rows, slots).astype(jnp.bfloat16)
        picks.append(pick)
        helds.append(dot(pick, hiddens[x], 1, 0).astype(jnp.bfloat16))
        prob_rows.append(table[:, x].reshape(rows, 1))
    scaled = jnp.concatenate(
        [(helds[x].astype(jnp.float32) * prob_rows[x]).astype(jnp.bfloat16) for x in range(2)], axis=1
    )
    scaleds = [scaled] + [shift(scaled, d) for d in range(1, n_dp)]

    layer_out = jnp.zeros((tok, n_dp * width), jnp.bfloat16)
    for d in range(n_dp):
        part = dot(scaleds[d], weights, 1, 0).astype(jnp.bfloat16)
        piece = lax.psum_scatter(
            part.reshape(chips, tok, width), "expert", scatter_dimension=0, axis_index_groups=same_core
        )
        piece = piece if d == 0 else shift(piece, -d)
        layer_out = lax.dynamic_update_slice_in_dim(
            layer_out, piece, ((replica + d) % n_dp) * width, axis=1
        )

    back = dot(grads[0], weights, 1, 1)
    for d in range(1, n_dp):
        part = dot(grads[d], weights, 1, 1).astype(jnp.bfloat16)
        back = back + shift(part, -d).astype(jnp.float32)
    spreads, inners = [], []
    for x in range(2):
        mine = back[:, x * ff : (x + 1) * ff]
        inners.append(jnp.sum(mine * helds[x].astype(jnp.float32), axis=1).reshape(chips, tok))
        mine = (mine * prob_rows[x]).astype(jnp.bfloat16)
        spreads.append(dot(picks[x], mine, 0, 0).astype(jnp.bfloat16))
    hidden_grad = spreads[0] + swap(spreads[1])
    hidden_grad = hidden_grad.reshape(cap, n_ex, ff).transpose(1, 0, 2)[None, None]

    total = dot(scaleds[0], grads[0], 0, 0)
    for d in range(1, n_dp):
        total = total + dot(scaleds[d], grads[d], 0, 0)
    weight_grad = total[:ff] + swap(total[ff:].astype(jnp.bfloat16)).astype(jnp.float32)

    inner = jnp.stack(inners, axis=1)
    inner = jnp.where(core == 0, inner, inner[:, ::-1])
    inner = lax.all_to_all(inner, "expert", 0, 0, tiled=True, axis_index_groups=same_core)
    inner = inner.reshape(n_ex, tok)
    mine = expert_ids[:, :, None] == jnp.arange(n_ex, dtype=jnp.int32)
    prob_grad = jnp.sum(jnp.where(mine, inner.T[:, None, :], 0.0), axis=2)
    return (layer_out, prob_grad, hidden_grad, weight_grad[None])


def solution(mesh):
    placed = (
        P(("dp", "expert"), None),
        P(("dp", "expert"), None),
        P("dp", "expert", None, None, None),
        P("expert", None, "dp"),
        P(("dp", "expert"), None),
    )
    return jax.shard_map(
        shards,
        mesh=mesh,
        in_specs=placed,
        out_specs=(
            P(("dp", "expert"), None),
            P(("dp", "expert"), None),
            P("dp", "expert", None, None, None),
            P("expert", None, "dp"),
        ),
        check_vma=False,
    )
```

time: 271 us -> 272 us (level)
  matrix products: 32.7 us -> 48.1 us
  blocking collectives: 24.1 us -> 10.4 us
  starting transfers between devices: 17.9 us -> 14.1 us
    dot_general x3 -> x10, matrix products: 24 us -> 47.9 us  [dot(): lax.dot_general(a, b, (((ca,), (cb,)), ((), ())), preferred_element_type=...]
    ppermute x0 -> x8, waiting for transfers between devices: none -> 22.7 us  [the longest x4 22.7 us: shift(): lax.ppermute(value, 'dp', [(i, (i + step) % n_dp) for i in range(n_dp)])]
    all_to_all x3 -> x1, starting transfers between devices: 17.8 us -> 6.09 us  [shards(): lax.all_to_all(table.reshape(chips, 2, tok), 'expert', 0, 0, tiled=True,...]
    reduce_scatter x2, waiting for transfers between devices: 78.3 us -> 67 us  [shards(): lax.psum_scatter(part.reshape(chips, tok, width), 'expert', scatter_dimen...]
    all_to_all x3 -> x1, waiting for transfers between devices: 16.1 us -> 6.43 us  [shards(): lax.all_to_all(table.reshape(chips, 2, tok), 'expert', 0, 0, tiled=True,...]
    all_to_all x2 -> x1, blocking collectives: 19.6 us -> 10.4 us  [shards(): lax.all_to_all(inner, 'expert', 0, 0, tiled=True, axis_index_groups=same_...]
    dot_general x3 -> x1, matrix products: 8.68 us -> 0.19 us  [shards(): position = jnp.einsum('set,ut->seu', taken, earlier).astype(jnp.int32)]
    broadcast_in_dim x0 -> x1, other arithmetic: none -> 7.95 us  [shards(): return (layer_out, prob_grad, hidden_grad, weight_grad[None])]
  transfers between devices with their start and end apart: 7 -> 13, of which waited for: 7 -> 7; matrix products, arithmetic and copies ran while one was open for 9% -> 19% of each run, Pallas kernels for 0% -> 0%
where the time goes in v3:
time: 272 us; the launch traced here: 271 us
  waiting for transfers between devices  162 us (60%)
  matrix products  48.1 us (18%)
  starting transfers between devices  14.1 us (5%)
  between operations  14 us (5%)
  local copies, waits for them, and re-layouts  12.2 us (4%)
  other arithmetic  10.7 us (4%)
  blocking collectives  10.4 us (4%)
    reduce_scatter x2, waiting for transfers between devices, shards(): lax.psum_scatter(part.reshape(chips, tok, width), 'expert', scatter_dimen...  67 us
    all_gather x2, waiting for transfers between devices, shards(): piece = lax.all_gather(piece, 'expert', axis=0, axis_index_groups=same_core)  64.8 us
    dot_general x10, matrix products, dot(): lax.dot_general(a, b, (((ca,), (cb,)), ((), ())), preferred_element_type=...  47.9 us
    ppermute x4, waiting for transfers between devices, shift(): lax.ppermute(value, 'dp', [(i, (i + step) % n_dp) for i in range(n_dp)])  22.7 us
    all_to_all x1, blocking collectives, shards(): lax.all_to_all(inner, 'expert', 0, 0, tiled=True, axis_index_groups=same_...  10.4 us
    unnamed x27, local copies, waits for them, and re-layouts  8.53 us
    broadcast_in_dim x1, other arithmetic, shards(): return (layer_out, prob_grad, hidden_grad, weight_grad[None])  7.95 us
    ppermute x4, starting transfers between devices, shift(): lax.ppermute(value, 'dp', [(i, (i + step) % n_dp) for i in range(n_dp)])  7.41 us
  transfers between devices with their start and end apart: 13, of which 7 were waited for; matrix products, arithmetic and copies ran while one was open for 19% of the time, Pallas kernels for 0%

profile of v3, /device:TPU:0, one launch (start us, length us, event | category | flops | bytes accessed | tf_op | source)
XLA Modules:
  0.0 271.3 jit_solution(15487423675342572228)
XLA Ops:
  7.2 0.0 all-gather.7.cloned.1.call-start
  7.2 1.7 constant_dynamic-slice_fusion
  9.0 2.9 %collective-permute-start.4 = (bf16[48,2048]{1,0:T(8,128)(2,1)S(1)}, bf16[48,2048]{1,0:T(8,128)(2,1)S(1)}, u32[]{:S(2)}, u32[]{:S(2)}) collective-permute-start(bf16[48,2048]{1,0:T(8,128)(2,1)S(1)} %get-tuple-element.8), channel_id=1, source_target_pairs={{0,16},{16,0},{1,17},{17,1},{2,18},{18,2},{3,19},{19,3},{4,20},{20... | collective-permute-start | bytes 589832 | tf_op jit(solution)/shard_map/ppermute | solution.py:29
  11.9 4.9 %collective-permute-done.4 = bf16[48,2048]{1,0:T(8,128)(2,1)S(1)} collective-permute-done((bf16[48,2048]{1,0:T(8,128)(2,1)S(1)}, bf16[48,2048]{1,0:T(8,128)(2,1)S(1)}, u32[]{:S(2)}, u32[]{:S(2)}) %collective-permute-start.4) | collective-permute-done | bytes 196640 | tf_op jit(solution)/shard_map/ppermute | solution.py:29
  16.8 0.7 copy-done.7
  17.5 0.0 all-gather.7.cloned.1.call-update
  17.5 0.0 all-gather.5.cloned.1.call-start
  17.6 0.1 collective-permute-start.1
  17.6 0.6 all-gather.5.cloned.1.call-update
  18.3 1.3 select_reduce_fusion.1
  19.6 6.1 %all-to-all-start = ((f32[8,2,48]{2,1,0:T(2,128)}), f32[8,2,48]{2,1,0:T(2,128)S(1)}, u32[]{:S(2)}, u32[]{:S(2)}) async-start(f32[8,2,48]{2,1,0:T(2,128)} %bitcast.2), calls=%async_computation | async-start | bytes 16384 | tf_op jit(solution)/shard_map/all_to_all | solution.py:50
  25.7 0.0 reduce-scatter.3.cloned.1.call-start
  25.7 0.1 collective-permute-start
  25.9 0.1 broadcast_compare_fusion
  25.9 6.4 %all-to-all-done = f32[8,2,48]{2,1,0:T(2,128)S(1)} async-done(((f32[8,2,48]{2,1,0:T(2,128)}), f32[8,2,48]{2,1,0:T(2,128)S(1)}, u32[]{:S(2)}, u32[]{:S(2)}) %all-to-all-start) | async-done | bytes 3104 | tf_op jit(solution)/shard_map/all_to_all | solution.py:50
  32.4 31.0 %all-gather.7.cloned.1.call-done = bf16[384,2048]{1,0:T(8,128)(2,1)} async-done(((bf16[48,2048]{1,0:T(8,128)(2,1)}), bf16[384,2048]{1,0:T(8,128)(2,1)}) %all-gather.7.cloned.1.call-update) | async-done | bytes 1572880 | tf_op jit(solution)/shard_map/all_gather | solution.py:41
  63.4 7.0 %convolution_convert_fusion = bf16[384,1536]{1,0:T(8,128)(2,1)} fusion(bf16[384,2048]{1,0:T(8,128)(2,1)} %all-gather.7.cloned.1.call-done, bf16[768,2048]{1,0:T(8,128)(2,1)} %collective-permute-done.1, bf16[768,2048]{1,0:T(8,128)(2,1)} %bitcast.61), kind=kOutput, calls=%fused_computation.6 | convolution fusion | flops 2429091840 | bytes 9043968 | tf_op jit(solution)/shard_map/dot_general | solution.py:8
  70.3 1.5 collective-permute-start.5
  71.8 0.1 mul.54
  71.9 0.1 mul.57
  72.0 0.2 fusion.6
  72.2 0.1 eq.121
  72.3 0.1 eq.114
  72.3 0.4 bitcast_and_fusion
  72.8 0.0 copy-start.4
  72.8 0.2 compare_and_fusion
  73.0 1.5 convolution_convert_fusion.6
  74.5 33.9 %all-gather.5.cloned.1.call-done = bf16[384,2048]{1,0:T(8,128)(2,1)} async-done(((bf16[48,2048]{1,0:T(8,128)(2,1)}), bf16[384,2048]{1,0:T(8,128)(2,1)}) %all-gather.5.cloned.1.call-update) | async-done | bytes 1572880 | tf_op jit(solution)/shard_map/all_gather | solution.py:41
  108.3 6.0 %convolution_add_fusion.1 = f32[384,1536]{1,0:T(8,128)S(1)} fusion(bf16[384,2048]{1,0:T(8,128)(2,1)} %all-gather.5.cloned.1.call-done, bf16[384,1536]{1,0:T(8,128)(2,1)S(1)} %collective-permute-done.5, bf16[768,2048]{1,0:T(8,128)(2,1)} %collective-permute-done.1, bf16[768,2048]{1,0:T(8,128)(2,1)} %bitcast.62), kind=kOutput, calls=%fused_computation.5 | convolution fusion | flops 2429681664 | bytes 11403264 | tf_op jit(solution)/shard_map/dot_general | solution.py:8
  114.3 0.0 copy-start.1
  114.4 0.0 copy-start.9
  114.4 2.9 %fusion.5 = (f32[384]{0:T(512)S(1)}, f32[384]{0:T(512)S(1)}, bf16[384,768]{1,0:T(8,128)(2,1)S(1)}, bf16[384,768]{1,0:T(8,128)(2,1)S(1)}) fusion(f32[384,1536]{1,0:T(8,128)S(1)} %convolution_add_fusion.1, bf16[384,768]{1,0:T(8,128)(2,1)S(1)} %copy-done.12, f32[384]{0:T(512)S(1)} %mul.54, f32[384]{0:T(512)S(1)} %mul.57, ...), kind=kOutput, calls=%fused_computation.23 | convolution fusion | flops 342981888 | bytes 5240832 | tf_op jit(solution)/shard_map/dot_general | solution.py:8
  117.3 0.1 copy-done.9
  117.4 5.7 %convolution_convert_fusion.2 = bf16[384,2048]{1,0:T(8,128)(2,1)} fusion(bf16[768,2048]{1,0:T(8,128)(2,1)} %collective-permute-done.1, bf16[768,2048]{1,0:T(8,128)(2,1)S(1)} %bitcast.63, bf16[384,768]{1,0:T(8,128)(2,1)S(1)} %get-tuple-element.7, bf16[384,768]{1,0:T(8,128)(2,1)S(1)} %get-tuple-element.6), kind=kOutput, calls=%fused_computation.8 | convolution fusion | flops 2431647744 | bytes 9043968 | tf_op jit(solution)/shard_map/dot_general | solution.py:8
  123.1 0.0 reduce-scatter.3.cloned.1.call-update
  123.1 0.2 reduce-scatter.5.cloned.1.call-start
  123.3 0.1 pad_maximum_fusion.1
  123.4 0.0 copy-start.10
  123.4 1.5 collective-permute-start.2
  125.0 7.8 %fusion.25 = f32[1536,2048]{1,0:T(8,128)} fusion(bf16[384,2048]{1,0:T(8,128)(2,1)} %all-gather.5.cloned.1.call-done, bf16[384,768]{1,0:T(8,128)(2,1)S(1)} %get-tuple-element.7, bf16[384,768]{1,0:T(8,128)(2,1)S(1)} %get-tuple-element.6), kind=kOutput, calls=%fused_computation.69 | convolution fusion | flops 2418278400 | bytes 15335424 | tf_op jit(solution)/shard_map/dot_general | solution.py:8
  132.8 17.8 %collective-permute-done.2 = bf16[384,1536]{1,0:T(8,128)(2,1)S(1)} collective-permute-done((bf16[384,1536]{1,0:T(8,128)(2,1)S(1)}, bf16[384,1536]{1,0:T(8,128)(2,1)S(1)}, u32[]{:S(2)}, u32[]{:S(2)}) %collective-permute-start.2) | collective-permute-done | bytes 1179680 | tf_op jit(solution)/shard_map/ppermute | solution.py:29
  150.6 5.7 %convolution_convert_fusion.1 = bf16[384,2048]{1,0:T(8,128)(2,1)} fusion(bf16[384,1536]{1,0:T(8,128)(2,1)S(1)} %collective-permute-done.2, bf16[768,2048]{1,0:T(8,128)(2,1)} %collective-permute-done.1, bf16[768,2048]{1,0:T(8,128)(2,1)S(1)} %bitcast.64), kind=kOutput, calls=%fused_computation.7 | convolution fusion | flops 2429288448 | bytes 9043968 | tf_op jit(solution)/shard_map/dot_general | solution.py:8
  156.3 0.0 reduce-scatter.5.cloned.1.call-update
  156.3 1.4 copy-done.3
  157.7 6.5 %convolution_add_fusion = f32[1536,2048]{1,0:T(8,128)S(1)} fusion(f32[1536,2048]{1,0:T(8,128)} %fusion.25, bf16[384,1536]{1,0:T(8,128)(2,1)S(1)} %collective-permute-done.2, bf16[384,2048]{1,0:T(8,128)(2,1)S(1)} %copy-done.3), kind=kOutput, calls=%fused_computation | convolution fusion | flops 2419064832 | bytes 27918336 | tf_op jit(solution)/shard_map/dot_general | solution.py:8
  164.3 4.5 %copy-done = f32[1536,2048]{1,0:T(8,128)} copy-done((f32[1536,2048]{1,0:T(8,128)}, f32[1536,2048]{1,0:T(8,128)S(1)}, u32[]{:S(2)}) %copy-start) | copy-done | bytes 12582936
  168.8 0.5 slice.52
  169.3 0.0 copy-start.8
  169.3 0.1 collective-permute-start.7
  169.4 1.1 copy-done.2
  170.5 1.7 convolution_convert_fusion.3
  172.1 0.0 collective-permute-start.6
  172.1 0.1 stack_reshape.7
  172.2 0.1 stack_reshape.6
  172.3 10.4 %all_to_all.10 = f32[8,2,48]{2,1,0:T(2,128)S(1)} all-to-all(f32[8,2,48]{2,1,0:T(2,128)S(1)} %copy.21), channel_id=1, replica_groups={{0,2,4,6,8,10,12,14},{1,3,5,7,9,11,13,15},{16,18,20,22,24,26,28,30},{17..., dimensions={0} | all-to-all | bytes 6144 | tf_op jit(solution)/shard_map/all_to_all | solution.py:106
  182.7 0.6 select_reduce_fusion
  183.4 3.2 %fusion.1 = bf16[576,768]{1,0:T(8,128)(2,1)} fusion(bf16[576,768]{1,0:T(8,128)(2,1)} %collective-permute-done.6, pred[384,576]{1,0:T(32,128)(4,1)S(1)} %get-tuple-element.10, f32[384,1536]{1,0:T(8,128)} %copy-done.1, f32[384]{0:T(512)S(1)} %mul.54), kind=kOutput, calls=%fused_computation.17 | convolution fusion | flops 341213184 | bytes 3171840 | tf_op jit(solution)/shard_map/dot_general | solution.py:8
  186.6 0.4 reduce-scatter.3.cloned.1.call-done
  187.0 0.9 bitcast_dynamic-update-slice_fusion
  188.0 66.5 %reduce-scatter.5.cloned.1.call-done = bf16[1,48,2048]{2,1,0:T(8,128)(2,1)} async-done(((bf16[8,48,2048]{2,1,0:T(8,128)(2,1)}), bf16[1,48,2048]{2,1,0:T(8,128)(2,1)}) %reduce-scatter.5.cloned.1.call-update) | async-done | bytes 196624 | tf_op jit(solution)/shard_map/reduce_scatter | solution.py:78
  254.5 1.5 collective-permute-start.3
  256.0 8.0 %fusion = f32[1,768,2048]{2,1,0:T(8,128)} fusion(f32[1536,2048]{1,0:T(8,128)} %copy-done, bf16[768,2048]{1,0:T(8,128)(2,1)} %collective-permute-done.7), kind=kLoop, calls=%fused_computation.3 | loop fusion | flops 3145728 | bytes 15728640 | tf_op jit(solution)/shard_map/broadcast_in_dim | solution.py:110
  264.0 0.0 copy-start.6
  264.0 0.7 copy-done.6
  (34 shorter events, 0.1 us)
Async XLA Ops:
  7.2 56.2 %all-gather.7.cloned.1.call-start = ((), (), s32[]{:S(2)}) async-start(), calls=%async_computation.7 | async-start | bytes 1769472 | tf_op jit(solution)/shard_map/all_gather | solution.py:41
  9.0 7.8 %collective-permute-start.4 = (bf16[48,2048]{1,0:T(8,128)(2,1)S(1)}, bf16[48,2048]{1,0:T(8,128)(2,1)S(1)}, u32[]{:S(2)}, u32[]{:S(2)}) collective-permute-start(bf16[48,2048]{1,0:T(8,128)(2,1)S(1)} %get-tuple-element.8), channel_id=1, source_target_pairs={{0,16},{16,0},{1,17},{17,1},{2,18},{18,2},{3,19},{19,3},{4,20},{20... | collective-permute-start | bytes 589832 | tf_op jit(solution)/shard_map/ppermute | solution.py:29
  16.8 0.7 copy-start.7
  17.5 90.8 %all-gather.5.cloned.1.call-start = ((), (), s32[]{:S(2)}) async-start(), calls=%async_computation.6 | async-start | bytes 1769472 | tf_op jit(solution)/shard_map/all_gather | solution.py:41
  17.6 45.8 %collective-permute-start.1 = (bf16[768,2048]{1,0:T(8,128)(2,1)}, bf16[768,2048]{1,0:T(8,128)(2,1)}, u32[]{:S(2)}, u32[]{:S(2)}) collective-permute-start(bf16[768,2048]{1,0:T(8,128)(2,1)} %bitcast.60), channel_id=1, source_target_pairs={{0,1},{1,0},{2,3},{3,2},{4,5},{5,4},{6,7},{7,6},{8,9},{9,8},{10,11... | collective-permute-start | bytes 9437192 | tf_op jit(solution)/shard_map/ppermute | solution.py:32
  19.6 12.8 %all-to-all-start = ((f32[8,2,48]{2,1,0:T(2,128)}), f32[8,2,48]{2,1,0:T(2,128)S(1)}, u32[]{:S(2)}, u32[]{:S(2)}) async-start(f32[8,2,48]{2,1,0:T(2,128)} %bitcast.2), calls=%async_computation | async-start | bytes 16384 | tf_op jit(solution)/shard_map/all_to_all | solution.py:50
  25.7 161.3 %reduce-scatter.3.cloned.1.call-start = ((), (), s32[]{:S(2)}) async-start(), calls=%async_computation.4 | async-start | bytes 1769472 | tf_op jit(solution)/shard_map/reduce_scatter | solution.py:78
  25.7 88.6 %collective-permute-start = (bf16[576,768]{1,0:T(8,128)(2,1)}, bf16[576,768]{1,0:T(8,128)(2,1)}, u32[]{:S(2)}, u32[]{:S(2)}) collective-permute-start(bf16[576,768]{1,0:T(8,128)(2,1)} %bitcast.65), channel_id=1, source_target_pairs={{0,1},{1,0},{2,3},{3,2},{4,5},{5,4},{6,7},{7,6},{8,9},{9,8},{10,11... | collective-permute-start | bytes 2654216 | tf_op jit(solution)/shard_map/ppermute | solution.py:32
  32.4 40.6 %copy-start.11 = (bf16[1,1,16,36,768]{4,2,3,1,0:T(8,128)(2,1)S(1)}, bf16[1,1,16,36,768]{4,2,3,1,0:T(8,128)(2,1)}, u32[]{:S(2)}) copy-start(bf16[1,1,16,36,768]{4,2,3,1,0:T(8,128)(2,1)} %param.7) | copy-start | bytes 2654212
  70.3 38.0 %collective-permute-start.5 = (bf16[384,1536]{1,0:T(8,128)(2,1)}, bf16[384,1536]{1,0:T(8,128)(2,1)S(1)}, u32[]{:S(2)}, u32[]{:S(2)}) collective-permute-start(bf16[384,1536]{1,0:T(8,128)(2,1)} %convolution_convert_fusion), channel_id=1, source_target_pairs={{0,16},{16,0},{1,17},{17,1},{2,18},{18,2},{3,19},{19,3},{4,20},{20... | collective-permute-start | bytes 3538952 | tf_op jit(solution)/shard_map/ppermute | solution.py:29
  72.8 41.6 %copy-start.4 = (pred[384,576]{1,0:T(32,128)(4,1)}, pred[384,576]{1,0:T(32,128)(4,1)S(1)}, u32[]{:S(2)}) copy-start(pred[384,576]{1,0:T(32,128)(4,1)S(1)} %get-tuple-element.11) | copy-start | bytes 663556
  108.3 6.1 %copy-start.12 = (bf16[384,768]{1,0:T(8,128)(2,1)S(1)}, bf16[384,768]{1,0:T(8,128)(2,1)}, u32[]{:S(2)}) copy-start(bf16[384,768]{1,0:T(8,128)(2,1)} %convolution_convert_fusion.6) | copy-start | bytes 1769476
  114.3 8.7 %copy-start.1 = (f32[384,1536]{1,0:T(8,128)}, f32[384,1536]{1,0:T(8,128)S(1)}, u32[]{:S(2)}) copy-start(f32[384,1536]{1,0:T(8,128)S(1)} %convolution_add_fusion.1) | copy-start | bytes 7077892
  114.4 3.0 %copy-start.9 = (bf16[1,768,2048]{2,1,0:T(8,128)(2,1)S(1)}, bf16[1,768,2048]{2,1,0:T(8,128)(2,1)}, u32[]{:S(2)}) copy-start(bf16[1,768,2048]{2,1,0:T(8,128)(2,1)} %param.8) | copy-start | bytes 9437188
  123.1 131.4 %reduce-scatter.5.cloned.1.call-start = ((), (), s32[]{:S(2)}) async-start(), calls=%async_computation.5 | async-start | bytes 1769472 | tf_op jit(solution)/shard_map/reduce_scatter | solution.py:78
  123.4 27.2 %copy-start.10 = (bf16[1,768,2048]{2,1,0:T(8,128)(2,1)S(1)}, bf16[1,768,2048]{2,1,0:T(8,128)(2,1)}, u32[]{:S(2)}) copy-start(bf16[1,768,2048]{2,1,0:T(8,128)(2,1)} %param.8) | copy-start | bytes 9437188
  123.4 27.2 %collective-permute-start.2 = (bf16[384,1536]{1,0:T(8,128)(2,1)S(1)}, bf16[384,1536]{1,0:T(8,128)(2,1)S(1)}, u32[]{:S(2)}, u32[]{:S(2)}) collective-permute-start(bf16[384,1536]{1,0:T(8,128)(2,1)S(1)} %pad_maximum_fusion.1), channel_id=1, source_target_pairs={{0,16},{16,0},{1,17},{17,1},{2,18},{18,2},{3,19},{19,3},{4,20},{20... | collective-permute-start | bytes 3538952 | tf_op jit(solution)/shard_map/ppermute | solution.py:29
  156.3 1.4 copy-start.3
  164.3 4.5 %copy-start = (f32[1536,2048]{1,0:T(8,128)}, f32[1536,2048]{1,0:T(8,128)S(1)}, u32[]{:S(2)}) copy-start(f32[1536,2048]{1,0:T(8,128)S(1)} %convolution_add_fusion) | copy-start | bytes 37748740
  168.8 1.7 copy-start.2
  168.8 1.7 copy-start.5
  169.3 13.5 %copy-start.8 = (s32[48,8]{0,1:T(8,128)S(1)}, s32[48,8]{0,1:T(8,128)}, u32[]{:S(2)}) copy-start(s32[48,8]{0,1:T(8,128)} %param.5) | copy-start | bytes 4612
  169.3 86.7 %collective-permute-start.7 = (bf16[768,2048]{1,0:T(8,128)(2,1)S(1)}, bf16[768,2048]{1,0:T(8,128)(2,1)}, u32[]{:S(2)}, u32[]{:S(2)}) collective-permute-start(bf16[768,2048]{1,0:T(8,128)(2,1)S(1)} %slice.52), channel_id=1, source_target_pairs={{0,1},{1,0},{2,3},{3,2},{4,5},{5,4},{6,7},{7,6},{8,9},{9,8},{10,11... | collective-permute-start | bytes 9437192 | tf_op jit(solution)/shard_map/ppermute | solution.py:32
  172.1 11.2 %collective-permute-start.6 = (bf16[576,768]{1,0:T(8,128)(2,1)}, bf16[576,768]{1,0:T(8,128)(2,1)}, u32[]{:S(2)}, u32[]{:S(2)}) collective-permute-start(bf16[576,768]{1,0:T(8,128)(2,1)} %convolution_convert_fusion.3), channel_id=1, source_target_pairs={{0,1},{1,0},{2,3},{3,2},{4,5},{5,4},{6,7},{7,6},{8,9},{9,8},{10,11... | collective-permute-start | bytes 2654216 | tf_op jit(solution)/shard_map/ppermute | solution.py:32
  254.5 9.4 %collective-permute-start.3 = (bf16[48,2048]{1,0:T(8,128)(2,1)}, bf16[48,2048]{1,0:T(8,128)(2,1)S(1)}, u32[]{:S(2)}, u32[]{:S(2)}) collective-permute-start(bf16[48,2048]{1,0:T(8,128)(2,1)} %bitcast.67), channel_id=1, source_target_pairs={{0,16},{16,0},{1,17},{17,1},{2,18},{18,2},{3,19},{19,3},{4,20},{20... | collective-permute-start | bytes 589832 | tf_op jit(solution)/shard_map/ppermute | solution.py:29
  264.0 0.7 copy-start.6
Sparse Core Ops, SparseCore 0:
  17.6 45.6 all-gather.6
  65.5 42.7 all-gather.4
  123.2 63.7 reduce-scatter.2
  190.7 63.8 reduce-scatter.4

commit v4 on v2

v4 whole, which is shorter than its diff:
```python
import functools

import jax
import jax.numpy as jnp
import numpy as np
from jax import lax
from jax.experimental import pallas as pl
from jax.experimental.pallas import tpu as pltpu
from jax.sharding import PartitionSpec as P

VMEM_BYTES = 48 * 1024 * 1024


def dot(a, b, ca, cb):
    return lax.dot_general(a, b, (((ca,), (cb,)), ((), ())), preferred_element_type=jnp.float32)


def after(value, *done):
    return lax.optimization_barrier((value, *done))[0]


def chip_ring(mesh):
    chips = mesh.shape["expert"] // 2
    devices = mesh.devices.reshape(mesh.shape["dp"], -1)
    if not hasattr(devices[0, 0], "coords"):
        return list(range(chips))
    at = [tuple(devices[0, 2 * chip].coords)[1:] for chip in range(chips)]
    rows = max(z for _, z in at) + 1
    cols = max(y for y, _ in at) + 1
    if rows * cols != chips or rows % 2:
        return list(range(chips))
    walk = [(0, z) for z in range(rows)]
    for step, z in enumerate(reversed(range(rows))):
        span = range(1, cols)
        walk += [(y, z) for y in (span if step % 2 == 0 else reversed(span))]
    return [at.index(place) for place in walk]


def back_kernel(n_blocks, *refs):
    blocks, w_ref, out_ref = refs[:n_blocks], refs[n_blocks], refs[n_blocks + 1]
    n_dp, tok, _ = blocks[0].shape
    for d in range(n_dp):
        rows = jnp.concatenate([block[d] for block in blocks], axis=0)
        out_ref[d] = dot(rows, w_ref[...], 1, 1).astype(jnp.bfloat16)


def back_product(blocks, weights):
    n_dp, tok, width = blocks[0].shape
    ff2 = weights.shape[0]
    rows = len(blocks) * tok
    tile = 256
    return pl.pallas_call(
        functools.partial(back_kernel, len(blocks)),
        grid=(ff2 // tile,),
        in_specs=[
            pl.BlockSpec((n_dp, tok, width), lambda i: (0, 0, 0), pipeline_mode=pl.Buffered(1))
            for _ in blocks
        ]
        + [pl.BlockSpec((tile, width), lambda i: (i, 0))],
        out_specs=pl.BlockSpec((n_dp, rows, tile), lambda i: (0, 0, i)),
        out_shape=jax.ShapeDtypeStruct((n_dp, rows, ff2), jnp.bfloat16),
        compiler_params=pltpu.CompilerParams(vmem_limit_bytes=VMEM_BYTES),
        cost_estimate=pl.CostEstimate(
            flops=2 * n_dp * rows * width * ff2,
            bytes_accessed=2 * (n_dp * rows * (width + ff2) + ff2 * width),
            transcendentals=0,
        ),
        name="back_product",
    )(*blocks, weights)


def weight_kernel(n_blocks, n_dp, *refs):
    blocks, held = refs[:n_blocks], refs[n_blocks : n_blocks + n_dp]
    own_ref, other_ref = refs[n_blocks + n_dp :]
    ff = own_ref.shape[0]
    own, other = None, None
    for d in range(n_dp):
        rows = jnp.concatenate([block[d] for block in blocks], axis=0)
        mine = dot(held[d][:ff, :], rows, 1, 0)
        theirs = dot(held[d][ff:, :], rows, 1, 0)
        own = mine if own is None else own + mine
        other = theirs if other is None else other + theirs
    own_ref[...] = own
    other_ref[...] = other.astype(jnp.bfloat16)


def weight_product(blocks, helds):
    n_dp, tok, width = blocks[0].shape
    ff2, rows = helds[0].shape
    tile = 512
    return pl.pallas_call(
        functools.partial(weight_kernel, len(blocks), n_dp),
        grid=(width // tile,),
        in_specs=[pl.BlockSpec((n_dp, tok, tile), lambda i: (0, 0, i)) for _ in blocks]
        + [
            pl.BlockSpec((ff2, rows), lambda i: (0, 0), pipeline_mode=pl.Buffered(1))
            for _ in helds
        ],
        out_specs=[pl.BlockSpec((ff2 // 2, tile), lambda i: (0, i))] * 2,
        out_shape=[
            jax.ShapeDtypeStruct((ff2 // 2, width), jnp.float32),
            jax.ShapeDtypeStruct((ff2 // 2, width), jnp.bfloat16),
        ],
        compiler_params=pltpu.CompilerParams(vmem_limit_bytes=VMEM_BYTES),
        cost_estimate=pl.CostEstimate(
            flops=2 * n_dp * rows * width * ff2,
            bytes_accessed=2 * n_dp * rows * (width + ff2) + 3 * ff2 * width,
            transcendentals=0,
        ),
        name="weight_product",
    )(*blocks, *helds)


def body(ring):
    chips = len(ring)
    half = chips // 2
    offsets = [0]
    for step in range(1, half):
        offsets += [-step, step]
    offsets.append(half)
    place_of = {chip: at for at, chip in enumerate(ring)}
    order_table = np.asarray(
        [[ring[(place_of[c] + off) % chips] for off in offsets] for c in range(chips)], np.int32
    )
    inverse_table = np.argsort(order_table, axis=1).astype(np.int32)

    def along(step):
        return [
            (2 * ring[at] + core, 2 * ring[(at + step) % chips] + core)
            for at in range(chips)
            for core in range(2)
        ]

    forward, backward = along(1), along(-1)
    sibling = [(e, e ^ 1) for e in range(2 * chips)]
    same_core = [[2 * chip + c for chip in range(chips)] for c in range(2)]

    def shards(expert_ids, route_probs, expert_hidden, down_weight, out_grad):
        tok, top = expert_ids.shape
        n_dp = lax.axis_size("dp")
        n_ex = lax.axis_size("expert")
        cap = expert_hidden.shape[3]
        slots = cap * n_ex
        ff = down_weight.shape[1]
        width = down_weight.shape[2]
        weight = down_weight[0]
        replica = lax.axis_index("dp")
        expert = lax.axis_index("expert")
        core = expert % 2
        rows = chips * tok
        per = n_dp // 2
        groups = [list(range(per)), list(range(per, n_dp))]
        order = lax.dynamic_index_in_dim(jnp.asarray(order_table), expert // 2, 0, keepdims=False)
        inverse = lax.dynamic_index_in_dim(jnp.asarray(inverse_table), expert // 2, 0, keepdims=False)

        def shift(value, step):
            return lax.ppermute(value, "dp", [(i, (i + step) % n_dp) for i in range(n_dp)])

        def ring_send(value, step):
            return lax.ppermute(value, "expert", forward if step > 0 else backward)

        def swap(value):
            return lax.ppermute(value, "expert", sibling)

        def width_shard(d):
            at = ((replica + d) % n_dp) * width
            return lax.dynamic_slice_in_dim(out_grad, at, width, axis=1)

        blocks = {0: jnp.stack([width_shard(0)] + [shift(width_shard(d), d) for d in range(1, n_dp)])}
        for step in range(1, half):
            blocks[-step] = ring_send(blocks[1 - step], 1)
            blocks[step] = ring_send(blocks[step - 1], -1)
        blocks[half] = jnp.concatenate(
            [ring_send(blocks[1 - half][:per], 1), ring_send(blocks[half - 1][per:], -1)], axis=0
        )
        grads = [blocks[off] for off in offsets]

        weights = jnp.concatenate([weight, swap(weight)], axis=0)
        hidden = expert_hidden[0, 0].transpose(1, 0, 2).reshape(slots, ff)
        hiddens = [hidden, swap(hidden)]

        names = expert_ids.T[None] == jnp.arange(n_ex, dtype=jnp.int32)[:, None, None]
        table = jnp.sum(jnp.where(names, route_probs.T[None], 0.0), axis=1)
        table = lax.all_to_all(
            table.reshape(chips, 2, tok), "expert", 0, 0, tiled=True, axis_index_groups=same_core
        )
        table = jnp.where(core == 0, table, table[:, ::-1])[order]
        taken = (table > 0.0).astype(jnp.float32)
        earlier = jnp.tril(jnp.ones((tok, tok), jnp.float32), -1)
        position = jnp.einsum("set,ut->seu", taken, earlier).astype(jnp.int32)
        position = jnp.where(table > 0.0, position, -1)

        slot_c = jnp.arange(slots, dtype=jnp.int32) // n_ex
        slot_s = jnp.arange(slots, dtype=jnp.int32) % n_ex
        here = (2 * order + core)[:, None, None] == slot_s
        picks, helds, prob_rows = [], [], []
        for x in range(2):
            pick = (position[:, x, :, None] == slot_c) & here
            pick = pick.reshape(rows, slots).astype(jnp.bfloat16)
            picks.append(pick)
            helds.append(dot(hiddens[x], pick, 0, 1).astype(jnp.bfloat16))
            prob_rows.append(table[:, x].reshape(1, rows))
        scaled = jnp.concatenate(
            [(helds[x].astype(jnp.float32) * prob_rows[x]).astype(jnp.bfloat16) for x in range(2)],
            axis=0,
        )
        scaleds = [scaled] + [shift(scaled, d) for d in range(1, n_dp)]

        layer_out = jnp.zeros((tok, n_dp * width), jnp.bfloat16)
        for g, group in enumerate(groups):
            parts = [dot(scaleds[d], weights, 0, 0).astype(jnp.bfloat16) for d in group]
            parts = [part.reshape(chips, tok, width) for part in parts]

            def term(off):
                index = offsets.index(off)
                return jnp.stack([part[index] for part in parts])

            total = term(0).astype(jnp.float32)
            for direction in (1, -1):
                first = half if (direction == 1) == (g == 0) else half - 1
                carry = None
                for hop in range(first, 0, -1):
                    value = term(half if hop == half else hop * direction)
                    if carry is not None:
                        value = (value.astype(jnp.float32) + carry.astype(jnp.float32)).astype(jnp.bfloat16)
                    carry = ring_send(value, direction)
                total = total + carry.astype(jnp.float32)
            total = total.astype(jnp.bfloat16)
            for i, d in enumerate(group):
                piece = total[i] if d == 0 else shift(total[i], -d)
                layer_out = lax.dynamic_update_slice_in_dim(
                    layer_out, piece, ((replica + d) % n_dp) * width, axis=1
                )

        backs = back_product(grads, weights)
        back = backs[0].astype(jnp.float32)
        for d in range(1, n_dp):
            back = back + shift(backs[d], -d).astype(jnp.float32)
        spreads, inners = [], []
        for x in range(2):
            mine = back[:, x * ff : (x + 1) * ff]
            inner = jnp.sum(mine * helds[x].T.astype(jnp.float32), axis=1)
            inners.append(inner.reshape(chips, tok))
            mine = (mine * prob_rows[x].reshape(rows, 1)).astype(jnp.bfloat16)
            spreads.append(dot(picks[x], mine, 0, 0).astype(jnp.bfloat16))
        hidden_grad = spreads[0] + swap(spreads[1])
        hidden_grad = hidden_grad.reshape(cap, n_ex, ff).transpose(1, 0, 2)[None, None]

        own, other = weight_product(grads, scaleds)
        weight_grad = own + swap(other).astype(jnp.float32)

        inner = jnp.stack(inners, axis=1)[inverse]
        inner = jnp.where(core == 0, inner, inner[:, ::-1])
        inner = lax.all_to_all(inner, "expert", 0, 0, tiled=True, axis_index_groups=same_core)
        inner = inner.reshape(n_ex, tok)
        mine = expert_ids[:, :, None] == jnp.arange(n_ex, dtype=jnp.int32)
        prob_grad = jnp.sum(jnp.where(mine, inner.T[:, None, :], 0.0), axis=2)
        return (layer_out, prob_grad, hidden_grad, weight_grad[None])

    return shards


def solution(mesh):
    placed = (
        P(("dp", "expert"), None),
        P(("dp", "expert"), None),
        P("dp", "expert", None, None, None),
        P("expert", None, "dp"),
        P(("dp", "expert"), None),
    )
    return jax.shard_map(
        body(chip_ring(mesh)),
        mesh=mesh,
        in_specs=placed,
        out_specs=(
            P(("dp", "expert"), None),
            P(("dp", "expert"), None),
            P("dp", "expert", None, None, None),
            P("expert", None, "dp"),
        ),
        check_vma=False,
    )
```

time: 231 us -> 186 us (0.81)
  blocking collectives: 43 us -> 0 us
  Pallas kernels: 0 us -> 17.7 us
  matrix products: 40.5 us -> 23.3 us
  waiting for transfers between devices: 42.5 us -> 58.9 us
  local copies, waits for them, and re-layouts: 29 us -> 15.8 us
  between operations: 12.9 us -> 1.01 us
  other arithmetic: 19.8 us -> 26.9 us
    all_gather x1 -> x0, blocking collectives: 43 us -> none  [shards(): facts = lax.all_gather(facts, ('dp', 'expert'), axis=0)]
    ppermute x4, waiting for transfers between devices: 1.48 us -> 22.7 us  [shift(): lax.ppermute(value, 'dp', [(i, (i + step) % n_dp) for i in range(n_dp)])]
    dot_general x10 -> x6, matrix products: 40.4 us -> 22.4 us  [dot(): lax.dot_general(a, b, (((ca,), (cb,)), ((), ())), preferred_element_type=...]
    pallas_call x0 -> x2, Pallas kernels: none -> 17.7 us  [the longest x1 9.81 us: weight_product(): pl.pallas_call(functools.partial(weight_kernel, len(blocks), n_dp), grid=...]
    unnamed x53 -> x37, local copies, waits for them, and re-layouts: 16.8 us -> 4.26 us
    convert_element_type x11 -> x8, other arithmetic: 12.8 us -> 2.43 us  [shards(): (value.astype(jnp.float32) + carry.astype(jnp.float32)).astype(jnp.bfloat16)]
    all_to_all x1 -> x2, starting transfers between devices: 2.54 us -> 10.3 us  [the longest x1 6.08 us: shards(): lax.all_to_all(table.reshape(chips, 2, tok), 'expert', 0, 0, tiled=True,...]
    ppermute x28 -> x22, starting transfers between devices: 31.1 us -> 23.5 us  [ring_send(): return lax.ppermute(value, 'expert', forward if step > 0 else backward)]
  transfers between devices with their start and end apart: 51 -> 32, of which waited for: 21 -> 16; matrix products, arithmetic and copies ran while one was open for 36% -> 29% of each run, Pallas kernels for 0% -> 10%
where the time goes in v4:
time: 186 us; the launch traced here: 185 us
  waiting for transfers between devices  58.9 us (32%)
  starting transfers between devices  41.5 us (22%)
  other arithmetic  26.9 us (14%)
  matrix products  23.3 us (13%)
  Pallas kernels  17.7 us (10%)
  local copies, waits for them, and re-layouts  15.8 us (8%)
    ppermute x22, waiting for transfers between devices, ring_send(): return lax.ppermute(value, 'expert', forward if step > 0 else backward)  34.6 us
    ppermute x22, starting transfers between devices, ring_send(): return lax.ppermute(value, 'expert', forward if step > 0 else backward)  23.5 us
    ppermute x4, waiting for transfers between devices, shift(): lax.ppermute(value, 'dp', [(i, (i + step) % n_dp) for i in range(n_dp)])  22.7 us
    dot_general x6, matrix products, dot(): lax.dot_general(a, b, (((ca,), (cb,)), ((), ())), preferred_element_type=...  22.4 us
    pallas_call x1, Pallas kernels, weight_product(): pl.pallas_call(functools.partial(weight_kernel, len(blocks), n_dp), grid=...  9.81 us
    pallas_call x1, Pallas kernels, back_product(): pl.pallas_call(functools.partial(back_kernel, len(blocks)), grid=(ff2 //...  7.89 us
    ppermute x4, starting transfers between devices, shift(): lax.ppermute(value, 'dp', [(i, (i + step) % n_dp) for i in range(n_dp)])  7.19 us
    concatenate x1, other arithmetic, shards(): weights = jnp.concatenate([weight, swap(weight)], axis=0)  6.68 us
  transfers between devices with their start and end apart: 32, of which 16 were waited for; matrix products, arithmetic and copies ran while one was open for 29% of the time, Pallas kernels for 10%

profile of v4, /device:TPU:0, one launch (start us, length us, event | category | flops | bytes accessed | tf_op | source)
XLA Modules:
  0.0 185.1 jit_solution(13992254996991618122)
XLA Ops:
  1.1 1.0 dynamic-slice_bitcast_fusion
  2.2 2.6 %collective-permute-start.18 = (bf16[48,2048]{1,0:T(8,128)(2,1)S(1)}, bf16[48,2048]{1,0:T(8,128)(2,1)S(1)}, u32[]{:S(2)}, u32[]{:S(2)}) collective-permute-start(bf16[48,2048]{1,0:T(8,128)(2,1)S(1)} %get-tuple-element.25), channel_id=1, source_target_pairs={{0,16},{16,0},{1,17},{17,1},{2,18},{18,2},{3,19},{19,3},{4,20},{20... | collective-permute-start | bytes 589832 | tf_op jit(solution)/shard_map/ppermute | solution.py:157
  4.8 5.5 %collective-permute-done.18 = bf16[48,2048]{1,0:T(8,128)(2,1)S(1)} collective-permute-done((bf16[48,2048]{1,0:T(8,128)(2,1)S(1)}, bf16[48,2048]{1,0:T(8,128)(2,1)S(1)}, u32[]{:S(2)}, u32[]{:S(2)}) %collective-permute-start.18) | collective-permute-done | bytes 196640 | tf_op jit(solution)/shard_map/ppermute | solution.py:157
  10.4 1.9 %collective-permute-start.19 = (bf16[2,48,2048]{2,1,0:T(8,128)(2,1)S(1)}, bf16[2,48,2048]{2,1,0:T(8,128)(2,1)S(1)}, u32[]{:S(2)}, u32[]{:S(2)}) collective-permute-start(bf16[2,48,2048]{2,1,0:T(8,128)(2,1)S(1)} %pad_maximum_fusion.2.refs_0_), channel_id=1, source_target_pairs={{0,4},{1,5},{4,8},{5,9},{8,12},{9,13},{12,14},{13,15},{14,10},{15,... | collective-permute-start | bytes 1179656 | tf_op jit(solution)/shard_map/ppermute | solution.py:160
  12.4 1.3 select_reduce_fusion.1
  13.8 6.1 %all-to-all-start = ((f32[8,2,48]{2,1,0:T(2,128)}), f32[8,2,48]{2,1,0:T(2,128)S(1)}, u32[]{:S(2)}, u32[]{:S(2)}) async-start(f32[8,2,48]{2,1,0:T(2,128)} %bitcast.2), calls=%async_computation | async-start | bytes 16384 | tf_op jit(solution)/shard_map/all_to_all | solution.py:184
  19.9 1.4 collective-permute-done.19.refs_1_
  21.3 1.7 collective-permute-start.21
  25.3 6.4 %collective-permute-done.21.refs_3_ = bf16[2,48,2048]{2,1,0:T(8,128)(2,1)S(1)} collective-permute-done((bf16[2,48,2048]{2,1,0:T(8,128)(2,1)S(1)}, bf16[2,48,2048]{2,1,0:T(8,128)(2,1)S(1)}, u32[]{:S(2)}, u32[]{:S(2)}) %collective-permute-start.21) | collective-permute-done | bytes 393248 | tf_op jit(solution)/shard_map/ppermute | solution.py:160
  31.7 1.7 collective-permute-start.23
  35.1 6.3 %collective-permute-done.23.refs_5_ = bf16[2,48,2048]{2,1,0:T(8,128)(2,1)S(1)} collective-permute-done((bf16[2,48,2048]{2,1,0:T(8,128)(2,1)S(1)}, bf16[2,48,2048]{2,1,0:T(8,128)(2,1)S(1)}, u32[]{:S(2)}, u32[]{:S(2)}) %collective-permute-start.23) | collective-permute-done | bytes 393248 | tf_op jit(solution)/shard_map/ppermute | solution.py:160
  41.4 1.6 collective-permute-start.25
  45.4 1.8 collective-permute-done.25
  47.2 3.4 %collective-permute-done.26 = bf16[1,48,2048]{2,1,0:T(8,128)(2,1)S(1)} collective-permute-done((bf16[1,48,2048]{2,1,0:T(8,128)(2,1)S(1)}, bf16[1,48,2048]{2,1,0:T(8,128)(2,1)S(1)}, u32[]{:S(2)}, u32[]{:S(2)}) %collective-permute-start.26) | collective-permute-done | bytes 196640 | tf_op jit(solution)/shard_map/ppermute | solution.py:160
  50.5 6.7 %pad_maximum_fusion.refs_8_ = bf16[1536,2048]{1,0:T(8,128)(2,1)} fusion(bf16[768,2048]{1,0:T(8,128)(2,1)} %collective-permute-done.1, bf16[768,2048]{1,0:T(8,128)(2,1)} %bitcast.146), kind=kLoop, calls=%fused_computation.2 | loop fusion | flops 12582912 | bytes 12582912 | tf_op jit(solution)/shard_map/concatenate | solution.py:178
  57.2 7.9 %back_product.1 = bf16[2,384,1536]{2,1,0:T(8,128)(2,1)S(1)} custom-call(bf16[2,48,2048]{2,1,0:T(8,128)(2,1)S(1)} %pad_maximum_fusion.2.refs_0_, bf16[2,48,2048]{2,1,0:T(8,128)(2,1)S(1)} %collective-permute-done.19.refs_1_, bf16[2,48,2048]{2,1,0:T(8,128)(2,1)S(1)} %collective-permute-done.20.refs_2_, ...), custom_call_target="tpu_custom_call" | custom-call | flops 4831838208 | bytes 11796480 | tf_op jit(solution)/shard_map/back_product/pallas_call | solution.py:52
  65.1 1.2 fusion.47
  66.3 2.4 %copy.32 = bf16[1,384,1536]{1,2,0:T(8,128)(2,1)} copy(bf16[1,384,1536]{2,1,0:T(8,128)(2,1)} %get-tuple-element.13) | data formatting | bytes 2359296
  68.7 1.5 collective-permute-start.27
  70.8 1.4 gather_fusion
  72.2 0.9 fusion.5
  73.6 1.6 compare_and_fusion
  75.9 1.3 mul.60
  78.0 0.8 eq.121
  78.7 1.3 eq.114
  80.1 2.0 %fusion.6 = (bf16[384,576]{1,0:T(8,128)(2,1)}, pred[384,576]{1,0:T(32,128)(4,1)}) fusion(s32[576]{0:T(1024)} %add_select_fusion, s32[384]{0:T(512)S(1)} %eq.121, pred[8,576]{1,0:T(8,128)(4,1)S(1)} %broadcast_compare_fusion, s32[384]{0:T(512)} %eq.114), kind=kLoop, calls=%fused_computation.27 | loop fusion | flops 1105920 | bytes 673536
  82.1 2.9 %convolution_convert_fusion.5 = bf16[384,768]{0,1:T(8,128)(2,1)} fusion(pred[384,576]{1,0:T(8,128)(4,1)} %bitcast.151, bf16[576,768]{1,0:T(8,128)(2,1)} %bitcast.162), kind=kOutput, calls=%fused_computation.17 | convolution fusion | flops 340033536 | bytes 1695744 | tf_op jit(solution)/shard_map/dot_general | solution.py:15
  85.0 1.4 copy.31
  86.4 6.9 %collective-permute-done.27 = bf16[384,1536]{0,1:T(8,128)(2,1)} collective-permute-done((bf16[384,1536]{0,1:T(8,128)(2,1)}, bf16[384,1536]{0,1:T(8,128)(2,1)}, u32[]{:S(2)}, u32[]{:S(2)}) %collective-permute-start.27) | collective-permute-done | bytes 1179680 | tf_op jit(solution)/shard_map/ppermute | solution.py:157
  93.3 1.9 %convert_add_fusion = f32[384,1536]{0,1:T(8,128)S(1)} fusion(bf16[384,1536]{0,1:T(8,128)(2,1)} %collective-permute-done.27, bf16[1,384,1536]{1,2,0:T(8,128)(2,1)} %copy.31), kind=kLoop, calls=%fused_computation.6 | loop fusion | flops 1769472 | bytes 4718592 | tf_op jit(solution)/shard_map/add | solution.py:238
  95.2 3.0 %fusion.2 = (f32[384]{0:T(512)S(1)}, f32[384]{0:T(512)S(1)}, bf16[768,384]{1,0:T(8,128)(2,1)S(1)}, bf16[768,384]{1,0:T(8,128)(2,1)S(1)}) fusion(bf16[384,768]{0,1:T(8,128)(2,1)S(1)} %copy-done.16, f32[384,1536]{0,1:T(8,128)S(1)} %convert_add_fusion, f32[384]{0:T(512)S(1)} %copy-done.15, f32[384]{0:T(512)S(1)} %mul.57, pred[384,576]{1,0:T(32,128)(4,1)S(1)} %copy-done.11, ...), kind=kOutput, calls=%fused_computation.19 | convolution fusion | flops 342981888 | bytes 5240832 | tf_op jit(solution)/shard_map/dot_general | solution.py:15
  98.4 4.6 %convolution_convert_fusion.1 = bf16[384,2048]{1,0:T(8,128)(2,1)S(1)} fusion(bf16[768,384]{1,0:T(8,128)(2,1)S(1)} %get-tuple-element.22, bf16[768,384]{1,0:T(8,128)(2,1)S(1)} %get-tuple-element.23, bf16[768,2048]{1,0:T(8,128)(2,1)} %collective-permute-done.1, bf16[768,2048]{1,0:T(8,128)(2,1)S(1)} %bitcast.148), kind=kOutput, calls=%fused_computation.5 | convolution fusion | flops 2431647744 | bytes 9043968 | tf_op jit(solution)/shard_map/dot_general | solution.py:15
  102.9 0.9 slice_bitcast_fusion.11
  104.2 1.2 collective-permute-start.2
  105.4 1.5 collective-permute-start.9
  108.4 4.2 %all-to-all-start.1 = ((f32[8,2,48]{2,1,0:T(2,128)}), f32[8,2,48]{2,1,0:T(2,128)S(1)}, u32[]{:S(2)}, u32[]{:S(2)}) async-start(f32[8,2,48]{2,1,0:T(2,128)} %bitcast.144), calls=%async_computation.1 | async-start | bytes 16384 | tf_op jit(solution)/shard_map/all_to_all | solution.py:254
  112.6 3.0 %convolution_convert_fusion.2 = bf16[576,768]{1,0:T(8,128)(2,1)} fusion(f32[384,1536]{0,1:T(8,128)} %copy-done.4, f32[384]{0:T(512)} %mul.60, pred[384,576]{1,0:T(32,128)(4,1)} %get-tuple-element.27), kind=kOutput, calls=%fused_computation.13 | convolution fusion | flops 340992000 | bytes 2312192 | tf_op jit(solution)/shard_map/dot_general | solution.py:15
  115.6 2.0 %collective-permute-start.6 = (bf16[1,48,2048]{2,1,0:T(8,128)(2,1)}, bf16[1,48,2048]{2,1,0:T(8,128)(2,1)}, u32[]{:S(2)}, u32[]{:S(2)}) collective-permute-start(bf16[1,48,2048]{2,1,0:T(8,128)(2,1)} %get-tuple-element.21), channel_id=1, source_target_pairs={{0,2},{1,3},{4,0},{5,1},{8,4},{9,5},{12,8},{13,9},{14,12},{15,13},... | collective-permute-start | bytes 589832 | tf_op jit(solution)/shard_map/ppermute | solution.py:160
  117.6 1.5 all-to-all-done.1
  119.1 1.3 select_reduce_fusion
  120.4 1.1 fusion.21
  122.1 6.3 %collective-permute-done.9.refs_9_ = bf16[1536,384]{1,0:T(8,128)(2,1)} collective-permute-done((bf16[1536,384]{1,0:T(8,128)(2,1)S(1)}, bf16[1536,384]{1,0:T(8,128)(2,1)}, u32[]{:S(2)}, u32[]{:S(2)}) %collective-permute-start.9) | collective-permute-done | bytes 1179680 | tf_op jit(solution)/shard_map/ppermute | solution.py:157
  128.5 5.9 %convolution_convert_fusion = bf16[384,2048]{1,0:T(8,128)(2,1)S(1)} fusion(bf16[1536,384]{1,0:T(8,128)(2,1)} %collective-permute-done.9.refs_9_, bf16[768,2048]{1,0:T(8,128)(2,1)} %collective-permute-done.1, bf16[768,2048]{1,0:T(8,128)(2,1)} %bitcast.147), kind=kOutput, calls=%fused_computation.4 | convolution fusion | flops 2429288448 | bytes 9043968 | tf_op jit(solution)/shard_map/dot_general | solution.py:15
  134.4 1.2 collective-permute-start.10
  135.6 1.4 collective-permute-start.4
  137.7 2.4 %collective-permute-done.10 = bf16[1,48,2048]{2,1,0:T(8,128)(2,1)S(1)} collective-permute-done((bf16[1,48,2048]{2,1,0:T(8,128)(2,1)S(1)}, bf16[1,48,2048]{2,1,0:T(8,128)(2,1)S(1)}, u32[]{:S(2)}, u32[]{:S(2)}) %collective-permute-start.10) | collective-permute-done | bytes 196640 | tf_op jit(solution)/shard_map/ppermute | solution.py:160
  140.1 1.2 collective-permute-start.11
  141.3 9.8 %weight_product.1 = (f32[768,2048]{1,0:T(8,128)}, bf16[768,2048]{1,0:T(8,128)(2,1)}) custom-call(bf16[2,48,2048]{2,1,0:T(8,128)(2,1)S(1)} %pad_maximum_fusion.2.refs_0_, bf16[2,48,2048]{2,1,0:T(8,128)(2,1)S(1)} %collective-permute-done.19.refs_1_, bf16[2,48,2048]{2,1,0:T(8,128)(2,1)S(1)} %collective-permute-done.20.refs_2_, ...), custom_call_target="tpu_custom_call" | custom-call | flops 4831838208 | bytes 14942208 | tf_op jit(solution)/shard_map/weight_product/pallas_call | solution.py:91
  151.4 0.9 collective-permute-start.14
  152.3 1.0 fusion.23
  153.3 1.1 collective-permute-start.7
  154.4 1.0 collective-permute-start.5
  155.4 3.7 %collective-permute-done.14 = bf16[1,48,2048]{2,1,0:T(8,128)(2,1)S(1)} collective-permute-done((bf16[1,48,2048]{2,1,0:T(8,128)(2,1)S(1)}, bf16[1,48,2048]{2,1,0:T(8,128)(2,1)S(1)}, u32[]{:S(2)}, u32[]{:S(2)}) %collective-permute-start.14) | collective-permute-done | bytes 196640 | tf_op jit(solution)/shard_map/ppermute | solution.py:160
  159.2 0.9 collective-permute-start.15
  160.1 3.2 %collective-permute-done.7 = bf16[1,48,2048]{2,1,0:T(8,128)(2,1)S(1)} collective-permute-done((bf16[1,48,2048]{2,1,0:T(8,128)(2,1)S(1)}, bf16[1,48,2048]{2,1,0:T(8,128)(2,1)S(1)}, u32[]{:S(2)}, u32[]{:S(2)}) %collective-permute-start.7) | collective-permute-done | bytes 196640 | tf_op jit(solution)/shard_map/ppermute | solution.py:160
  163.4 0.9 collective-permute-start.8
  164.3 3.2 %collective-permute-done.15 = bf16[1,48,2048]{2,1,0:T(8,128)(2,1)S(1)} collective-permute-done((bf16[1,48,2048]{2,1,0:T(8,128)(2,1)S(1)}, bf16[1,48,2048]{2,1,0:T(8,128)(2,1)S(1)}, u32[]{:S(2)}, u32[]{:S(2)}) %collective-permute-start.15) | collective-permute-done | bytes 196640 | tf_op jit(solution)/shard_map/ppermute | solution.py:160
  167.5 1.4 collective-permute-start.12
  169.7 3.1 %fusion = bf16[576,768]{1,0:T(8,128)(2,1)} fusion(bf16[576,768]{1,0:T(8,128)(2,1)} %collective-permute-done.28, bf16[384,576]{1,0:T(8,128)(2,1)S(1)} %copy-done.8, f32[384,1536]{0,1:T(8,128)S(1)} %copy-done.5, f32[384]{0:T(512)S(1)} %copy-done.14), kind=kOutput, calls=%fused_computation.15 | convolution fusion | flops 341213184 | bytes 3442688 | tf_op jit(solution)/shard_map/dot_general | solution.py:15
  172.8 0.9 collective-permute-done.12
  173.7 1.9 %collective-permute-done.16 = bf16[1,48,2048]{2,1,0:T(8,128)(2,1)S(1)} collective-permute-done((bf16[1,48,2048]{2,1,0:T(8,128)(2,1)S(1)}, bf16[1,48,2048]{2,1,0:T(8,128)(2,1)S(1)}, u32[]{:S(2)}, u32[]{:S(2)}) %collective-permute-start.16) | collective-permute-done | bytes 196640 | tf_op jit(solution)/shard_map/ppermute | solution.py:160
  175.6 1.6 collective-permute-start.17
  177.4 4.0 %collective-permute-done.17 = bf16[48,2048]{1,0:T(8,128)(2,1)S(1)} collective-permute-done((bf16[48,2048]{1,0:T(8,128)(2,1)S(1)}, bf16[48,2048]{1,0:T(8,128)(2,1)S(1)}, u32[]{:S(2)}, u32[]{:S(2)}) %collective-permute-start.17) | collective-permute-done | bytes 196640 | tf_op jit(solution)/shard_map/ppermute | solution.py:157
  181.4 3.6 %add_bitcast_fusion = f32[1,768,2048]{2,1,0:T(8,128)} fusion(f32[768,2048]{1,0:T(8,128)S(1)} %copy-done.6, bf16[768,2048]{1,0:T(8,128)(2,1)S(1)} %collective-permute-done.29), kind=kLoop, calls=%fused_computation.3 | loop fusion | flops 3145728 | bytes 15728640 | tf_op jit(solution)/shard_map/broadcast_in_dim | solution.py:258
  (98 shorter events, 14.5 us)
Async XLA Ops:
  0.6 49.9 %collective-permute-start.1 = (bf16[768,2048]{1,0:T(8,128)(2,1)}, bf16[768,2048]{1,0:T(8,128)(2,1)}, u32[]{:S(2)}, u32[]{:S(2)}) collective-permute-start(bf16[768,2048]{1,0:T(8,128)(2,1)} %bitcast.145), channel_id=1, source_target_pairs={{0,1},{1,0},{2,3},{3,2},{4,5},{5,4},{6,7},{7,6},{8,9},{9,8},{10,11... | collective-permute-start | bytes 9437192 | tf_op jit(solution)/shard_map/ppermute | solution.py:163
  2.2 8.1 %collective-permute-start.18 = (bf16[48,2048]{1,0:T(8,128)(2,1)S(1)}, bf16[48,2048]{1,0:T(8,128)(2,1)S(1)}, u32[]{:S(2)}, u32[]{:S(2)}) collective-permute-start(bf16[48,2048]{1,0:T(8,128)(2,1)S(1)} %get-tuple-element.25), channel_id=1, source_target_pairs={{0,16},{16,0},{1,17},{17,1},{2,18},{18,2},{3,19},{19,3},{4,20},{20... | collective-permute-start | bytes 589832 | tf_op jit(solution)/shard_map/ppermute | solution.py:157
  10.4 11.0 %collective-permute-start.19 = (bf16[2,48,2048]{2,1,0:T(8,128)(2,1)S(1)}, bf16[2,48,2048]{2,1,0:T(8,128)(2,1)S(1)}, u32[]{:S(2)}, u32[]{:S(2)}) collective-permute-start(bf16[2,48,2048]{2,1,0:T(8,128)(2,1)S(1)} %pad_maximum_fusion.2.refs_0_), channel_id=1, source_target_pairs={{0,4},{1,5},{4,8},{5,9},{8,12},{9,13},{12,14},{13,15},{14,10},{15,... | collective-permute-start | bytes 1179656 | tf_op jit(solution)/shard_map/ppermute | solution.py:160
  12.2 12.0 %collective-permute-start.20 = (bf16[2,48,2048]{2,1,0:T(8,128)(2,1)S(1)}, bf16[2,48,2048]{2,1,0:T(8,128)(2,1)S(1)}, u32[]{:S(2)}, u32[]{:S(2)}) collective-permute-start(bf16[2,48,2048]{2,1,0:T(8,128)(2,1)S(1)} %pad_maximum_fusion.2.refs_0_), channel_id=1, source_target_pairs={{0,2},{1,3},{4,0},{5,1},{8,4},{9,5},{12,8},{13,9},{14,12},{15,13},... | collective-permute-start | bytes 1179656 | tf_op jit(solution)/shard_map/ppermute | solution.py:160
  13.8 30.4 %all-to-all-start = ((f32[8,2,48]{2,1,0:T(2,128)}), f32[8,2,48]{2,1,0:T(2,128)S(1)}, u32[]{:S(2)}, u32[]{:S(2)}) async-start(f32[8,2,48]{2,1,0:T(2,128)} %bitcast.2), calls=%async_computation | async-start | bytes 16384 | tf_op jit(solution)/shard_map/all_to_all | solution.py:184
  19.9 75.3 %collective-permute-start = (bf16[576,768]{1,0:T(8,128)(2,1)}, bf16[576,768]{1,0:T(8,128)(2,1)}, u32[]{:S(2)}, u32[]{:S(2)}) collective-permute-start(bf16[576,768]{1,0:T(8,128)(2,1)} %bitcast.161), channel_id=1, source_target_pairs={{0,1},{1,0},{2,3},{3,2},{4,5},{5,4},{6,7},{7,6},{8,9},{9,8},{10,11... | collective-permute-start | bytes 2654216 | tf_op jit(solution)/shard_map/ppermute | solution.py:163
  21.3 10.4 %collective-permute-start.21 = (bf16[2,48,2048]{2,1,0:T(8,128)(2,1)S(1)}, bf16[2,48,2048]{2,1,0:T(8,128)(2,1)S(1)}, u32[]{:S(2)}, u32[]{:S(2)}) collective-permute-start(bf16[2,48,2048]{2,1,0:T(8,128)(2,1)S(1)} %collective-permute-done.19.refs_1_), channel_id=1, source_target_pairs={{0,4},{1,5},{4,8},{5,9},{8,12},{9,13},{12,14},{13,15},{14,10},{15,... | collective-permute-start | bytes 1179656 | tf_op jit(solution)/shard_map/ppermute | solution.py:160
  24.3 10.4 %collective-permute-start.22 = (bf16[2,48,2048]{2,1,0:T(8,128)(2,1)S(1)}, bf16[2,48,2048]{2,1,0:T(8,128)(2,1)S(1)}, u32[]{:S(2)}, u32[]{:S(2)}) collective-permute-start(bf16[2,48,2048]{2,1,0:T(8,128)(2,1)S(1)} %collective-permute-done.20.refs_2_), channel_id=1, source_target_pairs={{0,2},{1,3},{4,0},{5,1},{8,4},{9,5},{12,8},{13,9},{14,12},{15,13},... | collective-permute-start | bytes 1179656 | tf_op jit(solution)/shard_map/ppermute | solution.py:160
  31.7 25.5 %copy-start = (bf16[2,48,2048]{2,1,0:T(8,128)(2,1)}, bf16[2,48,2048]{2,1,0:T(8,128)(2,1)S(1)}, u32[]{:S(2)}) copy-start(bf16[2,48,2048]{2,1,0:T(8,128)(2,1)S(1)} %collective-permute-done.21.refs_3_) | copy-start | bytes 1179652
  31.7 9.7 %collective-permute-start.23 = (bf16[2,48,2048]{2,1,0:T(8,128)(2,1)S(1)}, bf16[2,48,2048]{2,1,0:T(8,128)(2,1)S(1)}, u32[]{:S(2)}, u32[]{:S(2)}) collective-permute-start(bf16[2,48,2048]{2,1,0:T(8,128)(2,1)S(1)} %collective-permute-done.21.refs_3_), channel_id=1, source_target_pairs={{0,4},{1,5},{4,8},{5,9},{8,12},{9,13},{12,14},{13,15},{14,10},{15,... | collective-permute-start | bytes 1179656 | tf_op jit(solution)/shard_map/ppermute | solution.py:160
  34.7 22.5 %copy-start.2 = (bf16[2,48,2048]{2,1,0:T(8,128)(2,1)}, bf16[2,48,2048]{2,1,0:T(8,128)(2,1)S(1)}, u32[]{:S(2)}) copy-start(bf16[2,48,2048]{2,1,0:T(8,128)(2,1)S(1)} %collective-permute-done.22.refs_4_) | copy-start | bytes 1179652
  34.7 10.1 %collective-permute-start.24 = (bf16[2,48,2048]{2,1,0:T(8,128)(2,1)S(1)}, bf16[2,48,2048]{2,1,0:T(8,128)(2,1)S(1)}, u32[]{:S(2)}, u32[]{:S(2)}) collective-permute-start(bf16[2,48,2048]{2,1,0:T(8,128)(2,1)S(1)} %collective-permute-done.22.refs_4_), channel_id=1, source_target_pairs={{0,2},{1,3},{4,0},{5,1},{8,4},{9,5},{12,8},{13,9},{14,12},{15,13},... | collective-permute-start | bytes 1179656 | tf_op jit(solution)/shard_map/ppermute | solution.py:160
  41.4 5.7 %collective-permute-start.25 = (bf16[1,48,2048]{2,1,0:T(8,128)(2,1)S(1)}, bf16[1,48,2048]{2,1,0:T(8,128)(2,1)S(1)}, u32[]{:S(2)}, u32[]{:S(2)}) collective-permute-start(bf16[1,48,2048]{2,1,0:T(8,128)(2,1)S(1)} %slice.156), channel_id=1, source_target_pairs={{0,4},{1,5},{4,8},{5,9},{8,12},{9,13},{12,14},{13,15},{14,10},{15,... | collective-permute-start | bytes 589832 | tf_op jit(solution)/shard_map/ppermute | solution.py:160
  44.8 5.7 %collective-permute-start.26 = (bf16[1,48,2048]{2,1,0:T(8,128)(2,1)S(1)}, bf16[1,48,2048]{2,1,0:T(8,128)(2,1)S(1)}, u32[]{:S(2)}, u32[]{:S(2)}) collective-permute-start(bf16[1,48,2048]{2,1,0:T(8,128)(2,1)S(1)} %slice.157), channel_id=1, source_target_pairs={{0,2},{1,3},{4,0},{5,1},{8,4},{9,5},{12,8},{13,9},{14,12},{15,13},... | collective-permute-start | bytes 589832 | tf_op jit(solution)/shard_map/ppermute | solution.py:160
  68.7 24.6 %collective-permute-start.27 = (bf16[384,1536]{0,1:T(8,128)(2,1)}, bf16[384,1536]{0,1:T(8,128)(2,1)}, u32[]{:S(2)}, u32[]{:S(2)}) collective-permute-start(bf16[384,1536]{0,1:T(8,128)(2,1)} %bitcast.149), channel_id=1, source_target_pairs={{0,16},{16,0},{1,17},{17,1},{2,18},{18,2},{3,19},{19,3},{4,20},{20... | collective-permute-start | bytes 3538952 | tf_op jit(solution)/shard_map/ppermute | solution.py:157
  78.0 17.2 %copy-start.13 = (f32[384]{0:T(512)}, f32[384]{0:T(512)S(1)}, u32[]{:S(2)}) copy-start(f32[384]{0:T(512)S(1)} %mul.57) | copy-start | bytes 4612
  86.4 8.8 %copy-start.11 = (pred[384,576]{1,0:T(32,128)(4,1)S(1)}, pred[384,576]{1,0:T(32,128)(4,1)}, u32[]{:S(2)}) copy-start(pred[384,576]{1,0:T(32,128)(4,1)} %get-tuple-element.27) | copy-start | bytes 663556
  86.4 8.8 %copy-start.15 = (f32[384]{0:T(512)S(1)}, f32[384]{0:T(512)}, u32[]{:S(2)}) copy-start(f32[384]{0:T(512)} %mul.60) | copy-start | bytes 4612
  86.4 8.8 %copy-start.16 = (bf16[384,768]{0,1:T(8,128)(2,1)S(1)}, bf16[384,768]{0,1:T(8,128)(2,1)}, u32[]{:S(2)}) copy-start(bf16[384,768]{0,1:T(8,128)(2,1)} %convolution_convert_fusion.5) | copy-start | bytes 1769476
  95.1 3.1 %copy-start.4 = (f32[384,1536]{0,1:T(8,128)}, f32[384,1536]{0,1:T(8,128)S(1)}, u32[]{:S(2)}) copy-start(f32[384,1536]{0,1:T(8,128)S(1)} %convert_add_fusion) | copy-start | bytes 7077892
  95.2 3.2 %copy-start.7 = (bf16[1,768,2048]{2,1,0:T(8,128)(2,1)S(1)}, bf16[1,768,2048]{2,1,0:T(8,128)(2,1)}, u32[]{:S(2)}) copy-start(bf16[1,768,2048]{2,1,0:T(8,128)(2,1)} %param.10) | copy-start | bytes 9437188
  102.9 1.3 copy-start.9
  104.2 16.2 %collective-permute-start.2 = (bf16[1,48,2048]{2,1,0:T(8,128)(2,1)}, bf16[1,48,2048]{2,1,0:T(8,128)(2,1)}, u32[]{:S(2)}, u32[]{:S(2)}) collective-permute-start(bf16[1,48,2048]{2,1,0:T(8,128)(2,1)} %get-tuple-element.20), channel_id=1, source_target_pairs={{0,4},{1,5},{4,8},{5,9},{8,12},{9,13},{12,14},{13,15},{14,10},{15,... | collective-permute-start | bytes 589832 | tf_op jit(solution)/shard_map/ppermute | solution.py:160
  105.4 23.1 %collective-permute-start.9 = (bf16[1536,384]{1,0:T(8,128)(2,1)S(1)}, bf16[1536,384]{1,0:T(8,128)(2,1)}, u32[]{:S(2)}, u32[]{:S(2)}) collective-permute-start(bf16[1536,384]{1,0:T(8,128)(2,1)S(1)} %pad_maximum_fusion.1.refs_8_), channel_id=1, source_target_pairs={{0,16},{16,0},{1,17},{17,1},{2,18},{18,2},{3,19},{19,3},{4,20},{20... | collective-permute-start | bytes 3538952 | tf_op jit(solution)/shard_map/ppermute | solution.py:157
  108.4 10.7 %all-to-all-start.1 = ((f32[8,2,48]{2,1,0:T(2,128)}), f32[8,2,48]{2,1,0:T(2,128)S(1)}, u32[]{:S(2)}, u32[]{:S(2)}) async-start(f32[8,2,48]{2,1,0:T(2,128)} %bitcast.144), calls=%async_computation.1 | async-start | bytes 16384 | tf_op jit(solution)/shard_map/all_to_all | solution.py:254
  115.6 36.7 %collective-permute-start.6 = (bf16[1,48,2048]{2,1,0:T(8,128)(2,1)}, bf16[1,48,2048]{2,1,0:T(8,128)(2,1)}, u32[]{:S(2)}, u32[]{:S(2)}) collective-permute-start(bf16[1,48,2048]{2,1,0:T(8,128)(2,1)} %get-tuple-element.21), channel_id=1, source_target_pairs={{0,2},{1,3},{4,0},{5,1},{8,4},{9,5},{12,8},{13,9},{14,12},{15,13},... | collective-permute-start | bytes 589832 | tf_op jit(solution)/shard_map/ppermute | solution.py:160
  117.6 51.4 %collective-permute-start.28 = (bf16[576,768]{1,0:T(8,128)(2,1)}, bf16[576,768]{1,0:T(8,128)(2,1)}, u32[]{:S(2)}, u32[]{:S(2)}) collective-permute-start(bf16[576,768]{1,0:T(8,128)(2,1)} %convolution_convert_fusion.2), channel_id=1, source_target_pairs={{0,1},{1,0},{2,3},{3,2},{4,5},{5,4},{6,7},{7,6},{8,9},{9,8},{10,11... | collective-permute-start | bytes 2654216 | tf_op jit(solution)/shard_map/ppermute | solution.py:163
  121.5 14.1 %copy-start.10 = (bf16[384,2048]{1,0:T(8,128)(2,1)S(1)}, bf16[384,2048]{1,0:T(8,128)(2,1)}, u32[]{:S(2)}) copy-start(bf16[384,2048]{1,0:T(8,128)(2,1)} %copy-done.9) | copy-start | bytes 4718596
  121.5 19.8 %copy-start.1 = (bf16[2,48,2048]{2,1,0:T(8,128)(2,1)S(1)}, bf16[2,48,2048]{2,1,0:T(8,128)(2,1)}, u32[]{:S(2)}) copy-start(bf16[2,48,2048]{2,1,0:T(8,128)(2,1)} %copy-done) | copy-start | bytes 1179652
  121.5 19.8 %copy-start.3 = (bf16[2,48,2048]{2,1,0:T(8,128)(2,1)S(1)}, bf16[2,48,2048]{2,1,0:T(8,128)(2,1)}, u32[]{:S(2)}) copy-start(bf16[2,48,2048]{2,1,0:T(8,128)(2,1)} %copy-done.2) | copy-start | bytes 1179652
  121.5 14.0 %collective-permute-start.3 = (bf16[1,48,2048]{2,1,0:T(8,128)(2,1)S(1)}, bf16[1,48,2048]{2,1,0:T(8,128)(2,1)S(1)}, u32[]{:S(2)}, u32[]{:S(2)}) collective-permute-start(bf16[1,48,2048]{2,1,0:T(8,128)(2,1)S(1)} %fusion.21), channel_id=1, source_target_pairs={{0,4},{1,5},{4,8},{5,9},{8,12},{9,13},{12,14},{13,15},{14,10},{15,... | collective-permute-start | bytes 589832 | tf_op jit(solution)/shard_map/ppermute | solution.py:160
  134.4 5.7 %collective-permute-start.10 = (bf16[1,48,2048]{2,1,0:T(8,128)(2,1)S(1)}, bf16[1,48,2048]{2,1,0:T(8,128)(2,1)S(1)}, u32[]{:S(2)}, u32[]{:S(2)}) collective-permute-start(bf16[1,48,2048]{2,1,0:T(8,128)(2,1)S(1)} %get-tuple-element.16), channel_id=1, source_target_pairs={{0,4},{1,5},{4,8},{5,9},{8,12},{9,13},{12,14},{13,15},{14,10},{15,... | collective-permute-start | bytes 589832 | tf_op jit(solution)/shard_map/ppermute | solution.py:160
  135.6 16.7 %collective-permute-start.4 = (bf16[1,48,2048]{2,1,0:T(8,128)(2,1)S(1)}, bf16[1,48,2048]{2,1,0:T(8,128)(2,1)S(1)}, u32[]{:S(2)}, u32[]{:S(2)}) collective-permute-start(bf16[1,48,2048]{2,1,0:T(8,128)(2,1)S(1)} %fusion.22), channel_id=1, source_target_pairs={{0,4},{1,5},{4,8},{5,9},{8,12},{9,13},{12,14},{13,15},{14,10},{15,... | collective-permute-start | bytes 589832 | tf_op jit(solution)/shard_map/ppermute | solution.py:160
  137.1 14.1 %collective-permute-start.13 = (bf16[1,48,2048]{2,1,0:T(8,128)(2,1)S(1)}, bf16[1,48,2048]{2,1,0:T(8,128)(2,1)S(1)}, u32[]{:S(2)}, u32[]{:S(2)}) collective-permute-start(bf16[1,48,2048]{2,1,0:T(8,128)(2,1)S(1)} %get-tuple-element.17), channel_id=1, source_target_pairs={{0,2},{1,3},{4,0},{5,1},{8,4},{9,5},{12,8},{13,9},{14,12},{15,13},... | collective-permute-start | bytes 589832 | tf_op jit(solution)/shard_map/ppermute | solution.py:160
  140.1 11.1 %collective-permute-start.11 = (bf16[1,48,2048]{2,1,0:T(8,128)(2,1)S(1)}, bf16[1,48,2048]{2,1,0:T(8,128)(2,1)S(1)}, u32[]{:S(2)}, u32[]{:S(2)}) collective-permute-start(bf16[1,48,2048]{2,1,0:T(8,128)(2,1)S(1)} %fusion.15), channel_id=1, source_target_pairs={{0,4},{1,5},{4,8},{5,9},{8,12},{9,13},{12,14},{13,15},{14,10},{15,... | collective-permute-start | bytes 589832 | tf_op jit(solution)/shard_map/ppermute | solution.py:160
  151.2 18.5 %copy-start.5 = (f32[384,1536]{0,1:T(8,128)S(1)}, f32[384,1536]{0,1:T(8,128)}, u32[]{:S(2)}) copy-start(f32[384,1536]{0,1:T(8,128)} %copy-done.4) | copy-start | bytes 7077892
  151.2 18.5 %copy-start.8 = (bf16[384,576]{1,0:T(8,128)(2,1)S(1)}, bf16[384,576]{1,0:T(8,128)(2,1)}, u32[]{:S(2)}) copy-start(bf16[384,576]{1,0:T(8,128)(2,1)} %get-tuple-element.26) | copy-start | bytes 1327108
  151.2 18.5 %copy-start.14 = (f32[384]{0:T(512)S(1)}, f32[384]{0:T(512)}, u32[]{:S(2)}) copy-start(f32[384]{0:T(512)} %copy-done.13) | copy-start | bytes 4612
  151.2 30.2 %collective-permute-start.29 = (bf16[768,2048]{1,0:T(8,128)(2,1)}, bf16[768,2048]{1,0:T(8,128)(2,1)S(1)}, u32[]{:S(2)}, u32[]{:S(2)}) collective-permute-start(bf16[768,2048]{1,0:T(8,128)(2,1)} %get-tuple-element.7), channel_id=1, source_target_pairs={{0,1},{1,0},{2,3},{3,2},{4,5},{5,4},{6,7},{7,6},{8,9},{9,8},{10,11... | collective-permute-start | bytes 9437192 | tf_op jit(solution)/shard_map/ppermute | solution.py:163
  151.4 7.7 %collective-permute-start.14 = (bf16[1,48,2048]{2,1,0:T(8,128)(2,1)S(1)}, bf16[1,48,2048]{2,1,0:T(8,128)(2,1)S(1)}, u32[]{:S(2)}, u32[]{:S(2)}) collective-permute-start(bf16[1,48,2048]{2,1,0:T(8,128)(2,1)S(1)} %get-tuple-element.15), channel_id=1, source_target_pairs={{0,2},{1,3},{4,0},{5,1},{8,4},{9,5},{12,8},{13,9},{14,12},{15,13},... | collective-permute-start | bytes 589832 | tf_op jit(solution)/shard_map/ppermute | solution.py:160
  153.3 10.0 %collective-permute-start.7 = (bf16[1,48,2048]{2,1,0:T(8,128)(2,1)S(1)}, bf16[1,48,2048]{2,1,0:T(8,128)(2,1)S(1)}, u32[]{:S(2)}, u32[]{:S(2)}) collective-permute-start(bf16[1,48,2048]{2,1,0:T(8,128)(2,1)S(1)} %get-tuple-element.19), channel_id=1, source_target_pairs={{0,2},{1,3},{4,0},{5,1},{8,4},{9,5},{12,8},{13,9},{14,12},{15,13},... | collective-permute-start | bytes 589832 | tf_op jit(solution)/shard_map/ppermute | solution.py:160
  154.4 22.8 %collective-permute-start.5 = (bf16[1,48,2048]{2,1,0:T(8,128)(2,1)S(1)}, bf16[1,48,2048]{2,1,0:T(8,128)(2,1)S(1)}, u32[]{:S(2)}, u32[]{:S(2)}) collective-permute-start(bf16[1,48,2048]{2,1,0:T(8,128)(2,1)S(1)} %get-tuple-element.18), channel_id=1, source_target_pairs={{0,4},{1,5},{4,8},{5,9},{8,12},{9,13},{12,14},{13,15},{14,10},{15,... | collective-permute-start | bytes 589832 | tf_op jit(solution)/shard_map/ppermute | solution.py:160
  159.2 8.4 %collective-permute-start.15 = (bf16[1,48,2048]{2,1,0:T(8,128)(2,1)S(1)}, bf16[1,48,2048]{2,1,0:T(8,128)(2,1)S(1)}, u32[]{:S(2)}, u32[]{:S(2)}) collective-permute-start(bf16[1,48,2048]{2,1,0:T(8,128)(2,1)S(1)} %fusion.13), channel_id=1, source_target_pairs={{0,2},{1,3},{4,0},{5,1},{8,4},{9,5},{12,8},{13,9},{14,12},{15,13},... | collective-permute-start | bytes 589832 | tf_op jit(solution)/shard_map/ppermute | solution.py:160
  163.4 13.9 %collective-permute-start.8 = (bf16[1,48,2048]{2,1,0:T(8,128)(2,1)S(1)}, bf16[1,48,2048]{2,1,0:T(8,128)(2,1)S(1)}, u32[]{:S(2)}, u32[]{:S(2)}) collective-permute-start(bf16[1,48,2048]{2,1,0:T(8,128)(2,1)S(1)} %fusion.20), channel_id=1, source_target_pairs={{0,2},{1,3},{4,0},{5,1},{8,4},{9,5},{12,8},{13,9},{14,12},{15,13},... | collective-permute-start | bytes 589832 | tf_op jit(solution)/shard_map/ppermute | solution.py:160
  167.5 6.1 %collective-permute-start.12 = (bf16[1,48,2048]{2,1,0:T(8,128)(2,1)S(1)}, bf16[1,48,2048]{2,1,0:T(8,128)(2,1)S(1)}, u32[]{:S(2)}, u32[]{:S(2)}) collective-permute-start(bf16[1,48,2048]{2,1,0:T(8,128)(2,1)S(1)} %get-tuple-element.14), channel_id=1, source_target_pairs={{0,4},{1,5},{4,8},{5,9},{8,12},{9,13},{12,14},{13,15},{14,10},{15,... | collective-permute-start | bytes 589832 | tf_op jit(solution)/shard_map/ppermute | solution.py:160
  168.9 12.5 %copy-start.6 = (f32[768,2048]{1,0:T(8,128)S(1)}, f32[768,2048]{1,0:T(8,128)}, u32[]{:S(2)}) copy-start(f32[768,2048]{1,0:T(8,128)} %get-tuple-element.6) | copy-start | bytes 18874372
  169.0 6.6 %collective-permute-start.16 = (bf16[1,48,2048]{2,1,0:T(8,128)(2,1)S(1)}, bf16[1,48,2048]{2,1,0:T(8,128)(2,1)S(1)}, u32[]{:S(2)}, u32[]{:S(2)}) collective-permute-start(bf16[1,48,2048]{2,1,0:T(8,128)(2,1)S(1)} %fusion.14), channel_id=1, source_target_pairs={{0,2},{1,3},{4,0},{5,1},{8,4},{9,5},{12,8},{13,9},{14,12},{15,13},... | collective-permute-start | bytes 589832 | tf_op jit(solution)/shard_map/ppermute | solution.py:160
  175.6 5.7 %collective-permute-start.17 = (bf16[48,2048]{1,0:T(8,128)(2,1)S(1)}, bf16[48,2048]{1,0:T(8,128)(2,1)S(1)}, u32[]{:S(2)}, u32[]{:S(2)}) collective-permute-start(bf16[48,2048]{1,0:T(8,128)(2,1)S(1)} %fusion.28), channel_id=1, source_target_pairs={{0,16},{16,0},{1,17},{17,1},{2,18},{18,2},{3,19},{19,3},{4,20},{20... | collective-permute-start | bytes 589832 | tf_op jit(solution)/shard_map/ppermute | solution.py:157
  181.4 3.7 %copy-start.12 = (bf16[48,4096]{1,0:T(8,128)(2,1)}, bf16[48,4096]{1,0:T(8,128)(2,1)S(1)}, u32[]{:S(2)}) copy-start(bf16[48,4096]{1,0:T(8,128)(2,1)S(1)} %constant_dynamic-update-slice_fusion.2) | copy-start | bytes 1179652

commit v5 on v4

v5 whole, which is shorter than its diff:
```python
import functools

import jax
import jax.numpy as jnp
import numpy as np
from jax import lax
from jax.experimental import pallas as pl
from jax.experimental.pallas import tpu as pltpu
from jax.sharding import PartitionSpec as P

VMEM_BYTES = 48 * 1024 * 1024


def dot(a, b, ca, cb):
    return lax.dot_general(a, b, (((ca,), (cb,)), ((), ())), preferred_element_type=jnp.float32)


def after(value, *done):
    return lax.optimization_barrier((value, *done))[0]


def chip_ring(mesh):
    chips = mesh.shape["expert"] // 2
    devices = mesh.devices.reshape(mesh.shape["dp"], -1)
    if not hasattr(devices[0, 0], "coords"):
        return list(range(chips))
    at = [tuple(devices[0, 2 * chip].coords)[1:] for chip in range(chips)]
    rows = max(z for _, z in at) + 1
    cols = max(y for y, _ in at) + 1
    if rows * cols != chips or rows % 2:
        return list(range(chips))
    walk = [(0, z) for z in range(rows)]
    for step, z in enumerate(reversed(range(rows))):
        span = range(1, cols)
        walk += [(y, z) for y in (span if step % 2 == 0 else reversed(span))]
    return [at.index(place) for place in walk]


def forward_kernel(keep, rows_of, table, hid_own, hid_sib, w_own, w_sib, *refs):
    part, scaled = refs[:2]
    held, index, prob = refs[2:5] if keep else (None, None, None)
    picked, facts = refs[-2:]
    n_ex, tok = table.shape
    chips = n_ex // 2
    slots = hid_own.shape[0]
    rows = chips * tok

    @pl.when(pl.program_id(0) == 0)
    def _():
        for j in range(n_ex):
            facts[j : j + 1, :] = table[pl.ds(rows_of[j], 1), :]
        weights = facts[...]
        taken = (weights > 0.0).astype(jnp.float32)
        row = lax.broadcasted_iota(jnp.int32, (tok, tok), 0)
        col = lax.broadcasted_iota(jnp.int32, (tok, tok), 1)
        position = dot((col < row).astype(jnp.float32), taken, 1, 1).astype(jnp.int32)
        column = lax.dot_general(
            (col == row).astype(jnp.float32),
            weights,
            (((1,), (1,)), ((), ())),
            precision=lax.Precision.HIGHEST,
            preferred_element_type=jnp.float32,
        )
        lane = lax.broadcasted_iota(jnp.int32, (tok, slots), 1)
        for x, hid in enumerate((hid_own, hid_sib)):
            columns = []
            for o in range(chips):
                j = x * chips + o
                here = column[:, j : j + 1]
                slot = jnp.where(here > 0.0, position[:, j : j + 1] * n_ex + rows_of[o], -1)
                picked[x, o * tok : (o + 1) * tok, :] = (lane == slot).astype(jnp.bfloat16)
                columns.append(here)
                if keep:
                    index[o * tok : (o + 1) * tok, x : x + 1] = slot
                    prob[o * tok : (o + 1) * tok, x : x + 1] = here
            found = dot(picked[x], hid[...], 1, 0)
            if keep:
                held[x] = found.astype(jnp.bfloat16)
            scaled[x] = (found * jnp.concatenate(columns, axis=0)).astype(jnp.bfloat16)

    value = dot(scaled[0], w_own[...], 1, 0) + dot(scaled[1], w_sib[...], 1, 0)
    part[...] = value.astype(jnp.bfloat16).reshape(part.shape)


def forward_product(keep, rows_of, table, hid_own, hid_sib, w_own, w_sib):
    n_ex, tok = table.shape
    chips = n_ex // 2
    rows = chips * tok
    slots, ff = hid_own.shape
    width = w_own.shape[1]
    tile = 512
    whole = lambda shape: pl.BlockSpec(shape, lambda i: (0,) * len(shape))
    out_specs = [pl.BlockSpec((chips, tok, tile), lambda i: (0, 0, i)), whole((2, rows, ff))]
    out_shape = [
        jax.ShapeDtypeStruct((chips, tok, width), jnp.bfloat16),
        jax.ShapeDtypeStruct((2, rows, ff), jnp.bfloat16),
    ]
    if keep:
        out_specs += [whole((2, rows, ff)), whole((rows, 2)), whole((rows, 2))]
        out_shape += [
            jax.ShapeDtypeStruct((2, rows, ff), jnp.bfloat16),
            jax.ShapeDtypeStruct((rows, 2), jnp.int32),
            jax.ShapeDtypeStruct((rows, 2), jnp.float32),
        ]
    return pl.pallas_call(
        functools.partial(forward_kernel, keep),
        grid=(width // tile,),
        in_specs=[pl.BlockSpec(memory_space=pltpu.SMEM), whole((n_ex, tok))]
        + [whole((slots, ff))] * 2
        + [pl.BlockSpec((ff, tile), lambda i: (0, i))] * 2,
        out_specs=out_specs,
        out_shape=out_shape,
        scratch_shapes=[
            pltpu.VMEM((2, rows, slots), jnp.bfloat16),
            pltpu.VMEM((n_ex, tok), jnp.float32),
        ],
        compiler_params=pltpu.CompilerParams(vmem_limit_bytes=VMEM_BYTES),
        cost_estimate=pl.CostEstimate(
            flops=4 * rows * ff * (width + slots),
            bytes_accessed=4 * ff * (width + slots) + 2 * rows * (width + 2 * ff),
            transcendentals=0,
        ),
        name="forward_product",
    )(rows_of, table, hid_own, hid_sib, w_own, w_sib)


def gathered(refs, layout, d):
    return jnp.concatenate([refs[where][at] for where, at in (row[d] for row in layout)], axis=0)


def back_kernel(n_refs, layout, *refs):
    blocks, (w_own, w_sib), outs = refs[:n_refs], refs[n_refs : n_refs + 2], refs[n_refs + 2 :]
    for d, out in enumerate(outs):
        rows = gathered(blocks, layout, d)
        out[0] = dot(rows, w_own[...], 1, 1).astype(jnp.bfloat16)
        out[1] = dot(rows, w_sib[...], 1, 1).astype(jnp.bfloat16)


def back_product(blocks, layout, w_own, w_sib):
    n_dp = len(layout[0])
    _, tok, width = blocks[0].shape
    ff = w_own.shape[0]
    rows = len(layout) * tok
    tile = 256
    return pl.pallas_call(
        functools.partial(back_kernel, len(blocks), layout),
        grid=(ff // tile,),
        in_specs=[
            pl.BlockSpec(block.shape, lambda i: (0, 0, 0), pipeline_mode=pl.Buffered(1))
            for block in blocks
        ]
        + [pl.BlockSpec((tile, width), lambda i: (i, 0))] * 2,
        out_specs=[pl.BlockSpec((2, rows, tile), lambda i: (0, 0, i))] * n_dp,
        out_shape=[jax.ShapeDtypeStruct((2, rows, ff), jnp.bfloat16)] * n_dp,
        compiler_params=pltpu.CompilerParams(vmem_limit_bytes=VMEM_BYTES),
        cost_estimate=pl.CostEstimate(
            flops=4 * n_dp * rows * width * ff,
            bytes_accessed=2 * (n_dp * rows * (width + 2 * ff) + 2 * ff * width),
            transcendentals=0,
        ),
        name="back_product",
    )(*blocks, w_own, w_sib)


def spread_kernel(n_parts, n_dp, *refs):
    rows_of, index, prob, held = refs[:4]
    backs = refs[4 : 4 + n_parts * n_dp]
    own, other, inner = refs[4 + n_parts * n_dp :]
    n_ex, tok = inner.shape
    chips = n_ex // 2
    rows, slots = index.shape[0], own.shape[0]
    ones = jnp.ones((8, held.shape[2]), jnp.float32)
    lane = lax.broadcasted_iota(jnp.int32, (rows, slots), 1)
    for x, out in enumerate((own, other)):
        back = None
        for d in range(n_dp):
            pieces = [backs[d * n_parts + i][x] for i in range(n_parts)]
            value = jnp.concatenate(pieces, axis=0).astype(jnp.float32)
            back = value if back is None else back + value
        product = back * held[x].astype(jnp.float32)
        sums = lax.dot_general(
            ones,
            product,
            (((1,), (1,)), ((), ())),
            precision=lax.Precision.HIGHEST,
            preferred_element_type=jnp.float32,
        )
        for o in range(chips):
            inner[pl.ds(rows_of[x * chips + o], 1), :] = sums[:1, o * tok : (o + 1) * tok]
        pick = (lane == index[:, x : x + 1]).astype(jnp.bfloat16)
        mine = (back * prob[:, x : x + 1]).astype(jnp.bfloat16)
        out[...] = dot(pick, mine, 0, 0).astype(jnp.bfloat16)


def spread_product(rows_of, index, prob, held, backs, slots, n_ex):
    n_dp, n_parts = len(backs), len(backs[0])
    _, rows, ff = held.shape
    flat = [part for parts in backs for part in parts]
    vmem = pl.BlockSpec(memory_space=pltpu.VMEM)
    return pl.pallas_call(
        functools.partial(spread_kernel, n_parts, n_dp),
        in_specs=[pl.BlockSpec(memory_space=pltpu.SMEM)] + [vmem] * (3 + len(flat)),
        out_specs=[vmem] * 3,
        out_shape=[
            jax.ShapeDtypeStruct((slots, ff), jnp.bfloat16),
            jax.ShapeDtypeStruct((slots, ff), jnp.bfloat16),
            jax.ShapeDtypeStruct((n_ex, 2 * rows // n_ex), jnp.float32),
        ],
        compiler_params=pltpu.CompilerParams(vmem_limit_bytes=VMEM_BYTES),
        cost_estimate=pl.CostEstimate(
            flops=4 * rows * slots * ff,
            bytes_accessed=4 * (2 + n_dp) * rows * ff,
            transcendentals=0,
        ),
        name="spread_product",
    )(rows_of, index, prob, held, *flat)


def weight_kernel(n_refs, n_dp, layout, *refs):
    blocks, scaleds = refs[:n_refs], refs[n_refs : n_refs + n_dp]
    own, other, turned = refs[n_refs + n_dp :]

    @pl.when(pl.program_id(0) == 0)
    def _():
        for d in range(n_dp):
            for x in range(2):
                turned[d, x] = scaleds[d][x].T

    rows = [gathered(blocks, layout, d) for d in range(n_dp)]
    for x, out in enumerate((own, other)):
        total = dot(turned[0, x], rows[0], 1, 0)
        for d in range(1, n_dp):
            total = total + dot(turned[d, x], rows[d], 1, 0)
        out[...] = total.astype(out.dtype)


def weight_product(blocks, layout, scaleds):
    n_dp = len(scaleds)
    _, tok, width = blocks[0].shape
    _, rows, ff = scaleds[0].shape
    tile = 512 if width >= 2048 else 256
    return pl.pallas_call(
        functools.partial(weight_kernel, len(blocks), n_dp, layout),
        grid=(width // tile,),
        in_specs=[pl.BlockSpec(block.shape[:2] + (tile,), lambda i: (0, 0, i)) for block in blocks]
        + [
            pl.BlockSpec((2, rows, ff), lambda i: (0, 0, 0), pipeline_mode=pl.Buffered(1))
            for _ in scaleds
        ],
        out_specs=[pl.BlockSpec((ff, tile), lambda i: (0, i))] * 2,
        out_shape=[
            jax.ShapeDtypeStruct((ff, width), jnp.float32),
            jax.ShapeDtypeStruct((ff, width), jnp.bfloat16),
        ],
        scratch_shapes=[pltpu.VMEM((n_dp, 2, ff, rows), jnp.bfloat16)],
        compiler_params=pltpu.CompilerParams(vmem_limit_bytes=VMEM_BYTES),
        cost_estimate=pl.CostEstimate(
            flops=4 * n_dp * rows * width * ff,
            bytes_accessed=2 * n_dp * rows * (width + 2 * ff) + 6 * ff * width,
            transcendentals=0,
        ),
        name="weight_product",
    )(*blocks, *scaleds)


def body(ring):
    chips = len(ring)
    half = chips // 2
    offsets = [0]
    for step in range(1, half):
        offsets += [-step, step]
    offsets.append(half)
    place_of = {chip: at for at, chip in enumerate(ring)}
    row_table = np.asarray(
        [
            [2 * ring[(place_of[e // 2] + off) % chips] + (e % 2 ^ x) for x in range(2) for off in offsets]
            for e in range(2 * chips)
        ],
        np.int32,
    )

    def along(step):
        return [
            (2 * ring[at] + core, 2 * ring[(at + step) % chips] + core)
            for at in range(chips)
            for core in range(2)
        ]

    forward, backward = along(1), along(-1)
    sibling = [(e, e ^ 1) for e in range(2 * chips)]
    same_core = [[2 * chip + c for chip in range(chips)] for c in range(2)]

    def shards(expert_ids, route_probs, expert_hidden, down_weight, out_grad):
        tok, top = expert_ids.shape
        n_dp = lax.axis_size("dp")
        n_ex = lax.axis_size("expert")
        cap = expert_hidden.shape[3]
        slots = cap * n_ex
        ff = down_weight.shape[1]
        width = down_weight.shape[2]
        weight = down_weight[0]
        replica = lax.axis_index("dp")
        expert = lax.axis_index("expert")
        per = n_dp // 2
        groups = [list(range(per)), list(range(per, n_dp))]
        rows_of = lax.dynamic_index_in_dim(jnp.asarray(row_table), expert, 0, keepdims=False)

        def shift(value, step):
            return lax.ppermute(value, "dp", [(i, (i + step) % n_dp) for i in range(n_dp)])

        def ring_send(value, step):
            return lax.ppermute(value, "expert", forward if step > 0 else backward)

        def swap(value):
            return lax.ppermute(value, "expert", sibling)

        def width_shard(d):
            at = ((replica + d) % n_dp) * width
            return lax.dynamic_slice_in_dim(out_grad, at, width, axis=1)

        blocks = {0: jnp.stack([width_shard(0)] + [shift(width_shard(d), d) for d in range(1, n_dp)])}
        for step in range(1, half):
            blocks[-step] = ring_send(blocks[1 - step], 1)
            blocks[step] = ring_send(blocks[step - 1], -1)
        last = [ring_send(blocks[1 - half][:per], 1), ring_send(blocks[half - 1][per:], -1)]

        cut = max(1, chips - 3)
        early = [blocks[off] for off in offsets[:cut]]
        late = [blocks[off] for off in offsets[cut:-1]]
        early_layout = [[(i, d) for d in range(n_dp)] for i in range(len(early))]
        late_layout = [[(i, d) for d in range(n_dp)] for i in range(len(late))]
        halves = lambda base: [(base + d // per, d % per) for d in range(n_dp)]
        full_layout = early_layout + [[(len(early) + i, d) for d in range(n_dp)] for i in range(len(late))]
        full_layout = full_layout + [halves(len(early) + len(late))]
        late_layout = late_layout + [halves(len(late))]

        sibling_weight = swap(weight)
        hidden = expert_hidden[0, 0].transpose(1, 0, 2).reshape(slots, ff)
        names = expert_ids.T[None] == jnp.arange(n_ex, dtype=jnp.int32)[:, None, None]
        table = jnp.sum(jnp.where(names, route_probs.T[None], 0.0), axis=1)
        table = lax.all_to_all(
            table.reshape(chips, 2 * tok), "expert", 0, 0, tiled=True, axis_index_groups=same_core
        ).reshape(n_ex, tok)
        tables = [table] + [shift(table, d) for d in range(1, n_dp)]
        hiddens = [hidden] + [shift(hidden, d) for d in range(1, n_dp)]
        hiddens = [(value, swap(value)) for value in hiddens]

        parts, scaleds = [], []
        for d in range(n_dp):
            made = forward_product(d == 0, rows_of, tables[d], *hiddens[d], weight, sibling_weight)
            parts.append(made[0])
            scaleds.append(made[1])
            if d == 0:
                held, index, prob = made[2:]
        layer_out = jnp.zeros((tok, n_dp * width), jnp.bfloat16)
        for g, group in enumerate(groups):

            def term(off):
                at = offsets.index(off)
                return jnp.stack([parts[d][at] for d in group])

            total = term(0).astype(jnp.float32)
            for direction in (1, -1):
                first = half if (direction == 1) == (g == 0) else half - 1
                carry = None
                for hop in range(first, 0, -1):
                    value = term(half if hop == half else hop * direction)
                    if carry is not None:
                        value = (value.astype(jnp.float32) + carry.astype(jnp.float32)).astype(jnp.bfloat16)
                    carry = ring_send(value, direction)
                total = total + carry.astype(jnp.float32)
            total = total.astype(jnp.bfloat16)
            for i, d in enumerate(group):
                piece = total[i] if d == 0 else shift(total[i], -d)
                layer_out = lax.dynamic_update_slice_in_dim(
                    layer_out, piece, ((replica + d) % n_dp) * width, axis=1
                )

        back_early = back_product(early, early_layout, weight, sibling_weight)
        back_late = back_product(late + last, late_layout, weight, sibling_weight)
        backs = [[back_early[0], back_late[0]]]
        for d in range(1, n_dp):
            backs.append([shift(back_early[d], -d), shift(back_late[d], -d)])
        spread, spread_other, inner = spread_product(rows_of, index, prob, held, backs, slots, n_ex)
        hidden_grad = spread + swap(spread_other)
        hidden_grad = hidden_grad.reshape(cap, n_ex, ff).transpose(1, 0, 2)[None, None]

        own, other = weight_product(early + late + last, full_layout, scaleds)
        weight_grad = own + swap(other).astype(jnp.float32)

        inner = lax.all_to_all(
            inner.reshape(chips, 2 * tok), "expert", 0, 0, tiled=True, axis_index_groups=same_core
        ).reshape(n_ex, tok)
        mine = expert_ids[:, :, None] == jnp.arange(n_ex, dtype=jnp.int32)
        prob_grad = jnp.sum(jnp.where(mine, inner.T[:, None, :], 0.0), axis=2)
        return (layer_out, prob_grad, hidden_grad, weight_grad[None])

    return shards


def solution(mesh):
    placed = (
        P(("dp", "expert"), None),
        P(("dp", "expert"), None),
        P("dp", "expert", None, None, None),
        P("expert", None, "dp"),
        P(("dp", "expert"), None),
    )
    return jax.shard_map(
        body(chip_ring(mesh)),
        mesh=mesh,
        in_specs=placed,
        out_specs=(
            P(("dp", "expert"), None),
            P(("dp", "expert"), None),
            P("dp", "expert", None, None, None),
            P("expert", None, "dp"),
        ),
        check_vma=False,
    )
```

time: 186 us -> 172 us (0.925)
  matrix products: 23.3 us -> 0 us
  Pallas kernels: 17.7 us -> 38.8 us
  other arithmetic: 26.9 us -> 17.7 us
  waiting for transfers between devices: 58.9 us -> 66.5 us
  local copies, waits for them, and re-layouts: 15.8 us -> 9.96 us
  starting transfers between devices: 41.5 us -> 37.1 us
    dot_general x7 -> x0, matrix products: 23.3 us -> none  [the longest x6 22.4 us: dot(): lax.dot_general(a, b, (((ca,), (cb,)), ((), ())), preferred_element_type=...]
    pallas_call x2 -> x6, Pallas kernels: 17.7 us -> 38.8 us  [the longest x2 14.4 us: forward_product(): pl.pallas_call(functools.partial(forward_kernel, keep), grid=(width // ti...]
    ppermute x22, waiting for transfers between devices: 34.6 us -> 44.3 us  [ring_send(): return lax.ppermute(value, 'expert', forward if step > 0 else backward)]
    ppermute x4 -> x6, waiting for transfers between devices: 22.7 us -> 14 us  [shift(): lax.ppermute(value, 'dp', [(i, (i + step) % n_dp) for i in range(n_dp)])]
    concatenate x2 -> x0, other arithmetic: 6.8 us -> none  [the longest x1 6.68 us: shards(): weights = jnp.concatenate([weight, swap(weight)], axis=0)]
    all_to_all x2, waiting for transfers between devices: 1.49 us -> 8.19 us  [the longest x1 5.7 us: shards(): lax.all_to_all(table.reshape(chips, 2 * tok), 'expert', 0, 0, tiled=True,...]
    broadcast_in_dim x1, other arithmetic: 3.64 us -> 7.89 us  [shards(): return (layer_out, prob_grad, hidden_grad, weight_grad[None])]
    ppermute x22, starting transfers between devices: 23.5 us -> 20.2 us  [ring_send(): return lax.ppermute(value, 'expert', forward if step > 0 else backward)]
  transfers between devices with their start and end apart: 32 -> 35, of which waited for: 16 -> 15; matrix products, arithmetic and copies ran while one was open for 29% -> 8% of each run, Pallas kernels for 10% -> 23%
where the time goes in v5:
time: 172 us; the launch traced here: 171 us
  waiting for transfers between devices  66.5 us (39%)
  Pallas kernels  38.8 us (23%)
  starting transfers between devices  37.1 us (22%)
  other arithmetic  17.7 us (10%)
  local copies, waits for them, and re-layouts  9.96 us (6%)
    ppermute x22, waiting for transfers between devices, ring_send(): return lax.ppermute(value, 'expert', forward if step > 0 else backward)  44.3 us
    ppermute x22, starting transfers between devices, ring_send(): return lax.ppermute(value, 'expert', forward if step > 0 else backward)  20.2 us
    pallas_call x2, Pallas kernels, forward_product(): pl.pallas_call(functools.partial(forward_kernel, keep), grid=(width // ti...  14.4 us
    ppermute x6, waiting for transfers between devices, shift(): lax.ppermute(value, 'dp', [(i, (i + step) % n_dp) for i in range(n_dp)])  14 us
    pallas_call x2, Pallas kernels, back_product(): pl.pallas_call(functools.partial(back_kernel, len(blocks), layout), grid=...  11.6 us
    pallas_call x1, Pallas kernels, weight_product(): pl.pallas_call(functools.partial(weight_kernel, len(blocks), n_dp, layout...  9.24 us
    broadcast_in_dim x1, other arithmetic, shards(): return (layer_out, prob_grad, hidden_grad, weight_grad[None])  7.89 us
    ppermute x6, starting transfers between devices, shift(): lax.ppermute(value, 'dp', [(i, (i + step) % n_dp) for i in range(n_dp)])  7.03 us
  transfers between devices with their start and end apart: 35, of which 15 were waited for; matrix products, arithmetic and copies ran while one was open for 8% of the time, Pallas kernels for 23%

profile of v5, /device:TPU:0, one launch (start us, length us, event | category | flops | bytes accessed | tf_op | source)
XLA Modules:
  0.0 171.1 jit_solution(3526481913886385594)
XLA Ops:
  0.7 0.5 collective-permute-start.1
  1.2 1.0 dynamic-slice_bitcast_fusion
  2.2 2.7 %collective-permute-start.20 = (bf16[48,2048]{1,0:T(8,128)(2,1)S(1)}, bf16[48,2048]{1,0:T(8,128)(2,1)S(1)}, u32[]{:S(2)}, u32[]{:S(2)}) collective-permute-start(bf16[48,2048]{1,0:T(8,128)(2,1)S(1)} %get-tuple-element.45), channel_id=1, source_target_pairs={{0,16},{16,0},{1,17},{17,1},{2,18},{18,2},{3,19},{19,3},{4,20},{20... | collective-permute-start | bytes 589832 | tf_op jit(solution)/shard_map/ppermute | solution.py:309
  5.0 5.7 %collective-permute-done.20 = bf16[48,2048]{1,0:T(8,128)(2,1)S(1)} collective-permute-done((bf16[48,2048]{1,0:T(8,128)(2,1)S(1)}, bf16[48,2048]{1,0:T(8,128)(2,1)S(1)}, u32[]{:S(2)}, u32[]{:S(2)}) %collective-permute-start.20) | collective-permute-done | bytes 196640 | tf_op jit(solution)/shard_map/ppermute | solution.py:309
  10.7 2.1 %collective-permute-start.22 = (bf16[2,48,2048]{2,1,0:T(8,128)(2,1)S(1)}, bf16[2,48,2048]{2,1,0:T(8,128)(2,1)S(1)}, u32[]{:S(2)}, u32[]{:S(2)}) collective-permute-start(bf16[2,48,2048]{2,1,0:T(8,128)(2,1)S(1)} %pad_maximum_fusion.refs_0_), channel_id=1, source_target_pairs={{0,2},{1,3},{4,0},{5,1},{8,4},{9,5},{12,8},{13,9},{14,12},{15,13},... | collective-permute-start | bytes 1179656 | tf_op jit(solution)/shard_map/ppermute | solution.py:312
  12.9 8.4 %collective-permute-done.22.refs_2_ = bf16[2,48,2048]{2,1,0:T(8,128)(2,1)S(1)} collective-permute-done((bf16[2,48,2048]{2,1,0:T(8,128)(2,1)S(1)}, bf16[2,48,2048]{2,1,0:T(8,128)(2,1)S(1)}, u32[]{:S(2)}, u32[]{:S(2)}) %collective-permute-start.22) | collective-permute-done | bytes 393248 | tf_op jit(solution)/shard_map/ppermute | solution.py:312
  21.3 1.5 collective-permute-start.24
  22.8 0.7 copy-done.14
  24.1 5.4 %collective-permute-done.10.hid_own = bf16[576,768]{1,0:T(8,128)(2,1)} collective-permute-done((bf16[576,768]{1,0:T(8,128)(2,1)}, bf16[576,768]{1,0:T(8,128)(2,1)}, u32[]{:S(2)}, u32[]{:S(2)}) %collective-permute-start.10) | collective-permute-done | bytes 884768 | tf_op jit(solution)/shard_map/ppermute | solution.py:309
  29.4 1.5 collective-permute-done.24.refs_4_
  30.9 1.1 collective-permute-start.26
  32.0 0.7 copy-done.18
  32.8 0.9 collective-permute-start.25
  33.7 7.3 %collective-permute-done.26.refs_1_.refs_6_ = bf16[2,48,2048]{2,1,0:T(8,128)(2,1)S(1)} collective-permute-done((bf16[2,48,2048]{2,1,0:T(8,128)(2,1)S(1)}, bf16[2,48,2048]{2,1,0:T(8,128)(2,1)S(1)}, u32[]{:S(2)}, u32[]{:S(2)}) %collective-permute-start.26) | collective-permute-done | bytes 393248 | tf_op jit(solution)/shard_map/ppermute | solution.py:312
  41.1 1.7 %collective-permute-start.28 = (bf16[1,48,2048]{2,1,0:T(8,128)(2,1)S(1)}, bf16[1,48,2048]{2,1,0:T(8,128)(2,1)S(1)}, u32[]{:S(2)}, u32[]{:S(2)}) collective-permute-start(bf16[1,48,2048]{2,1,0:T(8,128)(2,1)S(1)} %slice.73), channel_id=1, source_target_pairs={{0,2},{1,3},{4,0},{5,1},{8,4},{9,5},{12,8},{13,9},{14,12},{15,13},... | collective-permute-start | bytes 589832 | tf_op jit(solution)/shard_map/ppermute | solution.py:312
  43.7 0.7 all_to_all.12
  44.3 6.0 %all-to-all-start = ((f32[8,1,96]{2,1,0:T(1,128)}), f32[8,1,96]{2,1,0:T(1,128)S(1)}, u32[]{:S(2)}, u32[]{:S(2)}) async-start(f32[8,1,96]{2,1,0:T(1,128)} %bitcast.3), calls=%async_computation | async-start | bytes 8192 | tf_op jit(solution)/shard_map/all_to_all | solution.py:341
  50.3 0.7 fusion.3.rows_of.refs_0_
  51.0 5.7 %all-to-all-done = f32[8,1,96]{2,1,0:T(1,128)S(1)} async-done(((f32[8,1,96]{2,1,0:T(1,128)}), f32[8,1,96]{2,1,0:T(1,128)S(1)}, u32[]{:S(2)}, u32[]{:S(2)}) %all-to-all-start) | async-done | bytes 3104 | tf_op jit(solution)/shard_map/all_to_all | solution.py:341
  56.7 0.6 broadcast.12
  57.3 0.6 reduce.6
  58.0 1.5 collective-permute-start.9
  59.6 2.0 %copy-done = bf16[1,768,2048]{2,1,0:T(8,128)(2,1)S(1)} copy-done((bf16[1,768,2048]{2,1,0:T(8,128)(2,1)S(1)}, bf16[1,768,2048]{2,1,0:T(8,128)(2,1)}, u32[]{:S(2)}) %copy-start) | copy-done | bytes 3145752
  61.5 5.9 %back_product.3 = (bf16[2,144,768]{2,1,0:T(8,128)(2,1)S(1)}, bf16[2,144,768]{2,1,0:T(8,128)(2,1)S(1)}) custom-call(bf16[2,48,2048]{2,1,0:T(8,128)(2,1)S(1)} %collective-permute-done.25.refs_0_.refs_5_, bf16[2,48,2048]{2,1,0:T(8,128)(2,1)S(1)} %collective-permute-done.26.refs_1_.refs_6_, bf16[1,48,2048]{2,1,0:T(8,128)(2,1)S(1)} %collective-permute-done.27.refs_2_.refs_7_, ...), custom_call_target="tpu_custom_call" | custom-call | flops 1811939328 | bytes 8355840 | tf_op jit(solution)/shard_map/back_product/pallas_call | solution.py:145
  67.5 0.6 collective-permute-start.30
  68.1 7.3 %forward_product.3 = (bf16[8,48,2048]{2,1,0:T(8,128)(2,1)S(1)}, bf16[2,384,768]{2,1,0:T(8,128)(2,1)S(1)}) custom-call(s32[16]{0:T(128)S(1)} %fusion.3.rows_of.refs_0_, f32[16,48]{1,0:T(8,128)S(1)} %collective-permute-done.9.table, bf16[576,768]{1,0:T(8,128)(2,1)} %collective-permute-done.10.hid_own, bf16[576,768]{1,0:T(8,128)(2,1)} %collective-permute-done.11.hid_sib, ...), custom_call_target="tpu_custom_call" | custom-call | flops 3095396352 | bytes 10813440 | tf_op jit(solution)/shard_map/forward_product/pallas_call | solution.py:105
  75.5 0.6 collective-permute-start.12
  76.1 1.5 collective-permute-start.15
  77.6 7.1 %forward_product.2 = (bf16[8,48,2048]{2,1,0:T(8,128)(2,1)S(1)}, bf16[2,384,768]{2,1,0:T(8,128)(2,1)S(1)}, bf16[2,384,768]{2,1,0:T(8,128)(2,1)S(1)}, s32[384,2]{1,0:T(8,128)S(1)}, f32[384,2]{1,0:T(8,128)S(1)}) custom-call(s32[16]{0:T(128)S(1)} %fusion.3.rows_of.refs_0_, f32[16,48]{1,0:T(8,128)S(1)} %reshape.34.table, bf16[576,768]{1,0:T(8,128)(2,1)S(1)} %bitcast.36, ...), custom_call_target="tpu_custom_call" | custom-call | flops 3095396352 | bytes 10813440 | tf_op jit(solution)/shard_map/forward_product/pallas_call | solution.py:105
  84.7 0.7 fusion.5
  85.4 0.5 collective-permute-start.2
  86.0 1.5 collective-permute-start.6
  87.5 9.2 %weight_product.1 = (f32[768,2048]{1,0:T(8,128)}, bf16[768,2048]{1,0:T(8,128)(2,1)}) custom-call(bf16[2,48,2048]{2,1,0:T(8,128)(2,1)S(1)} %copy-done.6, bf16[2,48,2048]{2,1,0:T(8,128)(2,1)S(1)} %copy-done.17, bf16[2,48,2048]{2,1,0:T(8,128)(2,1)S(1)} %copy-done.15, bf16[2,48,2048]{2,1,0:T(8,128)(2,1)S(1)} %copy-done.21, bf16[2,48,2048]{2,1,0:T(8,128)(2,1)S(1)} %copy-done.19, ...), custom_call_target="tpu_custom_call" | custom-call | flops 4831838208 | bytes 14942208 | tf_op jit(solution)/shard_map/weight_product/pallas_call | solution.py:242
  96.8 5.7 %back_product.2 = (bf16[2,240,768]{2,1,0:T(8,128)(2,1)S(1)}, bf16[2,240,768]{2,1,0:T(8,128)(2,1)S(1)}) custom-call(bf16[2,48,2048]{2,1,0:T(8,128)(2,1)S(1)} %copy-done.6, bf16[2,48,2048]{2,1,0:T(8,128)(2,1)S(1)} %copy-done.17, bf16[2,48,2048]{2,1,0:T(8,128)(2,1)S(1)} %copy-done.15, bf16[2,48,2048]{2,1,0:T(8,128)(2,1)S(1)} %copy-done.21, ...), custom_call_target="tpu_custom_call" | custom-call | flops 3019898880 | bytes 9732096 | tf_op jit(solution)/shard_map/back_product/pallas_call | solution.py:145
  102.5 1.6 collective-permute-start.29
  104.1 0.6 collective-permute-start.13
  104.9 6.9 %collective-permute-done.13 = bf16[1,48,2048]{2,1,0:T(8,128)(2,1)S(1)} collective-permute-done((bf16[1,48,2048]{2,1,0:T(8,128)(2,1)S(1)}, bf16[1,48,2048]{2,1,0:T(8,128)(2,1)S(1)}, u32[]{:S(2)}, u32[]{:S(2)}) %collective-permute-start.13) | collective-permute-done | bytes 196640 | tf_op jit(solution)/shard_map/ppermute | solution.py:312
  112.3 5.1 %collective-permute-done.3 = bf16[1,48,2048]{2,1,0:T(8,128)(2,1)S(1)} collective-permute-done((bf16[1,48,2048]{2,1,0:T(8,128)(2,1)S(1)}, bf16[1,48,2048]{2,1,0:T(8,128)(2,1)S(1)}, u32[]{:S(2)}, u32[]{:S(2)}) %collective-permute-start.3) | collective-permute-done | bytes 196640 | tf_op jit(solution)/shard_map/ppermute | solution.py:312
  117.5 7.7 %collective-permute-done.16 = bf16[1,48,2048]{2,1,0:T(8,128)(2,1)S(1)} collective-permute-done((bf16[1,48,2048]{2,1,0:T(8,128)(2,1)S(1)}, bf16[1,48,2048]{2,1,0:T(8,128)(2,1)S(1)}, u32[]{:S(2)}, u32[]{:S(2)}) %collective-permute-start.16) | collective-permute-done | bytes 196640 | tf_op jit(solution)/shard_map/ppermute | solution.py:312
  125.6 0.7 add_convert_fusion.2
  126.3 0.7 collective-permute-start.14
  127.0 1.3 collective-permute-start.17
  128.3 3.6 %spread_product.1 = (bf16[576,768]{1,0:T(8,128)(2,1)S(1)}, bf16[576,768]{1,0:T(8,128)(2,1)S(1)}, f32[16,48]{1,0:T(8,128)S(1)}) custom-call(s32[16]{0:T(128)S(1)} %fusion.3.rows_of.refs_0_, s32[384,2]{1,0:T(8,128)S(1)} %get-tuple-element.22.refs_1_, f32[384,2]{1,0:T(8,128)S(1)} %get-tuple-element.23.refs_2_, ...), custom_call_target="tpu_custom_call" | custom-call | flops 679477248 | bytes 4718592 | tf_op jit(solution)/shard_map/spread_product/pallas_call | solution.py:200
  131.9 0.9 copy-done.3
  132.8 0.9 copy-done.13
  133.7 0.7 all_to_all.14
  134.4 3.3 %all-to-all-start.1 = ((f32[8,1,96]{2,1,0:T(1,128)}), f32[8,1,96]{2,1,0:T(1,128)S(1)}, u32[]{:S(2)}, u32[]{:S(2)}) async-start(f32[8,1,96]{2,1,0:T(1,128)} %bitcast.14), calls=%async_computation.1 | async-start | bytes 8192 | tf_op jit(solution)/shard_map/all_to_all | solution.py:391
  137.7 1.8 %add_convert_fusion.9 = (bf16[1,48,2048]{2,1,0:T(8,128)(2,1)S(1)}, bf16[1,48,2048]{2,1,0:T(8,128)(2,1)}) fusion(bf16[1,48,2048]{2,1,0:T(8,128)(2,1)} %collective-permute-done.4, bf16[8,48,2048]{2,1,0:T(8,128)(2,1)S(1)} %get-tuple-element.20, bf16[1,48,2048]{2,1,0:T(8,128)(2,1)} %collective-permute-done.6), kind=kLoop, calls=%fused_computation.11 | loop fusion | flops 786432 | bytes 1179648 | tf_op jit(solution)/shard_map/convert_element_type | solution.py:369
  139.5 1.9 %collective-permute-start.5 = (bf16[1,48,2048]{2,1,0:T(8,128)(2,1)S(1)}, bf16[1,48,2048]{2,1,0:T(8,128)(2,1)}, u32[]{:S(2)}, u32[]{:S(2)}) collective-permute-start(bf16[1,48,2048]{2,1,0:T(8,128)(2,1)S(1)} %get-tuple-element.40), channel_id=1, source_target_pairs={{0,4},{1,5},{4,8},{5,9},{8,12},{9,13},{12,14},{13,15},{14,10},{15,... | collective-permute-start | bytes 589832 | tf_op jit(solution)/shard_map/ppermute | solution.py:312
  141.5 2.5 %all-to-all-done.1 = f32[8,1,96]{2,1,0:T(1,128)S(1)} async-done(((f32[8,1,96]{2,1,0:T(1,128)}), f32[8,1,96]{2,1,0:T(1,128)S(1)}, u32[]{:S(2)}, u32[]{:S(2)}) %all-to-all-start.1) | async-done | bytes 3104 | tf_op jit(solution)/shard_map/all_to_all | solution.py:391
  144.0 0.6 reduce.7
  144.8 0.6 select_reduce_fusion
  145.4 1.0 add_convert_fusion.1
  146.4 1.0 collective-permute-done.7
  147.5 1.0 add_convert_fusion.7
  148.5 2.0 %collective-permute-start.8 = (bf16[1,48,2048]{2,1,0:T(8,128)(2,1)S(1)}, bf16[1,48,2048]{2,1,0:T(8,128)(2,1)S(1)}, u32[]{:S(2)}, u32[]{:S(2)}) collective-permute-start(bf16[1,48,2048]{2,1,0:T(8,128)(2,1)S(1)} %add_convert_fusion.7), channel_id=1, source_target_pairs={{0,2},{1,3},{4,0},{5,1},{8,4},{9,5},{12,8},{13,9},{14,12},{15,13},... | collective-permute-start | bytes 589832 | tf_op jit(solution)/shard_map/ppermute | solution.py:312
  150.5 4.8 %collective-permute-done.18 = bf16[1,48,2048]{2,1,0:T(8,128)(2,1)S(1)} collective-permute-done((bf16[1,48,2048]{2,1,0:T(8,128)(2,1)S(1)}, bf16[1,48,2048]{2,1,0:T(8,128)(2,1)S(1)}, u32[]{:S(2)}, u32[]{:S(2)}) %collective-permute-start.18) | collective-permute-done | bytes 196640 | tf_op jit(solution)/shard_map/ppermute | solution.py:312
  155.3 1.0 fusion.2
  156.3 0.6 collective-permute-start.19
  156.8 1.1 collective-permute-done.8
  158.0 1.0 fusion.1
  159.0 3.0 %collective-permute-done.19 = bf16[48,2048]{1,0:T(8,128)(2,1)S(1)} collective-permute-done((bf16[48,2048]{1,0:T(8,128)(2,1)S(1)}, bf16[48,2048]{1,0:T(8,128)(2,1)S(1)}, u32[]{:S(2)}, u32[]{:S(2)}) %collective-permute-start.19) | collective-permute-done | bytes 196640 | tf_op jit(solution)/shard_map/ppermute | solution.py:309
  162.0 1.1 add.93
  163.2 7.9 %add_bitcast_fusion = f32[1,768,2048]{2,1,0:T(8,128)} fusion(f32[768,2048]{1,0:T(8,128)} %get-tuple-element.34, bf16[768,2048]{1,0:T(8,128)(2,1)} %collective-permute-done.32), kind=kLoop, calls=%fused_computation | loop fusion | flops 3145728 | bytes 15728640 | tf_op jit(solution)/shard_map/broadcast_in_dim | solution.py:396
  (92 shorter events, 3.4 us)
Async XLA Ops:
  0.6 33.1 %copy-start.11 = (bf16[1,1,16,36,768]{4,2,3,1,0:T(8,128)(2,1)S(1)}, bf16[1,1,16,36,768]{4,2,3,1,0:T(8,128)(2,1)}, u32[]{:S(2)}) copy-start(bf16[1,1,16,36,768]{4,2,3,1,0:T(8,128)(2,1)} %param.8) | copy-start | bytes 2654212
  0.6 43.0 %copy-start.23 = (s32[48,8]{0,1:T(8,128)S(1)}, s32[48,8]{0,1:T(8,128)}, u32[]{:S(2)}) copy-start(s32[48,8]{0,1:T(8,128)} %param.6) | copy-start | bytes 4612
  0.7 43.0 %copy-start.24 = (f32[48,8]{0,1:T(8,128)S(1)}, f32[48,8]{0,1:T(8,128)}, u32[]{:S(2)}) copy-start(f32[48,8]{0,1:T(8,128)} %param.7) | copy-start | bytes 4612
  0.7 58.9 %collective-permute-start.1 = (bf16[768,2048]{1,0:T(8,128)(2,1)}, bf16[768,2048]{1,0:T(8,128)(2,1)}, u32[]{:S(2)}, u32[]{:S(2)}) collective-permute-start(bf16[768,2048]{1,0:T(8,128)(2,1)} %bitcast.29), channel_id=1, source_target_pairs={{0,1},{1,0},{2,3},{3,2},{4,5},{5,4},{6,7},{7,6},{8,9},{9,8},{10,11... | collective-permute-start | bytes 9437192 | tf_op jit(solution)/shard_map/ppermute | solution.py:315
  2.2 8.4 %collective-permute-start.20 = (bf16[48,2048]{1,0:T(8,128)(2,1)S(1)}, bf16[48,2048]{1,0:T(8,128)(2,1)S(1)}, u32[]{:S(2)}, u32[]{:S(2)}) collective-permute-start(bf16[48,2048]{1,0:T(8,128)(2,1)S(1)} %get-tuple-element.45), channel_id=1, source_target_pairs={{0,16},{16,0},{1,17},{17,1},{2,18},{18,2},{3,19},{19,3},{4,20},{20... | collective-permute-start | bytes 589832 | tf_op jit(solution)/shard_map/ppermute | solution.py:309
  4.9 24.5 %collective-permute-start.10 = (bf16[576,768]{1,0:T(8,128)(2,1)}, bf16[576,768]{1,0:T(8,128)(2,1)}, u32[]{:S(2)}, u32[]{:S(2)}) collective-permute-start(bf16[576,768]{1,0:T(8,128)(2,1)} %bitcast.34), channel_id=1, source_target_pairs={{0,16},{16,0},{1,17},{17,1},{2,18},{18,2},{3,19},{19,3},{4,20},{20... | collective-permute-start | bytes 2654216 | tf_op jit(solution)/shard_map/ppermute | solution.py:309
  10.7 32.5 %copy-start.5 = (bf16[2,48,2048]{2,1,0:T(8,128)(2,1)}, bf16[2,48,2048]{2,1,0:T(8,128)(2,1)S(1)}, u32[]{:S(2)}) copy-start(bf16[2,48,2048]{2,1,0:T(8,128)(2,1)S(1)} %pad_maximum_fusion.refs_0_) | copy-start | bytes 1179652
  10.7 10.6 %collective-permute-start.22 = (bf16[2,48,2048]{2,1,0:T(8,128)(2,1)S(1)}, bf16[2,48,2048]{2,1,0:T(8,128)(2,1)S(1)}, u32[]{:S(2)}, u32[]{:S(2)}) collective-permute-start(bf16[2,48,2048]{2,1,0:T(8,128)(2,1)S(1)} %pad_maximum_fusion.refs_0_), channel_id=1, source_target_pairs={{0,2},{1,3},{4,0},{5,1},{8,4},{9,5},{12,8},{13,9},{14,12},{15,13},... | collective-permute-start | bytes 1179656 | tf_op jit(solution)/shard_map/ppermute | solution.py:312
  12.8 10.8 %collective-permute-start.21 = (bf16[2,48,2048]{2,1,0:T(8,128)(2,1)S(1)}, bf16[2,48,2048]{2,1,0:T(8,128)(2,1)S(1)}, u32[]{:S(2)}, u32[]{:S(2)}) collective-permute-start(bf16[2,48,2048]{2,1,0:T(8,128)(2,1)S(1)} %pad_maximum_fusion.refs_0_), channel_id=1, source_target_pairs={{0,4},{1,5},{4,8},{5,9},{8,12},{9,13},{12,14},{13,15},{14,10},{15,... | collective-permute-start | bytes 1179656 | tf_op jit(solution)/shard_map/ppermute | solution.py:312
  21.3 9.7 %collective-permute-start.24 = (bf16[2,48,2048]{2,1,0:T(8,128)(2,1)S(1)}, bf16[2,48,2048]{2,1,0:T(8,128)(2,1)S(1)}, u32[]{:S(2)}, u32[]{:S(2)}) collective-permute-start(bf16[2,48,2048]{2,1,0:T(8,128)(2,1)S(1)} %collective-permute-done.22.refs_2_), channel_id=1, source_target_pairs={{0,2},{1,3},{4,0},{5,1},{8,4},{9,5},{12,8},{13,9},{14,12},{15,13},... | collective-permute-start | bytes 1179656 | tf_op jit(solution)/shard_map/ppermute | solution.py:312
  22.8 0.7 copy-start.14
  23.6 43.9 %copy-start.16 = (bf16[2,48,2048]{2,1,0:T(8,128)(2,1)}, bf16[2,48,2048]{2,1,0:T(8,128)(2,1)S(1)}, u32[]{:S(2)}) copy-start(bf16[2,48,2048]{2,1,0:T(8,128)(2,1)S(1)} %collective-permute-done.21.refs_1_) | copy-start | bytes 1179652
  23.6 9.2 %collective-permute-start.23 = (bf16[2,48,2048]{2,1,0:T(8,128)(2,1)S(1)}, bf16[2,48,2048]{2,1,0:T(8,128)(2,1)S(1)}, u32[]{:S(2)}, u32[]{:S(2)}) collective-permute-start(bf16[2,48,2048]{2,1,0:T(8,128)(2,1)S(1)} %collective-permute-done.21.refs_1_), channel_id=1, source_target_pairs={{0,4},{1,5},{4,8},{5,9},{8,12},{9,13},{12,14},{13,15},{14,10},{15,... | collective-permute-start | bytes 1179656 | tf_op jit(solution)/shard_map/ppermute | solution.py:312
  29.4 38.7 %collective-permute-start.11 = (bf16[576,768]{1,0:T(8,128)(2,1)}, bf16[576,768]{1,0:T(8,128)(2,1)}, u32[]{:S(2)}, u32[]{:S(2)}) collective-permute-start(bf16[576,768]{1,0:T(8,128)(2,1)} %collective-permute-done.10.hid_own), channel_id=1, source_target_pairs={{0,1},{1,0},{2,3},{3,2},{4,5},{5,4},{6,7},{7,6},{8,9},{9,8},{10,11... | collective-permute-start | bytes 2654216 | tf_op jit(solution)/shard_map/ppermute | solution.py:315
  30.9 10.1 %collective-permute-start.26 = (bf16[2,48,2048]{2,1,0:T(8,128)(2,1)S(1)}, bf16[2,48,2048]{2,1,0:T(8,128)(2,1)S(1)}, u32[]{:S(2)}, u32[]{:S(2)}) collective-permute-start(bf16[2,48,2048]{2,1,0:T(8,128)(2,1)S(1)} %collective-permute-done.24.refs_4_), channel_id=1, source_target_pairs={{0,2},{1,3},{4,0},{5,1},{8,4},{9,5},{12,8},{13,9},{14,12},{15,13},... | collective-permute-start | bytes 1179656 | tf_op jit(solution)/shard_map/ppermute | solution.py:312
  32.0 0.8 copy-start.18
  32.8 34.7 %copy-start.20 = (bf16[2,48,2048]{2,1,0:T(8,128)(2,1)}, bf16[2,48,2048]{2,1,0:T(8,128)(2,1)S(1)}, u32[]{:S(2)}) copy-start(bf16[2,48,2048]{2,1,0:T(8,128)(2,1)S(1)} %collective-permute-done.23.refs_3_) | copy-start | bytes 1179652
  32.8 10.4 %collective-permute-start.25 = (bf16[2,48,2048]{2,1,0:T(8,128)(2,1)S(1)}, bf16[2,48,2048]{2,1,0:T(8,128)(2,1)S(1)}, u32[]{:S(2)}, u32[]{:S(2)}) collective-permute-start(bf16[2,48,2048]{2,1,0:T(8,128)(2,1)S(1)} %collective-permute-done.23.refs_3_), channel_id=1, source_target_pairs={{0,4},{1,5},{4,8},{5,9},{8,12},{9,13},{12,14},{13,15},{14,10},{15,... | collective-permute-start | bytes 1179656 | tf_op jit(solution)/shard_map/ppermute | solution.py:312
  33.7 43.9 %collective-permute-start = (bf16[576,768]{1,0:T(8,128)(2,1)S(1)}, bf16[576,768]{1,0:T(8,128)(2,1)}, u32[]{:S(2)}, u32[]{:S(2)}) collective-permute-start(bf16[576,768]{1,0:T(8,128)(2,1)S(1)} %bitcast.35), channel_id=1, source_target_pairs={{0,1},{1,0},{2,3},{3,2},{4,5},{5,4},{6,7},{7,6},{8,9},{9,8},{10,11... | collective-permute-start | bytes 2654216 | tf_op jit(solution)/shard_map/ppermute | solution.py:315
  41.1 17.0 %collective-permute-start.28 = (bf16[1,48,2048]{2,1,0:T(8,128)(2,1)S(1)}, bf16[1,48,2048]{2,1,0:T(8,128)(2,1)S(1)}, u32[]{:S(2)}, u32[]{:S(2)}) collective-permute-start(bf16[1,48,2048]{2,1,0:T(8,128)(2,1)S(1)} %slice.73), channel_id=1, source_target_pairs={{0,2},{1,3},{4,0},{5,1},{8,4},{9,5},{12,8},{13,9},{14,12},{15,13},... | collective-permute-start | bytes 589832 | tf_op jit(solution)/shard_map/ppermute | solution.py:312
  43.2 24.2 %copy-start.1 = (bf16[2,48,2048]{2,1,0:T(8,128)(2,1)}, bf16[2,48,2048]{2,1,0:T(8,128)(2,1)S(1)}, u32[]{:S(2)}) copy-start(bf16[2,48,2048]{2,1,0:T(8,128)(2,1)S(1)} %collective-permute-done.25.refs_0_.refs_5_) | copy-start | bytes 1179652
  43.2 16.3 %collective-permute-start.27 = (bf16[1,48,2048]{2,1,0:T(8,128)(2,1)S(1)}, bf16[1,48,2048]{2,1,0:T(8,128)(2,1)S(1)}, u32[]{:S(2)}, u32[]{:S(2)}) collective-permute-start(bf16[1,48,2048]{2,1,0:T(8,128)(2,1)S(1)} %slice.72), channel_id=1, source_target_pairs={{0,4},{1,5},{4,8},{5,9},{8,12},{9,13},{12,14},{13,15},{14,10},{15,... | collective-permute-start | bytes 589832 | tf_op jit(solution)/shard_map/ppermute | solution.py:312
  44.3 12.4 %all-to-all-start = ((f32[8,1,96]{2,1,0:T(1,128)}), f32[8,1,96]{2,1,0:T(1,128)S(1)}, u32[]{:S(2)}, u32[]{:S(2)}) async-start(f32[8,1,96]{2,1,0:T(1,128)} %bitcast.3), calls=%async_computation | async-start | bytes 8192 | tf_op jit(solution)/shard_map/all_to_all | solution.py:341
  58.0 9.4 %copy-start.7 = (bf16[1,48,2048]{2,1,0:T(8,128)(2,1)}, bf16[1,48,2048]{2,1,0:T(8,128)(2,1)S(1)}, u32[]{:S(2)}) copy-start(bf16[1,48,2048]{2,1,0:T(8,128)(2,1)S(1)} %collective-permute-done.28.refs_3_.refs_8_) | copy-start | bytes 589828
  58.0 10.1 %collective-permute-start.9 = (f32[16,48]{1,0:T(8,128)S(1)}, f32[16,48]{1,0:T(8,128)S(1)}, u32[]{:S(2)}, u32[]{:S(2)}) collective-permute-start(f32[16,48]{1,0:T(8,128)S(1)} %reshape.34.table), channel_id=1, source_target_pairs={{0,16},{16,0},{1,17},{17,1},{2,18},{18,2},{3,19},{19,3},{4,20},{20... | collective-permute-start | bytes 9224 | tf_op jit(solution)/shard_map/ppermute | solution.py:309
  59.5 7.9 %copy-start.9 = (bf16[1,48,2048]{2,1,0:T(8,128)(2,1)}, bf16[1,48,2048]{2,1,0:T(8,128)(2,1)S(1)}, u32[]{:S(2)}) copy-start(bf16[1,48,2048]{2,1,0:T(8,128)(2,1)S(1)} %collective-permute-done.27.refs_2_.refs_7_) | copy-start | bytes 589828
  59.5 2.0 %copy-start = (bf16[1,768,2048]{2,1,0:T(8,128)(2,1)S(1)}, bf16[1,768,2048]{2,1,0:T(8,128)(2,1)}, u32[]{:S(2)}) copy-start(bf16[1,768,2048]{2,1,0:T(8,128)(2,1)} %param.9) | copy-start | bytes 9437188
  67.5 10.2 %copy-start.12 = (bf16[1,1,16,36,768]{4,2,3,1,0:T(8,128)(2,1)S(1)}, bf16[1,1,16,36,768]{4,2,3,1,0:T(8,128)(2,1)}, u32[]{:S(2)}) copy-start(bf16[1,1,16,36,768]{4,2,3,1,0:T(8,128)(2,1)} %param.8) | copy-start | bytes 2654212
  67.5 58.8 %collective-permute-start.30 = (bf16[2,144,768]{2,1,0:T(8,128)(2,1)S(1)}, bf16[2,144,768]{2,1,0:T(8,128)(2,1)S(1)}, u32[]{:S(2)}, u32[]{:S(2)}) collective-permute-start(bf16[2,144,768]{2,1,0:T(8,128)(2,1)S(1)} %get-tuple-element.28), channel_id=1, source_target_pairs={{0,16},{16,0},{1,17},{17,1},{2,18},{18,2},{3,19},{19,3},{4,20},{20... | collective-permute-start | bytes 1327112 | tf_op jit(solution)/shard_map/ppermute | solution.py:309
  75.5 27.0 %collective-permute-start.12 = (bf16[1,48,2048]{2,1,0:T(8,128)(2,1)S(1)}, bf16[1,48,2048]{2,1,0:T(8,128)(2,1)S(1)}, u32[]{:S(2)}, u32[]{:S(2)}) collective-permute-start(bf16[1,48,2048]{2,1,0:T(8,128)(2,1)S(1)} %get-tuple-element.38), channel_id=1, source_target_pairs={{0,4},{1,5},{4,8},{5,9},{8,12},{9,13},{12,14},{13,15},{14,10},{15,... | collective-permute-start | bytes 589832 | tf_op jit(solution)/shard_map/ppermute | solution.py:312
  76.0 11.4 %copy-start.2 = (bf16[2,48,2048]{2,1,0:T(8,128)(2,1)S(1)}, bf16[2,48,2048]{2,1,0:T(8,128)(2,1)}, u32[]{:S(2)}) copy-start(bf16[2,48,2048]{2,1,0:T(8,128)(2,1)} %copy-done.1) | copy-start | bytes 1179652
  76.0 11.4 %copy-start.6 = (bf16[2,48,2048]{2,1,0:T(8,128)(2,1)S(1)}, bf16[2,48,2048]{2,1,0:T(8,128)(2,1)}, u32[]{:S(2)}) copy-start(bf16[2,48,2048]{2,1,0:T(8,128)(2,1)} %copy-done.5) | copy-start | bytes 1179652
  76.1 11.4 %copy-start.8 = (bf16[1,48,2048]{2,1,0:T(8,128)(2,1)S(1)}, bf16[1,48,2048]{2,1,0:T(8,128)(2,1)}, u32[]{:S(2)}) copy-start(bf16[1,48,2048]{2,1,0:T(8,128)(2,1)} %copy-done.7) | copy-start | bytes 589828
  76.1 11.4 %copy-start.10 = (bf16[1,48,2048]{2,1,0:T(8,128)(2,1)S(1)}, bf16[1,48,2048]{2,1,0:T(8,128)(2,1)}, u32[]{:S(2)}) copy-start(bf16[1,48,2048]{2,1,0:T(8,128)(2,1)} %copy-done.9) | copy-start | bytes 589828
  76.1 11.4 %copy-start.15 = (bf16[2,48,2048]{2,1,0:T(8,128)(2,1)S(1)}, bf16[2,48,2048]{2,1,0:T(8,128)(2,1)}, u32[]{:S(2)}) copy-start(bf16[2,48,2048]{2,1,0:T(8,128)(2,1)} %copy-done.14) | copy-start | bytes 1179652
  76.1 11.4 %copy-start.17 = (bf16[2,48,2048]{2,1,0:T(8,128)(2,1)S(1)}, bf16[2,48,2048]{2,1,0:T(8,128)(2,1)}, u32[]{:S(2)}) copy-start(bf16[2,48,2048]{2,1,0:T(8,128)(2,1)} %copy-done.16) | copy-start | bytes 1179652
  76.1 11.4 %copy-start.19 = (bf16[2,48,2048]{2,1,0:T(8,128)(2,1)S(1)}, bf16[2,48,2048]{2,1,0:T(8,128)(2,1)}, u32[]{:S(2)}) copy-start(bf16[2,48,2048]{2,1,0:T(8,128)(2,1)} %copy-done.18) | copy-start | bytes 1179652
  76.1 11.4 %copy-start.21 = (bf16[2,48,2048]{2,1,0:T(8,128)(2,1)S(1)}, bf16[2,48,2048]{2,1,0:T(8,128)(2,1)}, u32[]{:S(2)}) copy-start(bf16[2,48,2048]{2,1,0:T(8,128)(2,1)} %copy-done.20) | copy-start | bytes 1179652
  76.1 28.7 %collective-permute-start.15 = (bf16[1,48,2048]{2,1,0:T(8,128)(2,1)S(1)}, bf16[1,48,2048]{2,1,0:T(8,128)(2,1)S(1)}, u32[]{:S(2)}, u32[]{:S(2)}) collective-permute-start(bf16[1,48,2048]{2,1,0:T(8,128)(2,1)S(1)} %get-tuple-element.39), channel_id=1, source_target_pairs={{0,2},{1,3},{4,0},{5,1},{8,4},{9,5},{12,8},{13,9},{14,12},{15,13},... | collective-permute-start | bytes 589832 | tf_op jit(solution)/shard_map/ppermute | solution.py:312
  85.4 18.7 %collective-permute-start.2 = (bf16[1,48,2048]{2,1,0:T(8,128)(2,1)S(1)}, bf16[1,48,2048]{2,1,0:T(8,128)(2,1)S(1)}, u32[]{:S(2)}, u32[]{:S(2)}) collective-permute-start(bf16[1,48,2048]{2,1,0:T(8,128)(2,1)S(1)} %get-tuple-element.42), channel_id=1, source_target_pairs={{0,4},{1,5},{4,8},{5,9},{8,12},{9,13},{12,14},{13,15},{14,10},{15,... | collective-permute-start | bytes 589832 | tf_op jit(solution)/shard_map/ppermute | solution.py:312
  86.0 51.7 %collective-permute-start.6 = (bf16[1,48,2048]{2,1,0:T(8,128)(2,1)}, bf16[1,48,2048]{2,1,0:T(8,128)(2,1)}, u32[]{:S(2)}, u32[]{:S(2)}) collective-permute-start(bf16[1,48,2048]{2,1,0:T(8,128)(2,1)} %get-tuple-element.43), channel_id=1, source_target_pairs={{0,2},{1,3},{4,0},{5,1},{8,4},{9,5},{12,8},{13,9},{14,12},{15,13},... | collective-permute-start | bytes 589832 | tf_op jit(solution)/shard_map/ppermute | solution.py:312
  102.5 24.5 %collective-permute-start.29 = (bf16[2,240,768]{2,1,0:T(8,128)(2,1)S(1)}, bf16[2,240,768]{2,1,0:T(8,128)(2,1)S(1)}, u32[]{:S(2)}, u32[]{:S(2)}) collective-permute-start(bf16[2,240,768]{2,1,0:T(8,128)(2,1)S(1)} %get-tuple-element.27), channel_id=1, source_target_pairs={{0,16},{16,0},{1,17},{17,1},{2,18},{18,2},{3,19},{19,3},{4,20},{20... | collective-permute-start | bytes 2211848 | tf_op jit(solution)/shard_map/ppermute | solution.py:309
  104.1 7.6 %collective-permute-start.13 = (bf16[1,48,2048]{2,1,0:T(8,128)(2,1)S(1)}, bf16[1,48,2048]{2,1,0:T(8,128)(2,1)S(1)}, u32[]{:S(2)}, u32[]{:S(2)}) collective-permute-start(bf16[1,48,2048]{2,1,0:T(8,128)(2,1)S(1)} %add_convert_fusion.5), channel_id=1, source_target_pairs={{0,4},{1,5},{4,8},{5,9},{8,12},{9,13},{12,14},{13,15},{14,10},{15,... | collective-permute-start | bytes 589832 | tf_op jit(solution)/shard_map/ppermute | solution.py:312
  104.8 58.4 %collective-permute-start.32 = (bf16[768,2048]{1,0:T(8,128)(2,1)}, bf16[768,2048]{1,0:T(8,128)(2,1)}, u32[]{:S(2)}, u32[]{:S(2)}) collective-permute-start(bf16[768,2048]{1,0:T(8,128)(2,1)} %get-tuple-element.35), channel_id=1, source_target_pairs={{0,1},{1,0},{2,3},{3,2},{4,5},{5,4},{6,7},{7,6},{8,9},{9,8},{10,11... | collective-permute-start | bytes 9437192 | tf_op jit(solution)/shard_map/ppermute | solution.py:315
  111.7 5.7 %collective-permute-start.3 = (bf16[1,48,2048]{2,1,0:T(8,128)(2,1)S(1)}, bf16[1,48,2048]{2,1,0:T(8,128)(2,1)S(1)}, u32[]{:S(2)}, u32[]{:S(2)}) collective-permute-start(bf16[1,48,2048]{2,1,0:T(8,128)(2,1)S(1)} %add_convert_fusion.11), channel_id=1, source_target_pairs={{0,4},{1,5},{4,8},{5,9},{8,12},{9,13},{12,14},{13,15},{14,10},{15,... | collective-permute-start | bytes 589832 | tf_op jit(solution)/shard_map/ppermute | solution.py:312
  117.4 7.8 %collective-permute-start.16 = (bf16[1,48,2048]{2,1,0:T(8,128)(2,1)S(1)}, bf16[1,48,2048]{2,1,0:T(8,128)(2,1)S(1)}, u32[]{:S(2)}, u32[]{:S(2)}) collective-permute-start(bf16[1,48,2048]{2,1,0:T(8,128)(2,1)S(1)} %get-tuple-element.37), channel_id=1, source_target_pairs={{0,2},{1,3},{4,0},{5,1},{8,4},{9,5},{12,8},{13,9},{14,12},{15,13},... | collective-permute-start | bytes 589832 | tf_op jit(solution)/shard_map/ppermute | solution.py:312
  125.2 12.6 %collective-permute-start.4 = (bf16[1,48,2048]{2,1,0:T(8,128)(2,1)S(1)}, bf16[1,48,2048]{2,1,0:T(8,128)(2,1)}, u32[]{:S(2)}, u32[]{:S(2)}) collective-permute-start(bf16[1,48,2048]{2,1,0:T(8,128)(2,1)S(1)} %add_convert_fusion.10), channel_id=1, source_target_pairs={{0,4},{1,5},{4,8},{5,9},{8,12},{9,13},{12,14},{13,15},{14,10},{15,... | collective-permute-start | bytes 589832 | tf_op jit(solution)/shard_map/ppermute | solution.py:312
  126.3 22.2 %collective-permute-start.14 = (bf16[1,48,2048]{2,1,0:T(8,128)(2,1)S(1)}, bf16[1,48,2048]{2,1,0:T(8,128)(2,1)}, u32[]{:S(2)}, u32[]{:S(2)}) collective-permute-start(bf16[1,48,2048]{2,1,0:T(8,128)(2,1)S(1)} %get-tuple-element.36), channel_id=1, source_target_pairs={{0,4},{1,5},{4,8},{5,9},{8,12},{9,13},{12,14},{13,15},{14,10},{15,... | collective-permute-start | bytes 589832 | tf_op jit(solution)/shard_map/ppermute | solution.py:312
  127.0 18.4 %collective-permute-start.17 = (bf16[1,48,2048]{2,1,0:T(8,128)(2,1)}, bf16[1,48,2048]{2,1,0:T(8,128)(2,1)}, u32[]{:S(2)}, u32[]{:S(2)}) collective-permute-start(bf16[1,48,2048]{2,1,0:T(8,128)(2,1)} %add_convert_fusion.2), channel_id=1, source_target_pairs={{0,2},{1,3},{4,0},{5,1},{8,4},{9,5},{12,8},{13,9},{14,12},{15,13},... | collective-permute-start | bytes 589832 | tf_op jit(solution)/shard_map/ppermute | solution.py:312
  131.9 0.9 copy-start.3
  132.8 0.9 copy-start.13
  134.4 9.6 %all-to-all-start.1 = ((f32[8,1,96]{2,1,0:T(1,128)}), f32[8,1,96]{2,1,0:T(1,128)S(1)}, u32[]{:S(2)}, u32[]{:S(2)}) async-start(f32[8,1,96]{2,1,0:T(1,128)} %bitcast.14), calls=%async_computation.1 | async-start | bytes 8192 | tf_op jit(solution)/shard_map/all_to_all | solution.py:391
  139.5 17.3 %collective-permute-start.5 = (bf16[1,48,2048]{2,1,0:T(8,128)(2,1)S(1)}, bf16[1,48,2048]{2,1,0:T(8,128)(2,1)}, u32[]{:S(2)}, u32[]{:S(2)}) collective-permute-start(bf16[1,48,2048]{2,1,0:T(8,128)(2,1)S(1)} %get-tuple-element.40), channel_id=1, source_target_pairs={{0,4},{1,5},{4,8},{5,9},{8,12},{9,13},{12,14},{13,15},{14,10},{15,... | collective-permute-start | bytes 589832 | tf_op jit(solution)/shard_map/ppermute | solution.py:312
  141.4 6.0 %collective-permute-start.7 = (bf16[1,48,2048]{2,1,0:T(8,128)(2,1)}, bf16[1,48,2048]{2,1,0:T(8,128)(2,1)}, u32[]{:S(2)}, u32[]{:S(2)}) collective-permute-start(bf16[1,48,2048]{2,1,0:T(8,128)(2,1)} %get-tuple-element.41), channel_id=1, source_target_pairs={{0,2},{1,3},{4,0},{5,1},{8,4},{9,5},{12,8},{13,9},{14,12},{15,13},... | collective-permute-start | bytes 589832 | tf_op jit(solution)/shard_map/ppermute | solution.py:312
  145.4 16.7 %collective-permute-start.31 = (bf16[576,768]{1,0:T(8,128)(2,1)}, bf16[576,768]{1,0:T(8,128)(2,1)S(1)}, u32[]{:S(2)}, u32[]{:S(2)}) collective-permute-start(bf16[576,768]{1,0:T(8,128)(2,1)} %copy-done.13), channel_id=1, source_target_pairs={{0,1},{1,0},{2,3},{3,2},{4,5},{5,4},{6,7},{7,6},{8,9},{9,8},{10,11... | collective-permute-start | bytes 2654216 | tf_op jit(solution)/shard_map/ppermute | solution.py:315
  146.4 15.7 %copy-start.4 = (bf16[576,768]{1,0:T(8,128)(2,1)S(1)}, bf16[576,768]{1,0:T(8,128)(2,1)}, u32[]{:S(2)}) copy-start(bf16[576,768]{1,0:T(8,128)(2,1)} %copy-done.3) | copy-start | bytes 2654212
  147.4 7.8 %collective-permute-start.18 = (bf16[1,48,2048]{2,1,0:T(8,128)(2,1)S(1)}, bf16[1,48,2048]{2,1,0:T(8,128)(2,1)S(1)}, u32[]{:S(2)}, u32[]{:S(2)}) collective-permute-start(bf16[1,48,2048]{2,1,0:T(8,128)(2,1)S(1)} %add_convert_fusion.1), channel_id=1, source_target_pairs={{0,2},{1,3},{4,0},{5,1},{8,4},{9,5},{12,8},{13,9},{14,12},{15,13},... | collective-permute-start | bytes 589832 | tf_op jit(solution)/shard_map/ppermute | solution.py:312
  148.5 9.4 %collective-permute-start.8 = (bf16[1,48,2048]{2,1,0:T(8,128)(2,1)S(1)}, bf16[1,48,2048]{2,1,0:T(8,128)(2,1)S(1)}, u32[]{:S(2)}, u32[]{:S(2)}) collective-permute-start(bf16[1,48,2048]{2,1,0:T(8,128)(2,1)S(1)} %add_convert_fusion.7), channel_id=1, source_target_pairs={{0,2},{1,3},{4,0},{5,1},{8,4},{9,5},{12,8},{13,9},{14,12},{15,13},... | collective-permute-start | bytes 589832 | tf_op jit(solution)/shard_map/ppermute | solution.py:312
  156.3 5.7 %collective-permute-start.19 = (bf16[48,2048]{1,0:T(8,128)(2,1)S(1)}, bf16[48,2048]{1,0:T(8,128)(2,1)S(1)}, u32[]{:S(2)}, u32[]{:S(2)}) collective-permute-start(bf16[48,2048]{1,0:T(8,128)(2,1)S(1)} %fusion.2), channel_id=1, source_target_pairs={{0,16},{16,0},{1,17},{17,1},{2,18},{18,2},{3,19},{19,3},{4,20},{20... | collective-permute-start | bytes 589832 | tf_op jit(solution)/shard_map/ppermute | solution.py:309
  162.0 9.1 %copy-start.22 = (bf16[48,4096]{1,0:T(8,128)(2,1)}, bf16[48,4096]{1,0:T(8,128)(2,1)S(1)}, u32[]{:S(2)}) copy-start(bf16[48,4096]{1,0:T(8,128)(2,1)S(1)} %constant_dynamic-update-slice_fusion) | copy-start | bytes 1179652

commit v6 on v5

--- a/solution.py
+++ b/solution.py
@@ -130,10 +130,12 @@
 
 def back_kernel(n_refs, layout, *refs):
     blocks, (w_own, w_sib), outs = refs[:n_refs], refs[n_refs : n_refs + 2], refs[n_refs + 2 :]
-    for d, out in enumerate(outs):
-        rows = gathered(blocks, layout, d)
-        out[0] = dot(rows, w_own[...], 1, 1).astype(jnp.bfloat16)
-        out[1] = dot(rows, w_sib[...], 1, 1).astype(jnp.bfloat16)
+    rows = jnp.concatenate([gathered(blocks, layout, d) for d in range(len(outs))], axis=0)
+    count = outs[0].shape[1]
+    for x, w_ref in enumerate((w_own, w_sib)):
+        value = dot(rows, w_ref[...], 1, 1).astype(jnp.bfloat16)
+        for d, out in enumerate(outs):
+            out[x] = value[d * count : (d + 1) * count]
 
 
 def back_product(blocks, layout, w_own, w_sib):
@@ -217,24 +219,23 @@
 
 
 def weight_kernel(n_refs, n_dp, layout, *refs):
-    blocks, scaleds = refs[:n_refs], refs[n_refs : n_refs + n_dp]
-    own, other, turned = refs[n_refs + n_dp :]
+    blocks, scaleds, more = refs[:n_refs], refs[n_refs : n_refs + n_dp], refs[n_refs + n_dp : -2]
+    out, turned = refs[-2:]
+    count = scaleds[0].shape[1]
 
     @pl.when(pl.program_id(0) == 0)
     def _():
         for d in range(n_dp):
-            for x in range(2):
-                turned[d, x] = scaleds[d][x].T
-
-    rows = [gathered(blocks, layout, d) for d in range(n_dp)]
-    for x, out in enumerate((own, other)):
-        total = dot(turned[0, x], rows[0], 1, 0)
-        for d in range(1, n_dp):
-            total = total + dot(turned[d, x], rows[d], 1, 0)
-        out[...] = total.astype(out.dtype)
-
-
-def weight_product(blocks, layout, scaleds):
+            turned[:, d * count : (d + 1) * count] = scaleds[d][0].T
+
+    rows = jnp.concatenate([gathered(blocks, layout, d) for d in range(n_dp)], axis=0)
+    total = dot(turned[...], rows, 1, 0)
+    for ref in more:
+        total = total + ref[...].astype(jnp.float32)
+    out[...] = total.astype(out.dtype)
+
+
+def weight_product(blocks, layout, scaleds, x, dtype, *more):
     n_dp = len(scaleds)
     _, tok, width = blocks[0].shape
     _, rows, ff = scaleds[0].shape
@@ -244,23 +245,21 @@
         grid=(width // tile,),
         in_specs=[pl.BlockSpec(block.shape[:2] + (tile,), lambda i: (0, 0, i)) for block in blocks]
         + [
-            pl.BlockSpec((2, rows, ff), lambda i: (0, 0, 0), pipeline_mode=pl.Buffered(1))
+            pl.BlockSpec((1, rows, ff), lambda i: (x, 0, 0), pipeline_mode=pl.Buffered(1))
             for _ in scaleds
-        ],
-        out_specs=[pl.BlockSpec((ff, tile), lambda i: (0, i))] * 2,
-        out_shape=[
-            jax.ShapeDtypeStruct((ff, width), jnp.float32),
-            jax.ShapeDtypeStruct((ff, width), jnp.bfloat16),
-        ],
-        scratch_shapes=[pltpu.VMEM((n_dp, 2, ff, rows), jnp.bfloat16)],
+        ]
+        + [pl.BlockSpec((ff, tile), lambda i: (0, i)) for _ in more],
+        out_specs=pl.BlockSpec((ff, tile), lambda i: (0, i)),
+        out_shape=jax.ShapeDtypeStruct((ff, width), dtype),
+        scratch_shapes=[pltpu.VMEM((ff, n_dp * rows), jnp.bfloat16)],
         compiler_params=pltpu.CompilerParams(vmem_limit_bytes=VMEM_BYTES),
         cost_estimate=pl.CostEstimate(
-            flops=4 * n_dp * rows * width * ff,
-            bytes_accessed=2 * n_dp * rows * (width + 2 * ff) + 6 * ff * width,
+            flops=2 * n_dp * rows * width * ff,
+            bytes_accessed=2 * n_dp * rows * (width + ff) + 4 * ff * width,
             transcendentals=0,
         ),
         name="weight_product",
-    )(*blocks, *scaleds)
+    )(*blocks, *scaleds, *more)
 
 
 def body(ring):
@@ -319,10 +318,38 @@
             return lax.dynamic_slice_in_dim(out_grad, at, width, axis=1)
 
         blocks = {0: jnp.stack([width_shard(0)] + [shift(width_shard(d), d) for d in range(1, n_dp)])}
+
+        sibling_weight = swap(weight)
+        hidden = expert_hidden[0, 0].transpose(1, 0, 2).reshape(slots, ff)
+        names = expert_ids.T[None] == jnp.arange(n_ex, dtype=jnp.int32)[:, None, None]
+        table = jnp.sum(jnp.where(names, route_probs.T[None], 0.0), axis=1)
+        table = lax.all_to_all(
+            table.reshape(chips, 2 * tok), "expert", 0, 0, tiled=True, axis_index_groups=same_core
+        ).reshape(n_ex, tok)
+        tables = [table] + [shift(table, d) for d in range(1, n_dp)]
+        hiddens = [hidden] + [shift(hidden, d) for d in range(1, n_dp)]
+
+        parts, scaleds, gate = [], [], (table,)
         for step in range(1, half):
-            blocks[-step] = ring_send(blocks[1 - step], 1)
-            blocks[step] = ring_send(blocks[step - 1], -1)
-        last = [ring_send(blocks[1 - half][:per], 1), ring_send(blocks[half - 1][per:], -1)]
+            sent = blocks[1 - step], blocks[step - 1]
+            if step > 1:
+                sent = after(sent[0], *gate), after(sent[1], *gate)
+            blocks[-step] = ring_send(sent[0], 1)
+            blocks[step] = ring_send(sent[1], -1)
+            arrived = blocks[-step], blocks[step]
+            for d in [step - 1] if step < half - 1 else range(step - 1, n_dp):
+                if d < n_dp:
+                    ours = after(hiddens[d], *parts[-1:])
+                    made = forward_product(
+                        d == 0, rows_of, after(tables[d], *arrived), ours, swap(ours), weight, sibling_weight
+                    )
+                    parts.append(made[0])
+                    scaleds.append(made[1])
+                    gate = (made[0],)
+                    if d == 0:
+                        held, index, prob = made[2:]
+        sent = after(blocks[1 - half][:per], *gate), after(blocks[half - 1][per:], *gate)
+        last = [ring_send(sent[0], 1), ring_send(sent[1], -1)]
 
         cut = max(1, chips - 3)
         early = [blocks[off] for off in offsets[:cut]]
@@ -334,59 +361,76 @@
         full_layout = full_layout + [halves(len(early) + len(late))]
         late_layout = late_layout + [halves(len(late))]
 
-        sibling_weight = swap(weight)
-        hidden = expert_hidden[0, 0].transpose(1, 0, 2).reshape(slots, ff)
-        names = expert_ids.T[None] == jnp.arange(n_ex, dtype=jnp.int32)[:, None, None]
-        table = jnp.sum(jnp.where(names, route_probs.T[None], 0.0), axis=1)
-        table = lax.all_to_all(
-            table.reshape(chips, 2 * tok), "expert", 0, 0, tiled=True, axis_index_groups=same_core
-        ).reshape(n_ex, tok)
-        tables = [table] + [shift(table, d) for d in range(1, n_dp)]
-        hiddens = [hidden] + [shift(hidden, d) for d in range(1, n_dp)]
-        hiddens = [(value, swap(value)) for value in hiddens]
-
-        parts, scaleds = [], []
-        for d in range(n_dp):
-            made = forward_product(d == 0, rows_of, tables[d], *hiddens[d], weight, sibling_weight)
-            parts.append(made[0])
-            scaleds.append(made[1])
-            if d == 0:
-                held, index, prob = made[2:]
+        def term(off, g):
+            at = offsets.index(off)
+            return jnp.stack([parts[d][at] for d in groups[g]])
+
+        carry = {}
+
+        def hop_on(hop, g, done):
+            for direction in (1, -1):
+                if hop == half and (direction == 1) != (g == 0):
+                    continue
+                value = term(half if hop == half else hop * direction, g)
+                if (g, direction) in carry:
+                    value = value.astype(jnp.float32) + carry[g, direction].astype(jnp.float32)
+                    value = value.astype(jnp.bfloat16)
+                carry[g, direction] = ring_send(after(value, *done), direction)
+
+        def carried():
+            return tuple(carry.values())
+
+        hop_on(half, 0, ())
+        hop_on(half, 1, ())
+        hop_on(half - 1, 0, ())
+        back_early = back_product([after(early[0], *parts)] + early[1:], early_layout, weight, sibling_weight)
+        held_up = carried()
+        hop_on(half - 1, 1, (back_early[0],))
+        for hop in range(half - 2, 1, -1):
+            hop_on(hop, 0, (back_early[0],))
+            if hop > 2:
+                hop_on(hop, 1, ())
+        back_late = back_product(
+            [after((late + last)[0], *held_up)] + (late + last)[1:], late_layout, weight, sibling_weight
+        )
+        other = weight_product(
+            [after(early[0], *carried(), back_late[0])] + early[1:] + late + last,
+            full_layout,
+            scaleds,
+            1,
+            jnp.bfloat16,
+        )
+        hop_on(1, 0, (back_late[0],))
+        hop_on(min(2, half - 2), 1, (back_late[0],))
+        backs = [[back_early[0], back_late[0]]]
+        for d in range(1, n_dp):
+            backs.append([shift(back_early[d], -d), shift(back_late[d], -d)])
+        spread, spread_other, inner = spread_product(
+            rows_of, index, after(prob, other), held, backs, slots, n_ex
+        )
+        hop_on(1, 1, (other,))
+
+        weight_grad = weight_product(
+            [after(early[0], spread)] + early[1:] + late + last,
+            full_layout,
+            scaleds,
+            0,
+            jnp.float32,
+            swap(other),
+        )
+        hidden_grad = spread + swap(spread_other)
+        hidden_grad = hidden_grad.reshape(cap, n_ex, ff).transpose(1, 0, 2)[None, None]
+
         layer_out = jnp.zeros((tok, n_dp * width), jnp.bfloat16)
-        for g, group in enumerate(groups):
-
-            def term(off):
-                at = offsets.index(off)
-                return jnp.stack([parts[d][at] for d in group])
-
-            total = term(0).astype(jnp.float32)
-            for direction in (1, -1):
-                first = half if (direction == 1) == (g == 0) else half - 1
-                carry = None
-                for hop in range(first, 0, -1):
-                    value = term(half if hop == half else hop * direction)
-                    if carry is not None:
-                        value = (value.astype(jnp.float32) + carry.astype(jnp.float32)).astype(jnp.bfloat16)
-                    carry = ring_send(value, direction)
-                total = total + carry.astype(jnp.float32)
+        for g in (1, 0):
+            total = term(0, g).astype(jnp.float32)
+            total = total + carry[g, 1].astype(jnp.float32) + carry[g, -1].astype(jnp.float32)
             total = total.astype(jnp.bfloat16)
-            for i, d in enumerate(group):
+            for i, d in enumerate(groups[g]):
                 piece = total[i] if d == 0 else shift(total[i], -d)
                 layer_out = lax.dynamic_update_slice_in_dim(
                     layer_out, piece, ((replica + d) % n_dp) * width, axis=1
                 )
-
-        back_early = back_product(early, early_layout, weight, sibling_weight)
-        back_late = back_product(late + last, late_layout, weight, sibling_weight)
-        backs = [[back_early[0], back_late[0]]]
-        for d in range(1, n_dp):
-            backs.append([shift(back_early[d], -d), shift(back_late[d], -d)])
-        spread, spread_other, inner = spread_product(rows_of, index, prob, held, backs, slots, n_ex)
-        hidden_grad = spread + swap(spread_other)
-        hidden_grad = hidden_grad.reshape(cap, n_ex, ff).transpose(1, 0, 2)[None, None]
-
-        own, other = weight_product(early + late + last, full_layout, scaleds)
-        weight_grad = own + swap(other).astype(jnp.float32)
 
         inner = lax.all_to_all(
             inner.reshape(chips, 2 * tok), "expert", 0, 0, tiled=True, axis_index_groups=same_core

time: 172 us -> 170 us (0.988)
  other arithmetic: 17.7 us -> 12.5 us
  starting transfers between devices: 37.1 us -> 39.6 us
    ppermute x6, waiting for transfers between devices: 14 us -> 26.5 us  [shift(): lax.ppermute(value, 'dp', [(i, (i + step) % n_dp) for i in range(n_dp)])]
    ppermute x22, waiting for transfers between devices: 44.3 us -> 33.2 us  [ring_send(): return lax.ppermute(value, 'expert', forward if step > 0 else backward)]
    broadcast_in_dim x1 -> x0, other arithmetic: 7.89 us -> none  [shards(): return (layer_out, prob_grad, hidden_grad, weight_grad[None])]
    pallas_call x1 -> x2, Pallas kernels: 9.24 us -> 11.7 us  [weight_product(): pl.pallas_call(functools.partial(weight_kernel, len(blocks), n_dp, layout...]
    all_to_all x1, waiting for transfers between devices: 2.49 us -> 0.01 us  [shards(): lax.all_to_all(inner.reshape(chips, 2 * tok), 'expert', 0, 0, tiled=True,...]
    unnamed x50 -> x48, local copies, waits for them, and re-layouts: 5.37 us -> 6.24 us
    convert_element_type x8 -> x6, other arithmetic: 4.7 us -> 5.03 us  [hop_on(): value = value.astype(jnp.bfloat16)]
  transfers between devices with their start and end apart: 35 -> 35, of which waited for: 15 -> 14; matrix products, arithmetic and copies ran while one was open for 8% -> 9% of each run, Pallas kernels for 23% -> 20%
where the time goes in v6:
time: 170 us
  waiting for transfers between devices  65.4 us (38%)
  Pallas kernels  40 us (24%)
  starting transfers between devices  39.6 us (23%)
  other arithmetic  12.5 us (7%)
  local copies, waits for them, and re-layouts  11.1 us (7%)
    ppermute x22, waiting for transfers between devices, ring_send(): return lax.ppermute(value, 'expert', forward if step > 0 else backward)  33.2 us
    ppermute x6, waiting for transfers between devices, shift(): lax.ppermute(value, 'dp', [(i, (i + step) % n_dp) for i in range(n_dp)])  26.5 us
    ppermute x22, starting transfers between devices, ring_send(): return lax.ppermute(value, 'expert', forward if step > 0 else backward)  21.1 us
    pallas_call x2, Pallas kernels, forward_product(): pl.pallas_call(functools.partial(forward_kernel, keep), grid=(width // ti...  14.1 us
    pallas_call x2, Pallas kernels, weight_product(): pl.pallas_call(functools.partial(weight_kernel, len(blocks), n_dp, layout...  11.7 us
    pallas_call x2, Pallas kernels, back_product(): pl.pallas_call(functools.partial(back_kernel, len(blocks), layout), grid=...  10.6 us
    ppermute x6, starting transfers between devices, shift(): lax.ppermute(value, 'dp', [(i, (i + step) % n_dp) for i in range(n_dp)])  8.12 us
    all_to_all x1, starting transfers between devices, shards(): lax.all_to_all(table.reshape(chips, 2 * tok), 'expert', 0, 0, tiled=True,...  6.28 us
  transfers between devices with their start and end apart: 35, of which 14 were waited for; matrix products, arithmetic and copies ran while one was open for 9% of the time, Pallas kernels for 20%

profile of v6, /device:TPU:0, one launch (start us, length us, event | category | flops | bytes accessed | tf_op | source)
XLA Modules:
  0.0 169.6 jit_solution(6346201947521200368)
XLA Ops:
  1.3 1.0 dynamic-slice_bitcast_fusion
  2.3 3.0 %collective-permute-start.1 = (bf16[48,2048]{1,0:T(8,128)(2,1)S(1)}, bf16[48,2048]{1,0:T(8,128)(2,1)S(1)}, u32[]{:S(2)}, u32[]{:S(2)}) collective-permute-start(bf16[48,2048]{1,0:T(8,128)(2,1)S(1)} %get-tuple-element.93), channel_id=1, source_target_pairs={{0,16},{16,0},{1,17},{17,1},{2,18},{18,2},{3,19},{19,3},{4,20},{20... | collective-permute-start | bytes 589832 | tf_op jit(solution)/shard_map/ppermute | solution.py:308
  5.4 5.6 %collective-permute-done.1 = bf16[48,2048]{1,0:T(8,128)(2,1)S(1)} collective-permute-done((bf16[48,2048]{1,0:T(8,128)(2,1)S(1)}, bf16[48,2048]{1,0:T(8,128)(2,1)S(1)}, u32[]{:S(2)}, u32[]{:S(2)}) %collective-permute-start.1) | collective-permute-done | bytes 196640 | tf_op jit(solution)/shard_map/ppermute | solution.py:308
  11.0 2.2 %collective-permute-start.2 = (bf16[2,48,2048]{2,1,0:T(8,128)(2,1)S(1)}, bf16[2,48,2048]{2,1,0:T(8,128)(2,1)S(1)}, u32[]{:S(2)}, u32[]{:S(2)}) collective-permute-start(bf16[2,48,2048]{2,1,0:T(8,128)(2,1)S(1)} %pad_maximum_fusion.refs_0_), channel_id=1, source_target_pairs={{0,4},{1,5},{4,8},{5,9},{8,12},{9,13},{12,14},{13,15},{14,10},{15,... | collective-permute-start | bytes 1179656 | tf_op jit(solution)/shard_map/ppermute | solution.py:311
  13.3 0.7 all_to_all.12
  13.9 6.3 %all-to-all-start = ((f32[8,1,96]{2,1,0:T(1,128)}), f32[8,1,96]{2,1,0:T(1,128)S(1)}, u32[]{:S(2)}, u32[]{:S(2)}) async-start(f32[8,1,96]{2,1,0:T(1,128)} %bitcast.3), calls=%async_computation | async-start | bytes 8192 | tf_op jit(solution)/shard_map/all_to_all | solution.py:326
  20.2 0.7 fusion.3.rows_of.refs_0_
  20.9 5.7 %all-to-all-done = f32[8,1,96]{2,1,0:T(1,128)S(1)} async-done(((f32[8,1,96]{2,1,0:T(1,128)}), f32[8,1,96]{2,1,0:T(1,128)S(1)}, u32[]{:S(2)}, u32[]{:S(2)}) %all-to-all-start) | async-done | bytes 3104 | tf_op jit(solution)/shard_map/all_to_all | solution.py:326
  26.6 0.6 broadcast.12
  27.2 0.7 reduce.6
  28.0 0.9 copy-done.16
  28.9 1.2 copy-done.15
  30.1 1.2 copy-done.17
  31.3 6.8 %forward_product.2 = (bf16[8,48,2048]{2,1,0:T(8,128)(2,1)S(1)}, bf16[2,384,768]{2,1,0:T(8,128)(2,1)S(1)}, bf16[2,384,768]{2,1,0:T(8,128)(2,1)S(1)}, s32[384,2]{1,0:T(8,128)S(1)}, f32[384,2]{1,0:T(8,128)S(1)}) custom-call(s32[16]{0:T(128)S(1)} %fusion.3.rows_of.refs_0_, f32[16,48]{1,0:T(8,128)S(1)} %reshape.34.table, bf16[576,768]{1,0:T(8,128)(2,1)S(1)} %bitcast.35, ...), custom_call_target="tpu_custom_call" | custom-call | flops 3095396352 | bytes 10813440 | tf_op jit(solution)/shard_map/forward_product/pallas_call | solution.py:105
  38.2 0.6 collective-permute-start.12
  38.8 1.5 collective-permute-start
  40.9 1.5 collective-permute-start.7
  42.4 3.6 %collective-permute-done.12 = bf16[1,48,2048]{2,1,0:T(8,128)(2,1)S(1)} collective-permute-done((bf16[1,48,2048]{2,1,0:T(8,128)(2,1)S(1)}, bf16[1,48,2048]{2,1,0:T(8,128)(2,1)S(1)}, u32[]{:S(2)}, u32[]{:S(2)}) %collective-permute-start.12) | collective-permute-done | bytes 196640 | tf_op jit(solution)/shard_map/ppermute | solution.py:311
  46.6 1.5 collective-permute-start.13
  48.1 6.3 %collective-permute-done.6.refs_3_ = bf16[2,48,2048]{2,1,0:T(8,128)(2,1)S(1)} collective-permute-done((bf16[2,48,2048]{2,1,0:T(8,128)(2,1)S(1)}, bf16[2,48,2048]{2,1,0:T(8,128)(2,1)S(1)}, u32[]{:S(2)}, u32[]{:S(2)}) %collective-permute-start.6) | collective-permute-done | bytes 393248 | tf_op jit(solution)/shard_map/ppermute | solution.py:311
  54.4 7.3 %forward_product.3 = (bf16[8,48,2048]{2,1,0:T(8,128)(2,1)S(1)}, bf16[2,384,768]{2,1,0:T(8,128)(2,1)S(1)}) custom-call(s32[16]{0:T(128)S(1)} %fusion.3.rows_of.refs_0_, f32[16,48]{1,0:T(8,128)S(1)} %collective-permute-done.table, bf16[576,768]{1,0:T(8,128)(2,1)} %collective-permute-done.8.hid_own, bf16[576,768]{1,0:T(8,128)(2,1)S(1)} %collective-permute-done.9.hid_sib, ...), custom_call_target="tpu_custom_call" | custom-call | flops 3095396352 | bytes 10813440 | tf_op jit(solution)/shard_map/forward_product/pallas_call | solution.py:105
  61.8 6.5 %back_product.2 = (bf16[2,240,768]{2,1,0:T(8,128)(2,1)S(1)}, bf16[2,240,768]{2,1,0:T(8,128)(2,1)S(1)}) custom-call(bf16[2,48,2048]{2,1,0:T(8,128)(2,1)S(1)} %pad_maximum_fusion.refs_0_, bf16[2,48,2048]{2,1,0:T(8,128)(2,1)S(1)} %collective-permute-done.2.refs_1_, bf16[2,48,2048]{2,1,0:T(8,128)(2,1)S(1)} %collective-permute-done.3.refs_2_, ...), custom_call_target="tpu_custom_call" | custom-call | flops 3019898880 | bytes 9732096 | tf_op jit(solution)/shard_map/back_product/pallas_call | solution.py:147
  68.3 0.6 collective-permute-start.10
  68.9 1.5 collective-permute-start.14
  71.0 1.5 collective-permute-start.16
  72.4 0.8 add_convert_fusion.6
  73.8 10.9 %collective-permute-done.11.refs_0_.refs_5_ = bf16[2,48,2048]{2,1,0:T(8,128)(2,1)S(1)} collective-permute-done((bf16[2,48,2048]{2,1,0:T(8,128)(2,1)S(1)}, bf16[2,48,2048]{2,1,0:T(8,128)(2,1)S(1)}, u32[]{:S(2)}, u32[]{:S(2)}) %collective-permute-start.11) | collective-permute-done | bytes 393248 | tf_op jit(solution)/shard_map/ppermute | solution.py:311
  85.2 1.5 collective-permute-start.17
  86.8 0.6 collective-permute-start.18
  87.4 0.8 add_convert_fusion.11
  88.2 0.8 collective-permute-start.21
  89.0 2.3 %collective-permute-done.17.refs_2_.refs_7_ = bf16[1,48,2048]{2,1,0:T(8,128)(2,1)S(1)} collective-permute-done((bf16[1,48,2048]{2,1,0:T(8,128)(2,1)S(1)}, bf16[1,48,2048]{2,1,0:T(8,128)(2,1)S(1)}, u32[]{:S(2)}, u32[]{:S(2)}) %collective-permute-start.17) | collective-permute-done | bytes 196640 | tf_op jit(solution)/shard_map/ppermute | solution.py:311
  91.4 3.1 %collective-permute-done.18.refs_3_.refs_8_ = bf16[1,48,2048]{2,1,0:T(8,128)(2,1)S(1)} collective-permute-done((bf16[1,48,2048]{2,1,0:T(8,128)(2,1)S(1)}, bf16[1,48,2048]{2,1,0:T(8,128)(2,1)S(1)}, u32[]{:S(2)}, u32[]{:S(2)}) %collective-permute-start.18) | collective-permute-done | bytes 196640 | tf_op jit(solution)/shard_map/ppermute | solution.py:311
  94.4 4.1 %back_product.3 = (bf16[2,144,768]{2,1,0:T(8,128)(2,1)S(1)}, bf16[2,144,768]{2,1,0:T(8,128)(2,1)S(1)}) custom-call(bf16[2,48,2048]{2,1,0:T(8,128)(2,1)S(1)} %collective-permute-done.11.refs_0_.refs_5_, bf16[2,48,2048]{2,1,0:T(8,128)(2,1)S(1)} %collective-permute-done.16.refs_1_.refs_6_, bf16[1,48,2048]{2,1,0:T(8,128)(2,1)S(1)} %collective-permute-done.17.refs_2_.refs_7_, ...), custom_call_target="tpu_custom_call" | custom-call | flops 1811939328 | bytes 8355840 | tf_op jit(solution)/shard_map/back_product/pallas_call | solution.py:147
  98.6 0.6 collective-permute-start.19
  99.2 4.8 %weight_product.2 = bf16[768,2048]{1,0:T(8,128)(2,1)} custom-call(bf16[2,48,2048]{2,1,0:T(8,128)(2,1)S(1)} %pad_maximum_fusion.refs_0_, bf16[2,48,2048]{2,1,0:T(8,128)(2,1)S(1)} %collective-permute-done.2.refs_1_, bf16[2,48,2048]{2,1,0:T(8,128)(2,1)S(1)} %copy-done.9, bf16[2,48,2048]{2,1,0:T(8,128)(2,1)S(1)} %collective-permute-done.6.refs_3_, ...), custom_call_target="tpu_custom_call" | custom-call | flops 2415919104 | bytes 10616832 | tf_op jit(solution)/shard_map/weight_product/pallas_call | solution.py:243
  104.5 0.8 add_convert_fusion.9
  105.3 1.1 collective-permute-start.24
  106.3 1.5 collective-permute-start.29
  108.4 1.0 collective-permute-start.23
  109.3 2.8 %collective-permute-done.24 = bf16[1,48,2048]{2,1,0:T(8,128)(2,1)S(1)} collective-permute-done((bf16[1,48,2048]{2,1,0:T(8,128)(2,1)S(1)}, bf16[1,48,2048]{2,1,0:T(8,128)(2,1)S(1)}, u32[]{:S(2)}, u32[]{:S(2)}) %collective-permute-start.24) | collective-permute-done | bytes 196640 | tf_op jit(solution)/shard_map/ppermute | solution.py:311
  112.2 0.7 add_convert_fusion.4
  112.9 1.5 collective-permute-start.25
  114.4 11.3 %collective-permute-done.29.refs_6_ = bf16[2,240,768]{2,1,0:T(8,128)(2,1)S(1)} collective-permute-done((bf16[2,240,768]{2,1,0:T(8,128)(2,1)S(1)}, bf16[2,240,768]{2,1,0:T(8,128)(2,1)S(1)}, u32[]{:S(2)}, u32[]{:S(2)}) %collective-permute-start.29) | collective-permute-done | bytes 737312 | tf_op jit(solution)/shard_map/ppermute | solution.py:308
  125.7 8.8 %collective-permute-done.30.refs_7_ = bf16[2,144,768]{2,1,0:T(8,128)(2,1)S(1)} collective-permute-done((bf16[2,144,768]{2,1,0:T(8,128)(2,1)S(1)}, bf16[2,144,768]{2,1,0:T(8,128)(2,1)S(1)}, u32[]{:S(2)}, u32[]{:S(2)}) %collective-permute-start.30) | collective-permute-done | bytes 442400 | tf_op jit(solution)/shard_map/ppermute | solution.py:308
  134.4 3.5 %spread_product.1 = (bf16[576,768]{1,0:T(8,128)(2,1)S(1)}, bf16[576,768]{1,0:T(8,128)(2,1)S(1)}, f32[16,48]{1,0:T(8,128)S(1)}) custom-call(s32[16]{0:T(128)S(1)} %fusion.3.rows_of.refs_0_, s32[384,2]{1,0:T(8,128)S(1)} %get-tuple-element.70.refs_1_, f32[384,2]{1,0:T(8,128)S(1)} %get-tuple-element.72.refs_2_, ...), custom_call_target="tpu_custom_call" | custom-call | flops 679477248 | bytes 4718592 | tf_op jit(solution)/shard_map/spread_product/pallas_call | solution.py:202
  138.0 0.9 copy-done.6
  138.9 1.0 copy-done.18
  139.9 0.7 all_to_all.14
  140.5 3.3 %all-to-all-start.1 = ((f32[8,1,96]{2,1,0:T(1,128)}), f32[8,1,96]{2,1,0:T(1,128)S(1)}, u32[]{:S(2)}, u32[]{:S(2)}) async-start(f32[8,1,96]{2,1,0:T(1,128)} %bitcast.14), calls=%async_computation.1 | async-start | bytes 8192 | tf_op jit(solution)/shard_map/all_to_all | solution.py:435
  143.9 1.9 %fusion = bf16[48,2048]{1,0:T(8,128)(2,1)} fusion(bf16[1,48,2048]{2,1,0:T(8,128)(2,1)} %collective-permute-done.25, bf16[1,48,2048]{2,1,0:T(8,128)(2,1)} %collective-permute-done.23, bf16[8,48,2048]{2,1,0:T(8,128)(2,1)} %copy-done.1), kind=kLoop, calls=%fused_computation.13 | loop fusion | flops 589824 | bytes 786432 | tf_op jit(solution)/shard_map/squeeze | solution.py:430
  145.8 1.5 collective-permute-start.26
  147.3 1.9 %add_convert_fusion.2 = (bf16[1,48,2048]{2,1,0:T(8,128)(2,1)}, bf16[1,48,2048]{2,1,0:T(8,128)(2,1)}) fusion(bf16[1,48,2048]{2,1,0:T(8,128)(2,1)} %copy-done.20, bf16[8,48,2048]{2,1,0:T(8,128)(2,1)S(1)} %get-tuple-element.43, bf16[1,48,2048]{2,1,0:T(8,128)(2,1)} %copy-done.21), kind=kLoop, calls=%fused_computation.3 | loop fusion | flops 786432 | bytes 1179648 | tf_op jit(solution)/shard_map/convert_element_type | solution.py:377
  149.2 1.8 %collective-permute-start.28 = (bf16[1,48,2048]{2,1,0:T(8,128)(2,1)}, bf16[1,48,2048]{2,1,0:T(8,128)(2,1)}, u32[]{:S(2)}, u32[]{:S(2)}) collective-permute-start(bf16[1,48,2048]{2,1,0:T(8,128)(2,1)} %get-tuple-element.69), channel_id=1, source_target_pairs={{0,2},{1,3},{4,0},{5,1},{8,4},{9,5},{12,8},{13,9},{14,12},{15,13},... | collective-permute-start | bytes 589832 | tf_op jit(solution)/shard_map/ppermute | solution.py:311
  151.2 0.7 reduce.7
  152.0 0.6 select_reduce_fusion
  152.6 0.8 collective-permute-done.26
  153.4 0.9 constant_dynamic-update-slice_fusion
  154.4 2.2 %collective-permute-done.28 = bf16[1,48,2048]{2,1,0:T(8,128)(2,1)} collective-permute-done((bf16[1,48,2048]{2,1,0:T(8,128)(2,1)}, bf16[1,48,2048]{2,1,0:T(8,128)(2,1)}, u32[]{:S(2)}, u32[]{:S(2)}) %collective-permute-start.28) | collective-permute-done | bytes 196640 | tf_op jit(solution)/shard_map/ppermute | solution.py:311
  156.7 1.5 collective-permute-done.27
  158.1 1.1 fusion.2
  159.2 2.4 %add.90 = bf16[576,768]{1,0:T(8,128)(2,1)} add(bf16[576,768]{1,0:T(8,128)(2,1)S(1)} %copy-done.7, bf16[576,768]{1,0:T(8,128)(2,1)} %collective-permute-done.31) | non-fusion elementwise | flops 442368 | bytes 2654208 | tf_op jit(solution)/shard_map/add | solution.py:421
  161.7 1.0 copy-done.14
  162.7 6.9 %weight_product.3 = f32[768,2048]{1,0:T(8,128)} custom-call(bf16[2,48,2048]{2,1,0:T(8,128)(2,1)S(1)} %pad_maximum_fusion.refs_0_, bf16[2,48,2048]{2,1,0:T(8,128)(2,1)S(1)} %collective-permute-done.2.refs_1_, bf16[2,48,2048]{2,1,0:T(8,128)(2,1)S(1)} %copy-done.10, bf16[2,48,2048]{2,1,0:T(8,128)(2,1)S(1)} %copy-done.12, bf16[2,48,2048]{2,1,0:T(8,128)(2,1)S(1)} %copy-done.14, ...), custom_call_target="tpu_custom_call" | custom-call | flops 2415919104 | bytes 10616832 | tf_op jit(solution)/shard_map/weight_product/pallas_call | solution.py:243
  (88 shorter events, 5.2 us)
Async XLA Ops:
  0.6 12.6 %copy-start.23 = (f32[48,8]{0,1:T(8,128)S(1)}, f32[48,8]{0,1:T(8,128)}, u32[]{:S(2)}) copy-start(f32[48,8]{0,1:T(8,128)} %param.7) | copy-start | bytes 4612
  0.6 12.6 %copy-start.22 = (s32[48,8]{0,1:T(8,128)S(1)}, s32[48,8]{0,1:T(8,128)}, u32[]{:S(2)}) copy-start(s32[48,8]{0,1:T(8,128)} %param.6) | copy-start | bytes 4612
  0.7 28.3 %collective-permute-start.5 = (bf16[768,2048]{1,0:T(8,128)(2,1)}, bf16[768,2048]{1,0:T(8,128)(2,1)}, u32[]{:S(2)}, u32[]{:S(2)}) collective-permute-start(bf16[768,2048]{1,0:T(8,128)(2,1)} %bitcast.28), channel_id=1, source_target_pairs={{0,1},{1,0},{2,3},{3,2},{4,5},{5,4},{6,7},{7,6},{8,9},{9,8},{10,11... | collective-permute-start | bytes 9437192 | tf_op jit(solution)/shard_map/ppermute | solution.py:314
  1.2 26.8 %collective-permute-start.4 = (bf16[576,768]{1,0:T(8,128)(2,1)}, bf16[576,768]{1,0:T(8,128)(2,1)S(1)}, u32[]{:S(2)}, u32[]{:S(2)}) collective-permute-start(bf16[576,768]{1,0:T(8,128)(2,1)} %bitcast.33), channel_id=1, source_target_pairs={{0,1},{1,0},{2,3},{3,2},{4,5},{5,4},{6,7},{7,6},{8,9},{9,8},{10,11... | collective-permute-start | bytes 2654216 | tf_op jit(solution)/shard_map/ppermute | solution.py:314
  2.3 8.7 %collective-permute-start.1 = (bf16[48,2048]{1,0:T(8,128)(2,1)S(1)}, bf16[48,2048]{1,0:T(8,128)(2,1)S(1)}, u32[]{:S(2)}, u32[]{:S(2)}) collective-permute-start(bf16[48,2048]{1,0:T(8,128)(2,1)S(1)} %get-tuple-element.93), channel_id=1, source_target_pairs={{0,16},{16,0},{1,17},{17,1},{2,18},{18,2},{3,19},{19,3},{4,20},{20... | collective-permute-start | bytes 589832 | tf_op jit(solution)/shard_map/ppermute | solution.py:308
  5.3 32.8 %collective-permute-start.8 = (bf16[576,768]{1,0:T(8,128)(2,1)}, bf16[576,768]{1,0:T(8,128)(2,1)}, u32[]{:S(2)}, u32[]{:S(2)}) collective-permute-start(bf16[576,768]{1,0:T(8,128)(2,1)} %bitcast.34), channel_id=1, source_target_pairs={{0,16},{16,0},{1,17},{17,1},{2,18},{18,2},{3,19},{19,3},{4,20},{20... | collective-permute-start | bytes 2654216 | tf_op jit(solution)/shard_map/ppermute | solution.py:308
  11.0 16.9 %collective-permute-start.2 = (bf16[2,48,2048]{2,1,0:T(8,128)(2,1)S(1)}, bf16[2,48,2048]{2,1,0:T(8,128)(2,1)S(1)}, u32[]{:S(2)}, u32[]{:S(2)}) collective-permute-start(bf16[2,48,2048]{2,1,0:T(8,128)(2,1)S(1)} %pad_maximum_fusion.refs_0_), channel_id=1, source_target_pairs={{0,4},{1,5},{4,8},{5,9},{8,12},{9,13},{12,14},{13,15},{14,10},{15,... | collective-permute-start | bytes 1179656 | tf_op jit(solution)/shard_map/ppermute | solution.py:311
  13.2 14.8 %collective-permute-start.3 = (bf16[2,48,2048]{2,1,0:T(8,128)(2,1)S(1)}, bf16[2,48,2048]{2,1,0:T(8,128)(2,1)S(1)}, u32[]{:S(2)}, u32[]{:S(2)}) collective-permute-start(bf16[2,48,2048]{2,1,0:T(8,128)(2,1)S(1)} %pad_maximum_fusion.refs_0_), channel_id=1, source_target_pairs={{0,2},{1,3},{4,0},{5,1},{8,4},{9,5},{12,8},{13,9},{14,12},{15,13},... | collective-permute-start | bytes 1179656 | tf_op jit(solution)/shard_map/ppermute | solution.py:311
  13.9 12.7 %all-to-all-start = ((f32[8,1,96]{2,1,0:T(1,128)}), f32[8,1,96]{2,1,0:T(1,128)S(1)}, u32[]{:S(2)}, u32[]{:S(2)}) async-start(f32[8,1,96]{2,1,0:T(1,128)} %bitcast.3), calls=%async_computation | async-start | bytes 8192 | tf_op jit(solution)/shard_map/all_to_all | solution.py:326
  28.0 33.8 %copy-start.8 = (bf16[2,48,2048]{2,1,0:T(8,128)(2,1)}, bf16[2,48,2048]{2,1,0:T(8,128)(2,1)S(1)}, u32[]{:S(2)}) copy-start(bf16[2,48,2048]{2,1,0:T(8,128)(2,1)S(1)} %collective-permute-done.3.refs_2_) | copy-start | bytes 1179652
  28.0 0.9 copy-start.16
  28.9 1.2 copy-start.15
  30.1 1.2 copy-start.17
  38.1 61.1 %copy-start.2 = (bf16[2,384,768]{2,1,0:T(8,128)(2,1)}, bf16[2,384,768]{2,1,0:T(8,128)(2,1)S(1)}, u32[]{:S(2)}) copy-start(bf16[2,384,768]{2,1,0:T(8,128)(2,1)S(1)} %get-tuple-element.63.refs_9_) | copy-start | bytes 3538948
  38.1 16.3 %collective-permute-start.9 = (bf16[576,768]{1,0:T(8,128)(2,1)}, bf16[576,768]{1,0:T(8,128)(2,1)S(1)}, u32[]{:S(2)}, u32[]{:S(2)}) collective-permute-start(bf16[576,768]{1,0:T(8,128)(2,1)} %collective-permute-done.8.hid_own), channel_id=1, source_target_pairs={{0,1},{1,0},{2,3},{3,2},{4,5},{5,4},{6,7},{7,6},{8,9},{9,8},{10,11... | collective-permute-start | bytes 2654216 | tf_op jit(solution)/shard_map/ppermute | solution.py:314
  38.2 7.8 %collective-permute-start.12 = (bf16[1,48,2048]{2,1,0:T(8,128)(2,1)S(1)}, bf16[1,48,2048]{2,1,0:T(8,128)(2,1)S(1)}, u32[]{:S(2)}, u32[]{:S(2)}) collective-permute-start(bf16[1,48,2048]{2,1,0:T(8,128)(2,1)S(1)} %get-tuple-element.91), channel_id=1, source_target_pairs={{0,4},{1,5},{4,8},{5,9},{8,12},{9,13},{12,14},{13,15},{14,10},{15,... | collective-permute-start | bytes 589832 | tf_op jit(solution)/shard_map/ppermute | solution.py:311
  38.8 7.8 %collective-permute-start = (f32[16,48]{1,0:T(8,128)S(1)}, f32[16,48]{1,0:T(8,128)S(1)}, u32[]{:S(2)}, u32[]{:S(2)}) collective-permute-start(f32[16,48]{1,0:T(8,128)S(1)} %reshape.34.table), channel_id=1, source_target_pairs={{0,16},{16,0},{1,17},{17,1},{2,18},{18,2},{3,19},{19,3},{4,20},{20... | collective-permute-start | bytes 9224 | tf_op jit(solution)/shard_map/ppermute | solution.py:308
  40.3 14.1 %collective-permute-start.6 = (bf16[2,48,2048]{2,1,0:T(8,128)(2,1)S(1)}, bf16[2,48,2048]{2,1,0:T(8,128)(2,1)S(1)}, u32[]{:S(2)}, u32[]{:S(2)}) collective-permute-start(bf16[2,48,2048]{2,1,0:T(8,128)(2,1)S(1)} %collective-permute-done.2.refs_1_), channel_id=1, source_target_pairs={{0,4},{1,5},{4,8},{5,9},{8,12},{9,13},{12,14},{13,15},{14,10},{15,... | collective-permute-start | bytes 1179656 | tf_op jit(solution)/shard_map/ppermute | solution.py:311
  40.9 13.5 %collective-permute-start.7 = (bf16[2,48,2048]{2,1,0:T(8,128)(2,1)S(1)}, bf16[2,48,2048]{2,1,0:T(8,128)(2,1)S(1)}, u32[]{:S(2)}, u32[]{:S(2)}) collective-permute-start(bf16[2,48,2048]{2,1,0:T(8,128)(2,1)S(1)} %collective-permute-done.3.refs_2_), channel_id=1, source_target_pairs={{0,2},{1,3},{4,0},{5,1},{8,4},{9,5},{12,8},{13,9},{14,12},{15,13},... | collective-permute-start | bytes 1179656 | tf_op jit(solution)/shard_map/ppermute | solution.py:311
  46.0 25.0 %collective-permute-start.15 = (bf16[1,48,2048]{2,1,0:T(8,128)(2,1)S(1)}, bf16[1,48,2048]{2,1,0:T(8,128)(2,1)S(1)}, u32[]{:S(2)}, u32[]{:S(2)}) collective-permute-start(bf16[1,48,2048]{2,1,0:T(8,128)(2,1)S(1)} %get-tuple-element.90), channel_id=1, source_target_pairs={{0,2},{1,3},{4,0},{5,1},{8,4},{9,5},{12,8},{13,9},{14,12},{15,13},... | collective-permute-start | bytes 589832 | tf_op jit(solution)/shard_map/ppermute | solution.py:311
  46.6 25.9 %collective-permute-start.13 = (bf16[1,48,2048]{2,1,0:T(8,128)(2,1)S(1)}, bf16[1,48,2048]{2,1,0:T(8,128)(2,1)S(1)}, u32[]{:S(2)}, u32[]{:S(2)}) collective-permute-start(bf16[1,48,2048]{2,1,0:T(8,128)(2,1)S(1)} %add_convert_fusion.10), channel_id=1, source_target_pairs={{0,4},{1,5},{4,8},{5,9},{8,12},{9,13},{12,14},{13,15},{14,10},{15,... | collective-permute-start | bytes 589832 | tf_op jit(solution)/shard_map/ppermute | solution.py:311
  54.4 44.8 %copy-start.11 = (bf16[2,48,2048]{2,1,0:T(8,128)(2,1)}, bf16[2,48,2048]{2,1,0:T(8,128)(2,1)S(1)}, u32[]{:S(2)}) copy-start(bf16[2,48,2048]{2,1,0:T(8,128)(2,1)S(1)} %collective-permute-done.6.refs_3_) | copy-start | bytes 1179652
  54.4 44.8 %copy-start.13 = (bf16[2,48,2048]{2,1,0:T(8,128)(2,1)}, bf16[2,48,2048]{2,1,0:T(8,128)(2,1)S(1)}, u32[]{:S(2)}) copy-start(bf16[2,48,2048]{2,1,0:T(8,128)(2,1)S(1)} %collective-permute-done.7.refs_4_) | copy-start | bytes 1179652
  61.7 37.5 %copy-start.4 = (bf16[2,384,768]{2,1,0:T(8,128)(2,1)}, bf16[2,384,768]{2,1,0:T(8,128)(2,1)S(1)}, u32[]{:S(2)}) copy-start(bf16[2,384,768]{2,1,0:T(8,128)(2,1)S(1)} %get-tuple-element.64.refs_10_) | copy-start | bytes 3538948
  61.7 50.4 %copy-start.1 = (bf16[8,48,2048]{2,1,0:T(8,128)(2,1)}, bf16[8,48,2048]{2,1,0:T(8,128)(2,1)S(1)}, u32[]{:S(2)}) copy-start(bf16[8,48,2048]{2,1,0:T(8,128)(2,1)S(1)} %get-tuple-element.48) | copy-start | bytes 4718596
  68.3 18.4 %collective-permute-start.10 = (bf16[1,48,2048]{2,1,0:T(8,128)(2,1)S(1)}, bf16[1,48,2048]{2,1,0:T(8,128)(2,1)S(1)}, u32[]{:S(2)}, u32[]{:S(2)}) collective-permute-start(bf16[1,48,2048]{2,1,0:T(8,128)(2,1)S(1)} %get-tuple-element.51), channel_id=1, source_target_pairs={{0,4},{1,5},{4,8},{5,9},{8,12},{9,13},{12,14},{13,15},{14,10},{15,... | collective-permute-start | bytes 589832 | tf_op jit(solution)/shard_map/ppermute | solution.py:311
  68.9 25.5 %copy-start = (bf16[1,768,2048]{2,1,0:T(8,128)(2,1)S(1)}, bf16[1,768,2048]{2,1,0:T(8,128)(2,1)}, u32[]{:S(2)}) copy-start(bf16[1,768,2048]{2,1,0:T(8,128)(2,1)} %param.9) | copy-start | bytes 9437188
  68.9 18.5 %collective-permute-start.14 = (bf16[1,48,2048]{2,1,0:T(8,128)(2,1)S(1)}, bf16[1,48,2048]{2,1,0:T(8,128)(2,1)S(1)}, u32[]{:S(2)}, u32[]{:S(2)}) collective-permute-start(bf16[1,48,2048]{2,1,0:T(8,128)(2,1)S(1)} %get-tuple-element.87), channel_id=1, source_target_pairs={{0,2},{1,3},{4,0},{5,1},{8,4},{9,5},{12,8},{13,9},{14,12},{15,13},... | collective-permute-start | bytes 589832 | tf_op jit(solution)/shard_map/ppermute | solution.py:311
  70.4 14.2 %collective-permute-start.11 = (bf16[2,48,2048]{2,1,0:T(8,128)(2,1)S(1)}, bf16[2,48,2048]{2,1,0:T(8,128)(2,1)S(1)}, u32[]{:S(2)}, u32[]{:S(2)}) collective-permute-start(bf16[2,48,2048]{2,1,0:T(8,128)(2,1)S(1)} %collective-permute-done.6.refs_3_), channel_id=1, source_target_pairs={{0,4},{1,5},{4,8},{5,9},{8,12},{9,13},{12,14},{13,15},{14,10},{15,... | collective-permute-start | bytes 1179656 | tf_op jit(solution)/shard_map/ppermute | solution.py:311
  71.0 14.3 %collective-permute-start.16 = (bf16[2,48,2048]{2,1,0:T(8,128)(2,1)S(1)}, bf16[2,48,2048]{2,1,0:T(8,128)(2,1)S(1)}, u32[]{:S(2)}, u32[]{:S(2)}) collective-permute-start(bf16[2,48,2048]{2,1,0:T(8,128)(2,1)S(1)} %collective-permute-done.7.refs_4_), channel_id=1, source_target_pairs={{0,2},{1,3},{4,0},{5,1},{8,4},{9,5},{12,8},{13,9},{14,12},{15,13},... | collective-permute-start | bytes 1179656 | tf_op jit(solution)/shard_map/ppermute | solution.py:311
  73.2 25.9 %collective-permute-start.20 = (bf16[1,48,2048]{2,1,0:T(8,128)(2,1)}, bf16[1,48,2048]{2,1,0:T(8,128)(2,1)S(1)}, u32[]{:S(2)}, u32[]{:S(2)}) collective-permute-start(bf16[1,48,2048]{2,1,0:T(8,128)(2,1)} %get-tuple-element.59), channel_id=1, source_target_pairs={{0,4},{1,5},{4,8},{5,9},{8,12},{9,13},{12,14},{13,15},{14,10},{15,... | collective-permute-start | bytes 589832 | tf_op jit(solution)/shard_map/ppermute | solution.py:311
  84.7 14.5 %collective-permute-start.22 = (bf16[1,48,2048]{2,1,0:T(8,128)(2,1)S(1)}, bf16[1,48,2048]{2,1,0:T(8,128)(2,1)S(1)}, u32[]{:S(2)}, u32[]{:S(2)}) collective-permute-start(bf16[1,48,2048]{2,1,0:T(8,128)(2,1)S(1)} %get-tuple-element.61), channel_id=1, source_target_pairs={{0,2},{1,3},{4,0},{5,1},{8,4},{9,5},{12,8},{13,9},{14,12},{15,13},... | collective-permute-start | bytes 589832 | tf_op jit(solution)/shard_map/ppermute | solution.py:311
  85.2 6.1 %collective-permute-start.17 = (bf16[1,48,2048]{2,1,0:T(8,128)(2,1)S(1)}, bf16[1,48,2048]{2,1,0:T(8,128)(2,1)S(1)}, u32[]{:S(2)}, u32[]{:S(2)}) collective-permute-start(bf16[1,48,2048]{2,1,0:T(8,128)(2,1)S(1)} %slice.72), channel_id=1, source_target_pairs={{0,4},{1,5},{4,8},{5,9},{8,12},{9,13},{12,14},{13,15},{14,10},{15,... | collective-permute-start | bytes 589832 | tf_op jit(solution)/shard_map/ppermute | solution.py:311
  86.8 7.6 %collective-permute-start.18 = (bf16[1,48,2048]{2,1,0:T(8,128)(2,1)S(1)}, bf16[1,48,2048]{2,1,0:T(8,128)(2,1)S(1)}, u32[]{:S(2)}, u32[]{:S(2)}) collective-permute-start(bf16[1,48,2048]{2,1,0:T(8,128)(2,1)S(1)} %slice.73), channel_id=1, source_target_pairs={{0,2},{1,3},{4,0},{5,1},{8,4},{9,5},{12,8},{13,9},{14,12},{15,13},... | collective-permute-start | bytes 589832 | tf_op jit(solution)/shard_map/ppermute | solution.py:311
  88.2 11.0 %copy-start.9 = (bf16[2,48,2048]{2,1,0:T(8,128)(2,1)S(1)}, bf16[2,48,2048]{2,1,0:T(8,128)(2,1)}, u32[]{:S(2)}) copy-start(bf16[2,48,2048]{2,1,0:T(8,128)(2,1)} %copy-done.8) | copy-start | bytes 1179652
  88.2 10.9 %collective-permute-start.21 = (bf16[1,48,2048]{2,1,0:T(8,128)(2,1)}, bf16[1,48,2048]{2,1,0:T(8,128)(2,1)S(1)}, u32[]{:S(2)}, u32[]{:S(2)}) collective-permute-start(bf16[1,48,2048]{2,1,0:T(8,128)(2,1)} %get-tuple-element.60), channel_id=1, source_target_pairs={{0,2},{1,3},{4,0},{5,1},{8,4},{9,5},{12,8},{13,9},{14,12},{15,13},... | collective-permute-start | bytes 589832 | tf_op jit(solution)/shard_map/ppermute | solution.py:311
  98.6 5.9 %collective-permute-start.19 = (bf16[1,48,2048]{2,1,0:T(8,128)(2,1)}, bf16[1,48,2048]{2,1,0:T(8,128)(2,1)S(1)}, u32[]{:S(2)}, u32[]{:S(2)}) collective-permute-start(bf16[1,48,2048]{2,1,0:T(8,128)(2,1)} %get-tuple-element.58), channel_id=1, source_target_pairs={{0,4},{1,5},{4,8},{5,9},{8,12},{9,13},{12,14},{13,15},{14,10},{15,... | collective-permute-start | bytes 589832 | tf_op jit(solution)/shard_map/ppermute | solution.py:311
  99.2 4.9 %copy-start.20 = (bf16[1,48,2048]{2,1,0:T(8,128)(2,1)}, bf16[1,48,2048]{2,1,0:T(8,128)(2,1)S(1)}, u32[]{:S(2)}) copy-start(bf16[1,48,2048]{2,1,0:T(8,128)(2,1)S(1)} %collective-permute-done.20) | copy-start | bytes 589828
  99.2 4.9 %copy-start.21 = (bf16[1,48,2048]{2,1,0:T(8,128)(2,1)}, bf16[1,48,2048]{2,1,0:T(8,128)(2,1)S(1)}, u32[]{:S(2)}) copy-start(bf16[1,48,2048]{2,1,0:T(8,128)(2,1)S(1)} %collective-permute-done.22) | copy-start | bytes 589828
  104.1 57.6 %collective-permute-start.32 = (bf16[768,2048]{1,0:T(8,128)(2,1)}, bf16[768,2048]{1,0:T(8,128)(2,1)}, u32[]{:S(2)}, u32[]{:S(2)}) collective-permute-start(bf16[768,2048]{1,0:T(8,128)(2,1)} %weight_product.2), channel_id=1, source_target_pairs={{0,1},{1,0},{2,3},{3,2},{4,5},{5,4},{6,7},{7,6},{8,9},{9,8},{10,11... | collective-permute-start | bytes 9437192 | tf_op jit(solution)/shard_map/ppermute | solution.py:314
  105.3 6.9 %collective-permute-start.24 = (bf16[1,48,2048]{2,1,0:T(8,128)(2,1)S(1)}, bf16[1,48,2048]{2,1,0:T(8,128)(2,1)S(1)}, u32[]{:S(2)}, u32[]{:S(2)}) collective-permute-start(bf16[1,48,2048]{2,1,0:T(8,128)(2,1)S(1)} %get-tuple-element.66), channel_id=1, source_target_pairs={{0,2},{1,3},{4,0},{5,1},{8,4},{9,5},{12,8},{13,9},{14,12},{15,13},... | collective-permute-start | bytes 589832 | tf_op jit(solution)/shard_map/ppermute | solution.py:311
  106.3 19.3 %collective-permute-start.29 = (bf16[2,240,768]{2,1,0:T(8,128)(2,1)S(1)}, bf16[2,240,768]{2,1,0:T(8,128)(2,1)S(1)}, u32[]{:S(2)}, u32[]{:S(2)}) collective-permute-start(bf16[2,240,768]{2,1,0:T(8,128)(2,1)S(1)} %get-tuple-element.74), channel_id=1, source_target_pairs={{0,16},{16,0},{1,17},{17,1},{2,18},{18,2},{3,19},{19,3},{4,20},{20... | collective-permute-start | bytes 2211848 | tf_op jit(solution)/shard_map/ppermute | solution.py:308
  107.9 26.6 %collective-permute-start.30 = (bf16[2,144,768]{2,1,0:T(8,128)(2,1)S(1)}, bf16[2,144,768]{2,1,0:T(8,128)(2,1)S(1)}, u32[]{:S(2)}, u32[]{:S(2)}) collective-permute-start(bf16[2,144,768]{2,1,0:T(8,128)(2,1)S(1)} %get-tuple-element.75), channel_id=1, source_target_pairs={{0,16},{16,0},{1,17},{17,1},{2,18},{18,2},{3,19},{19,3},{4,20},{20... | collective-permute-start | bytes 1327112 | tf_op jit(solution)/shard_map/ppermute | solution.py:308
  108.4 35.6 %collective-permute-start.23 = (bf16[1,48,2048]{2,1,0:T(8,128)(2,1)}, bf16[1,48,2048]{2,1,0:T(8,128)(2,1)}, u32[]{:S(2)}, u32[]{:S(2)}) collective-permute-start(bf16[1,48,2048]{2,1,0:T(8,128)(2,1)} %get-tuple-element.65), channel_id=1, source_target_pairs={{0,4},{1,5},{4,8},{5,9},{8,12},{9,13},{12,14},{13,15},{14,10},{15,... | collective-permute-start | bytes 589832 | tf_op jit(solution)/shard_map/ppermute | solution.py:311
  112.9 31.1 %collective-permute-start.25 = (bf16[1,48,2048]{2,1,0:T(8,128)(2,1)}, bf16[1,48,2048]{2,1,0:T(8,128)(2,1)}, u32[]{:S(2)}, u32[]{:S(2)}) collective-permute-start(bf16[1,48,2048]{2,1,0:T(8,128)(2,1)} %add_convert_fusion.4), channel_id=1, source_target_pairs={{0,2},{1,3},{4,0},{5,1},{8,4},{9,5},{12,8},{13,9},{14,12},{15,13},... | collective-permute-start | bytes 589832 | tf_op jit(solution)/shard_map/ppermute | solution.py:311
  137.9 0.9 copy-start.6
  138.9 1.0 copy-start.18
  140.5 10.7 %all-to-all-start.1 = ((f32[8,1,96]{2,1,0:T(1,128)}), f32[8,1,96]{2,1,0:T(1,128)S(1)}, u32[]{:S(2)}, u32[]{:S(2)}) async-start(f32[8,1,96]{2,1,0:T(1,128)} %bitcast.14), calls=%async_computation.1 | async-start | bytes 8192 | tf_op jit(solution)/shard_map/all_to_all | solution.py:435
  143.8 15.4 %collective-permute-start.31 = (bf16[576,768]{1,0:T(8,128)(2,1)}, bf16[576,768]{1,0:T(8,128)(2,1)}, u32[]{:S(2)}, u32[]{:S(2)}) collective-permute-start(bf16[576,768]{1,0:T(8,128)(2,1)} %copy-done.18), channel_id=1, source_target_pairs={{0,1},{1,0},{2,3},{3,2},{4,5},{5,4},{6,7},{7,6},{8,9},{9,8},{10,11... | collective-permute-start | bytes 2654216 | tf_op jit(solution)/shard_map/ppermute | solution.py:314
  145.8 7.6 %collective-permute-start.26 = (bf16[48,2048]{1,0:T(8,128)(2,1)}, bf16[48,2048]{1,0:T(8,128)(2,1)}, u32[]{:S(2)}, u32[]{:S(2)}) collective-permute-start(bf16[48,2048]{1,0:T(8,128)(2,1)} %fusion), channel_id=1, source_target_pairs={{0,16},{16,0},{1,17},{17,1},{2,18},{18,2},{3,19},{19,3},{4,20},{20... | collective-permute-start | bytes 589832 | tf_op jit(solution)/shard_map/ppermute | solution.py:308
  149.2 7.4 %collective-permute-start.28 = (bf16[1,48,2048]{2,1,0:T(8,128)(2,1)}, bf16[1,48,2048]{2,1,0:T(8,128)(2,1)}, u32[]{:S(2)}, u32[]{:S(2)}) collective-permute-start(bf16[1,48,2048]{2,1,0:T(8,128)(2,1)} %get-tuple-element.69), channel_id=1, source_target_pairs={{0,2},{1,3},{4,0},{5,1},{8,4},{9,5},{12,8},{13,9},{14,12},{15,13},... | collective-permute-start | bytes 589832 | tf_op jit(solution)/shard_map/ppermute | solution.py:311
  151.0 7.1 %collective-permute-start.27 = (bf16[1,48,2048]{2,1,0:T(8,128)(2,1)}, bf16[1,48,2048]{2,1,0:T(8,128)(2,1)}, u32[]{:S(2)}, u32[]{:S(2)}) collective-permute-start(bf16[1,48,2048]{2,1,0:T(8,128)(2,1)} %get-tuple-element.68), channel_id=1, source_target_pairs={{0,4},{1,5},{4,8},{5,9},{8,12},{9,13},{12,14},{13,15},{14,10},{15,... | collective-permute-start | bytes 589832 | tf_op jit(solution)/shard_map/ppermute | solution.py:311
  152.0 7.2 %copy-start.7 = (bf16[576,768]{1,0:T(8,128)(2,1)S(1)}, bf16[576,768]{1,0:T(8,128)(2,1)}, u32[]{:S(2)}) copy-start(bf16[576,768]{1,0:T(8,128)(2,1)} %copy-done.6) | copy-start | bytes 2654212
  154.4 7.3 %copy-start.3 = (bf16[2,384,768]{2,1,0:T(8,128)(2,1)S(1)}, bf16[2,384,768]{2,1,0:T(8,128)(2,1)}, u32[]{:S(2)}) copy-start(bf16[2,384,768]{2,1,0:T(8,128)(2,1)} %copy-done.2) | copy-start | bytes 3538948
  154.4 7.3 %copy-start.5 = (bf16[2,384,768]{2,1,0:T(8,128)(2,1)S(1)}, bf16[2,384,768]{2,1,0:T(8,128)(2,1)}, u32[]{:S(2)}) copy-start(bf16[2,384,768]{2,1,0:T(8,128)(2,1)} %copy-done.4) | copy-start | bytes 3538948
  154.4 7.3 %copy-start.10 = (bf16[2,48,2048]{2,1,0:T(8,128)(2,1)S(1)}, bf16[2,48,2048]{2,1,0:T(8,128)(2,1)}, u32[]{:S(2)}) copy-start(bf16[2,48,2048]{2,1,0:T(8,128)(2,1)} %copy-done.8) | copy-start | bytes 1179652
  154.4 7.3 %copy-start.12 = (bf16[2,48,2048]{2,1,0:T(8,128)(2,1)S(1)}, bf16[2,48,2048]{2,1,0:T(8,128)(2,1)}, u32[]{:S(2)}) copy-start(bf16[2,48,2048]{2,1,0:T(8,128)(2,1)} %copy-done.11) | copy-start | bytes 1179652
  159.2 10.4 %copy-start.19 = (bf16[48,4096]{1,0:T(8,128)(2,1)}, bf16[48,4096]{1,0:T(8,128)(2,1)S(1)}, u32[]{:S(2)}) copy-start(bf16[48,4096]{1,0:T(8,128)(2,1)S(1)} %fusion.2) | copy-start | bytes 1179652
  161.7 1.0 copy-start.14

commit v7 on v2

v7 whole, which is shorter than its diff:
```python
import functools

import jax
import jax.numpy as jnp
import numpy as np
from jax import lax
from jax.experimental import pallas as pl
from jax.experimental.pallas import tpu as pltpu
from jax.sharding import PartitionSpec as P

VMEM_BYTES = 48 * 1024 * 1024


def dot(a, b, ca, cb):
    return lax.dot_general(a, b, (((ca,), (cb,)), ((), ())), preferred_element_type=jnp.float32)


def after(value, *done):
    return lax.optimization_barrier((value, *done))[0]


def chip_ring(mesh):
    chips = mesh.shape["expert"] // 2
    devices = mesh.devices.reshape(mesh.shape["dp"], -1)
    if not hasattr(devices[0, 0], "coords"):
        return list(range(chips))
    at = [tuple(devices[0, 2 * chip].coords)[1:] for chip in range(chips)]
    rows = max(z for _, z in at) + 1
    cols = max(y for y, _ in at) + 1
    if rows * cols != chips or rows % 2:
        return list(range(chips))
    walk = [(0, z) for z in range(rows)]
    for step, z in enumerate(reversed(range(rows))):
        span = range(1, cols)
        walk += [(y, z) for y in (span if step % 2 == 0 else reversed(span))]
    return [at.index(place) for place in walk]


def block_kernel(plan, refs_in, n_dp, n_ex, top, *refs):
    meta = refs[0]
    blocks = refs[1 : 1 + refs_in]
    at = 1 + refs_in
    replicas = sorted({item[2] for item in plan})
    hid = {d: refs[at + 2 * i : at + 2 * i + 2] for i, d in enumerate(replicas)}
    at += 2 * len(replicas)
    weights = refs[at : at + 2]
    at += 2
    parts = refs[at : at + len(plan)]
    at += len(plan)
    outs = {d: refs[at + 2 * i : at + 2 * i + 2] for i, d in enumerate(replicas)}
    at += 2 * len(replicas)
    index, prob = refs[at : at + 2] if 0 in replicas else (None, None)

    _, tok, full = blocks[0].shape
    ff, width = weights[0].shape
    slots = hid[replicas[0]][0].shape[0]
    count = len(plan) * tok
    rows = [blocks[where][place] for where, place, _, _ in plan]
    routes = jnp.concatenate([row[:, width:] for row in rows], axis=0).astype(jnp.float32)
    named = routes[:, :top]
    chance = routes[:, top : 2 * top] + routes[:, 2 * top : 3 * top] + routes[:, 3 * top : 4 * top]
    row = lax.broadcasted_iota(jnp.int32, (tok, tok), 0)
    col = lax.broadcasted_iota(jnp.int32, (tok, tok), 1)
    earlier = (col < row).astype(jnp.float32)
    lane = lax.broadcasted_iota(jnp.int32, (tok, slots), 1)
    spans = {d: [i for i, item in enumerate(plan) if item[2] == d] for d in replicas}
    helds, scaleds = [], []
    for x in range(2):
        mine = named == meta[x].astype(jnp.float32)
        here = jnp.sum(jnp.where(mine, chance, 0.0), axis=1, keepdims=True)
        taken = jnp.broadcast_to((here > 0.0).astype(jnp.float32), (count, 128))
        held = []
        for d in replicas:
            picks = []
            for n, i in enumerate(spans[d]):
                span = slice(i * tok, (i + 1) * tok)
                position = dot(earlier, taken[span], 1, 0)[:, :1].astype(jnp.int32)
                slot = jnp.where(here[span] > 0.0, position * n_ex + meta[2 + plan[i][3]], -1)
                picks.append((lane == slot).astype(jnp.bfloat16))
                if d == 0:
                    index[n * tok : (n + 1) * tok, x : x + 1] = slot
                    prob[n * tok : (n + 1) * tok, x : x + 1] = here[span]
            held.append(dot(jnp.concatenate(picks, axis=0), hid[d][x][...], 1, 0))
        held = jnp.concatenate(held, axis=0)
        scaled = (held * here).astype(jnp.bfloat16)
        base = 0
        for d in replicas:
            size = len(spans[d]) * tok
            outs[d][0][x] = scaled[base : base + size]
            base += size
        helds.append(held)
        scaleds.append(scaled)

    tile = 512
    for step in range(width // tile):
        cols = slice(step * tile, (step + 1) * tile)
        value = dot(scaleds[0], weights[0][:, cols], 1, 0) + dot(scaleds[1], weights[1][:, cols], 1, 0)
        value = value.astype(jnp.bfloat16)
        for i, out in enumerate(parts):
            out[:, cols] = value[i * tok : (i + 1) * tok]

    lhs = jnp.concatenate([row[:, :width] for row in rows], axis=0)
    lane = lax.broadcasted_iota(jnp.int32, (count, full - width), 1)
    extra = jnp.zeros((count, full - width), jnp.float32)
    for x in range(2):
        inner = jnp.zeros((count, 1), jnp.float32)
        step_ff = 256
        for step in range(ff // step_ff):
            cols = slice(step * step_ff, (step + 1) * step_ff)
            value = dot(lhs, weights[x][cols, :], 1, 1)
            inner = inner + jnp.sum(value * helds[x][:, cols], axis=1, keepdims=True)
            value = value.astype(jnp.bfloat16)
            base = 0
            for d in replicas:
                size = len(spans[d]) * tok
                outs[d][1][x, :, cols] = value[base : base + size]
                base += size
        high = inner.astype(jnp.bfloat16).astype(jnp.float32)
        extra = jnp.where(lane == meta[x], high, extra)
        extra = jnp.where(lane == meta[x] + n_ex, inner - high, extra)
    extra = extra.astype(jnp.bfloat16)
    for i, out in enumerate(parts):
        out[:, width:] = extra[i * tok : (i + 1) * tok]


def block_product(plan, meta, blocks, hiddens, w_own, w_sib, n_ex, top):
    n_dp = len(hiddens)
    _, tok, full = blocks[0].shape
    ff, width = w_own.shape
    slots = hiddens[0][0].shape[0]
    replicas = sorted({item[2] for item in plan})
    vmem = pl.BlockSpec(memory_space=pltpu.VMEM)
    bf16 = lambda *shape: jax.ShapeDtypeStruct(shape, jnp.bfloat16)
    out_shape = [bf16(tok, full) for _ in plan]
    sizes = {d: tok * sum(item[2] == d for item in plan) for d in replicas}
    for d in replicas:
        out_shape += [bf16(2, sizes[d], ff)] * 2
    if 0 in replicas:
        out_shape.append(jax.ShapeDtypeStruct((sizes[0], 2), jnp.int32))
        out_shape.append(jax.ShapeDtypeStruct((sizes[0], 2), jnp.float32))
    hid = [value for d in replicas for value in hiddens[d]]
    count = len(plan) * tok
    made = pl.pallas_call(
        functools.partial(block_kernel, plan, len(blocks), n_dp, n_ex, top),
        in_specs=[pl.BlockSpec(memory_space=pltpu.SMEM)] + [vmem] * (len(blocks) + len(hid) + 2),
        out_specs=[vmem] * len(out_shape),
        out_shape=out_shape,
        compiler_params=pltpu.CompilerParams(vmem_limit_bytes=VMEM_BYTES),
        cost_estimate=pl.CostEstimate(
            flops=8 * count * ff * width,
            bytes_accessed=4 * ff * width + 4 * count * (full + ff),
            transcendentals=0,
        ),
        name="block_product",
    )(meta, *blocks, *hid, w_own, w_sib)
    parts = made[: len(plan)]
    rest = made[len(plan) :]
    scaled = {d: rest[2 * i] for i, d in enumerate(replicas)}
    back = {d: rest[2 * i + 1] for i, d in enumerate(replicas)}
    return parts, scaled, back, rest[2 * len(replicas) :]


def spread_kernel(sizes, *refs):
    n_parts = len(sizes[0])
    index, prob = refs[:n_parts], refs[n_parts : 2 * n_parts]
    backs = list(refs[2 * n_parts : -2])
    outs = refs[-2:]
    slots = outs[0].shape[0]
    slot = jnp.concatenate([ref[...] for ref in index], axis=0)
    weight = jnp.concatenate([ref[...] for ref in prob], axis=0)
    lane = lax.broadcasted_iota(jnp.int32, (slot.shape[0], slots), 1)
    for x, out in enumerate(outs):
        back, at = None, 0
        for pieces in sizes:
            value = jnp.concatenate([ref[x] for ref in backs[at : at + len(pieces)]], axis=0)
            at += len(pieces)
            value = value.astype(jnp.float32)
            back = value if back is None else back + value
        pick = (lane == slot[:, x : x + 1]).astype(jnp.bfloat16)
        mine = (back * weight[:, x : x + 1]).astype(jnp.bfloat16)
        out[...] = dot(pick, mine, 0, 0).astype(jnp.bfloat16)


def spread_product(index, prob, backs, slots):
    sizes = [[part.shape[1] for part in parts] for parts in backs]
    ff = backs[0][0].shape[2]
    rows = sum(sizes[0])
    flat = [part for parts in backs for part in parts]
    vmem = pl.BlockSpec(memory_space=pltpu.VMEM)
    return pl.pallas_call(
        functools.partial(spread_kernel, sizes),
        in_specs=[vmem] * (2 * len(index) + len(flat)),
        out_specs=[vmem] * 2,
        out_shape=[jax.ShapeDtypeStruct((slots, ff), jnp.bfloat16)] * 2,
        compiler_params=pltpu.CompilerParams(vmem_limit_bytes=VMEM_BYTES),
        cost_estimate=pl.CostEstimate(
            flops=4 * rows * slots * ff,
            bytes_accessed=4 * (1 + len(backs)) * rows * ff,
            transcendentals=0,
        ),
        name="spread_product",
    )(*index, *prob, *flat)


def weight_kernel(n_refs, n_scaled, layout, *refs):
    blocks, scaleds, more = refs[:n_refs], refs[n_refs : n_refs + n_scaled], refs[n_refs + n_scaled : -2]
    out, turned = refs[-2:]

    @pl.when(pl.program_id(0) == 0)
    def _():
        turned[...] = jnp.concatenate([ref[0] for ref in scaleds], axis=0).T

    rows = jnp.concatenate([blocks[where][place] for where, place in layout], axis=0)
    total = dot(turned[...], rows, 1, 0)
    for ref in more:
        total = total + ref[...].astype(jnp.float32)
    out[...] = total.astype(out.dtype)


def weight_product(blocks, layout, scaleds, x, dtype, width, *more):
    tok = blocks[0].shape[1]
    ff = scaleds[0].shape[2]
    rows = len(layout) * tok
    tile = 512 if width >= 2048 else 256
    return pl.pallas_call(
        functools.partial(weight_kernel, len(blocks), len(scaleds), layout),
        grid=(width // tile,),
        in_specs=[pl.BlockSpec(block.shape[:2] + (tile,), lambda i: (0, 0, i)) for block in blocks]
        + [
            pl.BlockSpec((1,) + value.shape[1:], lambda i: (x, 0, 0), pipeline_mode=pl.Buffered(1))
            for value in scaleds
        ]
        + [pl.BlockSpec((ff, tile), lambda i: (0, i)) for _ in more],
        out_specs=pl.BlockSpec((ff, tile), lambda i: (0, i)),
        out_shape=jax.ShapeDtypeStruct((ff, width), dtype),
        scratch_shapes=[pltpu.VMEM((ff, rows), jnp.bfloat16)],
        compiler_params=pltpu.CompilerParams(vmem_limit_bytes=VMEM_BYTES),
        cost_estimate=pl.CostEstimate(
            flops=2 * rows * width * ff,
            bytes_accessed=2 * rows * (width + ff) + 4 * ff * width,
            transcendentals=0,
        ),
        name="weight_product",
    )(*blocks, *scaleds, *more)


def body(ring):
    chips = len(ring)
    half = chips // 2
    offsets = [0]
    for step in range(1, half):
        offsets += [-step, step]
    offsets.append(half)
    place_of = {chip: at for at, chip in enumerate(ring)}
    meta_table = np.asarray(
        [
            [e, e ^ 1] + [2 * ring[(place_of[e // 2] + off) % chips] + e % 2 for off in offsets]
            for e in range(2 * chips)
        ],
        np.int32,
    )

    def along(step):
        return [
            (2 * ring[at] + core, 2 * ring[(at + step) % chips] + core)
            for at in range(chips)
            for core in range(2)
        ]

    forward, backward = along(1), along(-1)
    sibling = [(e, e ^ 1) for e in range(2 * chips)]

    def shards(expert_ids, route_probs, expert_hidden, down_weight, out_grad):
        tok, top = expert_ids.shape
        n_dp = lax.axis_size("dp")
        n_ex = lax.axis_size("expert")
        cap = expert_hidden.shape[3]
        slots = cap * n_ex
        ff = down_weight.shape[1]
        width = down_weight.shape[2]
        weight = down_weight[0]
        replica = lax.axis_index("dp")
        expert = lax.axis_index("expert")
        per = n_dp // 2
        meta = lax.dynamic_index_in_dim(jnp.asarray(meta_table), expert, 0, keepdims=False)

        def shift(value, step):
            return lax.ppermute(value, "dp", [(i, (i + step) % n_dp) for i in range(n_dp)])

        def ring_send(value, step):
            return lax.ppermute(value, "expert", forward if step > 0 else backward)

        def swap(value):
            return lax.ppermute(value, "expert", sibling)

        room = 128 * -(-max(4 * top, 2 * n_ex) // 128)
        narrow = lambda value: lax.reduce_precision(value, 8, 7)
        high = narrow(route_probs)
        middle = narrow(route_probs - high)
        low = route_probs - high - middle
        routes = jnp.concatenate([expert_ids.astype(jnp.float32), high, middle, low], axis=1)
        routes = jnp.pad(routes.astype(jnp.bfloat16), ((0, 0), (0, room - 4 * top)))

        def width_shard(d):
            at = ((replica + d) % n_dp) * width
            return jnp.concatenate([lax.dynamic_slice_in_dim(out_grad, at, width, axis=1), routes], axis=1)

        blocks = {0: jnp.stack([width_shard(0)] + [shift(width_shard(d), d) for d in range(1, n_dp)])}

        sibling_weight = swap(weight)
        hidden = expert_hidden[0, 0].transpose(1, 0, 2).reshape(slots, ff)
        hiddens = [hidden] + [shift(hidden, d) for d in range(1, n_dp)]
        hiddens = [(value, swap(value)) for value in hiddens]

        parts, scaleds, layout, facts = {}, [], [], []
        own_back, sent_back = [], [[] for _ in range(1, n_dp)]
        refs = []

        def work(items, *done):
            used, plan = [], []
            for off, d in items:
                value = blocks[off][d // per] if off == half else blocks[off]
                if not any(value is other for other in used):
                    used.append(value)
                where = [value is other for other in used].index(True)
                plan.append((where, d % per if off == half else d, d, offsets.index(off)))
            if done:
                gated = [after(used[0], *done)] + used[1:]
            else:
                gated = used
            made, scaled, back, fact = block_product(
                tuple(plan), meta, gated, hiddens, weight, sibling_weight, n_ex, top
            )
            for item, part in zip(items, made):
                parts[item] = part
            for d in sorted(scaled):
                scaleds.append(scaled[d])
                for (off, e), (where, place, _, _) in zip(items, plan):
                    if e == d:
                        if not any(used[where] is other for other in refs):
                            refs.append(used[where])
                        layout.append(([used[where] is other for other in refs].index(True), place))
                if d == 0:
                    own_back.append(back[0])
                    facts.append(fact)
                else:
                    sent_back[d - 1].append(shift(back[d], -d))
            return made[0]

        both = lambda offs: [(off, d) for d in range(n_dp) for off in offs]
        gate = ()
        for step in range(1, half):
            sent = blocks[1 - step], blocks[step - 1]
            if gate:
                sent = after(sent[0], *gate), after(sent[1], *gate)
            blocks[-step] = ring_send(sent[0], 1)
            blocks[step] = ring_send(sent[1], -1)
            if step == 1:
                following = [(off, 0) for off in offsets[:3]]
            elif step == 2:
                following = [(off, d) for d in range(n_dp) for off in offsets[:5] if d > 0 or off not in offsets[:3]]
            else:
                following = both([-step, step])
            if step == half - 1:
                break
            if step > 1:
                gate = (ready,)
            ready = work(following)
        sent = after(blocks[1 - half][:per], ready), after(blocks[half - 1][per:], ready)
        blocks[half] = [ring_send(sent[0], 1), ring_send(sent[1], -1)]
        ready = work(following)
        work(both([half]), ready)

        carry = {}

        def hop_on(hop, *done):
            for direction in (1, -1):
                off = half if hop == half else hop * direction
                group = range(n_dp)
                if hop == half:
                    group = range(per) if direction == 1 else range(per, n_dp)
                first = 0 if direction == 1 else per
                values = []
                for d in group:
                    value = parts[off, d]
                    if hop == half - 1 and 0 <= d - first < per:
                        value = value.astype(jnp.float32) + carry[direction][d - first].astype(jnp.float32)
                    elif hop < half - 1:
                        value = value.astype(jnp.float32) + carry[direction][d].astype(jnp.float32)
                    values.append(value.astype(jnp.bfloat16))
                carry[direction] = ring_send(after(jnp.stack(values), *done), direction)
            return carry[1], carry[-1]

        first = hop_on(half)
        other = weight_product(
            [after(refs[0], parts[half, n_dp - 1])] + refs[1:], layout, scaleds, 1, jnp.bfloat16, width
        )
        swapped = swap(other)
        second = hop_on(half - 1, other)
        spread, spread_other = spread_product(
            [after(facts[0][0], *first)] + [fact[0] for fact in facts[1:]],
            [fact[1] for fact in facts],
            [own_back] + sent_back,
            slots,
        )
        spread_swapped = swap(spread_other)
        for hop in range(half - 2, 1, -1):
            hop_on(hop, spread)
        weight_grad = weight_product(
            [after(refs[0], *second)] + refs[1:], layout, scaleds, 0, jnp.float32, width, swapped
        )
        hop_on(1, weight_grad)
        hidden_grad = spread + spread_swapped
        hidden_grad = hidden_grad.reshape(cap, n_ex, ff).transpose(1, 0, 2)[None, None]

        layer_out = jnp.zeros((tok, n_dp * width), jnp.bfloat16)
        inner = jnp.zeros((tok, n_ex), jnp.float32)
        for d in reversed(range(n_dp)):
            total = parts[0, d].astype(jnp.float32)
            total = total + carry[1][d].astype(jnp.float32) + carry[-1][d].astype(jnp.float32)
            total = total.astype(jnp.bfloat16)
            piece = total if d == 0 else shift(total, -d)
            layer_out = lax.dynamic_update_slice_in_dim(
                layer_out, piece[:, :width], ((replica + d) % n_dp) * width, axis=1
            )
            found = piece[:, width:].astype(jnp.float32)
            inner = inner + found[:, :n_ex] + found[:, n_ex : 2 * n_ex]

        mine = expert_ids[:, :, None] == jnp.arange(n_ex, dtype=jnp.int32)
        prob_grad = jnp.sum(jnp.where(mine, inner[:, None, :], 0.0), axis=2)
        return (layer_out, prob_grad, hidden_grad, weight_grad[None])

    return shards


def solution(mesh):
    placed = (
        P(("dp", "expert"), None),
        P(("dp", "expert"), None),
        P("dp", "expert", None, None, None),
        P("expert", None, "dp"),
        P(("dp", "expert"), None),
    )
    return jax.shard_map(
        body(chip_ring(mesh)),
        mesh=mesh,
        in_specs=placed,
        out_specs=(
            P(("dp", "expert"), None),
            P(("dp", "expert"), None),
            P("dp", "expert", None, None, None),
            P("expert", None, "dp"),
        ),
        check_vma=False,
    )
```

time: 231 us -> 146 us (0.63)
  Pallas kernels: 0 us -> 48.8 us
  blocking collectives: 43 us -> 0 us
  matrix products: 40.5 us -> 0 us
  local copies, waits for them, and re-layouts: 29 us -> 5.09 us
  waiting for transfers between devices: 42.5 us -> 61.7 us
  starting transfers between devices: 42.2 us -> 24.6 us
  other arithmetic: 19.8 us -> 4.41 us
  between operations: 12.9 us -> 0.96 us
    pallas_call x0 -> x7, Pallas kernels: none -> 48.8 us  [the longest x4 33.8 us: block_product(): pl.pallas_call(functools.partial(block_kernel, plan, len(blocks), n_dp, n...]
    all_gather x1 -> x0, blocking collectives: 43 us -> none  [shards(): facts = lax.all_gather(facts, ('dp', 'expert'), axis=0)]
    dot_general x11 -> x0, matrix products: 40.5 us -> none  [the longest x10 40.4 us: dot(): lax.dot_general(a, b, (((ca,), (cb,)), ((), ())), preferred_element_type=...]
    ppermute x4 -> x6, waiting for transfers between devices: 1.48 us -> 26.3 us  [shift(): lax.ppermute(value, 'dp', [(i, (i + step) % n_dp) for i in range(n_dp)])]
    ppermute x28 -> x16, starting transfers between devices: 31.1 us -> 16.9 us  [ring_send(): return lax.ppermute(value, 'expert', forward if step > 0 else backward)]
    unnamed x53 -> x29, local copies, waits for them, and re-layouts: 16.8 us -> 2.9 us
    convert_element_type x11 -> x3, other arithmetic: 12.8 us -> 0.17 us  [the longest x1 0.16 us: shards(): total = total.astype(jnp.bfloat16)]
    gather x7 -> x0, local copies, waits for them, and re-layouts: 4 us -> none  [the longest x2 1.2 us: shards(): inner = inner[:, inverse].reshape(n_dp * n_ex, tok)]
  transfers between devices with their start and end apart: 51 -> 27, of which waited for: 21 -> 9; matrix products, arithmetic and copies ran while one was open for 36% -> 4% of each run, Pallas kernels for 0% -> 34%
where the time goes in v7:
time: 146 us
  waiting for transfers between devices  61.7 us (42%)
  Pallas kernels  48.8 us (33%)
  starting transfers between devices  24.6 us (17%)
  local copies, waits for them, and re-layouts  5.09 us (3%)
  other arithmetic  4.41 us (3%)
    ppermute x16, waiting for transfers between devices, ring_send(): return lax.ppermute(value, 'expert', forward if step > 0 else backward)  35.4 us
    pallas_call x4, Pallas kernels, block_product(): pl.pallas_call(functools.partial(block_kernel, plan, len(blocks), n_dp, n...  33.8 us
    ppermute x6, waiting for transfers between devices, shift(): lax.ppermute(value, 'dp', [(i, (i + step) % n_dp) for i in range(n_dp)])  26.3 us
    ppermute x16, starting transfers between devices, ring_send(): return lax.ppermute(value, 'expert', forward if step > 0 else backward)  16.9 us
    pallas_call x2, Pallas kernels, weight_product(): pl.pallas_call(functools.partial(weight_kernel, len(blocks), len(scaleds)...  13.7 us
    ppermute x6, starting transfers between devices, shift(): lax.ppermute(value, 'dp', [(i, (i + step) % n_dp) for i in range(n_dp)])  7 us
  transfers between devices with their start and end apart: 27, of which 9 were waited for; matrix products, arithmetic and copies ran while one was open for 4% of the time, Pallas kernels for 34%

profile of v7, /device:TPU:0, one launch (start us, length us, event | category | flops | bytes accessed | tf_op | source)
XLA Modules:
  0.0 145.6 jit_solution(1069528220887299468)
XLA Ops:
  0.6 0.5 collective-permute-start.8
  1.2 2.6 %collective-permute-start.6 = (bf16[576,768]{1,0:T(8,128)(2,1)}, bf16[576,768]{1,0:T(8,128)(2,1)S(1)}, u32[]{:S(2)}, u32[]{:S(2)}) collective-permute-start(bf16[576,768]{1,0:T(8,128)(2,1)} %bitcast.107), channel_id=1, source_target_pairs={{0,16},{16,0},{1,17},{17,1},{2,18},{18,2},{3,19},{19,3},{4,20},{20... | collective-permute-start | bytes 2654216 | tf_op jit(solution)/shard_map/ppermute | solution.py:288
  3.7 0.8 copy.18
  4.5 0.7 reduce-precision_convert_fusion.1
  5.2 0.1 copy.19
  5.3 0.1 copy.21
  5.4 0.7 convert_convert_fusion
  6.1 0.1 copy.20
  6.2 0.1 fusion.30
  6.3 1.1 constant_dynamic-slice_fusion.1
  7.4 0.2 collective-permute-start
  7.5 0.1 collective-permute-start.5
  7.7 16.8 %collective-permute-done.6.refs_8_.refs_5_ = bf16[576,768]{1,0:T(8,128)(2,1)S(1)} collective-permute-done((bf16[576,768]{1,0:T(8,128)(2,1)}, bf16[576,768]{1,0:T(8,128)(2,1)S(1)}, u32[]{:S(2)}, u32[]{:S(2)}) %collective-permute-start.6) | collective-permute-done | bytes 884768 | tf_op jit(solution)/shard_map/ppermute | solution.py:288
  24.4 4.2 %collective-permute-done = bf16[48,2176]{1,0:T(8,128)(2,1)S(1)} collective-permute-done((bf16[48,2176]{1,0:T(8,128)(2,1)S(1)}, bf16[48,2176]{1,0:T(8,128)(2,1)S(1)}, u32[]{:S(2)}, u32[]{:S(2)}) %collective-permute-start) | collective-permute-done | bytes 208928 | tf_op jit(solution)/shard_map/ppermute | solution.py:288
  28.7 1.8 %collective-permute-start.3 = (bf16[2,48,2176]{2,1,0:T(8,128)(2,1)S(1)}, bf16[2,48,2176]{2,1,0:T(8,128)(2,1)S(1)}, u32[]{:S(2)}, u32[]{:S(2)}) collective-permute-start(bf16[2,48,2176]{2,1,0:T(8,128)(2,1)S(1)} %pad_maximum_fusion.refs_3_.refs_1_.refs_0_), channel_id=1, source_target_pairs={{0,2},{1,3},{4,0},{5,1},{8,4},{9,5},{12,8},{13,9},{14,12},{15,13},... | collective-permute-start | bytes 1253384 | tf_op jit(solution)/shard_map/ppermute | solution.py:291
  30.5 0.2 collective-permute-start.1
  30.8 9.4 %collective-permute-done.3.refs_5_.refs_3_.refs_2_ = bf16[2,48,2176]{2,1,0:T(8,128)(2,1)S(1)} collective-permute-done((bf16[2,48,2176]{2,1,0:T(8,128)(2,1)S(1)}, bf16[2,48,2176]{2,1,0:T(8,128)(2,1)S(1)}, u32[]{:S(2)}, u32[]{:S(2)}) %collective-permute-start.3) | collective-permute-done | bytes 417824 | tf_op jit(solution)/shard_map/ppermute | solution.py:291
  40.1 1.6 %collective-permute-start.4 = (bf16[2,48,2176]{2,1,0:T(8,128)(2,1)S(1)}, bf16[2,48,2176]{2,1,0:T(8,128)(2,1)}, u32[]{:S(2)}, u32[]{:S(2)}) collective-permute-start(bf16[2,48,2176]{2,1,0:T(8,128)(2,1)S(1)} %collective-permute-done.3.refs_5_.refs_3_.refs_2_), channel_id=1, source_target_pairs={{0,2},{1,3},{4,0},{5,1},{8,4},{9,5},{12,8},{13,9},{14,12},{15,13},... | collective-permute-start | bytes 1253384 | tf_op jit(solution)/shard_map/ppermute | solution.py:291
  41.7 0.4 collective-permute-start.2
  42.2 0.7 fusion.31.refs_0_
  42.9 7.4 %block_product.5 = (bf16[48,2176]{1,0:T(8,128)(2,1)S(1)}, bf16[48,2176]{1,0:T(8,128)(2,1)S(1)}, bf16[48,2176]{1,0:T(8,128)(2,1)S(1)}, bf16[2,144,768]{2,1,0:T(8,...) custom-call(s32[10]{0:T(128)S(1)} %fusion.31.refs_0_, ...), custom_call_target="tpu_custom_call" | custom-call | flops 1811939328 | bytes 7987200 | tf_op jit(solution)/shard_map/block_product/pallas_call | solution.py:143
  50.4 0.7 copy-done.6
  51.0 0.7 copy-done.8
  51.7 1.6 %collective-permute-start.10 = (bf16[2,48,2176]{2,1,0:T(8,128)(2,1)}, bf16[2,48,2176]{2,1,0:T(8,128)(2,1)S(1)}, u32[]{:S(2)}, u32[]{:S(2)}) collective-permute-start(bf16[2,48,2176]{2,1,0:T(8,128)(2,1)} %collective-permute-done.4.refs_2_.refs_4_), channel_id=1, source_target_pairs={{0,2},{1,3},{4,0},{5,1},{8,4},{9,5},{12,8},{13,9},{14,12},{15,13},... | collective-permute-start | bytes 1253384 | tf_op jit(solution)/shard_map/ppermute | solution.py:291
  53.4 0.4 collective-permute-start.9
  53.8 10.7 %block_product.4 = (bf16[48,2176]{1,0:T(8,128)(2,1)S(1)}, bf16[48,2176]{1,0:T(8,128)(2,1)S(1)}, bf16[48,2176]{1,0:T(8,128)(2,1)S(1)}, bf16[48,2176]{1,0:T(8,128)...) custom-call(s32[10]{0:T(128)S(1)} %fusion.31.refs_0_, ...), custom_call_target="tpu_custom_call" | custom-call | flops 4227858432 | bytes 10248192 | tf_op jit(solution)/shard_map/block_product/pallas_call | solution.py:143
  64.5 1.6 %collective-permute-start.16 = (bf16[2,240,768]{2,1,0:T(8,128)(2,1)S(1)}, bf16[2,240,768]{2,1,0:T(8,128)(2,1)S(1)}, u32[]{:S(2)}, u32[]{:S(2)}) collective-permute-start(bf16[2,240,768]{2,1,0:T(8,128)(2,1)S(1)} %get-tuple-element.96), channel_id=1, source_target_pairs={{0,16},{16,0},{1,17},{17,1},{2,18},{18,2},{3,19},{19,3},{4,20},{20... | collective-permute-start | bytes 2211848 | tf_op jit(solution)/shard_map/ppermute | solution.py:288
  66.2 1.6 %collective-permute-start.12 = (bf16[1,48,2176]{2,1,0:T(8,128)(2,1)S(1)}, bf16[1,48,2176]{2,1,0:T(8,128)(2,1)S(1)}, u32[]{:S(2)}, u32[]{:S(2)}) collective-permute-start(bf16[1,48,2176]{2,1,0:T(8,128)(2,1)S(1)} %slice.89), channel_id=1, source_target_pairs={{0,2},{1,3},{4,0},{5,1},{8,4},{9,5},{12,8},{13,9},{14,12},{15,13},... | collective-permute-start | bytes 626696 | tf_op jit(solution)/shard_map/ppermute | solution.py:291
  67.8 0.7 collective-permute-start.11
  68.5 8.0 %block_product.6 = (bf16[48,2176]{1,0:T(8,128)(2,1)S(1)}, bf16[48,2176]{1,0:T(8,128)(2,1)S(1)}, bf16[48,2176]{1,0:T(8,128)(2,1)S(1)}, bf16[48,2176]{1,0:T(8,128)...) custom-call(s32[10]{0:T(128)S(1)} %fusion.31.refs_0_, ...), custom_call_target="tpu_custom_call" | custom-call | flops 2415919104 | bytes 8552448 | tf_op jit(solution)/shard_map/block_product/pallas_call | solution.py:143
  76.6 0.5 collective-permute-start.17
  77.1 7.6 %block_product.7 = (bf16[48,2176]{1,0:T(8,128)(2,1)S(1)}, bf16[48,2176]{1,0:T(8,128)(2,1)S(1)}, bf16[2,48,768]{2,1,0:T(8,128)(2,1)S(1)}, bf16[2,48,768]{2,1,0:T(...) custom-call(s32[10]{0:T(128)S(1)} %fusion.31.refs_0_, ...), custom_call_target="tpu_custom_call" | custom-call | flops 1207959552 | bytes 7421952 | tf_op jit(solution)/shard_map/block_product/pallas_call | solution.py:143
  84.7 0.0 copy-start.10
  84.7 1.7 %collective-permute-start.13 = (bf16[1,48,2176]{2,1,0:T(8,128)(2,1)S(1)}, bf16[1,48,2176]{2,1,0:T(8,128)(2,1)S(1)}, u32[]{:S(2)}, u32[]{:S(2)}) collective-permute-start(bf16[1,48,2176]{2,1,0:T(8,128)(2,1)S(1)} %bitcast.115), channel_id=1, source_target_pairs={{0,4},{1,5},{4,8},{5,9},{8,12},{9,13},{12,14},{13,15},{14,10},{15,... | collective-permute-start | bytes 626696 | tf_op jit(solution)/shard_map/ppermute | solution.py:291
  86.4 0.4 collective-permute-start.15
  86.8 1.5 %collective-permute-start.18 = (bf16[2,48,768]{2,1,0:T(8,128)(2,1)S(1)}, bf16[2,48,768]{2,1,0:T(8,128)(2,1)S(1)}, u32[]{:S(2)}, u32[]{:S(2)}) collective-permute-start(bf16[2,48,768]{2,1,0:T(8,128)(2,1)S(1)} %get-tuple-element.98), channel_id=1, source_target_pairs={{0,16},{16,0},{1,17},{17,1},{2,18},{18,2},{3,19},{19,3},{4,20},{20... | collective-permute-start | bytes 442376 | tf_op jit(solution)/shard_map/ppermute | solution.py:288
  88.4 6.2 %weight_product.2 = bf16[768,2048]{1,0:T(8,128)(2,1)} custom-call(bf16[2,48,2176]{2,1,0:T(8,128)(2,1)S(1)} %pad_maximum_fusion.refs_3_.refs_1_.refs_0_, bf16[2,48,2176]{2,1,0:T(8,128)(2,1)} %collective-permute-done.1.refs_4_.refs_2_.refs_1_, bf16[2,48,2176]{2,1,0:T(8,128)(2,1)S(1)} %collective-permute-done.3.refs_5_.refs_3_.refs_2_, ...), custom_call_target="tpu_custom_call" | custom-call | flops 2415919104 | bytes 10616832 | tf_op jit(solution)/shard_map/weight_product/pallas_call | solution.py:225
  94.6 0.1 collective-permute-start.21
  94.6 0.1 fusion.18
  94.8 1.6 %collective-permute-start.20 = (bf16[2,48,2176]{2,1,0:T(8,128)(2,1)S(1)}, bf16[2,48,2176]{2,1,0:T(8,128)(2,1)S(1)}, u32[]{:S(2)}, u32[]{:S(2)}) collective-permute-start(bf16[2,48,2176]{2,1,0:T(8,128)(2,1)S(1)} %pad_maximum_fusion.4), channel_id=1, source_target_pairs={{0,2},{1,3},{4,0},{5,1},{8,4},{9,5},{12,8},{13,9},{14,12},{15,13},... | collective-permute-start | bytes 1253384 | tf_op jit(solution)/shard_map/ppermute | solution.py:291
  96.3 0.1 fusion.13
  96.5 0.6 collective-permute-start.14
  97.0 1.3 spread_product.1
  98.4 8.5 %collective-permute-done.20 = bf16[2,48,2176]{2,1,0:T(8,128)(2,1)S(1)} collective-permute-done((bf16[2,48,2176]{2,1,0:T(8,128)(2,1)S(1)}, bf16[2,48,2176]{2,1,0:T(8,128)(2,1)S(1)}, u32[]{:S(2)}, u32[]{:S(2)}) %collective-permute-start.20) | collective-permute-done | bytes 417824 | tf_op jit(solution)/shard_map/ppermute | solution.py:291
  106.9 0.1 fusion.19
  107.0 1.6 %collective-permute-start.23 = (bf16[2,48,2176]{2,1,0:T(8,128)(2,1)S(1)}, bf16[2,48,2176]{2,1,0:T(8,128)(2,1)S(1)}, u32[]{:S(2)}, u32[]{:S(2)}) collective-permute-start(bf16[2,48,2176]{2,1,0:T(8,128)(2,1)S(1)} %pad_maximum_fusion.5), channel_id=1, source_target_pairs={{0,2},{1,3},{4,0},{5,1},{8,4},{9,5},{12,8},{13,9},{14,12},{15,13},... | collective-permute-start | bytes 1253384 | tf_op jit(solution)/shard_map/ppermute | solution.py:291
  108.6 0.1 fusion.14
  108.8 0.6 collective-permute-start.19
  109.4 9.0 %collective-permute-done.23 = bf16[2,48,2176]{2,1,0:T(8,128)(2,1)S(1)} collective-permute-done((bf16[2,48,2176]{2,1,0:T(8,128)(2,1)S(1)}, bf16[2,48,2176]{2,1,0:T(8,128)(2,1)S(1)}, u32[]{:S(2)}, u32[]{:S(2)}) %collective-permute-start.23) | collective-permute-done | bytes 417824 | tf_op jit(solution)/shard_map/ppermute | solution.py:291
  118.4 1.5 %collective-permute-done.19 = bf16[2,48,2176]{2,1,0:T(8,128)(2,1)S(1)} collective-permute-done((bf16[2,48,2176]{2,1,0:T(8,128)(2,1)S(1)}, bf16[2,48,2176]{2,1,0:T(8,128)(2,1)S(1)}, u32[]{:S(2)}, u32[]{:S(2)}) %collective-permute-start.19) | collective-permute-done | bytes 417824 | tf_op jit(solution)/shard_map/ppermute | solution.py:291
  119.8 0.2 fusion.16
  120.2 7.5 %weight_product.3 = f32[768,2048]{1,0:T(8,128)} custom-call(bf16[2,48,2176]{2,1,0:T(8,128)(2,1)S(1)} %pad_maximum_fusion.refs_3_.refs_1_.refs_0_, bf16[2,48,2176]{2,1,0:T(8,128)(2,1)} %collective-permute-done.1.refs_4_.refs_2_.refs_1_, bf16[2,48,2176]{2,1,0:T(8,128)(2,1)S(1)} %collective-permute-done.3.refs_5_.refs_3_.refs_2_, ...), custom_call_target="tpu_custom_call" | custom-call | flops 2415919104 | bytes 10616832 | tf_op jit(solution)/shard_map/weight_product/pallas_call | solution.py:225
  127.6 0.5 collective-permute-start.22
  128.2 1.5 %collective-permute-start.24 = (bf16[2,48,2176]{2,1,0:T(8,128)(2,1)S(1)}, bf16[2,48,2176]{2,1,0:T(8,128)(2,1)S(1)}, u32[]{:S(2)}, u32[]{:S(2)}) collective-permute-start(bf16[2,48,2176]{2,1,0:T(8,128)(2,1)S(1)} %pad_maximum_fusion.6), channel_id=1, source_target_pairs={{0,2},{1,3},{4,0},{5,1},{8,4},{9,5},{12,8},{13,9},{14,12},{15,13},... | collective-permute-start | bytes 1253384 | tf_op jit(solution)/shard_map/ppermute | solution.py:291
  129.7 1.2 add.104
  130.8 6.9 %collective-permute-done.22 = bf16[2,48,2176]{2,1,0:T(8,128)(2,1)S(1)} collective-permute-done((bf16[2,48,2176]{2,1,0:T(8,128)(2,1)S(1)}, bf16[2,48,2176]{2,1,0:T(8,128)(2,1)S(1)}, u32[]{:S(2)}, u32[]{:S(2)}) %collective-permute-start.22) | collective-permute-done | bytes 417824 | tf_op jit(solution)/shard_map/ppermute | solution.py:291
  137.7 0.2 collective-permute-done.24
  137.9 0.2 fusion
  138.1 0.6 collective-permute-start.25
  138.6 5.3 %collective-permute-done.25 = bf16[48,2176]{1,0:T(8,128)(2,1)S(1)} collective-permute-done((bf16[48,2176]{1,0:T(8,128)(2,1)S(1)}, bf16[48,2176]{1,0:T(8,128)(2,1)S(1)}, u32[]{:S(2)}, u32[]{:S(2)}) %collective-permute-start.25) | collective-permute-done | bytes 208928 | tf_op jit(solution)/shard_map/ppermute | solution.py:288
  144.0 0.1 slice_add_fusion
  144.0 0.1 copy.22
  144.1 0.6 select_reduce_fusion
  144.8 0.7 copy-done.12
  (60 shorter events, 0.6 us)
Async XLA Ops:
  0.6 42.3 %copy-start = (bf16[1,1,16,36,768]{4,2,3,1,0:T(8,128)(2,1)S(1)}, bf16[1,1,16,36,768]{4,2,3,1,0:T(8,128)(2,1)}, u32[]{:S(2)}) copy-start(bf16[1,1,16,36,768]{4,2,3,1,0:T(8,128)(2,1)} %param.8) | copy-start | bytes 2654212
  0.6 42.2 %collective-permute-start.8 = (bf16[768,2048]{1,0:T(8,128)(2,1)}, bf16[768,2048]{1,0:T(8,128)(2,1)}, u32[]{:S(2)}, u32[]{:S(2)}) collective-permute-start(bf16[768,2048]{1,0:T(8,128)(2,1)} %bitcast.117), channel_id=1, source_target_pairs={{0,1},{1,0},{2,3},{3,2},{4,5},{5,4},{6,7},{7,6},{8,9},{9,8},{10,11... | collective-permute-start | bytes 9437192 | tf_op jit(solution)/shard_map/ppermute | solution.py:294
  1.2 23.3 %collective-permute-start.6 = (bf16[576,768]{1,0:T(8,128)(2,1)}, bf16[576,768]{1,0:T(8,128)(2,1)S(1)}, u32[]{:S(2)}, u32[]{:S(2)}) collective-permute-start(bf16[576,768]{1,0:T(8,128)(2,1)} %bitcast.107), channel_id=1, source_target_pairs={{0,16},{16,0},{1,17},{17,1},{2,18},{18,2},{3,19},{19,3},{4,20},{20... | collective-permute-start | bytes 2654216 | tf_op jit(solution)/shard_map/ppermute | solution.py:288
  7.4 21.3 %collective-permute-start = (bf16[48,2176]{1,0:T(8,128)(2,1)S(1)}, bf16[48,2176]{1,0:T(8,128)(2,1)S(1)}, u32[]{:S(2)}, u32[]{:S(2)}) collective-permute-start(bf16[48,2176]{1,0:T(8,128)(2,1)S(1)} %get-tuple-element.127), channel_id=1, source_target_pairs={{0,16},{16,0},{1,17},{17,1},{2,18},{18,2},{3,19},{19,3},{4,20},{20... | collective-permute-start | bytes 626696 | tf_op jit(solution)/shard_map/ppermute | solution.py:288
  7.5 35.3 %collective-permute-start.5 = (bf16[576,768]{1,0:T(8,128)(2,1)}, bf16[576,768]{1,0:T(8,128)(2,1)S(1)}, u32[]{:S(2)}, u32[]{:S(2)}) collective-permute-start(bf16[576,768]{1,0:T(8,128)(2,1)} %bitcast.108), channel_id=1, source_target_pairs={{0,1},{1,0},{2,3},{3,2},{4,5},{5,4},{6,7},{7,6},{8,9},{9,8},{10,11... | collective-permute-start | bytes 2654216 | tf_op jit(solution)/shard_map/ppermute | solution.py:294
  24.4 25.9 %copy-start.4 = (bf16[576,768]{1,0:T(8,128)(2,1)}, bf16[576,768]{1,0:T(8,128)(2,1)S(1)}, u32[]{:S(2)}) copy-start(bf16[576,768]{1,0:T(8,128)(2,1)S(1)} %collective-permute-done.6.refs_8_.refs_5_) | copy-start | bytes 2654212
  24.4 29.4 %collective-permute-start.7 = (bf16[576,768]{1,0:T(8,128)(2,1)S(1)}, bf16[576,768]{1,0:T(8,128)(2,1)}, u32[]{:S(2)}, u32[]{:S(2)}) collective-permute-start(bf16[576,768]{1,0:T(8,128)(2,1)S(1)} %collective-permute-done.6.refs_8_.refs_5_), channel_id=1, source_target_pairs={{0,1},{1,0},{2,3},{3,2},{4,5},{5,4},{6,7},{7,6},{8,9},{9,8},{10,11... | collective-permute-start | bytes 2654216 | tf_op jit(solution)/shard_map/ppermute | solution.py:294
  28.7 11.4 %collective-permute-start.3 = (bf16[2,48,2176]{2,1,0:T(8,128)(2,1)S(1)}, bf16[2,48,2176]{2,1,0:T(8,128)(2,1)S(1)}, u32[]{:S(2)}, u32[]{:S(2)}) collective-permute-start(bf16[2,48,2176]{2,1,0:T(8,128)(2,1)S(1)} %pad_maximum_fusion.refs_3_.refs_1_.refs_0_), channel_id=1, source_target_pairs={{0,2},{1,3},{4,0},{5,1},{8,4},{9,5},{12,8},{13,9},{14,12},{15,13},... | collective-permute-start | bytes 1253384 | tf_op jit(solution)/shard_map/ppermute | solution.py:291
  30.5 11.2 %collective-permute-start.1 = (bf16[2,48,2176]{2,1,0:T(8,128)(2,1)S(1)}, bf16[2,48,2176]{2,1,0:T(8,128)(2,1)}, u32[]{:S(2)}, u32[]{:S(2)}) collective-permute-start(bf16[2,48,2176]{2,1,0:T(8,128)(2,1)S(1)} %pad_maximum_fusion.refs_3_.refs_1_.refs_0_), channel_id=1, source_target_pairs={{0,4},{1,5},{4,8},{5,9},{8,12},{9,13},{12,14},{13,15},{14,10},{15,... | collective-permute-start | bytes 1253384 | tf_op jit(solution)/shard_map/ppermute | solution.py:291
  40.1 11.6 %collective-permute-start.4 = (bf16[2,48,2176]{2,1,0:T(8,128)(2,1)S(1)}, bf16[2,48,2176]{2,1,0:T(8,128)(2,1)}, u32[]{:S(2)}, u32[]{:S(2)}) collective-permute-start(bf16[2,48,2176]{2,1,0:T(8,128)(2,1)S(1)} %collective-permute-done.3.refs_5_.refs_3_.refs_2_), channel_id=1, source_target_pairs={{0,2},{1,3},{4,0},{5,1},{8,4},{9,5},{12,8},{13,9},{14,12},{15,13},... | collective-permute-start | bytes 1253384 | tf_op jit(solution)/shard_map/ppermute | solution.py:291
  41.7 11.6 %collective-permute-start.2 = (bf16[2,48,2176]{2,1,0:T(8,128)(2,1)}, bf16[2,48,2176]{2,1,0:T(8,128)(2,1)}, u32[]{:S(2)}, u32[]{:S(2)}) collective-permute-start(bf16[2,48,2176]{2,1,0:T(8,128)(2,1)} %collective-permute-done.1.refs_4_.refs_2_.refs_1_), channel_id=1, source_target_pairs={{0,4},{1,5},{4,8},{5,9},{8,12},{9,13},{12,14},{13,15},{14,10},{15,... | collective-permute-start | bytes 1253384 | tf_op jit(solution)/shard_map/ppermute | solution.py:291
  42.9 7.5 %copy-start.2 = (bf16[576,768]{1,0:T(8,128)(2,1)}, bf16[576,768]{1,0:T(8,128)(2,1)S(1)}, u32[]{:S(2)}) copy-start(bf16[576,768]{1,0:T(8,128)(2,1)S(1)} %collective-permute-done.5.refs_7_.refs_5_.refs_4_) | copy-start | bytes 2654212
  50.4 0.7 copy-start.6
  51.0 0.7 copy-start.8
  51.7 16.8 %copy-start.1 = (bf16[1,1,16,36,768]{4,2,3,1,0:T(8,128)(2,1)S(1)}, bf16[1,1,16,36,768]{4,2,3,1,0:T(8,128)(2,1)}, u32[]{:S(2)}) copy-start(bf16[1,1,16,36,768]{4,2,3,1,0:T(8,128)(2,1)} %param.8) | copy-start | bytes 2654212
  51.7 16.8 %copy-start.3 = (bf16[576,768]{1,0:T(8,128)(2,1)S(1)}, bf16[576,768]{1,0:T(8,128)(2,1)}, u32[]{:S(2)}) copy-start(bf16[576,768]{1,0:T(8,128)(2,1)} %copy-done.2) | copy-start | bytes 2654212
  51.7 16.8 %copy-start.5 = (bf16[576,768]{1,0:T(8,128)(2,1)S(1)}, bf16[576,768]{1,0:T(8,128)(2,1)}, u32[]{:S(2)}) copy-start(bf16[576,768]{1,0:T(8,128)(2,1)} %copy-done.4) | copy-start | bytes 2654212
  51.7 14.4 %collective-permute-start.10 = (bf16[2,48,2176]{2,1,0:T(8,128)(2,1)}, bf16[2,48,2176]{2,1,0:T(8,128)(2,1)S(1)}, u32[]{:S(2)}, u32[]{:S(2)}) collective-permute-start(bf16[2,48,2176]{2,1,0:T(8,128)(2,1)} %collective-permute-done.4.refs_2_.refs_4_), channel_id=1, source_target_pairs={{0,2},{1,3},{4,0},{5,1},{8,4},{9,5},{12,8},{13,9},{14,12},{15,13},... | collective-permute-start | bytes 1253384 | tf_op jit(solution)/shard_map/ppermute | solution.py:291
  53.4 14.4 %collective-permute-start.9 = (bf16[2,48,2176]{2,1,0:T(8,128)(2,1)}, bf16[2,48,2176]{2,1,0:T(8,128)(2,1)S(1)}, u32[]{:S(2)}, u32[]{:S(2)}) collective-permute-start(bf16[2,48,2176]{2,1,0:T(8,128)(2,1)} %collective-permute-done.2.refs_1_.refs_3_), channel_id=1, source_target_pairs={{0,4},{1,5},{4,8},{5,9},{8,12},{9,13},{12,14},{13,15},{14,10},{15,... | collective-permute-start | bytes 1253384 | tf_op jit(solution)/shard_map/ppermute | solution.py:291
  64.5 32.5 %collective-permute-start.16 = (bf16[2,240,768]{2,1,0:T(8,128)(2,1)S(1)}, bf16[2,240,768]{2,1,0:T(8,128)(2,1)S(1)}, u32[]{:S(2)}, u32[]{:S(2)}) collective-permute-start(bf16[2,240,768]{2,1,0:T(8,128)(2,1)S(1)} %get-tuple-element.96), channel_id=1, source_target_pairs={{0,16},{16,0},{1,17},{17,1},{2,18},{18,2},{3,19},{19,3},{4,20},{20... | collective-permute-start | bytes 2211848 | tf_op jit(solution)/shard_map/ppermute | solution.py:288
  66.2 10.9 %collective-permute-start.12 = (bf16[1,48,2176]{2,1,0:T(8,128)(2,1)S(1)}, bf16[1,48,2176]{2,1,0:T(8,128)(2,1)S(1)}, u32[]{:S(2)}, u32[]{:S(2)}) collective-permute-start(bf16[1,48,2176]{2,1,0:T(8,128)(2,1)S(1)} %slice.89), channel_id=1, source_target_pairs={{0,2},{1,3},{4,0},{5,1},{8,4},{9,5},{12,8},{13,9},{14,12},{15,13},... | collective-permute-start | bytes 626696 | tf_op jit(solution)/shard_map/ppermute | solution.py:291
  67.8 9.3 %collective-permute-start.11 = (bf16[1,48,2176]{2,1,0:T(8,128)(2,1)S(1)}, bf16[1,48,2176]{2,1,0:T(8,128)(2,1)S(1)}, u32[]{:S(2)}, u32[]{:S(2)}) collective-permute-start(bf16[1,48,2176]{2,1,0:T(8,128)(2,1)S(1)} %slice.88), channel_id=1, source_target_pairs={{0,4},{1,5},{4,8},{5,9},{8,12},{9,13},{12,14},{13,15},{14,10},{15,... | collective-permute-start | bytes 626696 | tf_op jit(solution)/shard_map/ppermute | solution.py:291
  76.6 19.9 %collective-permute-start.17 = (bf16[2,96,768]{2,1,0:T(8,128)(2,1)S(1)}, bf16[2,96,768]{2,1,0:T(8,128)(2,1)S(1)}, u32[]{:S(2)}, u32[]{:S(2)}) collective-permute-start(bf16[2,96,768]{2,1,0:T(8,128)(2,1)S(1)} %get-tuple-element.97), channel_id=1, source_target_pairs={{0,16},{16,0},{1,17},{17,1},{2,18},{18,2},{3,19},{19,3},{4,20},{20... | collective-permute-start | bytes 884744 | tf_op jit(solution)/shard_map/ppermute | solution.py:288
  84.7 9.8 %copy-start.10 = (bf16[2,48,768]{2,1,0:T(8,128)(2,1)}, bf16[2,48,768]{2,1,0:T(8,128)(2,1)S(1)}, u32[]{:S(2)}) copy-start(bf16[2,48,768]{2,1,0:T(8,128)(2,1)S(1)} %get-tuple-element.79.refs_14_) | copy-start | bytes 442372
  84.7 10.0 %collective-permute-start.13 = (bf16[1,48,2176]{2,1,0:T(8,128)(2,1)S(1)}, bf16[1,48,2176]{2,1,0:T(8,128)(2,1)S(1)}, u32[]{:S(2)}, u32[]{:S(2)}) collective-permute-start(bf16[1,48,2176]{2,1,0:T(8,128)(2,1)S(1)} %bitcast.115), channel_id=1, source_target_pairs={{0,4},{1,5},{4,8},{5,9},{8,12},{9,13},{12,14},{13,15},{14,10},{15,... | collective-permute-start | bytes 626696 | tf_op jit(solution)/shard_map/ppermute | solution.py:291
  86.4 8.1 %collective-permute-start.15 = (bf16[1,48,2176]{2,1,0:T(8,128)(2,1)S(1)}, bf16[1,48,2176]{2,1,0:T(8,128)(2,1)S(1)}, u32[]{:S(2)}, u32[]{:S(2)}) collective-permute-start(bf16[1,48,2176]{2,1,0:T(8,128)(2,1)S(1)} %bitcast.116), channel_id=1, source_target_pairs={{0,2},{1,3},{4,0},{5,1},{8,4},{9,5},{12,8},{13,9},{14,12},{15,13},... | collective-permute-start | bytes 626696 | tf_op jit(solution)/shard_map/ppermute | solution.py:291
  86.8 10.2 %collective-permute-start.18 = (bf16[2,48,768]{2,1,0:T(8,128)(2,1)S(1)}, bf16[2,48,768]{2,1,0:T(8,128)(2,1)S(1)}, u32[]{:S(2)}, u32[]{:S(2)}) collective-permute-start(bf16[2,48,768]{2,1,0:T(8,128)(2,1)S(1)} %get-tuple-element.98), channel_id=1, source_target_pairs={{0,16},{16,0},{1,17},{17,1},{2,18},{18,2},{3,19},{19,3},{4,20},{20... | collective-permute-start | bytes 442376 | tf_op jit(solution)/shard_map/ppermute | solution.py:288
  94.6 25.6 %collective-permute-start.21 = (bf16[768,2048]{1,0:T(8,128)(2,1)}, bf16[768,2048]{1,0:T(8,128)(2,1)}, u32[]{:S(2)}, u32[]{:S(2)}) collective-permute-start(bf16[768,2048]{1,0:T(8,128)(2,1)} %weight_product.2), channel_id=1, source_target_pairs={{0,1},{1,0},{2,3},{3,2},{4,5},{5,4},{6,7},{7,6},{8,9},{9,8},{10,11... | collective-permute-start | bytes 9437192 | tf_op jit(solution)/shard_map/ppermute | solution.py:294
  94.8 12.1 %collective-permute-start.20 = (bf16[2,48,2176]{2,1,0:T(8,128)(2,1)S(1)}, bf16[2,48,2176]{2,1,0:T(8,128)(2,1)S(1)}, u32[]{:S(2)}, u32[]{:S(2)}) collective-permute-start(bf16[2,48,2176]{2,1,0:T(8,128)(2,1)S(1)} %pad_maximum_fusion.4), channel_id=1, source_target_pairs={{0,2},{1,3},{4,0},{5,1},{8,4},{9,5},{12,8},{13,9},{14,12},{15,13},... | collective-permute-start | bytes 1253384 | tf_op jit(solution)/shard_map/ppermute | solution.py:291
  96.5 12.2 %collective-permute-start.14 = (bf16[2,48,2176]{2,1,0:T(8,128)(2,1)S(1)}, bf16[2,48,2176]{2,1,0:T(8,128)(2,1)S(1)}, u32[]{:S(2)}, u32[]{:S(2)}) collective-permute-start(bf16[2,48,2176]{2,1,0:T(8,128)(2,1)S(1)} %pad_maximum_fusion.1), channel_id=1, source_target_pairs={{0,4},{1,5},{4,8},{5,9},{8,12},{9,13},{12,14},{13,15},{14,10},{15,... | collective-permute-start | bytes 1253384 | tf_op jit(solution)/shard_map/ppermute | solution.py:291
  97.0 22.8 %copy-start.7 = (bf16[48,2176]{1,0:T(8,128)(2,1)S(1)}, bf16[48,2176]{1,0:T(8,128)(2,1)}, u32[]{:S(2)}) copy-start(bf16[48,2176]{1,0:T(8,128)(2,1)} %copy-done.6) | copy-start | bytes 626692
  97.0 22.8 %copy-start.9 = (bf16[48,2176]{1,0:T(8,128)(2,1)S(1)}, bf16[48,2176]{1,0:T(8,128)(2,1)}, u32[]{:S(2)}) copy-start(bf16[48,2176]{1,0:T(8,128)(2,1)} %copy-done.8) | copy-start | bytes 626692
  107.0 13.1 %copy-start.11 = (bf16[2,48,768]{2,1,0:T(8,128)(2,1)S(1)}, bf16[2,48,768]{2,1,0:T(8,128)(2,1)}, u32[]{:S(2)}) copy-start(bf16[2,48,768]{2,1,0:T(8,128)(2,1)} %copy-done.10) | copy-start | bytes 442372
  107.0 11.3 %collective-permute-start.23 = (bf16[2,48,2176]{2,1,0:T(8,128)(2,1)S(1)}, bf16[2,48,2176]{2,1,0:T(8,128)(2,1)S(1)}, u32[]{:S(2)}, u32[]{:S(2)}) collective-permute-start(bf16[2,48,2176]{2,1,0:T(8,128)(2,1)S(1)} %pad_maximum_fusion.5), channel_id=1, source_target_pairs={{0,2},{1,3},{4,0},{5,1},{8,4},{9,5},{12,8},{13,9},{14,12},{15,13},... | collective-permute-start | bytes 1253384 | tf_op jit(solution)/shard_map/ppermute | solution.py:291
  108.8 11.0 %collective-permute-start.19 = (bf16[2,48,2176]{2,1,0:T(8,128)(2,1)S(1)}, bf16[2,48,2176]{2,1,0:T(8,128)(2,1)S(1)}, u32[]{:S(2)}, u32[]{:S(2)}) collective-permute-start(bf16[2,48,2176]{2,1,0:T(8,128)(2,1)S(1)} %pad_maximum_fusion.2), channel_id=1, source_target_pairs={{0,4},{1,5},{4,8},{5,9},{8,12},{9,13},{12,14},{13,15},{14,10},{15,... | collective-permute-start | bytes 1253384 | tf_op jit(solution)/shard_map/ppermute | solution.py:291
  109.3 20.3 %collective-permute-start.26 = (bf16[576,768]{1,0:T(8,128)(2,1)S(1)}, bf16[576,768]{1,0:T(8,128)(2,1)S(1)}, u32[]{:S(2)}, u32[]{:S(2)}) collective-permute-start(bf16[576,768]{1,0:T(8,128)(2,1)S(1)} %get-tuple-element.111), channel_id=1, source_target_pairs={{0,1},{1,0},{2,3},{3,2},{4,5},{5,4},{6,7},{7,6},{8,9},{9,8},{10,11... | collective-permute-start | bytes 2654216 | tf_op jit(solution)/shard_map/ppermute | solution.py:294
  127.6 16.5 %copy-start.13 = (s32[48,8]{0,1:T(8,128)S(1)}, s32[48,8]{0,1:T(8,128)}, u32[]{:S(2)}) copy-start(s32[48,8]{0,1:T(8,128)} %param.6) | copy-start | bytes 4612
  127.6 10.1 %collective-permute-start.22 = (bf16[2,48,2176]{2,1,0:T(8,128)(2,1)S(1)}, bf16[2,48,2176]{2,1,0:T(8,128)(2,1)S(1)}, u32[]{:S(2)}, u32[]{:S(2)}) collective-permute-start(bf16[2,48,2176]{2,1,0:T(8,128)(2,1)S(1)} %pad_maximum_fusion.3), channel_id=1, source_target_pairs={{0,4},{1,5},{4,8},{5,9},{8,12},{9,13},{12,14},{13,15},{14,10},{15,... | collective-permute-start | bytes 1253384 | tf_op jit(solution)/shard_map/ppermute | solution.py:291
  128.2 9.8 %collective-permute-start.24 = (bf16[2,48,2176]{2,1,0:T(8,128)(2,1)S(1)}, bf16[2,48,2176]{2,1,0:T(8,128)(2,1)S(1)}, u32[]{:S(2)}, u32[]{:S(2)}) collective-permute-start(bf16[2,48,2176]{2,1,0:T(8,128)(2,1)S(1)} %pad_maximum_fusion.6), channel_id=1, source_target_pairs={{0,2},{1,3},{4,0},{5,1},{8,4},{9,5},{12,8},{13,9},{14,12},{15,13},... | collective-permute-start | bytes 1253384 | tf_op jit(solution)/shard_map/ppermute | solution.py:291
  138.1 5.9 %collective-permute-start.25 = (bf16[48,2176]{1,0:T(8,128)(2,1)S(1)}, bf16[48,2176]{1,0:T(8,128)(2,1)S(1)}, u32[]{:S(2)}, u32[]{:S(2)}) collective-permute-start(bf16[48,2176]{1,0:T(8,128)(2,1)S(1)} %get-tuple-element.113), channel_id=1, source_target_pairs={{0,16},{16,0},{1,17},{17,1},{2,18},{18,2},{3,19},{19,3},{4,20},{20... | collective-permute-start | bytes 626696 | tf_op jit(solution)/shard_map/ppermute | solution.py:288
  144.8 0.7 copy-start.12

commit v8 on v7

--- a/solution.py
+++ b/solution.py
@@ -8,7 +8,11 @@
 from jax.experimental.pallas import tpu as pltpu
 from jax.sharding import PartitionSpec as P
 
-VMEM_BYTES = 48 * 1024 * 1024
+MIB = 1024 * 1024
+
+
+def kernel_memory(rows):
+    return pltpu.CompilerParams(vmem_limit_bytes=(20 if rows <= 1024 else 48) * MIB)
 
 
 def dot(a, b, ca, cb):
@@ -34,6 +38,133 @@
         span = range(1, cols)
         walk += [(y, z) for y in (span if step % 2 == 0 else reversed(span))]
     return [at.index(place) for place in walk]
+
+
+def pack_kernel(top, where, ids, probs, grads, *outs):
+    tok = grads.shape[0]
+    width = grads.shape[1] // len(outs)
+    room = outs[0].shape[1] - width
+    row = lax.broadcasted_iota(jnp.int32, (tok, tok), 0)
+    col = lax.broadcasted_iota(jnp.int32, (tok, tok), 1)
+    same = (row == col).astype(jnp.float32)
+
+    def columns(value):
+        return lax.dot_general(
+            same,
+            value,
+            (((1,), (1,)), ((), ())),
+            precision=lax.Precision.HIGHEST,
+            preferred_element_type=jnp.float32,
+        )
+
+    prob = columns(probs[...])
+    high = prob.astype(jnp.bfloat16)
+    middle = (prob - high.astype(jnp.float32)).astype(jnp.bfloat16)
+    low = (prob - high.astype(jnp.float32) - middle.astype(jnp.float32)).astype(jnp.bfloat16)
+    named = columns(ids[...].astype(jnp.float32)).astype(jnp.bfloat16)
+    blank = jnp.zeros((tok, room - 4 * top), jnp.bfloat16)
+    routes = jnp.concatenate([named, high, middle, low, blank], axis=1)
+    for d, out in enumerate(outs):
+        at = lax.rem(where[0] + d, len(outs)) * width
+        out[:, :width] = grads[:, pl.ds(pl.multiple_of(at, 128), width)]
+        out[:, width:] = routes
+
+
+def pack(where, ids, probs, grads, n_dp, room):
+    top, tok = ids.shape
+    width = grads.shape[1] // n_dp
+    vmem = pl.BlockSpec(memory_space=pltpu.VMEM)
+    return pl.pallas_call(
+        functools.partial(pack_kernel, top),
+        in_specs=[pl.BlockSpec(memory_space=pltpu.SMEM)] + [vmem] * 3,
+        out_specs=[vmem] * n_dp,
+        out_shape=[jax.ShapeDtypeStruct((tok, width + room), jnp.bfloat16)] * n_dp,
+        compiler_params=kernel_memory(tok),
+        name="pack",
+    )(where, ids, probs, grads)
+
+
+def sum_kernel(starts, n_out, *refs):
+    outs = refs[-n_out:]
+    at = 0
+    for out, (n_rows, arrives) in zip(outs, starts):
+        carry = refs[at + n_rows] if arrives else None
+        for i in range(n_rows):
+            value = refs[at + i][...]
+            if carry is not None and arrives[0] <= i < arrives[1]:
+                value = value.astype(jnp.float32) + carry[i - arrives[0]].astype(jnp.float32)
+            out[i] = value.astype(jnp.bfloat16)
+        at += n_rows + (1 if arrives else 0)
+
+
+def sums(jobs):
+    tok, full = jobs[0][0][0].shape
+    flat, starts, shapes = [], [], []
+    for parts, carry, first, last in jobs:
+        flat += list(parts) + [carry]
+        starts.append((len(parts), (first, last)))
+        shapes.append(jax.ShapeDtypeStruct((len(parts), tok, full), jnp.bfloat16))
+    vmem = pl.BlockSpec(memory_space=pltpu.VMEM)
+    return pl.pallas_call(
+        functools.partial(sum_kernel, tuple(starts), len(shapes)),
+        in_specs=[vmem] * len(flat),
+        out_specs=[vmem] * len(shapes),
+        out_shape=shapes,
+        compiler_params=kernel_memory(tok),
+        name="sums",
+    )(*flat)
+
+
+def close_kernel(n_dp, *refs):
+    parts, (one, two), outs = refs[:n_dp], refs[n_dp : n_dp + 2], refs[n_dp + 2 :]
+    for d, out in enumerate(outs):
+        value = parts[d][...].astype(jnp.float32) + one[d].astype(jnp.float32)
+        out[...] = (value + two[d].astype(jnp.float32)).astype(jnp.bfloat16)
+
+
+def close(parts, one, two):
+    vmem = pl.BlockSpec(memory_space=pltpu.VMEM)
+    return pl.pallas_call(
+        functools.partial(close_kernel, len(parts)),
+        in_specs=[vmem] * (len(parts) + 2),
+        out_specs=[vmem] * len(parts),
+        out_shape=[jax.ShapeDtypeStruct(part.shape, jnp.bfloat16) for part in parts],
+        compiler_params=kernel_memory(parts[0].shape[0]),
+        name="close",
+    )(*parts, one, two)
+
+
+def home_kernel(n_ex, where, ids, *refs):
+    pieces, (layer, prob) = refs[:-2], refs[-2:]
+    n_dp = len(pieces)
+    tok, top = ids.shape
+    width = layer.shape[1] // n_dp
+    inner = jnp.zeros((tok, n_ex), jnp.float32)
+    for d, piece in enumerate(pieces):
+        at = lax.rem(where[0] + d, n_dp) * width
+        layer[:, pl.ds(pl.multiple_of(at, 128), width)] = piece[:, :width]
+        more = piece[:, width:].astype(jnp.float32)
+        inner = inner + more[:, :n_ex] + more[:, n_ex : 2 * n_ex]
+    lane = lax.broadcasted_iota(jnp.int32, (tok, n_ex), 1)
+    for k in range(top):
+        mine = lane == ids[:, k : k + 1]
+        prob[:, k : k + 1] = jnp.sum(jnp.where(mine, inner, 0.0), axis=1, keepdims=True)
+
+
+def home(where, ids, pieces, width, n_ex):
+    tok, top = ids.shape
+    vmem = pl.BlockSpec(memory_space=pltpu.VMEM)
+    return pl.pallas_call(
+        functools.partial(home_kernel, n_ex),
+        in_specs=[pl.BlockSpec(memory_space=pltpu.SMEM)] + [vmem] * (1 + len(pieces)),
+        out_specs=[vmem] * 2,
+        out_shape=[
+            jax.ShapeDtypeStruct((tok, len(pieces) * width), jnp.bfloat16),
+            jax.ShapeDtypeStruct((tok, top), jnp.float32),
+        ],
+        compiler_params=kernel_memory(tok),
+        name="home",
+    )(where, ids, *pieces)
 
 
 def block_kernel(plan, refs_in, n_dp, n_ex, top, *refs):
@@ -140,12 +271,13 @@
         out_shape.append(jax.ShapeDtypeStruct((sizes[0], 2), jnp.float32))
     hid = [value for d in replicas for value in hiddens[d]]
     count = len(plan) * tok
+    chips_rows = n_ex * tok * n_dp // 2
     made = pl.pallas_call(
         functools.partial(block_kernel, plan, len(blocks), n_dp, n_ex, top),
         in_specs=[pl.BlockSpec(memory_space=pltpu.SMEM)] + [vmem] * (len(blocks) + len(hid) + 2),
         out_specs=[vmem] * len(out_shape),
         out_shape=out_shape,
-        compiler_params=pltpu.CompilerParams(vmem_limit_bytes=VMEM_BYTES),
+        compiler_params=kernel_memory(chips_rows),
         cost_estimate=pl.CostEstimate(
             flops=8 * count * ff * width,
             bytes_accessed=4 * ff * width + 4 * count * (full + ff),
@@ -192,7 +324,7 @@
         in_specs=[vmem] * (2 * len(index) + len(flat)),
         out_specs=[vmem] * 2,
         out_shape=[jax.ShapeDtypeStruct((slots, ff), jnp.bfloat16)] * 2,
-        compiler_params=pltpu.CompilerParams(vmem_limit_bytes=VMEM_BYTES),
+        compiler_params=kernel_memory(rows * len(backs)),
         cost_estimate=pl.CostEstimate(
             flops=4 * rows * slots * ff,
             bytes_accessed=4 * (1 + len(backs)) * rows * ff,
@@ -234,7 +366,7 @@
         out_specs=pl.BlockSpec((ff, tile), lambda i: (0, i)),
         out_shape=jax.ShapeDtypeStruct((ff, width), dtype),
         scratch_shapes=[pltpu.VMEM((ff, rows), jnp.bfloat16)],
-        compiler_params=pltpu.CompilerParams(vmem_limit_bytes=VMEM_BYTES),
+        compiler_params=kernel_memory(rows),
         cost_estimate=pl.CostEstimate(
             flops=2 * rows * width * ff,
             bytes_accessed=2 * rows * (width + ff) + 4 * ff * width,
@@ -294,23 +426,16 @@
             return lax.ppermute(value, "expert", sibling)
 
         room = 128 * -(-max(4 * top, 2 * n_ex) // 128)
-        narrow = lambda value: lax.reduce_precision(value, 8, 7)
-        high = narrow(route_probs)
-        middle = narrow(route_probs - high)
-        low = route_probs - high - middle
-        routes = jnp.concatenate([expert_ids.astype(jnp.float32), high, middle, low], axis=1)
-        routes = jnp.pad(routes.astype(jnp.bfloat16), ((0, 0), (0, room - 4 * top)))
-
-        def width_shard(d):
-            at = ((replica + d) % n_dp) * width
-            return jnp.concatenate([lax.dynamic_slice_in_dim(out_grad, at, width, axis=1), routes], axis=1)
-
-        blocks = {0: jnp.stack([width_shard(0)] + [shift(width_shard(d), d) for d in range(1, n_dp)])}
+        where = replica.reshape(1).astype(jnp.int32)
+        packed = pack(where, expert_ids.T, route_probs.T, out_grad, n_dp, room)
+        blocks = {0: jnp.stack([packed[0]] + [shift(packed[d], d) for d in range(1, n_dp)])}
 
         sibling_weight = swap(weight)
         hidden = expert_hidden[0, 0].transpose(1, 0, 2).reshape(slots, ff)
-        hiddens = [hidden] + [shift(hidden, d) for d in range(1, n_dp)]
-        hiddens = [(value, swap(value)) for value in hiddens]
+        hiddens = [(hidden, swap(hidden))]
+        for d in range(1, n_dp):
+            value = shift(after(hidden, blocks[0]), d)
+            hiddens.append((value, None))
 
         parts, scaleds, layout, facts = {}, [], [], []
         own_back, sent_back = [], [[] for _ in range(1, n_dp)]
@@ -365,8 +490,12 @@
                 break
             if step > 1:
                 gate = (ready,)
+            if step == 2:
+                for d in range(1, n_dp):
+                    value = hiddens[d][0]
+                    hiddens[d] = value, swap(after(value, blocks[-step], blocks[step], ready))
             ready = work(following)
-        sent = after(blocks[1 - half][:per], ready), after(blocks[half - 1][per:], ready)
+        sent = after(blocks[1 - half], ready)[:per], after(blocks[half - 1], ready)[per:]
         blocks[half] = [ring_send(sent[0], 1), ring_send(sent[1], -1)]
         ready = work(following)
         work(both([half]), ready)
@@ -374,60 +503,48 @@
         carry = {}
 
         def hop_on(hop, *done):
-            for direction in (1, -1):
-                off = half if hop == half else hop * direction
-                group = range(n_dp)
-                if hop == half:
-                    group = range(per) if direction == 1 else range(per, n_dp)
-                first = 0 if direction == 1 else per
-                values = []
-                for d in group:
-                    value = parts[off, d]
-                    if hop == half - 1 and 0 <= d - first < per:
-                        value = value.astype(jnp.float32) + carry[direction][d - first].astype(jnp.float32)
-                    elif hop < half - 1:
-                        value = value.astype(jnp.float32) + carry[direction][d].astype(jnp.float32)
-                    values.append(value.astype(jnp.bfloat16))
-                carry[direction] = ring_send(after(jnp.stack(values), *done), direction)
+            every = range(n_dp)
+            if hop == half:
+                values = [jnp.stack([parts[half, d] for d in every[:per]])]
+                values.append(jnp.stack([parts[half, d] for d in every[per:]]))
+            else:
+                first, last = ((0, per), (per, n_dp)) if hop == half - 1 else ((0, n_dp), (0, n_dp))
+                values = sums(
+                    [
+                        ([parts[hop, d] for d in every], carry[1], *first),
+                        ([parts[-hop, d] for d in every], carry[-1], *last),
+                    ]
+                )
+            values = [after(value, *done) for value in values]
+            carry[1] = ring_send(values[0], 1)
+            carry[-1] = ring_send(values[1], -1)
+            sending[:] = values
             return carry[1], carry[-1]
 
-        first = hop_on(half)
+        sending = []
+        hop_on(half)
+        second = hop_on(half - 1)
         other = weight_product(
-            [after(refs[0], parts[half, n_dp - 1])] + refs[1:], layout, scaleds, 1, jnp.bfloat16, width
+            [after(refs[0], *sending, *[value for sent in sent_back for value in sent[:-1]])] + refs[1:], layout, scaleds, 1, jnp.bfloat16, width
         )
-        swapped = swap(other)
-        second = hop_on(half - 1, other)
+        swapped = swap(after(other, *second))
+        third = hop_on(half - 2, other)
         spread, spread_other = spread_product(
-            [after(facts[0][0], *first)] + [fact[0] for fact in facts[1:]],
+            [after(facts[0][0], *second)] + [fact[0] for fact in facts[1:]],
             [fact[1] for fact in facts],
             [own_back] + sent_back,
             slots,
         )
-        spread_swapped = swap(spread_other)
-        for hop in range(half - 2, 1, -1):
+        hidden_grad = spread + swap(spread_other)
+        hidden_grad = hidden_grad.reshape(cap, n_ex, ff).transpose(1, 0, 2)[None, None]
+        for hop in range(half - 3, 0, -1):
             hop_on(hop, spread)
         weight_grad = weight_product(
-            [after(refs[0], *second)] + refs[1:], layout, scaleds, 0, jnp.float32, width, swapped
+            [after(refs[0], *third)] + refs[1:], layout, scaleds, 0, jnp.float32, width, swapped
         )
-        hop_on(1, weight_grad)
-        hidden_grad = spread + spread_swapped
-        hidden_grad = hidden_grad.reshape(cap, n_ex, ff).transpose(1, 0, 2)[None, None]
-
-        layer_out = jnp.zeros((tok, n_dp * width), jnp.bfloat16)
-        inner = jnp.zeros((tok, n_ex), jnp.float32)
-        for d in reversed(range(n_dp)):
-            total = parts[0, d].astype(jnp.float32)
-            total = total + carry[1][d].astype(jnp.float32) + carry[-1][d].astype(jnp.float32)
-            total = total.astype(jnp.bfloat16)
-            piece = total if d == 0 else shift(total, -d)
-            layer_out = lax.dynamic_update_slice_in_dim(
-                layer_out, piece[:, :width], ((replica + d) % n_dp) * width, axis=1
-            )
-            found = piece[:, width:].astype(jnp.float32)
-            inner = inner + found[:, :n_ex] + found[:, n_ex : 2 * n_ex]
-
-        mine = expert_ids[:, :, None] == jnp.arange(n_ex, dtype=jnp.int32)
-        prob_grad = jnp.sum(jnp.where(mine, inner[:, None, :], 0.0), axis=2)
+        totals = close([after(parts[0, 0], weight_grad)] + [parts[0, d] for d in range(1, n_dp)], carry[1], carry[-1])
+        pieces = [totals[0]] + [shift(totals[d], -d) for d in range(1, n_dp)]
+        layer_out, prob_grad = home(where, expert_ids, pieces, width, n_ex)
         return (layer_out, prob_grad, hidden_grad, weight_grad[None])
 
     return shards

time: 146 us -> 117 us (0.80)
  waiting for transfers between devices: 61.7 us -> 37.4 us
  Pallas kernels: 48.8 us -> 41.9 us
  local copies, waits for them, and re-layouts: 5.09 us -> 8.66 us
  other arithmetic: 4.41 us -> 1.17 us
  starting transfers between devices: 24.6 us -> 26.3 us
    ppermute x6, waiting for transfers between devices: 26.3 us -> 13.3 us  [shift(): lax.ppermute(value, 'dp', [(i, (i + step) % n_dp) for i in range(n_dp)])]
    ppermute x16, waiting for transfers between devices: 35.4 us -> 23.5 us  [ring_send(): return lax.ppermute(value, 'expert', forward if step > 0 else backward)]
    pallas_call x4, Pallas kernels: 33.8 us -> 26.3 us  [block_product(): pl.pallas_call(functools.partial(block_kernel, plan, len(blocks), n_dp, n...]
    unnamed x29 -> x24, local copies, waits for them, and re-layouts: 2.9 us -> 7.93 us
    another operation x16 -> x1, other arithmetic: 2.3 us -> 0.05 us  [shards(): jnp.stack([packed[0]] + [shift(packed[d], d) for d in range(1, n_dp)])]
    pallas_call x0 -> x6, Pallas kernels: none -> 2.2 us  [the longest x1 1.29 us: home(): pl.pallas_call(functools.partial(home_kernel, n_ex), in_specs=[pl.BlockSp...]
    ppermute x6, starting transfers between devices: 7 us -> 8.65 us  [shift(): lax.ppermute(value, 'dp', [(i, (i + step) % n_dp) for i in range(n_dp)])]
    pallas_call x2, Pallas kernels: 13.7 us -> 12 us  [weight_product(): pl.pallas_call(functools.partial(weight_kernel, len(blocks), len(scaleds)...]
  transfers between devices with their start and end apart: 27 -> 27, of which waited for: 9 -> 15; matrix products, arithmetic and copies ran while one was open for 4% -> 2% of each run, Pallas kernels for 34% -> 35%
where the time goes in v8:
time: 117 us; the launch traced here: 116 us
  Pallas kernels  41.9 us (36%)
  waiting for transfers between devices  37.4 us (32%)
  starting transfers between devices  26.3 us (22%)
  local copies, waits for them, and re-layouts  8.66 us (7%)
  other arithmetic  1.17 us (1%)
    pallas_call x4, Pallas kernels, block_product(): pl.pallas_call(functools.partial(block_kernel, plan, len(blocks), n_dp, n...  26.3 us
    ppermute x16, waiting for transfers between devices, ring_send(): return lax.ppermute(value, 'expert', forward if step > 0 else backward)  23.5 us
    ppermute x16, starting transfers between devices, ring_send(): return lax.ppermute(value, 'expert', forward if step > 0 else backward)  16.8 us
    ppermute x6, waiting for transfers between devices, shift(): lax.ppermute(value, 'dp', [(i, (i + step) % n_dp) for i in range(n_dp)])  13.3 us
    pallas_call x2, Pallas kernels, weight_product(): pl.pallas_call(functools.partial(weight_kernel, len(blocks), len(scaleds)...  12 us
    ppermute x6, starting transfers between devices, shift(): lax.ppermute(value, 'dp', [(i, (i + step) % n_dp) for i in range(n_dp)])  8.65 us
    unnamed x24, local copies, waits for them, and re-layouts  7.93 us
  transfers between devices with their start and end apart: 27, of which 15 were waited for; matrix products, arithmetic and copies ran while one was open for 2% of the time, Pallas kernels for 35%

profile of v8, /device:TPU:0, one launch (start us, length us, event | category | flops | bytes accessed | tf_op | source)
XLA Modules:
  0.0 116.2 jit_solution(15024818909536293654)
XLA Ops:
  0.6 0.5 collective-permute-start.4
  1.2 1.0 copy-done.7
  2.1 0.7 copy-done.8
  2.8 0.7 copy-done.10
  3.5 0.2 pack.1
  3.8 2.6 %collective-permute-start = (bf16[48,2176]{1,0:T(8,128)(2,1)S(1)}, bf16[48,2176]{1,0:T(8,128)(2,1)S(1)}, u32[]{:S(2)}, u32[]{:S(2)}) collective-permute-start(bf16[48,2176]{1,0:T(8,128)(2,1)S(1)} %get-tuple-element.73), channel_id=1, source_target_pairs={{0,16},{16,0},{1,17},{17,1},{2,18},{18,2},{3,19},{19,3},{4,20},{20... | collective-permute-start | bytes 626696 | tf_op jit(solution)/shard_map/ppermute | solution.py:420
  6.3 0.2 collective-permute-start.3
  6.6 5.6 %collective-permute-done = bf16[48,2176]{1,0:T(8,128)(2,1)S(1)} collective-permute-done((bf16[48,2176]{1,0:T(8,128)(2,1)S(1)}, bf16[48,2176]{1,0:T(8,128)(2,1)S(1)}, u32[]{:S(2)}, u32[]{:S(2)}) %collective-permute-start) | collective-permute-done | bytes 208928 | tf_op jit(solution)/shard_map/ppermute | solution.py:420
  12.2 1.8 %collective-permute-start.7 = (bf16[576,768]{1,0:T(8,128)(2,1)}, bf16[576,768]{1,0:T(8,128)(2,1)}, u32[]{:S(2)}, u32[]{:S(2)}) collective-permute-start(bf16[576,768]{1,0:T(8,128)(2,1)} %bitcast.27), channel_id=1, source_target_pairs={{0,16},{16,0},{1,17},{17,1},{2,18},{18,2},{3,19},{19,3},{4,20},{20... | collective-permute-start | bytes 2654216 | tf_op jit(solution)/shard_map/ppermute | solution.py:420
  14.0 1.6 %collective-permute-start.1 = (bf16[2,48,2176]{2,1,0:T(8,128)(2,1)S(1)}, bf16[2,48,2176]{2,1,0:T(8,128)(2,1)}, u32[]{:S(2)}, u32[]{:S(2)}) collective-permute-start(bf16[2,48,2176]{2,1,0:T(8,128)(2,1)S(1)} %pad_maximum_fusion.refs_1_.refs_3_.refs_0_), channel_id=1, source_target_pairs={{0,4},{1,5},{4,8},{5,9},{8,12},{9,13},{12,14},{13,15},{14,10},{15,... | collective-permute-start | bytes 1253384 | tf_op jit(solution)/shard_map/ppermute | solution.py:423
  15.6 0.4 collective-permute-start.2
  16.1 0.8 copy-done.4
  16.8 8.3 %collective-permute-done.1.refs_2_.refs_4_.refs_1_ = bf16[2,48,2176]{2,1,0:T(8,128)(2,1)} collective-permute-done((bf16[2,48,2176]{2,1,0:T(8,128)(2,1)S(1)}, bf16[2,48,2176]{2,1,0:T(8,128)(2,1)}, u32[]{:S(2)}, u32[]{:S(2)}) %collective-permute-start.1) | collective-permute-done | bytes 417824 | tf_op jit(solution)/shard_map/ppermute | solution.py:423
  25.1 1.6 %collective-permute-start.5 = (bf16[2,48,2176]{2,1,0:T(8,128)(2,1)}, bf16[2,48,2176]{2,1,0:T(8,128)(2,1)}, u32[]{:S(2)}, u32[]{:S(2)}) collective-permute-start(bf16[2,48,2176]{2,1,0:T(8,128)(2,1)} %collective-permute-done.1.refs_2_.refs_4_.refs_1_), channel_id=1, source_target_pairs={{0,4},{1,5},{4,8},{5,9},{8,12},{9,13},{12,14},{13,15},{14,10},{15,... | collective-permute-start | bytes 1253384 | tf_op jit(solution)/shard_map/ppermute | solution.py:423
  26.7 0.5 collective-permute-start.6
  27.1 0.7 dynamic-slice_bitcast_fusion.refs_0_
  27.8 1.9 %copy-done = bf16[1,768,2048]{2,1,0:T(8,128)(2,1)S(1)} copy-done((bf16[1,768,2048]{2,1,0:T(8,128)(2,1)S(1)}, bf16[1,768,2048]{2,1,0:T(8,128)(2,1)}, u32[]{:S(2)}) %copy-start) | copy-done | bytes 3145752
  29.7 1.2 %copy-done.2 = bf16[1,1,16,36,768]{4,2,3,1,0:T(8,128)(2,1)S(1)} copy-done((bf16[1,1,16,36,768]{4,2,3,1,0:T(8,128)(2,1)S(1)}, bf16[1,1,16,36,768]{4,2,3,1,0:T(8,128)(2,1)}, u32[]{:S(2)}) %copy-start.2) | copy-done | bytes 884760
  30.9 1.0 copy-done.5
  31.9 5.7 %block_product.4 = (bf16[48,2176]{1,0:T(8,128)(2,1)S(1)}, bf16[48,2176]{1,0:T(8,128)(2,1)S(1)}, bf16[48,2176]{1,0:T(8,128)(2,1)S(1)}, bf16[2,144,768]{2,1,0:T(8,...) custom-call(s32[10]{0:T(128)S(1)} %dynamic-slice_bitcast_fusion.refs_0_, ...), custom_call_target="tpu_custom_call" | custom-call | flops 1811939328 | bytes 7987200 | tf_op jit(solution)/shard_map/block_product/pallas_call | solution.py:275
  37.7 1.6 %collective-permute-start.10 = (bf16[2,48,2176]{2,1,0:T(8,128)(2,1)}, bf16[2,48,2176]{2,1,0:T(8,128)(2,1)S(1)}, u32[]{:S(2)}, u32[]{:S(2)}) collective-permute-start(bf16[2,48,2176]{2,1,0:T(8,128)(2,1)} %collective-permute-done.6.refs_2_.refs_4_), channel_id=1, source_target_pairs={{0,2},{1,3},{4,0},{5,1},{8,4},{9,5},{12,8},{13,9},{14,12},{15,13},... | collective-permute-start | bytes 1253384 | tf_op jit(solution)/shard_map/ppermute | solution.py:423
  39.3 0.5 collective-permute-start.9
  39.8 0.5 collective-permute-done.8.refs_9_.refs_6_
  40.3 8.3 %block_product.5 = (bf16[48,2176]{1,0:T(8,128)(2,1)S(1)}, bf16[48,2176]{1,0:T(8,128)(2,1)S(1)}, bf16[48,2176]{1,0:T(8,128)(2,1)S(1)}, bf16[48,2176]{1,0:T(8,128)...) custom-call(s32[10]{0:T(128)S(1)} %dynamic-slice_bitcast_fusion.refs, ...), custom_call_target="tpu_custom_call" | custom-call | flops 4227858432 | bytes 10248192 | tf_op jit(solution)/shard_map/block_product/pallas_call | solution.py:275
  48.7 1.3 %collective-permute-done.10.refs_2_.refs_6_ = bf16[2,48,2176]{2,1,0:T(8,128)(2,1)S(1)} collective-permute-done((bf16[2,48,2176]{2,1,0:T(8,128)(2,1)}, bf16[2,48,2176]{2,1,0:T(8,128)(2,1)S(1)}, u32[]{:S(2)}, u32[]{:S(2)}) %collective-permute-start.10) | collective-permute-done | bytes 417824 | tf_op jit(solution)/shard_map/ppermute | solution.py:423
  50.0 1.6 %collective-permute-start.12 = (bf16[1,48,2176]{2,1,0:T(8,128)(2,1)S(1)}, bf16[1,48,2176]{2,1,0:T(8,128)(2,1)S(1)}, u32[]{:S(2)}, u32[]{:S(2)}) collective-permute-start(bf16[1,48,2176]{2,1,0:T(8,128)(2,1)S(1)} %slice.7), channel_id=1, source_target_pairs={{0,2},{1,3},{4,0},{5,1},{8,4},{9,5},{12,8},{13,9},{14,12},{15,13},... | collective-permute-start | bytes 626696 | tf_op jit(solution)/shard_map/ppermute | solution.py:423
  51.6 0.7 collective-permute-start.11
  52.3 0.5 collective-permute-start.17
  52.8 6.4 %block_product.6 = (bf16[48,2176]{1,0:T(8,128)(2,1)S(1)}, bf16[48,2176]{1,0:T(8,128)(2,1)S(1)}, bf16[48,2176]{1,0:T(8,128)(2,1)S(1)}, bf16[48,2176]{1,0:T(8,128)...) custom-call(s32[10]{0:T(128)S(1)} %dynamic-slice_bitcast_fusion.refs, ...), custom_call_target="tpu_custom_call" | custom-call | flops 2415919104 | bytes 8552448 | tf_op jit(solution)/shard_map/block_product/pallas_call | solution.py:275
  59.2 5.9 %block_product.7 = (bf16[48,2176]{1,0:T(8,128)(2,1)S(1)}, bf16[48,2176]{1,0:T(8,128)(2,1)S(1)}, bf16[2,48,768]{2,1,0:T(8,128)(2,1)S(1)}, bf16[2,48,768]{2,1,0:T(...) custom-call(s32[10]{0:T(128)S(1)} %dynamic-slice_bitcast_fusion.refs, ...), custom_call_target="tpu_custom_call" | custom-call | flops 1207959552 | bytes 7421952 | tf_op jit(solution)/shard_map/block_product/pallas_call | solution.py:275
  65.1 1.7 %collective-permute-start.13 = (bf16[1,48,2176]{2,1,0:T(8,128)(2,1)S(1)}, bf16[1,48,2176]{2,1,0:T(8,128)(2,1)S(1)}, u32[]{:S(2)}, u32[]{:S(2)}) collective-permute-start(bf16[1,48,2176]{2,1,0:T(8,128)(2,1)S(1)} %bitcast.36), channel_id=1, source_target_pairs={{0,4},{1,5},{4,8},{5,9},{8,12},{9,13},{12,14},{13,15},{14,10},{15,... | collective-permute-start | bytes 626696 | tf_op jit(solution)/shard_map/ppermute | solution.py:423
  66.8 0.4 collective-permute-start.14
  67.2 1.5 %collective-permute-start.18 = (bf16[2,96,768]{2,1,0:T(8,128)(2,1)S(1)}, bf16[2,96,768]{2,1,0:T(8,128)(2,1)S(1)}, u32[]{:S(2)}, u32[]{:S(2)}) collective-permute-start(bf16[2,96,768]{2,1,0:T(8,128)(2,1)S(1)} %get-tuple-element.96), channel_id=1, source_target_pairs={{0,16},{16,0},{1,17},{17,1},{2,18},{18,2},{3,19},{19,3},{4,20},{20... | collective-permute-start | bytes 884744 | tf_op jit(solution)/shard_map/ppermute | solution.py:420
  68.8 2.3 %collective-permute-done.13.refs_2_ = bf16[1,48,2176]{2,1,0:T(8,128)(2,1)S(1)} collective-permute-done((bf16[1,48,2176]{2,1,0:T(8,128)(2,1)S(1)}, bf16[1,48,2176]{2,1,0:T(8,128)(2,1)S(1)}, u32[]{:S(2)}, u32[]{:S(2)}) %collective-permute-start.13) | collective-permute-done | bytes 208928 | tf_op jit(solution)/shard_map/ppermute | solution.py:423
  71.1 1.5 %collective-permute-done.14.refs_5_ = bf16[1,48,2176]{2,1,0:T(8,128)(2,1)S(1)} collective-permute-done((bf16[1,48,2176]{2,1,0:T(8,128)(2,1)S(1)}, bf16[1,48,2176]{2,1,0:T(8,128)(2,1)S(1)}, u32[]{:S(2)}, u32[]{:S(2)}) %collective-permute-start.14) | collective-permute-done | bytes 208928 | tf_op jit(solution)/shard_map/ppermute | solution.py:423
  72.6 0.1 sums.3
  72.7 1.6 %collective-permute-start.15 = (bf16[2,48,2176]{2,1,0:T(8,128)(2,1)S(1)}, bf16[2,48,2176]{2,1,0:T(8,128)(2,1)S(1)}, u32[]{:S(2)}, u32[]{:S(2)}) collective-permute-start(bf16[2,48,2176]{2,1,0:T(8,128)(2,1)S(1)} %get-tuple-element.91), channel_id=1, source_target_pairs={{0,4},{1,5},{4,8},{5,9},{8,12},{9,13},{12,14},{13,15},{14,10},{15,... | collective-permute-start | bytes 1253384 | tf_op jit(solution)/shard_map/ppermute | solution.py:423
  74.4 0.4 collective-permute-start.16
  74.8 1.3 %collective-permute-done.18.refs_13_ = bf16[2,96,768]{2,1,0:T(8,128)(2,1)S(1)} collective-permute-done((bf16[2,96,768]{2,1,0:T(8,128)(2,1)S(1)}, bf16[2,96,768]{2,1,0:T(8,128)(2,1)S(1)}, u32[]{:S(2)}, u32[]{:S(2)}) %collective-permute-start.18) | collective-permute-done | bytes 294944 | tf_op jit(solution)/shard_map/ppermute | solution.py:420
  76.1 5.3 %weight_product.2 = bf16[768,2048]{1,0:T(8,128)(2,1)S(1)} custom-call(bf16[2,48,2176]{2,1,0:T(8,128)(2,1)S(1)} %copy-done.6, bf16[2,48,2176]{2,1,0:T(8,128)(2,1)} %collective-permute-done.1.refs_2_.refs_4_.refs_1_, bf16[2,48,2176]{2,1,0:T(8,128)(2,1)} %collective-permute-done.2.refs_3_.refs_5_.refs_2_, ...), custom_call_target="tpu_custom_call" | custom-call | flops 2415919104 | bytes 10616832 | tf_op jit(solution)/shard_map/weight_product/pallas_call | solution.py:357
  81.4 0.6 collective-permute-done.15.refs_2_
  82.0 1.3 %collective-permute-done.16.refs_5_ = bf16[2,48,2176]{2,1,0:T(8,128)(2,1)S(1)} collective-permute-done((bf16[2,48,2176]{2,1,0:T(8,128)(2,1)S(1)}, bf16[2,48,2176]{2,1,0:T(8,128)(2,1)S(1)}, u32[]{:S(2)}, u32[]{:S(2)}) %collective-permute-start.16) | collective-permute-done | bytes 417824 | tf_op jit(solution)/shard_map/ppermute | solution.py:423
  83.3 1.5 %collective-permute-start.22 = (bf16[2,48,768]{2,1,0:T(8,128)(2,1)S(1)}, bf16[2,48,768]{2,1,0:T(8,128)(2,1)S(1)}, u32[]{:S(2)}, u32[]{:S(2)}) collective-permute-start(bf16[2,48,768]{2,1,0:T(8,128)(2,1)S(1)} %get-tuple-element.130), channel_id=1, source_target_pairs={{0,16},{16,0},{1,17},{17,1},{2,18},{18,2},{3,19},{19,3},{4,20},{20... | collective-permute-start | bytes 442376 | tf_op jit(solution)/shard_map/ppermute | solution.py:420
  84.8 0.2 sums.4
  85.0 0.5 collective-permute-start.20
  85.5 1.6 %collective-permute-start.19 = (bf16[2,48,2176]{2,1,0:T(8,128)(2,1)S(1)}, bf16[2,48,2176]{2,1,0:T(8,128)(2,1)S(1)}, u32[]{:S(2)}, u32[]{:S(2)}) collective-permute-start(bf16[2,48,2176]{2,1,0:T(8,128)(2,1)S(1)} %get-tuple-element.105), channel_id=1, source_target_pairs={{0,4},{1,5},{4,8},{5,9},{8,12},{9,13},{12,14},{13,15},{14,10},{15,... | collective-permute-start | bytes 1253384 | tf_op jit(solution)/shard_map/ppermute | solution.py:423
  87.1 2.5 %collective-permute-done.22.refs_14_ = bf16[2,48,768]{2,1,0:T(8,128)(2,1)S(1)} collective-permute-done((bf16[2,48,768]{2,1,0:T(8,128)(2,1)S(1)}, bf16[2,48,768]{2,1,0:T(8,128)(2,1)S(1)}, u32[]{:S(2)}, u32[]{:S(2)}) %collective-permute-start.22) | collective-permute-done | bytes 147488 | tf_op jit(solution)/shard_map/ppermute | solution.py:420
  89.6 1.3 %spread_product.1 = (bf16[576,768]{1,0:T(8,128)(2,1)S(1)}, bf16[576,768]{1,0:T(8,128)(2,1)S(1)}) custom-call(s32[144,2]{1,0:T(8,128)S(1)} %get-tuple-element.118.refs_0_, s32[96,2]{1,0:T(8,128)S(1)} %get-tuple-element.119.refs_1_, s32[96,2]{1,0:T(8,128)S(1)} %get-tuple-element.120.refs_2_, s32[48,2]{1,0:T(8,128)S(1)} %get-tuple-element.121.refs_3_, ...), custom_call_target="tpu_custom_call" | custom-call | flops 679477248 | bytes 3538944 | tf_op jit(solution)/shard_map/spread_product/pallas_call | solution.py:322
  90.9 0.1 collective-permute-start.26
  91.0 5.8 %collective-permute-done.20.refs_5_ = bf16[2,48,2176]{2,1,0:T(8,128)(2,1)S(1)} collective-permute-done((bf16[2,48,2176]{2,1,0:T(8,128)(2,1)S(1)}, bf16[2,48,2176]{2,1,0:T(8,128)(2,1)S(1)}, u32[]{:S(2)}, u32[]{:S(2)}) %collective-permute-start.20) | collective-permute-done | bytes 417824 | tf_op jit(solution)/shard_map/ppermute | solution.py:423
  96.8 0.2 collective-permute-done.19.refs_2_
  97.0 0.2 sums.5
  97.2 0.5 collective-permute-start.24
  97.7 1.6 %collective-permute-start.23 = (bf16[2,48,2176]{2,1,0:T(8,128)(2,1)S(1)}, bf16[2,48,2176]{2,1,0:T(8,128)(2,1)S(1)}, u32[]{:S(2)}, u32[]{:S(2)}) collective-permute-start(bf16[2,48,2176]{2,1,0:T(8,128)(2,1)S(1)} %get-tuple-element.132), channel_id=1, source_target_pairs={{0,4},{1,5},{4,8},{5,9},{8,12},{9,13},{12,14},{13,15},{14,10},{15,... | collective-permute-start | bytes 1253384 | tf_op jit(solution)/shard_map/ppermute | solution.py:423
  99.3 6.8 %weight_product.3 = f32[768,2048]{1,0:T(8,128)} custom-call(bf16[2,48,2176]{2,1,0:T(8,128)(2,1)S(1)} %copy-done.6, bf16[2,48,2176]{2,1,0:T(8,128)(2,1)} %collective-permute-done.1.refs_2_.refs_4_.refs_1_, bf16[2,48,2176]{2,1,0:T(8,128)(2,1)} %collective-permute-done.2.refs_3_.refs_5_.refs_2_, bf16[2,48,2176]{2,1,0:T(8,128)(2,1)} %collective-permute-done.5.refs_1_.refs_3_, ...), custom_call_target="tpu_custom_call" | custom-call | flops 2415919104 | bytes 10616832 | tf_op jit(solution)/shard_map/weight_product/pallas_call | solution.py:357
  106.1 2.0 %collective-permute-done.24.refs_3_ = bf16[2,48,2176]{2,1,0:T(8,128)(2,1)S(1)} collective-permute-done((bf16[2,48,2176]{2,1,0:T(8,128)(2,1)S(1)}, bf16[2,48,2176]{2,1,0:T(8,128)(2,1)S(1)}, u32[]{:S(2)}, u32[]{:S(2)}) %collective-permute-start.24) | collective-permute-done | bytes 417824 | tf_op jit(solution)/shard_map/ppermute | solution.py:423
  108.0 0.2 collective-permute-done.23.refs_2_
  108.2 0.2 close.1
  108.4 0.8 collective-permute-start.25
  109.1 0.1 copy.10.ids
  109.2 1.1 add.8
  110.3 3.9 %collective-permute-done.25.refs_1_ = bf16[48,2176]{1,0:T(8,128)(2,1)S(1)} collective-permute-done((bf16[48,2176]{1,0:T(8,128)(2,1)S(1)}, bf16[48,2176]{1,0:T(8,128)(2,1)S(1)}, u32[]{:S(2)}, u32[]{:S(2)}) %collective-permute-start.25) | collective-permute-done | bytes 208928 | tf_op jit(solution)/shard_map/ppermute | solution.py:420
  114.2 1.3 %home.1 = (bf16[48,4096]{1,0:T(8,128)(2,1)}, f32[48,8]{1,0:T(8,128)S(1)}) custom-call(s32[1]{0:T(128)} %bitcast.where, s32[48,8]{1,0:T(8,128)S(1)} %copy.10.ids, bf16[48,2176]{1,0:T(8,128)(2,1)S(1)} %get-tuple-element.135.refs_0_, bf16[48,2176]{1,0:T(8,128)(2,1)S(1)} %collective-permute-done.25.refs_1_), custom_call_target="tpu_custom_call" | custom-call | tf_op jit(solution)/shard_map/home/pallas_call | solution.py:157
  115.5 0.7 copy.11
  (32 shorter events, 0.2 us)
Async XLA Ops:
  0.6 27.2 %collective-permute-start.4 = (bf16[768,2048]{1,0:T(8,128)(2,1)}, bf16[768,2048]{1,0:T(8,128)(2,1)S(1)}, u32[]{:S(2)}, u32[]{:S(2)}) collective-permute-start(bf16[768,2048]{1,0:T(8,128)(2,1)} %bitcast.21), channel_id=1, source_target_pairs={{0,1},{1,0},{2,3},{3,2},{4,5},{5,4},{6,7},{7,6},{8,9},{9,8},{10,11... | collective-permute-start | bytes 9437192 | tf_op jit(solution)/shard_map/ppermute | solution.py:426
  1.1 1.0 copy-start.7
  2.1 0.7 copy-start.8
  2.8 0.7 copy-start.10
  3.8 8.4 %collective-permute-start = (bf16[48,2176]{1,0:T(8,128)(2,1)S(1)}, bf16[48,2176]{1,0:T(8,128)(2,1)S(1)}, u32[]{:S(2)}, u32[]{:S(2)}) collective-permute-start(bf16[48,2176]{1,0:T(8,128)(2,1)S(1)} %get-tuple-element.73), channel_id=1, source_target_pairs={{0,16},{16,0},{1,17},{17,1},{2,18},{18,2},{3,19},{19,3},{4,20},{20... | collective-permute-start | bytes 626696 | tf_op jit(solution)/shard_map/ppermute | solution.py:420
  6.3 21.5 %collective-permute-start.3 = (bf16[576,768]{1,0:T(8,128)(2,1)}, bf16[576,768]{1,0:T(8,128)(2,1)}, u32[]{:S(2)}, u32[]{:S(2)}) collective-permute-start(bf16[576,768]{1,0:T(8,128)(2,1)} %bitcast.26), channel_id=1, source_target_pairs={{0,1},{1,0},{2,3},{3,2},{4,5},{5,4},{6,7},{7,6},{8,9},{9,8},{10,11... | collective-permute-start | bytes 2654216 | tf_op jit(solution)/shard_map/ppermute | solution.py:426
  12.2 25.4 %collective-permute-start.7 = (bf16[576,768]{1,0:T(8,128)(2,1)}, bf16[576,768]{1,0:T(8,128)(2,1)}, u32[]{:S(2)}, u32[]{:S(2)}) collective-permute-start(bf16[576,768]{1,0:T(8,128)(2,1)} %bitcast.27), channel_id=1, source_target_pairs={{0,16},{16,0},{1,17},{17,1},{2,18},{18,2},{3,19},{19,3},{4,20},{20... | collective-permute-start | bytes 2654216 | tf_op jit(solution)/shard_map/ppermute | solution.py:420
  14.0 11.1 %collective-permute-start.1 = (bf16[2,48,2176]{2,1,0:T(8,128)(2,1)S(1)}, bf16[2,48,2176]{2,1,0:T(8,128)(2,1)}, u32[]{:S(2)}, u32[]{:S(2)}) collective-permute-start(bf16[2,48,2176]{2,1,0:T(8,128)(2,1)S(1)} %pad_maximum_fusion.refs_1_.refs_3_.refs_0_), channel_id=1, source_target_pairs={{0,4},{1,5},{4,8},{5,9},{8,12},{9,13},{12,14},{13,15},{14,10},{15,... | collective-permute-start | bytes 1253384 | tf_op jit(solution)/shard_map/ppermute | solution.py:423
  15.6 11.1 %collective-permute-start.2 = (bf16[2,48,2176]{2,1,0:T(8,128)(2,1)S(1)}, bf16[2,48,2176]{2,1,0:T(8,128)(2,1)}, u32[]{:S(2)}, u32[]{:S(2)}) collective-permute-start(bf16[2,48,2176]{2,1,0:T(8,128)(2,1)S(1)} %pad_maximum_fusion.refs_1_.refs_3_.refs_0_), channel_id=1, source_target_pairs={{0,2},{1,3},{4,0},{5,1},{8,4},{9,5},{12,8},{13,9},{14,12},{15,13},... | collective-permute-start | bytes 1253384 | tf_op jit(solution)/shard_map/ppermute | solution.py:423
  16.1 0.8 copy-start.4
  25.1 12.5 %collective-permute-start.5 = (bf16[2,48,2176]{2,1,0:T(8,128)(2,1)}, bf16[2,48,2176]{2,1,0:T(8,128)(2,1)}, u32[]{:S(2)}, u32[]{:S(2)}) collective-permute-start(bf16[2,48,2176]{2,1,0:T(8,128)(2,1)} %collective-permute-done.1.refs_2_.refs_4_.refs_1_), channel_id=1, source_target_pairs={{0,4},{1,5},{4,8},{5,9},{8,12},{9,13},{12,14},{13,15},{14,10},{15,... | collective-permute-start | bytes 1253384 | tf_op jit(solution)/shard_map/ppermute | solution.py:423
  26.7 10.9 %collective-permute-start.6 = (bf16[2,48,2176]{2,1,0:T(8,128)(2,1)}, bf16[2,48,2176]{2,1,0:T(8,128)(2,1)}, u32[]{:S(2)}, u32[]{:S(2)}) collective-permute-start(bf16[2,48,2176]{2,1,0:T(8,128)(2,1)} %collective-permute-done.2.refs_3_.refs_5_.refs_2_), channel_id=1, source_target_pairs={{0,2},{1,3},{4,0},{5,1},{8,4},{9,5},{12,8},{13,9},{14,12},{15,13},... | collective-permute-start | bytes 1253384 | tf_op jit(solution)/shard_map/ppermute | solution.py:423
  27.8 1.9 %copy-start = (bf16[1,768,2048]{2,1,0:T(8,128)(2,1)S(1)}, bf16[1,768,2048]{2,1,0:T(8,128)(2,1)}, u32[]{:S(2)}) copy-start(bf16[1,768,2048]{2,1,0:T(8,128)(2,1)} %param.9) | copy-start | bytes 9437188
  29.7 1.2 %copy-start.2 = (bf16[1,1,16,36,768]{4,2,3,1,0:T(8,128)(2,1)S(1)}, bf16[1,1,16,36,768]{4,2,3,1,0:T(8,128)(2,1)}, u32[]{:S(2)}) copy-start(bf16[1,1,16,36,768]{4,2,3,1,0:T(8,128)(2,1)} %param.8) | copy-start | bytes 2654212
  30.9 1.0 copy-start.5
  31.9 8.4 %copy-start.3 = (bf16[1,1,16,36,768]{4,2,3,1,0:T(8,128)(2,1)S(1)}, bf16[1,1,16,36,768]{4,2,3,1,0:T(8,128)(2,1)}, u32[]{:S(2)}) copy-start(bf16[1,1,16,36,768]{4,2,3,1,0:T(8,128)(2,1)} %param.8) | copy-start | bytes 2654212
  31.9 8.4 %copy-start.6 = (bf16[2,48,2176]{2,1,0:T(8,128)(2,1)S(1)}, bf16[2,48,2176]{2,1,0:T(8,128)(2,1)}, u32[]{:S(2)}) copy-start(bf16[2,48,2176]{2,1,0:T(8,128)(2,1)} %copy-done.4) | copy-start | bytes 1253380
  37.6 15.2 %copy-start.1 = (bf16[1,768,2048]{2,1,0:T(8,128)(2,1)S(1)}, bf16[1,768,2048]{2,1,0:T(8,128)(2,1)}, u32[]{:S(2)}) copy-start(bf16[1,768,2048]{2,1,0:T(8,128)(2,1)} %param.9) | copy-start | bytes 9437188
  37.6 2.7 %collective-permute-start.8 = (bf16[576,768]{1,0:T(8,128)(2,1)}, bf16[576,768]{1,0:T(8,128)(2,1)S(1)}, u32[]{:S(2)}, u32[]{:S(2)}) collective-permute-start(bf16[576,768]{1,0:T(8,128)(2,1)} %collective-permute-done.7.refs_8_.refs_5_), channel_id=1, source_target_pairs={{0,1},{1,0},{2,3},{3,2},{4,5},{5,4},{6,7},{7,6},{8,9},{9,8},{10,11... | collective-permute-start | bytes 2654216 | tf_op jit(solution)/shard_map/ppermute | solution.py:426
  37.7 12.3 %collective-permute-start.10 = (bf16[2,48,2176]{2,1,0:T(8,128)(2,1)}, bf16[2,48,2176]{2,1,0:T(8,128)(2,1)S(1)}, u32[]{:S(2)}, u32[]{:S(2)}) collective-permute-start(bf16[2,48,2176]{2,1,0:T(8,128)(2,1)} %collective-permute-done.6.refs_2_.refs_4_), channel_id=1, source_target_pairs={{0,2},{1,3},{4,0},{5,1},{8,4},{9,5},{12,8},{13,9},{14,12},{15,13},... | collective-permute-start | bytes 1253384 | tf_op jit(solution)/shard_map/ppermute | solution.py:423
  39.3 12.3 %collective-permute-start.9 = (bf16[2,48,2176]{2,1,0:T(8,128)(2,1)}, bf16[2,48,2176]{2,1,0:T(8,128)(2,1)S(1)}, u32[]{:S(2)}, u32[]{:S(2)}) collective-permute-start(bf16[2,48,2176]{2,1,0:T(8,128)(2,1)} %collective-permute-done.5.refs_1_.refs_3_), channel_id=1, source_target_pairs={{0,4},{1,5},{4,8},{5,9},{8,12},{9,13},{12,14},{13,15},{14,10},{15,... | collective-permute-start | bytes 1253384 | tf_op jit(solution)/shard_map/ppermute | solution.py:423
  50.0 9.2 %collective-permute-start.12 = (bf16[1,48,2176]{2,1,0:T(8,128)(2,1)S(1)}, bf16[1,48,2176]{2,1,0:T(8,128)(2,1)S(1)}, u32[]{:S(2)}, u32[]{:S(2)}) collective-permute-start(bf16[1,48,2176]{2,1,0:T(8,128)(2,1)S(1)} %slice.7), channel_id=1, source_target_pairs={{0,2},{1,3},{4,0},{5,1},{8,4},{9,5},{12,8},{13,9},{14,12},{15,13},... | collective-permute-start | bytes 626696 | tf_op jit(solution)/shard_map/ppermute | solution.py:423
  51.6 7.6 %collective-permute-start.11 = (bf16[1,48,2176]{2,1,0:T(8,128)(2,1)S(1)}, bf16[1,48,2176]{2,1,0:T(8,128)(2,1)S(1)}, u32[]{:S(2)}, u32[]{:S(2)}) collective-permute-start(bf16[1,48,2176]{2,1,0:T(8,128)(2,1)S(1)} %slice.6), channel_id=1, source_target_pairs={{0,4},{1,5},{4,8},{5,9},{8,12},{9,13},{12,14},{13,15},{14,10},{15,... | collective-permute-start | bytes 626696 | tf_op jit(solution)/shard_map/ppermute | solution.py:423
  52.3 23.8 %collective-permute-start.17 = (bf16[2,240,768]{2,1,0:T(8,128)(2,1)S(1)}, bf16[2,240,768]{2,1,0:T(8,128)(2,1)S(1)}, u32[]{:S(2)}, u32[]{:S(2)}) collective-permute-start(bf16[2,240,768]{2,1,0:T(8,128)(2,1)S(1)} %get-tuple-element.95), channel_id=1, source_target_pairs={{0,16},{16,0},{1,17},{17,1},{2,18},{18,2},{3,19},{19,3},{4,20},{20... | collective-permute-start | bytes 2211848 | tf_op jit(solution)/shard_map/ppermute | solution.py:420
  65.1 5.9 %collective-permute-start.13 = (bf16[1,48,2176]{2,1,0:T(8,128)(2,1)S(1)}, bf16[1,48,2176]{2,1,0:T(8,128)(2,1)S(1)}, u32[]{:S(2)}, u32[]{:S(2)}) collective-permute-start(bf16[1,48,2176]{2,1,0:T(8,128)(2,1)S(1)} %bitcast.36), channel_id=1, source_target_pairs={{0,4},{1,5},{4,8},{5,9},{8,12},{9,13},{12,14},{13,15},{14,10},{15,... | collective-permute-start | bytes 626696 | tf_op jit(solution)/shard_map/ppermute | solution.py:423
  66.8 5.8 %collective-permute-start.14 = (bf16[1,48,2176]{2,1,0:T(8,128)(2,1)S(1)}, bf16[1,48,2176]{2,1,0:T(8,128)(2,1)S(1)}, u32[]{:S(2)}, u32[]{:S(2)}) collective-permute-start(bf16[1,48,2176]{2,1,0:T(8,128)(2,1)S(1)} %bitcast.35), channel_id=1, source_target_pairs={{0,2},{1,3},{4,0},{5,1},{8,4},{9,5},{12,8},{13,9},{14,12},{15,13},... | collective-permute-start | bytes 626696 | tf_op jit(solution)/shard_map/ppermute | solution.py:423
  67.2 8.9 %collective-permute-start.18 = (bf16[2,96,768]{2,1,0:T(8,128)(2,1)S(1)}, bf16[2,96,768]{2,1,0:T(8,128)(2,1)S(1)}, u32[]{:S(2)}, u32[]{:S(2)}) collective-permute-start(bf16[2,96,768]{2,1,0:T(8,128)(2,1)S(1)} %get-tuple-element.96), channel_id=1, source_target_pairs={{0,16},{16,0},{1,17},{17,1},{2,18},{18,2},{3,19},{19,3},{4,20},{20... | collective-permute-start | bytes 884744 | tf_op jit(solution)/shard_map/ppermute | solution.py:420
  72.7 9.3 %collective-permute-start.15 = (bf16[2,48,2176]{2,1,0:T(8,128)(2,1)S(1)}, bf16[2,48,2176]{2,1,0:T(8,128)(2,1)S(1)}, u32[]{:S(2)}, u32[]{:S(2)}) collective-permute-start(bf16[2,48,2176]{2,1,0:T(8,128)(2,1)S(1)} %get-tuple-element.91), channel_id=1, source_target_pairs={{0,4},{1,5},{4,8},{5,9},{8,12},{9,13},{12,14},{13,15},{14,10},{15,... | collective-permute-start | bytes 1253384 | tf_op jit(solution)/shard_map/ppermute | solution.py:423
  74.4 9.0 %collective-permute-start.16 = (bf16[2,48,2176]{2,1,0:T(8,128)(2,1)S(1)}, bf16[2,48,2176]{2,1,0:T(8,128)(2,1)S(1)}, u32[]{:S(2)}, u32[]{:S(2)}) collective-permute-start(bf16[2,48,2176]{2,1,0:T(8,128)(2,1)S(1)} %get-tuple-element.93), channel_id=1, source_target_pairs={{0,2},{1,3},{4,0},{5,1},{8,4},{9,5},{12,8},{13,9},{14,12},{15,13},... | collective-permute-start | bytes 1253384 | tf_op jit(solution)/shard_map/ppermute | solution.py:423
  83.3 16.0 %collective-permute-start.21 = (bf16[768,2048]{1,0:T(8,128)(2,1)S(1)}, bf16[768,2048]{1,0:T(8,128)(2,1)S(1)}, u32[]{:S(2)}, u32[]{:S(2)}) collective-permute-start(bf16[768,2048]{1,0:T(8,128)(2,1)S(1)} %weight_product.2), channel_id=1, source_target_pairs={{0,1},{1,0},{2,3},{3,2},{4,5},{5,4},{6,7},{7,6},{8,9},{9,8},{10,11... | collective-permute-start | bytes 9437192 | tf_op jit(solution)/shard_map/ppermute | solution.py:426
  83.3 6.3 %collective-permute-start.22 = (bf16[2,48,768]{2,1,0:T(8,128)(2,1)S(1)}, bf16[2,48,768]{2,1,0:T(8,128)(2,1)S(1)}, u32[]{:S(2)}, u32[]{:S(2)}) collective-permute-start(bf16[2,48,768]{2,1,0:T(8,128)(2,1)S(1)} %get-tuple-element.130), channel_id=1, source_target_pairs={{0,16},{16,0},{1,17},{17,1},{2,18},{18,2},{3,19},{19,3},{4,20},{20... | collective-permute-start | bytes 442376 | tf_op jit(solution)/shard_map/ppermute | solution.py:420
  85.0 11.8 %collective-permute-start.20 = (bf16[2,48,2176]{2,1,0:T(8,128)(2,1)S(1)}, bf16[2,48,2176]{2,1,0:T(8,128)(2,1)S(1)}, u32[]{:S(2)}, u32[]{:S(2)}) collective-permute-start(bf16[2,48,2176]{2,1,0:T(8,128)(2,1)S(1)} %get-tuple-element.107), channel_id=1, source_target_pairs={{0,2},{1,3},{4,0},{5,1},{8,4},{9,5},{12,8},{13,9},{14,12},{15,13},... | collective-permute-start | bytes 1253384 | tf_op jit(solution)/shard_map/ppermute | solution.py:423
  85.5 11.5 %collective-permute-start.19 = (bf16[2,48,2176]{2,1,0:T(8,128)(2,1)S(1)}, bf16[2,48,2176]{2,1,0:T(8,128)(2,1)S(1)}, u32[]{:S(2)}, u32[]{:S(2)}) collective-permute-start(bf16[2,48,2176]{2,1,0:T(8,128)(2,1)S(1)} %get-tuple-element.105), channel_id=1, source_target_pairs={{0,4},{1,5},{4,8},{5,9},{8,12},{9,13},{12,14},{13,15},{14,10},{15,... | collective-permute-start | bytes 1253384 | tf_op jit(solution)/shard_map/ppermute | solution.py:423
  90.9 18.3 %collective-permute-start.26 = (bf16[576,768]{1,0:T(8,128)(2,1)S(1)}, bf16[576,768]{1,0:T(8,128)(2,1)S(1)}, u32[]{:S(2)}, u32[]{:S(2)}) collective-permute-start(bf16[576,768]{1,0:T(8,128)(2,1)S(1)} %get-tuple-element.139), channel_id=1, source_target_pairs={{0,1},{1,0},{2,3},{3,2},{4,5},{5,4},{6,7},{7,6},{8,9},{9,8},{10,11... | collective-permute-start | bytes 2654216 | tf_op jit(solution)/shard_map/ppermute | solution.py:426
  97.2 10.8 %collective-permute-start.24 = (bf16[2,48,2176]{2,1,0:T(8,128)(2,1)S(1)}, bf16[2,48,2176]{2,1,0:T(8,128)(2,1)S(1)}, u32[]{:S(2)}, u32[]{:S(2)}) collective-permute-start(bf16[2,48,2176]{2,1,0:T(8,128)(2,1)S(1)} %get-tuple-element.134), channel_id=1, source_target_pairs={{0,2},{1,3},{4,0},{5,1},{8,4},{9,5},{12,8},{13,9},{14,12},{15,13},... | collective-permute-start | bytes 1253384 | tf_op jit(solution)/shard_map/ppermute | solution.py:423
  97.7 11.4 %copy-start.9 = (s32[48,8]{0,1:T(8,128)S(1)}, s32[48,8]{0,1:T(8,128)}, u32[]{:S(2)}) copy-start(s32[48,8]{0,1:T(8,128)} %param.6) | copy-start | bytes 4612
  97.7 10.5 %collective-permute-start.23 = (bf16[2,48,2176]{2,1,0:T(8,128)(2,1)S(1)}, bf16[2,48,2176]{2,1,0:T(8,128)(2,1)S(1)}, u32[]{:S(2)}, u32[]{:S(2)}) collective-permute-start(bf16[2,48,2176]{2,1,0:T(8,128)(2,1)S(1)} %get-tuple-element.132), channel_id=1, source_target_pairs={{0,4},{1,5},{4,8},{5,9},{8,12},{9,13},{12,14},{13,15},{14,10},{15,... | collective-permute-start | bytes 1253384 | tf_op jit(solution)/shard_map/ppermute | solution.py:423
  108.4 5.9 %collective-permute-start.25 = (bf16[48,2176]{1,0:T(8,128)(2,1)S(1)}, bf16[48,2176]{1,0:T(8,128)(2,1)S(1)}, u32[]{:S(2)}, u32[]{:S(2)}) collective-permute-start(bf16[48,2176]{1,0:T(8,128)(2,1)S(1)} %get-tuple-element.136), channel_id=1, source_target_pairs={{0,16},{16,0},{1,17},{17,1},{2,18},{18,2},{3,19},{19,3},{4,20},{20... | collective-permute-start | bytes 626696 | tf_op jit(solution)/shard_map/ppermute | solution.py:420

commit v9 on v8

--- a/solution.py
+++ b/solution.py
@@ -428,14 +428,12 @@
         room = 128 * -(-max(4 * top, 2 * n_ex) // 128)
         where = replica.reshape(1).astype(jnp.int32)
         packed = pack(where, expert_ids.T, route_probs.T, out_grad, n_dp, room)
-        blocks = {0: jnp.stack([packed[0]] + [shift(packed[d], d) for d in range(1, n_dp)])}
+        seeds = [packed[0]] + [shift(packed[d], d) for d in range(1, n_dp)]
+        blocks = {0: [jnp.stack(seeds[:per]), jnp.stack(seeds[per:])]}
 
         sibling_weight = swap(weight)
         hidden = expert_hidden[0, 0].transpose(1, 0, 2).reshape(slots, ff)
         hiddens = [(hidden, swap(hidden))]
-        for d in range(1, n_dp):
-            value = shift(after(hidden, blocks[0]), d)
-            hiddens.append((value, None))
 
         parts, scaleds, layout, facts = {}, [], [], []
         own_back, sent_back = [], [[] for _ in range(1, n_dp)]
@@ -444,11 +442,11 @@
         def work(items, *done):
             used, plan = [], []
             for off, d in items:
-                value = blocks[off][d // per] if off == half else blocks[off]
+                value = blocks[off][d // per]
                 if not any(value is other for other in used):
                     used.append(value)
                 where = [value is other for other in used].index(True)
-                plan.append((where, d % per if off == half else d, d, offsets.index(off)))
+                plan.append((where, d % per, d, offsets.index(off)))
             if done:
                 gated = [after(used[0], *done)] + used[1:]
             else:
@@ -472,33 +470,36 @@
                     sent_back[d - 1].append(shift(back[d], -d))
             return made[0]
 
-        both = lambda offs: [(off, d) for d in range(n_dp) for off in offs]
-        gate = ()
+        near = offsets[: 2 * min(2, half - 1) + 1]
         for step in range(1, half):
-            sent = blocks[1 - step], blocks[step - 1]
-            if gate:
+            sent = blocks[1 - step][0], blocks[step - 1][0]
+            if step == 2:
+                sent = after(sent[0], *seeds[1:]), after(sent[1], *seeds[1:])
+            if step > 2:
+                gate = blocks[2 - step][1], blocks[step - 2][1]
                 sent = after(sent[0], *gate), after(sent[1], *gate)
-            blocks[-step] = ring_send(sent[0], 1)
-            blocks[step] = ring_send(sent[1], -1)
+            blocks[-step], blocks[step] = [ring_send(sent[0], 1)], [ring_send(sent[1], -1)]
+            blocks[-step].append(ring_send(blocks[1 - step][1], 1))
+            blocks[step].append(ring_send(blocks[step - 1][1], -1))
             if step == 1:
-                following = [(off, 0) for off in offsets[:3]]
-            elif step == 2:
-                following = [(off, d) for d in range(n_dp) for off in offsets[:5] if d > 0 or off not in offsets[:3]]
-            else:
-                following = both([-step, step])
-            if step == half - 1:
-                break
-            if step > 1:
-                gate = (ready,)
-            if step == 2:
                 for d in range(1, n_dp):
-                    value = hiddens[d][0]
-                    hiddens[d] = value, swap(after(value, blocks[-step], blocks[step], ready))
-            ready = work(following)
-        sent = after(blocks[1 - half], ready)[:per], after(blocks[half - 1], ready)[per:]
-        blocks[half] = [ring_send(sent[0], 1), ring_send(sent[1], -1)]
-        ready = work(following)
-        work(both([half]), ready)
+                    value = shift(after(hidden, *seeds[1:], blocks[-1][0], blocks[1][0]), d)
+                    hiddens.append((value, None))
+            if step == min(2, half - 1):
+                ready = work([(off, 0) for off in near])
+        gate = blocks[2 - half][1], blocks[half - 2][1], ready
+        blocks[half] = [
+            ring_send(after(blocks[1 - half][0], *gate), 1),
+            ring_send(after(blocks[half - 1][1], ready), -1),
+        ]
+        for d in range(1, n_dp):
+            value = hiddens[d][0]
+            hiddens[d] = value, swap(after(value, *gate, blocks[1 - half][0], blocks[half - 1][0]))
+        later = [[(off, d) for off in near for d in range(1, n_dp)]]
+        later.append([(off, d) for off in offsets for d in range(n_dp) if off not in near])
+        for items in later:
+            for at in range(0, len(items), 12):
+                ready = work(sorted(items[at : at + 12], key=lambda item: item[1]), ready)
 
         carry = {}
 
@@ -528,7 +529,7 @@
             [after(refs[0], *sending, *[value for sent in sent_back for value in sent[:-1]])] + refs[1:], layout, scaleds, 1, jnp.bfloat16, width
         )
         swapped = swap(after(other, *second))
-        third = hop_on(half - 2, other)
+        third = hop_on(half - 2, other, *[sent[-1] for sent in sent_back])
         spread, spread_other = spread_product(
             [after(facts[0][0], *second)] + [fact[0] for fact in facts[1:]],
             [fact[1] for fact in facts],

time: 117 us -> 133 us (1.14)
  waiting for transfers between devices: 37.4 us -> 52.9 us
  starting transfers between devices: 26.3 us -> 31 us
  Pallas kernels: 41.9 us -> 38.6 us
  local copies, waits for them, and re-layouts: 8.66 us -> 6.87 us
    ppermute x16 -> x22, waiting for transfers between devices: 23.5 us -> 36.7 us  [ring_send(): return lax.ppermute(value, 'expert', forward if step > 0 else backward)]
    ppermute x16 -> x22, starting transfers between devices: 16.8 us -> 25.6 us  [ring_send(): return lax.ppermute(value, 'expert', forward if step > 0 else backward)]
    pallas_call x4 -> x3, Pallas kernels: 26.3 us -> 21 us  [block_product(): pl.pallas_call(functools.partial(block_kernel, plan, len(blocks), n_dp, n...]
    ppermute x6 -> x5, starting transfers between devices: 8.65 us -> 4.68 us  [shift(): lax.ppermute(value, 'dp', [(i, (i + step) % n_dp) for i in range(n_dp)])]
    ppermute x6 -> x5, waiting for transfers between devices: 13.3 us -> 16.2 us  [shift(): lax.ppermute(value, 'dp', [(i, (i + step) % n_dp) for i in range(n_dp)])]
    pallas_call x2, Pallas kernels: 12 us -> 14.1 us  [weight_product(): pl.pallas_call(functools.partial(weight_kernel, len(blocks), len(scaleds)...]
    unnamed x24 -> x18, local copies, waits for them, and re-layouts: 7.93 us -> 6.18 us
  transfers between devices with their start and end apart: 27 -> 32, of which waited for: 15 -> 19; matrix products, arithmetic and copies ran while one was open for 2% -> 2% of each run, Pallas kernels for 35% -> 28%
where the time goes in v9:
time: 133 us
  waiting for transfers between devices  52.9 us (40%)
  Pallas kernels  38.6 us (29%)
  starting transfers between devices  31 us (23%)
  local copies, waits for them, and re-layouts  6.87 us (5%)
  other arithmetic  2.29 us (2%)
    ppermute x22, waiting for transfers between devices, ring_send(): return lax.ppermute(value, 'expert', forward if step > 0 else backward)  36.7 us
    ppermute x22, starting transfers between devices, ring_send(): return lax.ppermute(value, 'expert', forward if step > 0 else backward)  25.6 us
    pallas_call x3, Pallas kernels, block_product(): pl.pallas_call(functools.partial(block_kernel, plan, len(blocks), n_dp, n...  21 us
    ppermute x5, waiting for transfers between devices, shift(): lax.ppermute(value, 'dp', [(i, (i + step) % n_dp) for i in range(n_dp)])  16.2 us
    pallas_call x2, Pallas kernels, weight_product(): pl.pallas_call(functools.partial(weight_kernel, len(blocks), len(scaleds)...  14.1 us
    unnamed x18, local copies, waits for them, and re-layouts  6.18 us
    ppermute x5, starting transfers between devices, shift(): lax.ppermute(value, 'dp', [(i, (i + step) % n_dp) for i in range(n_dp)])  4.68 us
  transfers between devices with their start and end apart: 32, of which 19 were waited for; matrix products, arithmetic and copies ran while one was open for 2% of the time, Pallas kernels for 28%

profile of v9, /device:TPU:0, one launch (start us, length us, event | category | flops | bytes accessed | tf_op | source)
XLA Modules:
  0.0 132.5 jit_solution(1792701526008089356)
XLA Ops:
  0.6 0.5 collective-permute-start.6
  1.2 1.0 copy-done
  2.2 0.7 copy-done.1
  2.9 0.7 copy-done.3
  3.6 0.2 pack.1
  3.9 3.0 %collective-permute-start.1 = (bf16[1,48,2176]{2,1,0:T(8,128)(2,1)S(1)}, bf16[1,48,2176]{2,1,0:T(8,128)(2,1)S(1)}, u32[]{:S(2)}, u32[]{:S(2)}) collective-permute-start(bf16[1,48,2176]{2,1,0:T(8,128)(2,1)S(1)} %bitcast.21), channel_id=1, source_target_pairs={{0,2},{1,3},{4,0},{5,1},{8,4},{9,5},{12,8},{13,9},{14,12},{15,13},... | collective-permute-start | bytes 626696 | tf_op jit(solution)/shard_map/ppermute | solution.py:423
  6.9 1.5 %collective-permute-start.2 = (bf16[48,2176]{1,0:T(8,128)(2,1)S(1)}, bf16[48,2176]{1,0:T(8,128)(2,1)S(1)}, u32[]{:S(2)}, u32[]{:S(2)}) collective-permute-start(bf16[48,2176]{1,0:T(8,128)(2,1)S(1)} %get-tuple-element.66), channel_id=1, source_target_pairs={{0,16},{16,0},{1,17},{17,1},{2,18},{18,2},{3,19},{19,3},{4,20},{20... | collective-permute-start | bytes 626696 | tf_op jit(solution)/shard_map/ppermute | solution.py:420
  8.3 0.5 collective-permute-start
  8.9 3.5 %collective-permute-done.1.refs_3_.refs_2_ = bf16[1,48,2176]{2,1,0:T(8,128)(2,1)S(1)} collective-permute-done((bf16[1,48,2176]{2,1,0:T(8,128)(2,1)S(1)}, bf16[1,48,2176]{2,1,0:T(8,128)(2,1)S(1)}, u32[]{:S(2)}, u32[]{:S(2)}) %collective-permute-start.1) | collective-permute-done | bytes 208928 | tf_op jit(solution)/shard_map/ppermute | solution.py:423
  12.3 1.4 %collective-permute-done.2 = bf16[48,2176]{1,0:T(8,128)(2,1)S(1)} collective-permute-done((bf16[48,2176]{1,0:T(8,128)(2,1)S(1)}, bf16[48,2176]{1,0:T(8,128)(2,1)S(1)}, u32[]{:S(2)}, u32[]{:S(2)}) %collective-permute-start.2) | collective-permute-done | bytes 208928 | tf_op jit(solution)/shard_map/ppermute | solution.py:420
  13.7 1.2 collective-permute-done.refs_2_.refs_1_
  14.9 0.5 collective-permute-start.11
  15.5 0.4 collective-permute-start.3
  15.9 1.7 %collective-permute-start.7 = (bf16[1,48,2176]{2,1,0:T(8,128)(2,1)S(1)}, bf16[1,48,2176]{2,1,0:T(8,128)(2,1)S(1)}, u32[]{:S(2)}, u32[]{:S(2)}) collective-permute-start(bf16[1,48,2176]{2,1,0:T(8,128)(2,1)S(1)} %bitcast.26), channel_id=1, source_target_pairs={{0,4},{1,5},{4,8},{5,9},{8,12},{9,13},{12,14},{13,15},{14,10},{15,... | collective-permute-start | bytes 626696 | tf_op jit(solution)/shard_map/ppermute | solution.py:423
  17.6 5.6 %collective-permute-done.3.refs_4_.refs_3_ = bf16[1,48,2176]{2,1,0:T(8,128)(2,1)S(1)} collective-permute-done((bf16[1,48,2176]{2,1,0:T(8,128)(2,1)S(1)}, bf16[1,48,2176]{2,1,0:T(8,128)(2,1)S(1)}, u32[]{:S(2)}, u32[]{:S(2)}) %collective-permute-start.3) | collective-permute-done | bytes 208928 | tf_op jit(solution)/shard_map/ppermute | solution.py:423
  23.2 1.6 %collective-permute-start.8 = (bf16[1,48,2176]{2,1,0:T(8,128)(2,1)S(1)}, bf16[1,48,2176]{2,1,0:T(8,128)(2,1)S(1)}, u32[]{:S(2)}, u32[]{:S(2)}) collective-permute-start(bf16[1,48,2176]{2,1,0:T(8,128)(2,1)S(1)} %bitcast.27), channel_id=1, source_target_pairs={{0,2},{1,3},{4,0},{5,1},{8,4},{9,5},{12,8},{13,9},{14,12},{15,13},... | collective-permute-start | bytes 626696 | tf_op jit(solution)/shard_map/ppermute | solution.py:423
  24.8 0.7 collective-permute-done.7.refs_2_.refs_6_
  25.4 1.6 %collective-permute-start.4 = (bf16[1,48,2176]{2,1,0:T(8,128)(2,1)S(1)}, bf16[1,48,2176]{2,1,0:T(8,128)(2,1)S(1)}, u32[]{:S(2)}, u32[]{:S(2)}) collective-permute-start(bf16[1,48,2176]{2,1,0:T(8,128)(2,1)S(1)} %collective-permute-done.1.refs_3_.refs_2_), channel_id=1, source_target_pairs={{0,2},{1,3},{4,0},{5,1},{8,4},{9,5},{12,8},{13,9},{14,12},{15,13},... | collective-permute-start | bytes 626696 | tf_op jit(solution)/shard_map/ppermute | solution.py:423
  27.0 0.7 dynamic-slice_bitcast_fusion.refs_0_
  27.7 2.3 %collective-permute-done.8.refs_3_.refs_7_ = bf16[1,48,2176]{2,1,0:T(8,128)(2,1)S(1)} collective-permute-done((bf16[1,48,2176]{2,1,0:T(8,128)(2,1)S(1)}, bf16[1,48,2176]{2,1,0:T(8,128)(2,1)S(1)}, u32[]{:S(2)}, u32[]{:S(2)}) %collective-permute-start.8) | collective-permute-done | bytes 208928 | tf_op jit(solution)/shard_map/ppermute | solution.py:423
  30.0 0.9 collective-permute-start.12
  30.9 2.1 %collective-permute-done.4.refs_5_.refs_4_ = bf16[1,48,2176]{2,1,0:T(8,128)(2,1)S(1)} collective-permute-done((bf16[1,48,2176]{2,1,0:T(8,128)(2,1)S(1)}, bf16[1,48,2176]{2,1,0:T(8,128)(2,1)S(1)}, u32[]{:S(2)}, u32[]{:S(2)}) %collective-permute-start.4) | collective-permute-done | bytes 208928 | tf_op jit(solution)/shard_map/ppermute | solution.py:423
  32.9 1.6 %collective-permute-start.13 = (bf16[1,48,2176]{2,1,0:T(8,128)(2,1)S(1)}, bf16[1,48,2176]{2,1,0:T(8,128)(2,1)S(1)}, u32[]{:S(2)}, u32[]{:S(2)}) collective-permute-start(bf16[1,48,2176]{2,1,0:T(8,128)(2,1)S(1)} %collective-permute-done.4.refs_5_.refs_4_), channel_id=1, source_target_pairs={{0,2},{1,3},{4,0},{5,1},{8,4},{9,5},{12,8},{13,9},{14,12},{15,13},... | collective-permute-start | bytes 626696 | tf_op jit(solution)/shard_map/ppermute | solution.py:423
  34.5 1.6 %collective-permute-start.10 = (bf16[1,48,2176]{2,1,0:T(8,128)(2,1)S(1)}, bf16[1,48,2176]{2,1,0:T(8,128)(2,1)S(1)}, u32[]{:S(2)}, u32[]{:S(2)}) collective-permute-start(bf16[1,48,2176]{2,1,0:T(8,128)(2,1)S(1)} %collective-permute-done.8.refs_3_.refs_7_), channel_id=1, source_target_pairs={{0,2},{1,3},{4,0},{5,1},{8,4},{9,5},{12,8},{13,9},{14,12},{15,13},... | collective-permute-start | bytes 626696 | tf_op jit(solution)/shard_map/ppermute | solution.py:423
  36.1 0.4 collective-permute-start.9
  36.6 1.9 %copy-done.4 = bf16[1,768,2048]{2,1,0:T(8,128)(2,1)S(1)} copy-done((bf16[1,768,2048]{2,1,0:T(8,128)(2,1)S(1)}, bf16[1,768,2048]{2,1,0:T(8,128)(2,1)}, u32[]{:S(2)}) %copy-start.4) | copy-done | bytes 3145752
  38.5 1.2 copy-done.6
  39.6 6.7 %block_product.3 = (bf16[48,2176]{1,0:T(8,128)(2,1)S(1)}, bf16[48,2176]{1,0:T(8,128)(2,1)S(1)}, bf16[48,2176]{1,0:T(8,128)(2,1)S(1)}, bf16[48,2176]{1,0:T(8,128)...) custom-call(s32[10]{0:T(128)S(1)} %dynamic-slice_bitcast_fusion.refs, ...), custom_call_target="tpu_custom_call" | custom-call | flops 3019898880 | bytes 9117696 | tf_op jit(solution)/shard_map/block_product/pallas_call | solution.py:275
  46.5 1.6 %collective-permute-start.17 = (bf16[1,48,2176]{2,1,0:T(8,128)(2,1)S(1)}, bf16[1,48,2176]{2,1,0:T(8,128)(2,1)S(1)}, u32[]{:S(2)}, u32[]{:S(2)}) collective-permute-start(bf16[1,48,2176]{2,1,0:T(8,128)(2,1)S(1)} %collective-permute-done.10.refs_5_.refs_9_), channel_id=1, source_target_pairs={{0,2},{1,3},{4,0},{5,1},{8,4},{9,5},{12,8},{13,9},{14,12},{15,13},... | collective-permute-start | bytes 626696 | tf_op jit(solution)/shard_map/ppermute | solution.py:423
  48.1 0.4 collective-permute-start.16
  48.6 0.4 collective-permute-start.15
  49.0 5.0 %collective-permute-done.17.refs_5_.refs_14_ = bf16[1,48,2176]{2,1,0:T(8,128)(2,1)S(1)} collective-permute-done((bf16[1,48,2176]{2,1,0:T(8,128)(2,1)S(1)}, bf16[1,48,2176]{2,1,0:T(8,128)(2,1)S(1)}, u32[]{:S(2)}, u32[]{:S(2)}) %collective-permute-start.17) | collective-permute-done | bytes 208928 | tf_op jit(solution)/shard_map/ppermute | solution.py:423
  54.1 1.6 %collective-permute-start.18 = (bf16[1,48,2176]{2,1,0:T(8,128)(2,1)S(1)}, bf16[1,48,2176]{2,1,0:T(8,128)(2,1)S(1)}, u32[]{:S(2)}, u32[]{:S(2)}) collective-permute-start(bf16[1,48,2176]{2,1,0:T(8,128)(2,1)S(1)} %collective-permute-done.17.refs_5_.refs_14_), channel_id=1, source_target_pairs={{0,2},{1,3},{4,0},{5,1},{8,4},{9,5},{12,8},{13,9},{14,12},{15,13},... | collective-permute-start | bytes 626696 | tf_op jit(solution)/shard_map/ppermute | solution.py:423
  55.6 6.6 %block_product.4 = (bf16[48,2176]{1,0:T(8,128)(2,1)S(1)}, bf16[48,2176]{1,0:T(8,128)(2,1)S(1)}, bf16[48,2176]{1,0:T(8,128)(2,1)S(1)}, bf16[48,2176]{1,0:T(8,128)...) custom-call(s32[10]{0:T(128)S(1)} %dynamic-slice_bitcast_fusion.refs_0_,, ...), custom_call_target="tpu_custom_call" | custom-call | flops 3019898880 | bytes 9117696 | tf_op jit(solution)/shard_map/block_product/pallas_call | solution.py:275
  62.3 1.5 %collective-permute-start.23 = (bf16[2,240,768]{2,1,0:T(8,128)(2,1)S(1)}, bf16[2,240,768]{2,1,0:T(8,128)(2,1)S(1)}, u32[]{:S(2)}, u32[]{:S(2)}) collective-permute-start(bf16[2,240,768]{2,1,0:T(8,128)(2,1)S(1)} %get-tuple-element.92), channel_id=1, source_target_pairs={{0,16},{16,0},{1,17},{17,1},{2,18},{18,2},{3,19},{19,3},{4,20},{20... | collective-permute-start | bytes 2211848 | tf_op jit(solution)/shard_map/ppermute | solution.py:420
  63.8 7.6 %block_product.5 = (bf16[48,2176]{1,0:T(8,128)(2,1)S(1)}, bf16[48,2176]{1,0:T(8,128)(2,1)S(1)}, bf16[48,2176]{1,0:T(8,128)(2,1)S(1)}, bf16[48,2176]{1,0:T(8,128)...) custom-call(s32[10]{0:T(128)S(1)} %dynamic-slice_bitcast_fusion.refs, ...), custom_call_target="tpu_custom_call" | custom-call | flops 3623878656 | bytes 9682944 | tf_op jit(solution)/shard_map/block_product/pallas_call | solution.py:275
  71.4 0.5 collective-permute-start.19
  71.9 1.6 %collective-permute-start.20 = (bf16[1,48,2176]{2,1,0:T(8,128)(2,1)S(1)}, bf16[1,48,2176]{2,1,0:T(8,128)(2,1)S(1)}, u32[]{:S(2)}, u32[]{:S(2)}) collective-permute-start(bf16[1,48,2176]{2,1,0:T(8,128)(2,1)S(1)} %bitcast.41), channel_id=1, source_target_pairs={{0,2},{1,3},{4,0},{5,1},{8,4},{9,5},{12,8},{13,9},{14,12},{15,13},... | collective-permute-start | bytes 626696 | tf_op jit(solution)/shard_map/ppermute | solution.py:423
  73.5 4.2 %collective-permute-done.19.refs_2_ = bf16[1,48,2176]{2,1,0:T(8,128)(2,1)S(1)} collective-permute-done((bf16[1,48,2176]{2,1,0:T(8,128)(2,1)S(1)}, bf16[1,48,2176]{2,1,0:T(8,128)(2,1)S(1)}, u32[]{:S(2)}, u32[]{:S(2)}) %collective-permute-start.19) | collective-permute-done | bytes 208928 | tf_op jit(solution)/shard_map/ppermute | solution.py:423
  77.7 0.2 collective-permute-done.20.refs_5_
  78.0 0.5 collective-permute-start.21
  78.5 1.6 %collective-permute-start.22 = (bf16[2,48,2176]{2,1,0:T(8,128)(2,1)S(1)}, bf16[2,48,2176]{2,1,0:T(8,128)(2,1)S(1)}, u32[]{:S(2)}, u32[]{:S(2)}) collective-permute-start(bf16[2,48,2176]{2,1,0:T(8,128)(2,1)S(1)} %get-tuple-element.90), channel_id=1, source_target_pairs={{0,2},{1,3},{4,0},{5,1},{8,4},{9,5},{12,8},{13,9},{14,12},{15,13},... | collective-permute-start | bytes 1253384 | tf_op jit(solution)/shard_map/ppermute | solution.py:423
  80.1 6.4 %weight_product.2 = bf16[768,2048]{1,0:T(8,128)(2,1)S(1)} custom-call(bf16[1,48,2176]{2,1,0:T(8,128)(2,1)S(1)} %bitcast.24, bf16[1,48,2176]{2,1,0:T(8,128)(2,1)S(1)} %collective-permute-done.refs_2_.refs_1_, bf16[1,48,2176]{2,1,0:T(8,128)(2,1)S(1)} %collective-permute-done.1.refs_3_.refs_2_, bf16[1,48,2176]{2,1,0:T(8,128)(2,1)S(1)} %collective-permute-done.3.refs_4_.refs_3_, ...), custom_call_target="tpu_custom_call" | custom-call | flops 2415919104 | bytes 10616832 | tf_op jit(solution)/shard_map/weight_product/pallas_call | solution.py:357
  86.6 1.0 collective-permute-done.21.refs_2_
  87.6 0.2 collective-permute-done.22.refs_5_
  87.8 0.6 collective-permute-start.24
  88.3 0.2 sums.4
  88.5 11.8 %collective-permute-done.24.refs_7_ = bf16[2,144,768]{2,1,0:T(8,128)(2,1)S(1)} collective-permute-done((bf16[2,144,768]{2,1,0:T(8,128)(2,1)S(1)}, bf16[2,144,768]{2,1,0:T(8,128)(2,1)S(1)}, u32[]{:S(2)}, u32[]{:S(2)}) %collective-permute-start.24) | collective-permute-done | bytes 442400 | tf_op jit(solution)/shard_map/ppermute | solution.py:420
  100.4 1.6 %collective-permute-start.26 = (bf16[2,48,2176]{2,1,0:T(8,128)(2,1)S(1)}, bf16[2,48,2176]{2,1,0:T(8,128)(2,1)S(1)}, u32[]{:S(2)}, u32[]{:S(2)}) collective-permute-start(bf16[2,48,2176]{2,1,0:T(8,128)(2,1)S(1)} %get-tuple-element.101), channel_id=1, source_target_pairs={{0,2},{1,3},{4,0},{5,1},{8,4},{9,5},{12,8},{13,9},{14,12},{15,13},... | collective-permute-start | bytes 1253384 | tf_op jit(solution)/shard_map/ppermute | solution.py:423
  101.9 0.4 collective-permute-start.25
  102.4 1.3 spread_product.1
  103.8 7.8 %collective-permute-done.26.refs_5_ = bf16[2,48,2176]{2,1,0:T(8,128)(2,1)S(1)} collective-permute-done((bf16[2,48,2176]{2,1,0:T(8,128)(2,1)S(1)}, bf16[2,48,2176]{2,1,0:T(8,128)(2,1)S(1)}, u32[]{:S(2)}, u32[]{:S(2)}) %collective-permute-start.26) | collective-permute-done | bytes 417824 | tf_op jit(solution)/shard_map/ppermute | solution.py:423
  111.6 1.3 collective-permute-done.25.refs_2_
  112.9 0.2 sums.5
  113.1 1.6 %collective-permute-start.29 = (bf16[2,48,2176]{2,1,0:T(8,128)(2,1)S(1)}, bf16[2,48,2176]{2,1,0:T(8,128)(2,1)S(1)}, u32[]{:S(2)}, u32[]{:S(2)}) collective-permute-start(bf16[2,48,2176]{2,1,0:T(8,128)(2,1)S(1)} %get-tuple-element.120), channel_id=1, source_target_pairs={{0,2},{1,3},{4,0},{5,1},{8,4},{9,5},{12,8},{13,9},{14,12},{15,13},... | collective-permute-start | bytes 1253384 | tf_op jit(solution)/shard_map/ppermute | solution.py:423
  114.8 0.5 collective-permute-start.28
  115.2 7.7 %weight_product.3 = f32[768,2048]{1,0:T(8,128)} custom-call(bf16[1,48,2176]{2,1,0:T(8,128)(2,1)S(1)} %bitcast.25, bf16[1,48,2176]{2,1,0:T(8,128)(2,1)S(1)} %collective-permute-done.refs_2_.refs_1_, bf16[1,48,2176]{2,1,0:T(8,128)(2,1)S(1)} %collective-permute-done.1.refs_3_.refs_2_, bf16[1,48,2176]{2,1,0:T(8,128)(2,1)S(1)} %collective-permute-done.3.refs_4_.refs_3_, ...), custom_call_target="tpu_custom_call" | custom-call | flops 2415919104 | bytes 10616832 | tf_op jit(solution)/shard_map/weight_product/pallas_call | solution.py:357
  122.9 0.4 collective-permute-done.29.refs_3_
  123.3 1.3 collective-permute-done.28.refs_2_
  124.7 0.6 collective-permute-start.30
  125.4 2.3 %add.8 = bf16[576,768]{1,0:T(8,128)(2,1)} add(bf16[576,768]{1,0:T(8,128)(2,1)S(1)} %get-tuple-element.117, bf16[576,768]{1,0:T(8,128)(2,1)} %collective-permute-done.31) | non-fusion elementwise | flops 442368 | bytes 2654208 | tf_op jit(solution)/shard_map/add | solution.py:539
  127.7 2.9 %collective-permute-done.30.refs_1_ = bf16[48,2176]{1,0:T(8,128)(2,1)S(1)} collective-permute-done((bf16[48,2176]{1,0:T(8,128)(2,1)S(1)}, bf16[48,2176]{1,0:T(8,128)(2,1)S(1)}, u32[]{:S(2)}, u32[]{:S(2)}) %collective-permute-start.30) | collective-permute-done | bytes 208928 | tf_op jit(solution)/shard_map/ppermute | solution.py:420
  130.6 1.3 home.1
  131.9 0.7 copy.11
  (32 shorter events, 0.7 us)
Async XLA Ops:
  0.6 35.5 %collective-permute-start.6 = (bf16[768,2048]{1,0:T(8,128)(2,1)}, bf16[768,2048]{1,0:T(8,128)(2,1)}, u32[]{:S(2)}, u32[]{:S(2)}) collective-permute-start(bf16[768,2048]{1,0:T(8,128)(2,1)} %bitcast.33), channel_id=1, source_target_pairs={{0,1},{1,0},{2,3},{3,2},{4,5},{5,4},{6,7},{7,6},{8,9},{9,8},{10,11... | collective-permute-start | bytes 9437192 | tf_op jit(solution)/shard_map/ppermute | solution.py:426
  1.1 33.4 %collective-permute-start.5 = (bf16[576,768]{1,0:T(8,128)(2,1)}, bf16[576,768]{1,0:T(8,128)(2,1)S(1)}, u32[]{:S(2)}, u32[]{:S(2)}) collective-permute-start(bf16[576,768]{1,0:T(8,128)(2,1)} %bitcast.37), channel_id=1, source_target_pairs={{0,1},{1,0},{2,3},{3,2},{4,5},{5,4},{6,7},{7,6},{8,9},{9,8},{10,11... | collective-permute-start | bytes 2654216 | tf_op jit(solution)/shard_map/ppermute | solution.py:426
  1.2 1.0 copy-start
  2.2 0.7 copy-start.1
  2.9 0.7 copy-start.3
  3.9 8.5 %collective-permute-start.1 = (bf16[1,48,2176]{2,1,0:T(8,128)(2,1)S(1)}, bf16[1,48,2176]{2,1,0:T(8,128)(2,1)S(1)}, u32[]{:S(2)}, u32[]{:S(2)}) collective-permute-start(bf16[1,48,2176]{2,1,0:T(8,128)(2,1)S(1)} %bitcast.21), channel_id=1, source_target_pairs={{0,2},{1,3},{4,0},{5,1},{8,4},{9,5},{12,8},{13,9},{14,12},{15,13},... | collective-permute-start | bytes 626696 | tf_op jit(solution)/shard_map/ppermute | solution.py:423
  6.9 6.9 %collective-permute-start.2 = (bf16[48,2176]{1,0:T(8,128)(2,1)S(1)}, bf16[48,2176]{1,0:T(8,128)(2,1)S(1)}, u32[]{:S(2)}, u32[]{:S(2)}) collective-permute-start(bf16[48,2176]{1,0:T(8,128)(2,1)S(1)} %get-tuple-element.66), channel_id=1, source_target_pairs={{0,16},{16,0},{1,17},{17,1},{2,18},{18,2},{3,19},{19,3},{4,20},{20... | collective-permute-start | bytes 626696 | tf_op jit(solution)/shard_map/ppermute | solution.py:420
  8.3 6.6 %collective-permute-start = (bf16[1,48,2176]{2,1,0:T(8,128)(2,1)S(1)}, bf16[1,48,2176]{2,1,0:T(8,128)(2,1)S(1)}, u32[]{:S(2)}, u32[]{:S(2)}) collective-permute-start(bf16[1,48,2176]{2,1,0:T(8,128)(2,1)S(1)} %bitcast.22), channel_id=1, source_target_pairs={{0,4},{1,5},{4,8},{5,9},{8,12},{9,13},{12,14},{13,15},{14,10},{15,... | collective-permute-start | bytes 626696 | tf_op jit(solution)/shard_map/ppermute | solution.py:423
  14.9 31.5 %collective-permute-start.11 = (bf16[576,768]{1,0:T(8,128)(2,1)}, bf16[576,768]{1,0:T(8,128)(2,1)S(1)}, u32[]{:S(2)}, u32[]{:S(2)}) collective-permute-start(bf16[576,768]{1,0:T(8,128)(2,1)} %bitcast.38), channel_id=1, source_target_pairs={{0,16},{16,0},{1,17},{17,1},{2,18},{18,2},{3,19},{19,3},{4,20},{20... | collective-permute-start | bytes 2654216 | tf_op jit(solution)/shard_map/ppermute | solution.py:420
  15.5 7.7 %collective-permute-start.3 = (bf16[1,48,2176]{2,1,0:T(8,128)(2,1)S(1)}, bf16[1,48,2176]{2,1,0:T(8,128)(2,1)S(1)}, u32[]{:S(2)}, u32[]{:S(2)}) collective-permute-start(bf16[1,48,2176]{2,1,0:T(8,128)(2,1)S(1)} %collective-permute-done.refs_2_.refs_1_), channel_id=1, source_target_pairs={{0,4},{1,5},{4,8},{5,9},{8,12},{9,13},{12,14},{13,15},{14,10},{15,... | collective-permute-start | bytes 626696 | tf_op jit(solution)/shard_map/ppermute | solution.py:423
  15.9 9.5 %collective-permute-start.7 = (bf16[1,48,2176]{2,1,0:T(8,128)(2,1)S(1)}, bf16[1,48,2176]{2,1,0:T(8,128)(2,1)S(1)}, u32[]{:S(2)}, u32[]{:S(2)}) collective-permute-start(bf16[1,48,2176]{2,1,0:T(8,128)(2,1)S(1)} %bitcast.26), channel_id=1, source_target_pairs={{0,4},{1,5},{4,8},{5,9},{8,12},{9,13},{12,14},{13,15},{14,10},{15,... | collective-permute-start | bytes 626696 | tf_op jit(solution)/shard_map/ppermute | solution.py:423
  23.2 6.8 %collective-permute-start.8 = (bf16[1,48,2176]{2,1,0:T(8,128)(2,1)S(1)}, bf16[1,48,2176]{2,1,0:T(8,128)(2,1)S(1)}, u32[]{:S(2)}, u32[]{:S(2)}) collective-permute-start(bf16[1,48,2176]{2,1,0:T(8,128)(2,1)S(1)} %bitcast.27), channel_id=1, source_target_pairs={{0,2},{1,3},{4,0},{5,1},{8,4},{9,5},{12,8},{13,9},{14,12},{15,13},... | collective-permute-start | bytes 626696 | tf_op jit(solution)/shard_map/ppermute | solution.py:423
  25.4 7.5 %collective-permute-start.4 = (bf16[1,48,2176]{2,1,0:T(8,128)(2,1)S(1)}, bf16[1,48,2176]{2,1,0:T(8,128)(2,1)S(1)}, u32[]{:S(2)}, u32[]{:S(2)}) collective-permute-start(bf16[1,48,2176]{2,1,0:T(8,128)(2,1)S(1)} %collective-permute-done.1.refs_3_.refs_2_), channel_id=1, source_target_pairs={{0,2},{1,3},{4,0},{5,1},{8,4},{9,5},{12,8},{13,9},{14,12},{15,13},... | collective-permute-start | bytes 626696 | tf_op jit(solution)/shard_map/ppermute | solution.py:423
  30.0 16.4 %collective-permute-start.12 = (bf16[1,48,2176]{2,1,0:T(8,128)(2,1)S(1)}, bf16[1,48,2176]{2,1,0:T(8,128)(2,1)S(1)}, u32[]{:S(2)}, u32[]{:S(2)}) collective-permute-start(bf16[1,48,2176]{2,1,0:T(8,128)(2,1)S(1)} %collective-permute-done.3.refs_4_.refs_3_), channel_id=1, source_target_pairs={{0,4},{1,5},{4,8},{5,9},{8,12},{9,13},{12,14},{13,15},{14,10},{15,... | collective-permute-start | bytes 626696 | tf_op jit(solution)/shard_map/ppermute | solution.py:423
  32.9 13.4 %collective-permute-start.13 = (bf16[1,48,2176]{2,1,0:T(8,128)(2,1)S(1)}, bf16[1,48,2176]{2,1,0:T(8,128)(2,1)S(1)}, u32[]{:S(2)}, u32[]{:S(2)}) collective-permute-start(bf16[1,48,2176]{2,1,0:T(8,128)(2,1)S(1)} %collective-permute-done.4.refs_5_.refs_4_), channel_id=1, source_target_pairs={{0,2},{1,3},{4,0},{5,1},{8,4},{9,5},{12,8},{13,9},{14,12},{15,13},... | collective-permute-start | bytes 626696 | tf_op jit(solution)/shard_map/ppermute | solution.py:423
  34.5 11.8 %collective-permute-start.10 = (bf16[1,48,2176]{2,1,0:T(8,128)(2,1)S(1)}, bf16[1,48,2176]{2,1,0:T(8,128)(2,1)S(1)}, u32[]{:S(2)}, u32[]{:S(2)}) collective-permute-start(bf16[1,48,2176]{2,1,0:T(8,128)(2,1)S(1)} %collective-permute-done.8.refs_3_.refs_7_), channel_id=1, source_target_pairs={{0,2},{1,3},{4,0},{5,1},{8,4},{9,5},{12,8},{13,9},{14,12},{15,13},... | collective-permute-start | bytes 626696 | tf_op jit(solution)/shard_map/ppermute | solution.py:423
  36.1 10.3 %collective-permute-start.9 = (bf16[1,48,2176]{2,1,0:T(8,128)(2,1)S(1)}, bf16[1,48,2176]{2,1,0:T(8,128)(2,1)S(1)}, u32[]{:S(2)}, u32[]{:S(2)}) collective-permute-start(bf16[1,48,2176]{2,1,0:T(8,128)(2,1)S(1)} %collective-permute-done.7.refs_2_.refs_6_), channel_id=1, source_target_pairs={{0,4},{1,5},{4,8},{5,9},{8,12},{9,13},{12,14},{13,15},{14,10},{15,... | collective-permute-start | bytes 626696 | tf_op jit(solution)/shard_map/ppermute | solution.py:423
  36.6 1.9 %copy-start.4 = (bf16[1,768,2048]{2,1,0:T(8,128)(2,1)S(1)}, bf16[1,768,2048]{2,1,0:T(8,128)(2,1)}, u32[]{:S(2)}) copy-start(bf16[1,768,2048]{2,1,0:T(8,128)(2,1)} %param.9) | copy-start | bytes 9437188
  38.5 1.2 copy-start.6
  39.6 16.0 %copy-start.5 = (bf16[1,768,2048]{2,1,0:T(8,128)(2,1)S(1)}, bf16[1,768,2048]{2,1,0:T(8,128)(2,1)}, u32[]{:S(2)}) copy-start(bf16[1,768,2048]{2,1,0:T(8,128)(2,1)} %param.9) | copy-start | bytes 9437188
  46.4 17.4 %copy-start.7 = (bf16[1,1,16,36,768]{4,2,3,1,0:T(8,128)(2,1)S(1)}, bf16[1,1,16,36,768]{4,2,3,1,0:T(8,128)(2,1)}, u32[]{:S(2)}) copy-start(bf16[1,1,16,36,768]{4,2,3,1,0:T(8,128)(2,1)} %param.8) | copy-start | bytes 2654212
  46.4 9.2 %collective-permute-start.14 = (bf16[576,768]{1,0:T(8,128)(2,1)S(1)}, bf16[576,768]{1,0:T(8,128)(2,1)S(1)}, u32[]{:S(2)}, u32[]{:S(2)}) collective-permute-start(bf16[576,768]{1,0:T(8,128)(2,1)S(1)} %collective-permute-done.11.refs_6_.refs_9_), channel_id=1, source_target_pairs={{0,1},{1,0},{2,3},{3,2},{4,5},{5,4},{6,7},{7,6},{8,9},{9,8},{10,11... | collective-permute-start | bytes 2654216 | tf_op jit(solution)/shard_map/ppermute | solution.py:426
  46.5 7.6 %collective-permute-start.17 = (bf16[1,48,2176]{2,1,0:T(8,128)(2,1)S(1)}, bf16[1,48,2176]{2,1,0:T(8,128)(2,1)S(1)}, u32[]{:S(2)}, u32[]{:S(2)}) collective-permute-start(bf16[1,48,2176]{2,1,0:T(8,128)(2,1)S(1)} %collective-permute-done.10.refs_5_.refs_9_), channel_id=1, source_target_pairs={{0,2},{1,3},{4,0},{5,1},{8,4},{9,5},{12,8},{13,9},{14,12},{15,13},... | collective-permute-start | bytes 626696 | tf_op jit(solution)/shard_map/ppermute | solution.py:423
  48.1 15.7 %collective-permute-start.16 = (bf16[1,48,2176]{2,1,0:T(8,128)(2,1)S(1)}, bf16[1,48,2176]{2,1,0:T(8,128)(2,1)S(1)}, u32[]{:S(2)}, u32[]{:S(2)}) collective-permute-start(bf16[1,48,2176]{2,1,0:T(8,128)(2,1)S(1)} %collective-permute-done.9.refs_4_.refs_8_), channel_id=1, source_target_pairs={{0,4},{1,5},{4,8},{5,9},{8,12},{9,13},{12,14},{13,15},{14,10},{15,... | collective-permute-start | bytes 626696 | tf_op jit(solution)/shard_map/ppermute | solution.py:423
  48.6 15.2 %collective-permute-start.15 = (bf16[1,48,2176]{2,1,0:T(8,128)(2,1)S(1)}, bf16[1,48,2176]{2,1,0:T(8,128)(2,1)S(1)}, u32[]{:S(2)}, u32[]{:S(2)}) collective-permute-start(bf16[1,48,2176]{2,1,0:T(8,128)(2,1)S(1)} %collective-permute-done.12.refs_1_.refs_10_), channel_id=1, source_target_pairs={{0,4},{1,5},{4,8},{5,9},{8,12},{9,13},{12,14},{13,15},{14,10},{15,... | collective-permute-start | bytes 626696 | tf_op jit(solution)/shard_map/ppermute | solution.py:423
  54.1 9.7 %collective-permute-start.18 = (bf16[1,48,2176]{2,1,0:T(8,128)(2,1)S(1)}, bf16[1,48,2176]{2,1,0:T(8,128)(2,1)S(1)}, u32[]{:S(2)}, u32[]{:S(2)}) collective-permute-start(bf16[1,48,2176]{2,1,0:T(8,128)(2,1)S(1)} %collective-permute-done.17.refs_5_.refs_14_), channel_id=1, source_target_pairs={{0,2},{1,3},{4,0},{5,1},{8,4},{9,5},{12,8},{13,9},{14,12},{15,13},... | collective-permute-start | bytes 626696 | tf_op jit(solution)/shard_map/ppermute | solution.py:423
  62.3 17.8 %collective-permute-start.23 = (bf16[2,240,768]{2,1,0:T(8,128)(2,1)S(1)}, bf16[2,240,768]{2,1,0:T(8,128)(2,1)S(1)}, u32[]{:S(2)}, u32[]{:S(2)}) collective-permute-start(bf16[2,240,768]{2,1,0:T(8,128)(2,1)S(1)} %get-tuple-element.92), channel_id=1, source_target_pairs={{0,16},{16,0},{1,17},{17,1},{2,18},{18,2},{3,19},{19,3},{4,20},{20... | collective-permute-start | bytes 2211848 | tf_op jit(solution)/shard_map/ppermute | solution.py:420
  71.4 6.3 %collective-permute-start.19 = (bf16[1,48,2176]{2,1,0:T(8,128)(2,1)S(1)}, bf16[1,48,2176]{2,1,0:T(8,128)(2,1)S(1)}, u32[]{:S(2)}, u32[]{:S(2)}) collective-permute-start(bf16[1,48,2176]{2,1,0:T(8,128)(2,1)S(1)} %bitcast.42), channel_id=1, source_target_pairs={{0,4},{1,5},{4,8},{5,9},{8,12},{9,13},{12,14},{13,15},{14,10},{15,... | collective-permute-start | bytes 626696 | tf_op jit(solution)/shard_map/ppermute | solution.py:423
  71.9 5.9 %collective-permute-start.20 = (bf16[1,48,2176]{2,1,0:T(8,128)(2,1)S(1)}, bf16[1,48,2176]{2,1,0:T(8,128)(2,1)S(1)}, u32[]{:S(2)}, u32[]{:S(2)}) collective-permute-start(bf16[1,48,2176]{2,1,0:T(8,128)(2,1)S(1)} %bitcast.41), channel_id=1, source_target_pairs={{0,2},{1,3},{4,0},{5,1},{8,4},{9,5},{12,8},{13,9},{14,12},{15,13},... | collective-permute-start | bytes 626696 | tf_op jit(solution)/shard_map/ppermute | solution.py:423
  78.0 9.7 %collective-permute-start.21 = (bf16[2,48,2176]{2,1,0:T(8,128)(2,1)S(1)}, bf16[2,48,2176]{2,1,0:T(8,128)(2,1)S(1)}, u32[]{:S(2)}, u32[]{:S(2)}) collective-permute-start(bf16[2,48,2176]{2,1,0:T(8,128)(2,1)S(1)} %get-tuple-element.87), channel_id=1, source_target_pairs={{0,4},{1,5},{4,8},{5,9},{8,12},{9,13},{12,14},{13,15},{14,10},{15,... | collective-permute-start | bytes 1253384 | tf_op jit(solution)/shard_map/ppermute | solution.py:423
  78.5 9.3 %collective-permute-start.22 = (bf16[2,48,2176]{2,1,0:T(8,128)(2,1)S(1)}, bf16[2,48,2176]{2,1,0:T(8,128)(2,1)S(1)}, u32[]{:S(2)}, u32[]{:S(2)}) collective-permute-start(bf16[2,48,2176]{2,1,0:T(8,128)(2,1)S(1)} %get-tuple-element.90), channel_id=1, source_target_pairs={{0,2},{1,3},{4,0},{5,1},{8,4},{9,5},{12,8},{13,9},{14,12},{15,13},... | collective-permute-start | bytes 1253384 | tf_op jit(solution)/shard_map/ppermute | solution.py:423
  87.8 27.5 %collective-permute-start.27 = (bf16[768,2048]{1,0:T(8,128)(2,1)S(1)}, bf16[768,2048]{1,0:T(8,128)(2,1)S(1)}, u32[]{:S(2)}, u32[]{:S(2)}) collective-permute-start(bf16[768,2048]{1,0:T(8,128)(2,1)S(1)} %weight_product.2), channel_id=1, source_target_pairs={{0,1},{1,0},{2,3},{3,2},{4,5},{5,4},{6,7},{7,6},{8,9},{9,8},{10,11... | collective-permute-start | bytes 9437192 | tf_op jit(solution)/shard_map/ppermute | solution.py:426
  87.8 12.6 %collective-permute-start.24 = (bf16[2,144,768]{2,1,0:T(8,128)(2,1)S(1)}, bf16[2,144,768]{2,1,0:T(8,128)(2,1)S(1)}, u32[]{:S(2)}, u32[]{:S(2)}) collective-permute-start(bf16[2,144,768]{2,1,0:T(8,128)(2,1)S(1)} %get-tuple-element.98), channel_id=1, source_target_pairs={{0,16},{16,0},{1,17},{17,1},{2,18},{18,2},{3,19},{19,3},{4,20},{20... | collective-permute-start | bytes 1327112 | tf_op jit(solution)/shard_map/ppermute | solution.py:420
  100.4 11.3 %collective-permute-start.26 = (bf16[2,48,2176]{2,1,0:T(8,128)(2,1)S(1)}, bf16[2,48,2176]{2,1,0:T(8,128)(2,1)S(1)}, u32[]{:S(2)}, u32[]{:S(2)}) collective-permute-start(bf16[2,48,2176]{2,1,0:T(8,128)(2,1)S(1)} %get-tuple-element.101), channel_id=1, source_target_pairs={{0,2},{1,3},{4,0},{5,1},{8,4},{9,5},{12,8},{13,9},{14,12},{15,13},... | collective-permute-start | bytes 1253384 | tf_op jit(solution)/shard_map/ppermute | solution.py:423
  101.9 11.0 %collective-permute-start.25 = (bf16[2,48,2176]{2,1,0:T(8,128)(2,1)S(1)}, bf16[2,48,2176]{2,1,0:T(8,128)(2,1)S(1)}, u32[]{:S(2)}, u32[]{:S(2)}) collective-permute-start(bf16[2,48,2176]{2,1,0:T(8,128)(2,1)S(1)} %get-tuple-element.99), channel_id=1, source_target_pairs={{0,4},{1,5},{4,8},{5,9},{8,12},{9,13},{12,14},{13,15},{14,10},{15,... | collective-permute-start | bytes 1253384 | tf_op jit(solution)/shard_map/ppermute | solution.py:423
  103.7 21.7 %collective-permute-start.31 = (bf16[576,768]{1,0:T(8,128)(2,1)S(1)}, bf16[576,768]{1,0:T(8,128)(2,1)}, u32[]{:S(2)}, u32[]{:S(2)}) collective-permute-start(bf16[576,768]{1,0:T(8,128)(2,1)S(1)} %get-tuple-element.125), channel_id=1, source_target_pairs={{0,1},{1,0},{2,3},{3,2},{4,5},{5,4},{6,7},{7,6},{8,9},{9,8},{10,11... | collective-permute-start | bytes 2654216 | tf_op jit(solution)/shard_map/ppermute | solution.py:426
  113.1 10.1 %collective-permute-start.29 = (bf16[2,48,2176]{2,1,0:T(8,128)(2,1)S(1)}, bf16[2,48,2176]{2,1,0:T(8,128)(2,1)S(1)}, u32[]{:S(2)}, u32[]{:S(2)}) collective-permute-start(bf16[2,48,2176]{2,1,0:T(8,128)(2,1)S(1)} %get-tuple-element.120), channel_id=1, source_target_pairs={{0,2},{1,3},{4,0},{5,1},{8,4},{9,5},{12,8},{13,9},{14,12},{15,13},... | collective-permute-start | bytes 1253384 | tf_op jit(solution)/shard_map/ppermute | solution.py:423
  114.8 10.6 %copy-start.2 = (s32[48,8]{0,1:T(8,128)S(1)}, s32[48,8]{0,1:T(8,128)}, u32[]{:S(2)}) copy-start(s32[48,8]{0,1:T(8,128)} %param.6) | copy-start | bytes 4612
  114.8 9.8 %collective-permute-start.28 = (bf16[2,48,2176]{2,1,0:T(8,128)(2,1)S(1)}, bf16[2,48,2176]{2,1,0:T(8,128)(2,1)S(1)}, u32[]{:S(2)}, u32[]{:S(2)}) collective-permute-start(bf16[2,48,2176]{2,1,0:T(8,128)(2,1)S(1)} %get-tuple-element.118), channel_id=1, source_target_pairs={{0,4},{1,5},{4,8},{5,9},{8,12},{9,13},{12,14},{13,15},{14,10},{15,... | collective-permute-start | bytes 1253384 | tf_op jit(solution)/shard_map/ppermute | solution.py:423
  124.7 5.9 %collective-permute-start.30 = (bf16[48,2176]{1,0:T(8,128)(2,1)S(1)}, bf16[48,2176]{1,0:T(8,128)(2,1)S(1)}, u32[]{:S(2)}, u32[]{:S(2)}) collective-permute-start(bf16[48,2176]{1,0:T(8,128)(2,1)S(1)} %get-tuple-element.122), channel_id=1, source_target_pairs={{0,16},{16,0},{1,17},{17,1},{2,18},{18,2},{3,19},{19,3},{4,20},{20... | collective-permute-start | bytes 626696 | tf_op jit(solution)/shard_map/ppermute | solution.py:420

commit v10 on v8

--- a/solution.py
+++ b/solution.py
@@ -40,7 +40,16 @@
     return [at.index(place) for place in walk]
 
 
-def pack_kernel(top, where, ids, probs, grads, *outs):
+def pack_kernel(top, n_out, where, ids_in, probs_in, grads_in, *refs):
+    outs, (ids, probs, grads, sems) = refs[:n_out], refs[n_out:]
+    copies = [
+        pltpu.make_async_copy(source, target, sems.at[i])
+        for i, (source, target) in enumerate([(ids_in, ids), (probs_in, probs), (grads_in, grads)])
+    ]
+    for copy in copies:
+        copy.start()
+    for copy in copies:
+        copy.wait()
     tok = grads.shape[0]
     width = grads.shape[1] // len(outs)
     room = outs[0].shape[1] - width
@@ -75,13 +84,42 @@
     width = grads.shape[1] // n_dp
     vmem = pl.BlockSpec(memory_space=pltpu.VMEM)
     return pl.pallas_call(
-        functools.partial(pack_kernel, top),
-        in_specs=[pl.BlockSpec(memory_space=pltpu.SMEM)] + [vmem] * 3,
+        functools.partial(pack_kernel, top, n_dp),
+        in_specs=[pl.BlockSpec(memory_space=pltpu.SMEM)] + [pl.BlockSpec(memory_space=pl.ANY)] * 3,
         out_specs=[vmem] * n_dp,
         out_shape=[jax.ShapeDtypeStruct((tok, width + room), jnp.bfloat16)] * n_dp,
+        scratch_shapes=[
+            pltpu.VMEM(ids.shape, ids.dtype),
+            pltpu.VMEM(probs.shape, probs.dtype),
+            pltpu.VMEM(grads.shape, grads.dtype),
+            pltpu.SemaphoreType.DMA((3,)),
+        ],
         compiler_params=kernel_memory(tok),
         name="pack",
     )(where, ids, probs, grads)
+
+
+def turn_kernel(value, out):
+    rows, cols = value.shape
+    step = 256
+    for i in range(rows // step):
+        for j in range(cols // step):
+            tile = value[i * step : (i + 1) * step, j * step : (j + 1) * step]
+            out[j * step : (j + 1) * step, i * step : (i + 1) * step] = tile.T
+
+
+def turn(value):
+    rows, cols = value.shape
+    vmem = pl.BlockSpec(memory_space=pltpu.VMEM)
+    return pl.pallas_call(
+        turn_kernel,
+        in_specs=[vmem],
+        out_specs=vmem,
+        out_shape=jax.ShapeDtypeStruct((cols, rows), value.dtype),
+        compiler_params=kernel_memory(rows),
+        cost_estimate=pl.CostEstimate(flops=0, bytes_accessed=4 * rows * cols, transcendentals=0),
+        name="turn",
+    )(value)
 
 
 def sum_kernel(starts, n_out, *refs):
@@ -174,8 +212,8 @@
     replicas = sorted({item[2] for item in plan})
     hid = {d: refs[at + 2 * i : at + 2 * i + 2] for i, d in enumerate(replicas)}
     at += 2 * len(replicas)
-    weights = refs[at : at + 2]
-    at += 2
+    weights, turned = refs[at : at + 2], refs[at + 2 : at + 4]
+    at += 4
     parts = refs[at : at + len(plan)]
     at += len(plan)
     outs = {d: refs[at + 2 * i : at + 2 * i + 2] for i, d in enumerate(replicas)}
@@ -238,7 +276,7 @@
         step_ff = 256
         for step in range(ff // step_ff):
             cols = slice(step * step_ff, (step + 1) * step_ff)
-            value = dot(lhs, weights[x][cols, :], 1, 1)
+            value = dot(lhs, turned[x][:, cols], 1, 0)
             inner = inner + jnp.sum(value * helds[x][:, cols], axis=1, keepdims=True)
             value = value.astype(jnp.bfloat16)
             base = 0
@@ -254,10 +292,10 @@
         out[:, width:] = extra[i * tok : (i + 1) * tok]
 
 
-def block_product(plan, meta, blocks, hiddens, w_own, w_sib, n_ex, top):
+def block_product(plan, meta, blocks, hiddens, weights, n_ex, top):
     n_dp = len(hiddens)
     _, tok, full = blocks[0].shape
-    ff, width = w_own.shape
+    ff, width = weights[0].shape
     slots = hiddens[0][0].shape[0]
     replicas = sorted({item[2] for item in plan})
     vmem = pl.BlockSpec(memory_space=pltpu.VMEM)
@@ -274,7 +312,7 @@
     chips_rows = n_ex * tok * n_dp // 2
     made = pl.pallas_call(
         functools.partial(block_kernel, plan, len(blocks), n_dp, n_ex, top),
-        in_specs=[pl.BlockSpec(memory_space=pltpu.SMEM)] + [vmem] * (len(blocks) + len(hid) + 2),
+        in_specs=[pl.BlockSpec(memory_space=pltpu.SMEM)] + [vmem] * (len(blocks) + len(hid) + 4),
         out_specs=[vmem] * len(out_shape),
         out_shape=out_shape,
         compiler_params=kernel_memory(chips_rows),
@@ -284,7 +322,7 @@
             transcendentals=0,
         ),
         name="block_product",
-    )(meta, *blocks, *hid, w_own, w_sib)
+    )(meta, *blocks, *hid, *weights)
     parts = made[: len(plan)]
     rest = made[len(plan) :]
     scaled = {d: rest[2 * i] for i, d in enumerate(replicas)}
@@ -431,6 +469,7 @@
         blocks = {0: jnp.stack([packed[0]] + [shift(packed[d], d) for d in range(1, n_dp)])}
 
         sibling_weight = swap(weight)
+        weights = [weight, sibling_weight, turn(weight), turn(sibling_weight)]
         hidden = expert_hidden[0, 0].transpose(1, 0, 2).reshape(slots, ff)
         hiddens = [(hidden, swap(hidden))]
         for d in range(1, n_dp):
@@ -454,7 +493,7 @@
             else:
                 gated = used
             made, scaled, back, fact = block_product(
-                tuple(plan), meta, gated, hiddens, weight, sibling_weight, n_ex, top
+                tuple(plan), meta, gated, hiddens, weights, n_ex, top
             )
             for item, part in zip(items, made):
                 parts[item] = part
@@ -473,10 +512,10 @@
             return made[0]
 
         both = lambda offs: [(off, d) for d in range(n_dp) for off in offs]
-        gate = ()
+        gate = tuple(weights[2:])
         for step in range(1, half):
             sent = blocks[1 - step], blocks[step - 1]
-            if gate:
+            if step > 1:
                 sent = after(sent[0], *gate), after(sent[1], *gate)
             blocks[-step] = ring_send(sent[0], 1)
             blocks[step] = ring_send(sent[1], -1)
@@ -509,12 +548,8 @@
                 values.append(jnp.stack([parts[half, d] for d in every[per:]]))
             else:
                 first, last = ((0, per), (per, n_dp)) if hop == half - 1 else ((0, n_dp), (0, n_dp))
-                values = sums(
-                    [
-                        ([parts[hop, d] for d in every], carry[1], *first),
-                        ([parts[-hop, d] for d in every], carry[-1], *last),
-                    ]
-                )
+                values = sums([([parts[hop, d] for d in every], carry[1], *first)])
+                values += sums([([parts[-hop, d] for d in every], carry[-1], *last)])
             values = [after(value, *done) for value in values]
             carry[1] = ring_send(values[0], 1)
             carry[-1] = ring_send(values[1], -1)
@@ -525,7 +560,7 @@
         hop_on(half)
         second = hop_on(half - 1)
         other = weight_product(
-            [after(refs[0], *sending, *[value for sent in sent_back for value in sent[:-1]])] + refs[1:], layout, scaleds, 1, jnp.bfloat16, width
+            [after(refs[0], *sending, *[value for sent in sent_back for value in sent])] + refs[1:], layout, scaleds, 1, jnp.bfloat16, width
         )
         swapped = swap(after(other, *second))
         third = hop_on(half - 2, other)

time: 117 us -> 120 us (1.026)
  waiting for transfers between devices: 37.4 us -> 28.7 us
  local copies, waits for them, and re-layouts: 8.66 us -> 15 us
  Pallas kernels: 41.9 us -> 47 us
    ppermute x16, waiting for transfers between devices: 23.5 us -> 15 us  [ring_send(): return lax.ppermute(value, 'expert', forward if step > 0 else backward)]
    unnamed x24 -> x30, local copies, waits for them, and re-layouts: 7.93 us -> 14.3 us
    pallas_call x1 -> x3, Pallas kernels: 0.25 us -> 4.22 us  [the longest x2 3.75 us: turn(): pl.pallas_call(turn_kernel, in_specs=[vmem], out_specs=vmem, out_shape=ja...]
  transfers between devices with their start and end apart: 27 -> 27, of which waited for: 15 -> 10; matrix products, arithmetic and copies ran while one was open for 2% -> 2% of each run, Pallas kernels for 35% -> 38%
where the time goes in v10:
time: 120 us
  Pallas kernels  47 us (39%)
  waiting for transfers between devices  28.7 us (24%)
  starting transfers between devices  27 us (22%)
  local copies, waits for them, and re-layouts  15 us (12%)
    pallas_call x4, Pallas kernels, block_product(): pl.pallas_call(functools.partial(block_kernel, plan, len(blocks), n_dp, n...  27.4 us
    ppermute x16, starting transfers between devices, ring_send(): return lax.ppermute(value, 'expert', forward if step > 0 else backward)  16.9 us
    ppermute x16, waiting for transfers between devices, ring_send(): return lax.ppermute(value, 'expert', forward if step > 0 else backward)  15 us
    unnamed x30, local copies, waits for them, and re-layouts  14.3 us
    ppermute x6, waiting for transfers between devices, shift(): lax.ppermute(value, 'dp', [(i, (i + step) % n_dp) for i in range(n_dp)])  13.2 us
    pallas_call x2, Pallas kernels, weight_product(): pl.pallas_call(functools.partial(weight_kernel, len(blocks), len(scaleds)...  12 us
    ppermute x6, starting transfers between devices, shift(): lax.ppermute(value, 'dp', [(i, (i + step) % n_dp) for i in range(n_dp)])  9.11 us
    pallas_call x2, Pallas kernels, turn(): pl.pallas_call(turn_kernel, in_specs=[vmem], out_specs=vmem, out_shape=ja...  3.75 us
  transfers between devices with their start and end apart: 27, of which 10 were waited for; matrix products, arithmetic and copies ran while one was open for 2% of the time, Pallas kernels for 38%

profile of v10, /device:TPU:0, one launch (start us, length us, event | category | flops | bytes accessed | tf_op | source)
XLA Modules:
  0.0 119.8 jit_solution(3231441185375977254)
XLA Ops:
  0.6 0.5 collective-permute-start.4
  1.2 1.0 copy-done.10
  2.1 0.7 copy-done.11
  2.8 0.7 copy-done.13
  3.5 0.5 pack.1
  4.0 2.6 %collective-permute-start = (bf16[48,2176]{1,0:T(8,128)(2,1)S(1)}, bf16[48,2176]{1,0:T(8,128)(2,1)S(1)}, u32[]{:S(2)}, u32[]{:S(2)}) collective-permute-start(bf16[48,2176]{1,0:T(8,128)(2,1)S(1)} %get-tuple-element.69), channel_id=1, source_target_pairs={{0,16},{16,0},{1,17},{17,1},{2,18},{18,2},{3,19},{19,3},{4,20},{20... | collective-permute-start | bytes 626696 | tf_op jit(solution)/shard_map/ppermute | solution.py:458
  6.6 0.2 collective-permute-start.3
  6.8 5.6 %collective-permute-done = bf16[48,2176]{1,0:T(8,128)(2,1)S(1)} collective-permute-done((bf16[48,2176]{1,0:T(8,128)(2,1)S(1)}, bf16[48,2176]{1,0:T(8,128)(2,1)S(1)}, u32[]{:S(2)}, u32[]{:S(2)}) %collective-permute-start) | collective-permute-done | bytes 208928 | tf_op jit(solution)/shard_map/ppermute | solution.py:458
  12.5 1.8 %collective-permute-start.7 = (bf16[576,768]{1,0:T(8,128)(2,1)}, bf16[576,768]{1,0:T(8,128)(2,1)}, u32[]{:S(2)}, u32[]{:S(2)}) collective-permute-start(bf16[576,768]{1,0:T(8,128)(2,1)} %bitcast.28), channel_id=1, source_target_pairs={{0,16},{16,0},{1,17},{17,1},{2,18},{18,2},{3,19},{19,3},{4,20},{20... | collective-permute-start | bytes 2654216 | tf_op jit(solution)/shard_map/ppermute | solution.py:458
  14.3 1.6 %collective-permute-start.1 = (bf16[2,48,2176]{2,1,0:T(8,128)(2,1)S(1)}, bf16[2,48,2176]{2,1,0:T(8,128)(2,1)}, u32[]{:S(2)}, u32[]{:S(2)}) collective-permute-start(bf16[2,48,2176]{2,1,0:T(8,128)(2,1)S(1)} %pad_maximum_fusion.refs_1_.refs_3_.refs_0_), channel_id=1, source_target_pairs={{0,4},{1,5},{4,8},{5,9},{8,12},{9,13},{12,14},{13,15},{14,10},{15,... | collective-permute-start | bytes 1253384 | tf_op jit(solution)/shard_map/ppermute | solution.py:461
  15.8 0.4 collective-permute-start.2
  16.3 1.9 %copy-done = bf16[1,768,2048]{2,1,0:T(8,128)(2,1)S(1)} copy-done((bf16[1,768,2048]{2,1,0:T(8,128)(2,1)S(1)}, bf16[1,768,2048]{2,1,0:T(8,128)(2,1)}, u32[]{:S(2)}) %copy-start) | copy-done | bytes 3145752
  18.2 0.9 turn.2.refs_8_.refs_12_.refs_9_
  19.1 1.7 %copy-done.2 = bf16[2048,768]{1,0:T(8,128)(2,1)} copy-done((bf16[2048,768]{1,0:T(8,128)(2,1)}, bf16[2048,768]{1,0:T(8,128)(2,1)S(1)}, u32[]{:S(2)}) %copy-start.2) | copy-done | bytes 3145752
  20.7 2.9 %turn.3.refs_9_.refs_13_.refs_10_ = bf16[2048,768]{1,0:T(8,128)(2,1)S(1)} custom-call(bf16[768,2048]{1,0:T(8,128)(2,1)} %collective-permute-done.4.value.refs_7_.refs_11_.refs_8_), custom_call_target="tpu_custom_call" | custom-call | bytes 6291456 | tf_op jit(solution)/shard_map/turn/pallas_call | solution.py:114
  23.6 1.7 %copy-done.4 = bf16[2048,768]{1,0:T(8,128)(2,1)} copy-done((bf16[2048,768]{1,0:T(8,128)(2,1)}, bf16[2048,768]{1,0:T(8,128)(2,1)S(1)}, u32[]{:S(2)}) %copy-start.4) | copy-done | bytes 3145752
  25.3 1.6 %collective-permute-start.5 = (bf16[2,48,2176]{2,1,0:T(8,128)(2,1)}, bf16[2,48,2176]{2,1,0:T(8,128)(2,1)}, u32[]{:S(2)}, u32[]{:S(2)}) collective-permute-start(bf16[2,48,2176]{2,1,0:T(8,128)(2,1)} %collective-permute-done.1.refs_2_.refs_4_.refs_1_), channel_id=1, source_target_pairs={{0,4},{1,5},{4,8},{5,9},{8,12},{9,13},{12,14},{13,15},{14,10},{15,... | collective-permute-start | bytes 1253384 | tf_op jit(solution)/shard_map/ppermute | solution.py:461
  26.9 0.5 collective-permute-start.6
  27.4 0.7 dynamic-slice_bitcast_fusion.refs_0_
  28.1 1.9 %copy-done.3 = bf16[2048,768]{1,0:T(8,128)(2,1)S(1)} copy-done((bf16[2048,768]{1,0:T(8,128)(2,1)S(1)}, bf16[2048,768]{1,0:T(8,128)(2,1)}, u32[]{:S(2)}) %copy-start.3) | copy-done | bytes 3145752
  30.0 1.9 %copy-done.5 = bf16[2048,768]{1,0:T(8,128)(2,1)S(1)} copy-done((bf16[2048,768]{1,0:T(8,128)(2,1)S(1)}, bf16[2048,768]{1,0:T(8,128)(2,1)}, u32[]{:S(2)}) %copy-start.5) | copy-done | bytes 3145752
  31.8 1.2 copy-done.6
  33.0 1.0 copy-done.9
  34.0 5.5 %block_product.4 = (bf16[48,2176]{1,0:T(8,128)(2,1)S(1)}, bf16[48,2176]{1,0:T(8,128)(2,1)S(1)}, bf16[48,2176]{1,0:T(8,128)(2,1)S(1)}, bf16[2,144,768]{2,1,0:T(8,...) custom-call(s32[10]{0:T(128)S(1)} %dynamic-slice_bitcast_fusion.refs_0_, ...), custom_call_target="tpu_custom_call" | custom-call | flops 1811939328 | bytes 7987200 | tf_op jit(solution)/shard_map/block_product/pallas_call | solution.py:313
  39.6 1.6 %collective-permute-start.10 = (bf16[2,48,2176]{2,1,0:T(8,128)(2,1)}, bf16[2,48,2176]{2,1,0:T(8,128)(2,1)S(1)}, u32[]{:S(2)}, u32[]{:S(2)}) collective-permute-start(bf16[2,48,2176]{2,1,0:T(8,128)(2,1)} %collective-permute-done.6.refs_2_.refs_4_), channel_id=1, source_target_pairs={{0,2},{1,3},{4,0},{5,1},{8,4},{9,5},{12,8},{13,9},{14,12},{15,13},... | collective-permute-start | bytes 1253384 | tf_op jit(solution)/shard_map/ppermute | solution.py:461
  41.2 0.5 collective-permute-start.9
  41.7 0.5 collective-permute-done.8.refs_9_.refs_6_
  42.3 9.3 %block_product.5 = (bf16[48,2176]{1,0:T(8,128)(2,1)S(1)}, bf16[48,2176]{1,0:T(8,128)(2,1)S(1)}, bf16[48,2176]{1,0:T(8,128)(2,1)S(1)}, bf16[48,2176]{1,0:T(8,128)...) custom-call(s32[10]{0:T(128)S(1)} %dynamic-slice_bitcast_fusion.refs, ...), custom_call_target="tpu_custom_call" | custom-call | flops 4227858432 | bytes 10248192 | tf_op jit(solution)/shard_map/block_product/pallas_call | solution.py:313
  51.6 0.3 collective-permute-done.10.refs_2_.refs_6_
  51.9 1.6 %collective-permute-start.12 = (bf16[1,48,2176]{2,1,0:T(8,128)(2,1)S(1)}, bf16[1,48,2176]{2,1,0:T(8,128)(2,1)S(1)}, u32[]{:S(2)}, u32[]{:S(2)}) collective-permute-start(bf16[1,48,2176]{2,1,0:T(8,128)(2,1)S(1)} %slice.7), channel_id=1, source_target_pairs={{0,2},{1,3},{4,0},{5,1},{8,4},{9,5},{12,8},{13,9},{14,12},{15,13},... | collective-permute-start | bytes 626696 | tf_op jit(solution)/shard_map/ppermute | solution.py:461
  53.5 0.7 collective-permute-start.11
  54.3 0.5 collective-permute-start.16
  54.8 6.6 %block_product.6 = (bf16[48,2176]{1,0:T(8,128)(2,1)S(1)}, bf16[48,2176]{1,0:T(8,128)(2,1)S(1)}, bf16[48,2176]{1,0:T(8,128)(2,1)S(1)}, bf16[48,2176]{1,0:T(8,128)...) custom-call(s32[10]{0:T(128)S(1)} %dynamic-slice_bitcast_fusion.refs, ...), custom_call_target="tpu_custom_call" | custom-call | flops 2415919104 | bytes 8552448 | tf_op jit(solution)/shard_map/block_product/pallas_call | solution.py:313
  61.4 6.0 %block_product.7 = (bf16[48,2176]{1,0:T(8,128)(2,1)S(1)}, bf16[48,2176]{1,0:T(8,128)(2,1)S(1)}, bf16[2,48,768]{2,1,0:T(8,128)(2,1)S(1)}, bf16[2,48,768]{2,1,0:T(...) custom-call(s32[10]{0:T(128)S(1)} %dynamic-slice_bitcast_fusion.refs, ...), custom_call_target="tpu_custom_call" | custom-call | flops 1207959552 | bytes 7421952 | tf_op jit(solution)/shard_map/block_product/pallas_call | solution.py:313
  67.4 1.6 %collective-permute-start.15 = (bf16[1,48,2176]{2,1,0:T(8,128)(2,1)S(1)}, bf16[1,48,2176]{2,1,0:T(8,128)(2,1)S(1)}, u32[]{:S(2)}, u32[]{:S(2)}) collective-permute-start(bf16[1,48,2176]{2,1,0:T(8,128)(2,1)S(1)} %bitcast.37), channel_id=1, source_target_pairs={{0,2},{1,3},{4,0},{5,1},{8,4},{9,5},{12,8},{13,9},{14,12},{15,13},... | collective-permute-start | bytes 626696 | tf_op jit(solution)/shard_map/ppermute | solution.py:461
  69.1 0.4 collective-permute-start.13
  69.5 1.5 %collective-permute-start.17 = (bf16[2,96,768]{2,1,0:T(8,128)(2,1)S(1)}, bf16[2,96,768]{2,1,0:T(8,128)(2,1)S(1)}, u32[]{:S(2)}, u32[]{:S(2)}) collective-permute-start(bf16[2,96,768]{2,1,0:T(8,128)(2,1)S(1)} %get-tuple-element.90), channel_id=1, source_target_pairs={{0,16},{16,0},{1,17},{17,1},{2,18},{18,2},{3,19},{19,3},{4,20},{20... | collective-permute-start | bytes 884744 | tf_op jit(solution)/shard_map/ppermute | solution.py:458
  71.1 2.5 %collective-permute-done.15.refs_2_ = bf16[1,48,2176]{2,1,0:T(8,128)(2,1)S(1)} collective-permute-done((bf16[1,48,2176]{2,1,0:T(8,128)(2,1)S(1)}, bf16[1,48,2176]{2,1,0:T(8,128)(2,1)S(1)}, u32[]{:S(2)}, u32[]{:S(2)}) %collective-permute-start.15) | collective-permute-done | bytes 208928 | tf_op jit(solution)/shard_map/ppermute | solution.py:461
  73.6 1.6 %collective-permute-start.20 = (bf16[2,48,2176]{2,1,0:T(8,128)(2,1)S(1)}, bf16[2,48,2176]{2,1,0:T(8,128)(2,1)S(1)}, u32[]{:S(2)}, u32[]{:S(2)}) collective-permute-start(bf16[2,48,2176]{2,1,0:T(8,128)(2,1)S(1)} %sums.8), channel_id=1, source_target_pairs={{0,2},{1,3},{4,0},{5,1},{8,4},{9,5},{12,8},{13,9},{14,12},{15,13},... | collective-permute-start | bytes 1253384 | tf_op jit(solution)/shard_map/ppermute | solution.py:461
  75.3 0.5 collective-permute-start.14
  75.8 1.5 %collective-permute-start.18 = (bf16[2,48,768]{2,1,0:T(8,128)(2,1)S(1)}, bf16[2,48,768]{2,1,0:T(8,128)(2,1)S(1)}, u32[]{:S(2)}, u32[]{:S(2)}) collective-permute-start(bf16[2,48,768]{2,1,0:T(8,128)(2,1)S(1)} %get-tuple-element.91), channel_id=1, source_target_pairs={{0,16},{16,0},{1,17},{17,1},{2,18},{18,2},{3,19},{19,3},{4,20},{20... | collective-permute-start | bytes 442376 | tf_op jit(solution)/shard_map/ppermute | solution.py:458
  77.3 2.2 %collective-permute-done.17.refs_13_ = bf16[2,96,768]{2,1,0:T(8,128)(2,1)S(1)} collective-permute-done((bf16[2,96,768]{2,1,0:T(8,128)(2,1)S(1)}, bf16[2,96,768]{2,1,0:T(8,128)(2,1)S(1)}, u32[]{:S(2)}, u32[]{:S(2)}) %collective-permute-start.17) | collective-permute-done | bytes 294944 | tf_op jit(solution)/shard_map/ppermute | solution.py:458
  79.5 1.8 %collective-permute-done.18.refs_14_ = bf16[2,48,768]{2,1,0:T(8,128)(2,1)S(1)} collective-permute-done((bf16[2,48,768]{2,1,0:T(8,128)(2,1)S(1)}, bf16[2,48,768]{2,1,0:T(8,128)(2,1)S(1)}, u32[]{:S(2)}, u32[]{:S(2)}) %collective-permute-start.18) | collective-permute-done | bytes 147488 | tf_op jit(solution)/shard_map/ppermute | solution.py:458
  81.4 5.3 %weight_product.2 = bf16[768,2048]{1,0:T(8,128)(2,1)S(1)} custom-call(bf16[2,48,2176]{2,1,0:T(8,128)(2,1)S(1)} %copy-done.9, bf16[2,48,2176]{2,1,0:T(8,128)(2,1)} %collective-permute-done.1.refs_2_.refs_4_.refs_1_, bf16[2,48,2176]{2,1,0:T(8,128)(2,1)} %collective-permute-done.2.refs_3_.refs_5_.refs_2_, ...), custom_call_target="tpu_custom_call" | custom-call | flops 2415919104 | bytes 10616832 | tf_op jit(solution)/shard_map/weight_product/pallas_call | solution.py:395
  86.8 0.1 sums.9
  86.9 1.6 %collective-permute-start.21 = (bf16[2,48,2176]{2,1,0:T(8,128)(2,1)S(1)}, bf16[2,48,2176]{2,1,0:T(8,128)(2,1)S(1)}, u32[]{:S(2)}, u32[]{:S(2)}) collective-permute-start(bf16[2,48,2176]{2,1,0:T(8,128)(2,1)S(1)} %sums.9), channel_id=1, source_target_pairs={{0,2},{1,3},{4,0},{5,1},{8,4},{9,5},{12,8},{13,9},{14,12},{15,13},... | collective-permute-start | bytes 1253384 | tf_op jit(solution)/shard_map/ppermute | solution.py:461
  88.5 0.1 sums.7
  88.6 0.6 collective-permute-start.19
  89.1 1.3 %spread_product.1 = (bf16[576,768]{1,0:T(8,128)(2,1)S(1)}, bf16[576,768]{1,0:T(8,128)(2,1)S(1)}) custom-call(s32[144,2]{1,0:T(8,128)S(1)} %get-tuple-element.110.refs_0_, s32[96,2]{1,0:T(8,128)S(1)} %get-tuple-element.111.refs_1_, s32[96,2]{1,0:T(8,128)S(1)} %get-tuple-element.112.refs_2_, s32[48,2]{1,0:T(8,128)S(1)} %get-tuple-element.113.refs_3_, ...), custom_call_target="tpu_custom_call" | custom-call | flops 679477248 | bytes 3538944 | tf_op jit(solution)/shard_map/spread_product/pallas_call | solution.py:360
  90.5 8.5 %collective-permute-done.21.refs_2_ = bf16[2,48,2176]{2,1,0:T(8,128)(2,1)S(1)} collective-permute-done((bf16[2,48,2176]{2,1,0:T(8,128)(2,1)S(1)}, bf16[2,48,2176]{2,1,0:T(8,128)(2,1)S(1)}, u32[]{:S(2)}, u32[]{:S(2)}) %collective-permute-start.21) | collective-permute-done | bytes 417824 | tf_op jit(solution)/shard_map/ppermute | solution.py:461
  99.0 0.1 sums.11
  99.1 1.6 %collective-permute-start.24 = (bf16[2,48,2176]{2,1,0:T(8,128)(2,1)S(1)}, bf16[2,48,2176]{2,1,0:T(8,128)(2,1)S(1)}, u32[]{:S(2)}, u32[]{:S(2)}) collective-permute-start(bf16[2,48,2176]{2,1,0:T(8,128)(2,1)S(1)} %sums.11), channel_id=1, source_target_pairs={{0,2},{1,3},{4,0},{5,1},{8,4},{9,5},{12,8},{13,9},{14,12},{15,13},... | collective-permute-start | bytes 1253384 | tf_op jit(solution)/shard_map/ppermute | solution.py:461
  100.7 0.1 sums.10
  100.8 0.6 collective-permute-start.23
  101.3 6.8 %weight_product.3 = f32[768,2048]{1,0:T(8,128)} custom-call(bf16[2,48,2176]{2,1,0:T(8,128)(2,1)S(1)} %copy-done.9, bf16[2,48,2176]{2,1,0:T(8,128)(2,1)} %collective-permute-done.1.refs_2_.refs_4_.refs_1_, bf16[2,48,2176]{2,1,0:T(8,128)(2,1)} %collective-permute-done.2.refs_3_.refs_5_.refs_2_, bf16[2,48,2176]{2,1,0:T(8,128)(2,1)} %collective-permute-done.5.refs_1_.refs_3_, ...), custom_call_target="tpu_custom_call" | custom-call | flops 2415919104 | bytes 10616832 | tf_op jit(solution)/shard_map/weight_product/pallas_call | solution.py:395
  108.1 2.3 %collective-permute-done.24.refs_3_ = bf16[2,48,2176]{2,1,0:T(8,128)(2,1)S(1)} collective-permute-done((bf16[2,48,2176]{2,1,0:T(8,128)(2,1)S(1)}, bf16[2,48,2176]{2,1,0:T(8,128)(2,1)S(1)}, u32[]{:S(2)}, u32[]{:S(2)}) %collective-permute-start.24) | collective-permute-done | bytes 417824 | tf_op jit(solution)/shard_map/ppermute | solution.py:461
  110.4 1.4 %collective-permute-done.23.refs_2_ = bf16[2,48,2176]{2,1,0:T(8,128)(2,1)S(1)} collective-permute-done((bf16[2,48,2176]{2,1,0:T(8,128)(2,1)S(1)}, bf16[2,48,2176]{2,1,0:T(8,128)(2,1)S(1)}, u32[]{:S(2)}, u32[]{:S(2)}) %collective-permute-start.23) | collective-permute-done | bytes 417824 | tf_op jit(solution)/shard_map/ppermute | solution.py:461
  111.8 0.2 close.1
  112.0 1.1 collective-permute-start.25
  113.1 0.1 copy.10.ids
  113.2 1.1 add.8
  114.3 3.5 %collective-permute-done.25.refs_1_ = bf16[48,2176]{1,0:T(8,128)(2,1)S(1)} collective-permute-done((bf16[48,2176]{1,0:T(8,128)(2,1)S(1)}, bf16[48,2176]{1,0:T(8,128)(2,1)S(1)}, u32[]{:S(2)}, u32[]{:S(2)}) %collective-permute-start.25) | collective-permute-done | bytes 208928 | tf_op jit(solution)/shard_map/ppermute | solution.py:458
  117.8 1.3 %home.1 = (bf16[48,4096]{1,0:T(8,128)(2,1)}, f32[48,8]{1,0:T(8,128)S(1)}) custom-call(s32[1]{0:T(128)} %bitcast.where, s32[48,8]{1,0:T(8,128)S(1)} %copy.10.ids, bf16[48,2176]{1,0:T(8,128)(2,1)S(1)} %get-tuple-element.127.refs_0_, bf16[48,2176]{1,0:T(8,128)(2,1)S(1)} %collective-permute-done.25.refs_1_), custom_call_target="tpu_custom_call" | custom-call | tf_op jit(solution)/shard_map/home/pallas_call | solution.py:195
  119.1 0.7 copy.11
  (43 shorter events, 0.5 us)
Async XLA Ops:
  0.6 20.1 %collective-permute-start.4 = (bf16[768,2048]{1,0:T(8,128)(2,1)}, bf16[768,2048]{1,0:T(8,128)(2,1)}, u32[]{:S(2)}, u32[]{:S(2)}) collective-permute-start(bf16[768,2048]{1,0:T(8,128)(2,1)} %bitcast.21), channel_id=1, source_target_pairs={{0,1},{1,0},{2,3},{3,2},{4,5},{5,4},{6,7},{7,6},{8,9},{9,8},{10,11... | collective-permute-start | bytes 9437192 | tf_op jit(solution)/shard_map/ppermute | solution.py:464
  1.1 1.0 copy-start.10
  2.1 0.7 copy-start.11
  2.8 0.7 copy-start.13
  4.0 8.4 %collective-permute-start = (bf16[48,2176]{1,0:T(8,128)(2,1)S(1)}, bf16[48,2176]{1,0:T(8,128)(2,1)S(1)}, u32[]{:S(2)}, u32[]{:S(2)}) collective-permute-start(bf16[48,2176]{1,0:T(8,128)(2,1)S(1)} %get-tuple-element.69), channel_id=1, source_target_pairs={{0,16},{16,0},{1,17},{17,1},{2,18},{18,2},{3,19},{19,3},{4,20},{20... | collective-permute-start | bytes 626696 | tf_op jit(solution)/shard_map/ppermute | solution.py:458
  6.6 21.5 %collective-permute-start.3 = (bf16[576,768]{1,0:T(8,128)(2,1)}, bf16[576,768]{1,0:T(8,128)(2,1)}, u32[]{:S(2)}, u32[]{:S(2)}) collective-permute-start(bf16[576,768]{1,0:T(8,128)(2,1)} %bitcast.27), channel_id=1, source_target_pairs={{0,1},{1,0},{2,3},{3,2},{4,5},{5,4},{6,7},{7,6},{8,9},{9,8},{10,11... | collective-permute-start | bytes 2654216 | tf_op jit(solution)/shard_map/ppermute | solution.py:464
  12.4 11.2 %copy-start.8 = (bf16[2,48,2176]{2,1,0:T(8,128)(2,1)}, bf16[2,48,2176]{2,1,0:T(8,128)(2,1)S(1)}, u32[]{:S(2)}) copy-start(bf16[2,48,2176]{2,1,0:T(8,128)(2,1)S(1)} %pad_maximum_fusion.refs_1_.refs_3_.refs_0_) | copy-start | bytes 1253380
  12.5 27.1 %collective-permute-start.7 = (bf16[576,768]{1,0:T(8,128)(2,1)}, bf16[576,768]{1,0:T(8,128)(2,1)}, u32[]{:S(2)}, u32[]{:S(2)}) collective-permute-start(bf16[576,768]{1,0:T(8,128)(2,1)} %bitcast.28), channel_id=1, source_target_pairs={{0,16},{16,0},{1,17},{17,1},{2,18},{18,2},{3,19},{19,3},{4,20},{20... | collective-permute-start | bytes 2654216 | tf_op jit(solution)/shard_map/ppermute | solution.py:458
  14.3 11.1 %collective-permute-start.1 = (bf16[2,48,2176]{2,1,0:T(8,128)(2,1)S(1)}, bf16[2,48,2176]{2,1,0:T(8,128)(2,1)}, u32[]{:S(2)}, u32[]{:S(2)}) collective-permute-start(bf16[2,48,2176]{2,1,0:T(8,128)(2,1)S(1)} %pad_maximum_fusion.refs_1_.refs_3_.refs_0_), channel_id=1, source_target_pairs={{0,4},{1,5},{4,8},{5,9},{8,12},{9,13},{12,14},{13,15},{14,10},{15,... | collective-permute-start | bytes 1253384 | tf_op jit(solution)/shard_map/ppermute | solution.py:461
  15.8 11.1 %collective-permute-start.2 = (bf16[2,48,2176]{2,1,0:T(8,128)(2,1)S(1)}, bf16[2,48,2176]{2,1,0:T(8,128)(2,1)}, u32[]{:S(2)}, u32[]{:S(2)}) collective-permute-start(bf16[2,48,2176]{2,1,0:T(8,128)(2,1)S(1)} %pad_maximum_fusion.refs_1_.refs_3_.refs_0_), channel_id=1, source_target_pairs={{0,2},{1,3},{4,0},{5,1},{8,4},{9,5},{12,8},{13,9},{14,12},{15,13},... | collective-permute-start | bytes 1253384 | tf_op jit(solution)/shard_map/ppermute | solution.py:461
  16.3 1.9 %copy-start = (bf16[1,768,2048]{2,1,0:T(8,128)(2,1)S(1)}, bf16[1,768,2048]{2,1,0:T(8,128)(2,1)}, u32[]{:S(2)}) copy-start(bf16[1,768,2048]{2,1,0:T(8,128)(2,1)} %param.9) | copy-start | bytes 9437188
  19.0 1.7 %copy-start.2 = (bf16[2048,768]{1,0:T(8,128)(2,1)}, bf16[2048,768]{1,0:T(8,128)(2,1)S(1)}, u32[]{:S(2)}) copy-start(bf16[2048,768]{1,0:T(8,128)(2,1)S(1)} %turn.2.refs_8_.refs_12_.refs_9_) | copy-start | bytes 9437188
  20.7 7.4 %copy-start.1 = (bf16[1,768,2048]{2,1,0:T(8,128)(2,1)S(1)}, bf16[1,768,2048]{2,1,0:T(8,128)(2,1)}, u32[]{:S(2)}) copy-start(bf16[1,768,2048]{2,1,0:T(8,128)(2,1)} %param.9) | copy-start | bytes 9437188
  23.6 1.7 %copy-start.4 = (bf16[2048,768]{1,0:T(8,128)(2,1)}, bf16[2048,768]{1,0:T(8,128)(2,1)S(1)}, u32[]{:S(2)}) copy-start(bf16[2048,768]{1,0:T(8,128)(2,1)S(1)} %turn.3.refs_9_.refs_13_.refs_10_) | copy-start | bytes 9437188
  25.3 14.2 %collective-permute-start.5 = (bf16[2,48,2176]{2,1,0:T(8,128)(2,1)}, bf16[2,48,2176]{2,1,0:T(8,128)(2,1)}, u32[]{:S(2)}, u32[]{:S(2)}) collective-permute-start(bf16[2,48,2176]{2,1,0:T(8,128)(2,1)} %collective-permute-done.1.refs_2_.refs_4_.refs_1_), channel_id=1, source_target_pairs={{0,4},{1,5},{4,8},{5,9},{8,12},{9,13},{12,14},{13,15},{14,10},{15,... | collective-permute-start | bytes 1253384 | tf_op jit(solution)/shard_map/ppermute | solution.py:461
  26.9 12.6 %collective-permute-start.6 = (bf16[2,48,2176]{2,1,0:T(8,128)(2,1)}, bf16[2,48,2176]{2,1,0:T(8,128)(2,1)}, u32[]{:S(2)}, u32[]{:S(2)}) collective-permute-start(bf16[2,48,2176]{2,1,0:T(8,128)(2,1)} %collective-permute-done.2.refs_3_.refs_5_.refs_2_), channel_id=1, source_target_pairs={{0,2},{1,3},{4,0},{5,1},{8,4},{9,5},{12,8},{13,9},{14,12},{15,13},... | collective-permute-start | bytes 1253384 | tf_op jit(solution)/shard_map/ppermute | solution.py:461
  28.1 1.9 %copy-start.3 = (bf16[2048,768]{1,0:T(8,128)(2,1)S(1)}, bf16[2048,768]{1,0:T(8,128)(2,1)}, u32[]{:S(2)}) copy-start(bf16[2048,768]{1,0:T(8,128)(2,1)} %copy-done.2) | copy-start | bytes 9437188
  30.0 1.9 %copy-start.5 = (bf16[2048,768]{1,0:T(8,128)(2,1)S(1)}, bf16[2048,768]{1,0:T(8,128)(2,1)}, u32[]{:S(2)}) copy-start(bf16[2048,768]{1,0:T(8,128)(2,1)} %copy-done.4) | copy-start | bytes 9437188
  31.8 1.2 copy-start.6
  33.0 1.0 copy-start.9
  39.6 15.2 %copy-start.7 = (bf16[1,1,16,36,768]{4,2,3,1,0:T(8,128)(2,1)S(1)}, bf16[1,1,16,36,768]{4,2,3,1,0:T(8,128)(2,1)}, u32[]{:S(2)}) copy-start(bf16[1,1,16,36,768]{4,2,3,1,0:T(8,128)(2,1)} %param.8) | copy-start | bytes 2654212
  39.6 2.7 %collective-permute-start.8 = (bf16[576,768]{1,0:T(8,128)(2,1)}, bf16[576,768]{1,0:T(8,128)(2,1)S(1)}, u32[]{:S(2)}, u32[]{:S(2)}) collective-permute-start(bf16[576,768]{1,0:T(8,128)(2,1)} %collective-permute-done.7.refs_8_.refs_5_), channel_id=1, source_target_pairs={{0,1},{1,0},{2,3},{3,2},{4,5},{5,4},{6,7},{7,6},{8,9},{9,8},{10,11... | collective-permute-start | bytes 2654216 | tf_op jit(solution)/shard_map/ppermute | solution.py:464
  39.6 12.3 %collective-permute-start.10 = (bf16[2,48,2176]{2,1,0:T(8,128)(2,1)}, bf16[2,48,2176]{2,1,0:T(8,128)(2,1)S(1)}, u32[]{:S(2)}, u32[]{:S(2)}) collective-permute-start(bf16[2,48,2176]{2,1,0:T(8,128)(2,1)} %collective-permute-done.6.refs_2_.refs_4_), channel_id=1, source_target_pairs={{0,2},{1,3},{4,0},{5,1},{8,4},{9,5},{12,8},{13,9},{14,12},{15,13},... | collective-permute-start | bytes 1253384 | tf_op jit(solution)/shard_map/ppermute | solution.py:461
  41.2 12.3 %collective-permute-start.9 = (bf16[2,48,2176]{2,1,0:T(8,128)(2,1)}, bf16[2,48,2176]{2,1,0:T(8,128)(2,1)S(1)}, u32[]{:S(2)}, u32[]{:S(2)}) collective-permute-start(bf16[2,48,2176]{2,1,0:T(8,128)(2,1)} %collective-permute-done.5.refs_1_.refs_3_), channel_id=1, source_target_pairs={{0,4},{1,5},{4,8},{5,9},{8,12},{9,13},{12,14},{13,15},{14,10},{15,... | collective-permute-start | bytes 1253384 | tf_op jit(solution)/shard_map/ppermute | solution.py:461
  51.9 9.5 %collective-permute-start.12 = (bf16[1,48,2176]{2,1,0:T(8,128)(2,1)S(1)}, bf16[1,48,2176]{2,1,0:T(8,128)(2,1)S(1)}, u32[]{:S(2)}, u32[]{:S(2)}) collective-permute-start(bf16[1,48,2176]{2,1,0:T(8,128)(2,1)S(1)} %slice.7), channel_id=1, source_target_pairs={{0,2},{1,3},{4,0},{5,1},{8,4},{9,5},{12,8},{13,9},{14,12},{15,13},... | collective-permute-start | bytes 626696 | tf_op jit(solution)/shard_map/ppermute | solution.py:461
  53.5 7.9 %collective-permute-start.11 = (bf16[1,48,2176]{2,1,0:T(8,128)(2,1)S(1)}, bf16[1,48,2176]{2,1,0:T(8,128)(2,1)S(1)}, u32[]{:S(2)}, u32[]{:S(2)}) collective-permute-start(bf16[1,48,2176]{2,1,0:T(8,128)(2,1)S(1)} %slice.6), channel_id=1, source_target_pairs={{0,4},{1,5},{4,8},{5,9},{8,12},{9,13},{12,14},{13,15},{14,10},{15,... | collective-permute-start | bytes 626696 | tf_op jit(solution)/shard_map/ppermute | solution.py:461
  54.3 27.1 %collective-permute-start.16 = (bf16[2,240,768]{2,1,0:T(8,128)(2,1)S(1)}, bf16[2,240,768]{2,1,0:T(8,128)(2,1)S(1)}, u32[]{:S(2)}, u32[]{:S(2)}) collective-permute-start(bf16[2,240,768]{2,1,0:T(8,128)(2,1)S(1)} %get-tuple-element.89), channel_id=1, source_target_pairs={{0,16},{16,0},{1,17},{17,1},{2,18},{18,2},{3,19},{19,3},{4,20},{20... | collective-permute-start | bytes 2211848 | tf_op jit(solution)/shard_map/ppermute | solution.py:458
  67.4 6.1 %collective-permute-start.15 = (bf16[1,48,2176]{2,1,0:T(8,128)(2,1)S(1)}, bf16[1,48,2176]{2,1,0:T(8,128)(2,1)S(1)}, u32[]{:S(2)}, u32[]{:S(2)}) collective-permute-start(bf16[1,48,2176]{2,1,0:T(8,128)(2,1)S(1)} %bitcast.37), channel_id=1, source_target_pairs={{0,2},{1,3},{4,0},{5,1},{8,4},{9,5},{12,8},{13,9},{14,12},{15,13},... | collective-permute-start | bytes 626696 | tf_op jit(solution)/shard_map/ppermute | solution.py:461
  69.1 6.1 %collective-permute-start.13 = (bf16[1,48,2176]{2,1,0:T(8,128)(2,1)S(1)}, bf16[1,48,2176]{2,1,0:T(8,128)(2,1)S(1)}, u32[]{:S(2)}, u32[]{:S(2)}) collective-permute-start(bf16[1,48,2176]{2,1,0:T(8,128)(2,1)S(1)} %bitcast.36), channel_id=1, source_target_pairs={{0,4},{1,5},{4,8},{5,9},{8,12},{9,13},{12,14},{13,15},{14,10},{15,... | collective-permute-start | bytes 626696 | tf_op jit(solution)/shard_map/ppermute | solution.py:461
  69.5 10.0 %collective-permute-start.17 = (bf16[2,96,768]{2,1,0:T(8,128)(2,1)S(1)}, bf16[2,96,768]{2,1,0:T(8,128)(2,1)S(1)}, u32[]{:S(2)}, u32[]{:S(2)}) collective-permute-start(bf16[2,96,768]{2,1,0:T(8,128)(2,1)S(1)} %get-tuple-element.90), channel_id=1, source_target_pairs={{0,16},{16,0},{1,17},{17,1},{2,18},{18,2},{3,19},{19,3},{4,20},{20... | collective-permute-start | bytes 884744 | tf_op jit(solution)/shard_map/ppermute | solution.py:458
  73.6 13.1 %collective-permute-start.20 = (bf16[2,48,2176]{2,1,0:T(8,128)(2,1)S(1)}, bf16[2,48,2176]{2,1,0:T(8,128)(2,1)S(1)}, u32[]{:S(2)}, u32[]{:S(2)}) collective-permute-start(bf16[2,48,2176]{2,1,0:T(8,128)(2,1)S(1)} %sums.8), channel_id=1, source_target_pairs={{0,2},{1,3},{4,0},{5,1},{8,4},{9,5},{12,8},{13,9},{14,12},{15,13},... | collective-permute-start | bytes 1253384 | tf_op jit(solution)/shard_map/ppermute | solution.py:461
  75.3 11.4 %collective-permute-start.14 = (bf16[2,48,2176]{2,1,0:T(8,128)(2,1)S(1)}, bf16[2,48,2176]{2,1,0:T(8,128)(2,1)S(1)}, u32[]{:S(2)}, u32[]{:S(2)}) collective-permute-start(bf16[2,48,2176]{2,1,0:T(8,128)(2,1)S(1)} %sums.6), channel_id=1, source_target_pairs={{0,4},{1,5},{4,8},{5,9},{8,12},{9,13},{12,14},{13,15},{14,10},{15,... | collective-permute-start | bytes 1253384 | tf_op jit(solution)/shard_map/ppermute | solution.py:461
  75.8 5.6 %collective-permute-start.18 = (bf16[2,48,768]{2,1,0:T(8,128)(2,1)S(1)}, bf16[2,48,768]{2,1,0:T(8,128)(2,1)S(1)}, u32[]{:S(2)}, u32[]{:S(2)}) collective-permute-start(bf16[2,48,768]{2,1,0:T(8,128)(2,1)S(1)} %get-tuple-element.91), channel_id=1, source_target_pairs={{0,16},{16,0},{1,17},{17,1},{2,18},{18,2},{3,19},{19,3},{4,20},{20... | collective-permute-start | bytes 442376 | tf_op jit(solution)/shard_map/ppermute | solution.py:458
  86.7 14.7 %collective-permute-start.22 = (bf16[768,2048]{1,0:T(8,128)(2,1)S(1)}, bf16[768,2048]{1,0:T(8,128)(2,1)S(1)}, u32[]{:S(2)}, u32[]{:S(2)}) collective-permute-start(bf16[768,2048]{1,0:T(8,128)(2,1)S(1)} %weight_product.2), channel_id=1, source_target_pairs={{0,1},{1,0},{2,3},{3,2},{4,5},{5,4},{6,7},{7,6},{8,9},{9,8},{10,11... | collective-permute-start | bytes 9437192 | tf_op jit(solution)/shard_map/ppermute | solution.py:464
  86.9 12.1 %collective-permute-start.21 = (bf16[2,48,2176]{2,1,0:T(8,128)(2,1)S(1)}, bf16[2,48,2176]{2,1,0:T(8,128)(2,1)S(1)}, u32[]{:S(2)}, u32[]{:S(2)}) collective-permute-start(bf16[2,48,2176]{2,1,0:T(8,128)(2,1)S(1)} %sums.9), channel_id=1, source_target_pairs={{0,2},{1,3},{4,0},{5,1},{8,4},{9,5},{12,8},{13,9},{14,12},{15,13},... | collective-permute-start | bytes 1253384 | tf_op jit(solution)/shard_map/ppermute | solution.py:461
  88.6 12.1 %collective-permute-start.19 = (bf16[2,48,2176]{2,1,0:T(8,128)(2,1)S(1)}, bf16[2,48,2176]{2,1,0:T(8,128)(2,1)S(1)}, u32[]{:S(2)}, u32[]{:S(2)}) collective-permute-start(bf16[2,48,2176]{2,1,0:T(8,128)(2,1)S(1)} %sums.7), channel_id=1, source_target_pairs={{0,4},{1,5},{4,8},{5,9},{8,12},{9,13},{12,14},{13,15},{14,10},{15,... | collective-permute-start | bytes 1253384 | tf_op jit(solution)/shard_map/ppermute | solution.py:461
  90.4 22.8 %collective-permute-start.26 = (bf16[576,768]{1,0:T(8,128)(2,1)S(1)}, bf16[576,768]{1,0:T(8,128)(2,1)S(1)}, u32[]{:S(2)}, u32[]{:S(2)}) collective-permute-start(bf16[576,768]{1,0:T(8,128)(2,1)S(1)} %get-tuple-element.131), channel_id=1, source_target_pairs={{0,1},{1,0},{2,3},{3,2},{4,5},{5,4},{6,7},{7,6},{8,9},{9,8},{10,11... | collective-permute-start | bytes 2654216 | tf_op jit(solution)/shard_map/ppermute | solution.py:464
  99.1 11.3 %collective-permute-start.24 = (bf16[2,48,2176]{2,1,0:T(8,128)(2,1)S(1)}, bf16[2,48,2176]{2,1,0:T(8,128)(2,1)S(1)}, u32[]{:S(2)}, u32[]{:S(2)}) collective-permute-start(bf16[2,48,2176]{2,1,0:T(8,128)(2,1)S(1)} %sums.11), channel_id=1, source_target_pairs={{0,2},{1,3},{4,0},{5,1},{8,4},{9,5},{12,8},{13,9},{14,12},{15,13},... | collective-permute-start | bytes 1253384 | tf_op jit(solution)/shard_map/ppermute | solution.py:461
  100.8 12.4 %copy-start.12 = (s32[48,8]{0,1:T(8,128)S(1)}, s32[48,8]{0,1:T(8,128)}, u32[]{:S(2)}) copy-start(s32[48,8]{0,1:T(8,128)} %param.6) | copy-start | bytes 4612
  100.8 11.0 %collective-permute-start.23 = (bf16[2,48,2176]{2,1,0:T(8,128)(2,1)S(1)}, bf16[2,48,2176]{2,1,0:T(8,128)(2,1)S(1)}, u32[]{:S(2)}, u32[]{:S(2)}) collective-permute-start(bf16[2,48,2176]{2,1,0:T(8,128)(2,1)S(1)} %sums.10), channel_id=1, source_target_pairs={{0,4},{1,5},{4,8},{5,9},{8,12},{9,13},{12,14},{13,15},{14,10},{15,... | collective-permute-start | bytes 1253384 | tf_op jit(solution)/shard_map/ppermute | solution.py:461
  112.0 5.9 %collective-permute-start.25 = (bf16[48,2176]{1,0:T(8,128)(2,1)S(1)}, bf16[48,2176]{1,0:T(8,128)(2,1)S(1)}, u32[]{:S(2)}, u32[]{:S(2)}) collective-permute-start(bf16[48,2176]{1,0:T(8,128)(2,1)S(1)} %get-tuple-element.128), channel_id=1, source_target_pairs={{0,16},{16,0},{1,17},{17,1},{2,18},{18,2},{3,19},{19,3},{4,20},{20... | collective-permute-start | bytes 626696 | tf_op jit(solution)/shard_map/ppermute | solution.py:458

commit v11 on v8

--- a/solution.py
+++ b/solution.py
@@ -40,7 +40,16 @@
     return [at.index(place) for place in walk]
 
 
-def pack_kernel(top, where, ids, probs, grads, *outs):
+def pack_kernel(top, n_out, where, ids_in, probs_in, grads_in, *refs):
+    outs, (ids, probs, grads, sems) = refs[:n_out], refs[n_out:]
+    copies = [
+        pltpu.make_async_copy(source, target, sems.at[i])
+        for i, (source, target) in enumerate([(ids_in, ids), (probs_in, probs), (grads_in, grads)])
+    ]
+    for copy in copies:
+        copy.start()
+    for copy in copies:
+        copy.wait()
     tok = grads.shape[0]
     width = grads.shape[1] // len(outs)
     room = outs[0].shape[1] - width
@@ -75,10 +84,16 @@
     width = grads.shape[1] // n_dp
     vmem = pl.BlockSpec(memory_space=pltpu.VMEM)
     return pl.pallas_call(
-        functools.partial(pack_kernel, top),
-        in_specs=[pl.BlockSpec(memory_space=pltpu.SMEM)] + [vmem] * 3,
+        functools.partial(pack_kernel, top, n_dp),
+        in_specs=[pl.BlockSpec(memory_space=pltpu.SMEM)] + [pl.BlockSpec(memory_space=pltpu.HBM)] * 3,
         out_specs=[vmem] * n_dp,
         out_shape=[jax.ShapeDtypeStruct((tok, width + room), jnp.bfloat16)] * n_dp,
+        scratch_shapes=[
+            pltpu.VMEM(ids.shape, ids.dtype),
+            pltpu.VMEM(probs.shape, probs.dtype),
+            pltpu.VMEM(grads.shape, grads.dtype),
+            pltpu.SemaphoreType.DMA((3,)),
+        ],
         compiler_params=kernel_memory(tok),
         name="pack",
     )(where, ids, probs, grads)
@@ -428,13 +443,15 @@
         room = 128 * -(-max(4 * top, 2 * n_ex) // 128)
         where = replica.reshape(1).astype(jnp.int32)
         packed = pack(where, expert_ids.T, route_probs.T, out_grad, n_dp, room)
-        blocks = {0: jnp.stack([packed[0]] + [shift(packed[d], d) for d in range(1, n_dp)])}
+        seeds = [packed[0]] + [shift(packed[d], d) for d in range(1, n_dp)]
+        blocks = {0: [jnp.stack(seeds[:per]), jnp.stack(seeds[per:])]}
+        halves = {step: [ring_send(value, step) for value in blocks[0]] for step in (1, -1)}
 
         sibling_weight = swap(weight)
         hidden = expert_hidden[0, 0].transpose(1, 0, 2).reshape(slots, ff)
         hiddens = [(hidden, swap(hidden))]
         for d in range(1, n_dp):
-            value = shift(after(hidden, blocks[0]), d)
+            value = shift(after(hidden, *seeds[1:], halves[1][0], halves[-1][0]), d)
             hiddens.append((value, None))
 
         parts, scaleds, layout, facts = {}, [], [], []
@@ -444,11 +461,11 @@
         def work(items, *done):
             used, plan = [], []
             for off, d in items:
-                value = blocks[off][d // per] if off == half else blocks[off]
+                value = blocks[off][d // per] if off in (0, half) else blocks[off]
                 if not any(value is other for other in used):
                     used.append(value)
                 where = [value is other for other in used].index(True)
-                plan.append((where, d % per if off == half else d, d, offsets.index(off)))
+                plan.append((where, d % per if off in (0, half) else d, d, offsets.index(off)))
             if done:
                 gated = [after(used[0], *done)] + used[1:]
             else:
@@ -475,11 +492,15 @@
         both = lambda offs: [(off, d) for d in range(n_dp) for off in offs]
         gate = ()
         for step in range(1, half):
-            sent = blocks[1 - step], blocks[step - 1]
-            if gate:
-                sent = after(sent[0], *gate), after(sent[1], *gate)
-            blocks[-step] = ring_send(sent[0], 1)
-            blocks[step] = ring_send(sent[1], -1)
+            if step == 1:
+                blocks[-1] = jnp.concatenate(halves[1], axis=0)
+                blocks[1] = jnp.concatenate(halves[-1], axis=0)
+            else:
+                sent = blocks[1 - step], blocks[step - 1]
+                if gate:
+                    sent = after(sent[0], *gate), after(sent[1], *gate)
+                blocks[-step] = ring_send(sent[0], 1)
+                blocks[step] = ring_send(sent[1], -1)
             if step == 1:
                 following = [(off, 0) for off in offsets[:3]]
             elif step == 2:
@@ -509,12 +530,8 @@
                 values.append(jnp.stack([parts[half, d] for d in every[per:]]))
             else:
                 first, last = ((0, per), (per, n_dp)) if hop == half - 1 else ((0, n_dp), (0, n_dp))
-                values = sums(
-                    [
-                        ([parts[hop, d] for d in every], carry[1], *first),
-                        ([parts[-hop, d] for d in every], carry[-1], *last),
-                    ]
-                )
+                values = sums([([parts[hop, d] for d in every], carry[1], *first)])
+                values += sums([([parts[-hop, d] for d in every], carry[-1], *last)])
             values = [after(value, *done) for value in values]
             carry[1] = ring_send(values[0], 1)
             carry[-1] = ring_send(values[1], -1)
@@ -525,7 +542,7 @@
         hop_on(half)
         second = hop_on(half - 1)
         other = weight_product(
-            [after(refs[0], *sending, *[value for sent in sent_back for value in sent[:-1]])] + refs[1:], layout, scaleds, 1, jnp.bfloat16, width
+            [after(refs[0], *sending, *[value for sent in sent_back for value in sent])] + refs[1:], layout, scaleds, 1, jnp.bfloat16, width
         )
         swapped = swap(after(other, *second))
         third = hop_on(half - 2, other)

time: 117 us -> 117 us (level)
  waiting for transfers between devices: 37.4 us -> 32.4 us
  starting transfers between devices: 26.3 us -> 28.5 us
  local copies, waits for them, and re-layouts: 8.66 us -> 10.4 us
    ppermute x16 -> x18, waiting for transfers between devices: 23.5 us -> 17.1 us  [ring_send(): return lax.ppermute(value, 'expert', forward if step > 0 else backward)]
    ppermute x16 -> x18, starting transfers between devices: 16.8 us -> 19.9 us  [ring_send(): return lax.ppermute(value, 'expert', forward if step > 0 else backward)]
    concatenate x0 -> x2, local copies, waits for them, and re-layouts: none -> 1.38 us  [the longest x1 0.7 us: shards(): blocks[-1] = jnp.concatenate(halves[1], axis=0)]
    ppermute x6, waiting for transfers between devices: 13.3 us -> 14.7 us  [shift(): lax.ppermute(value, 'dp', [(i, (i + step) % n_dp) for i in range(n_dp)])]
  transfers between devices with their start and end apart: 27 -> 29, of which waited for: 15 -> 13; matrix products, arithmetic and copies ran while one was open for 2% -> 5% of each run, Pallas kernels for 35% -> 35%
where the time goes in v11:
time: 117 us
  Pallas kernels  42.3 us (36%)
  waiting for transfers between devices  32.4 us (28%)
  starting transfers between devices  28.5 us (24%)
  local copies, waits for them, and re-layouts  10.4 us (9%)
  other arithmetic  2.29 us (2%)
    pallas_call x4, Pallas kernels, block_product(): pl.pallas_call(functools.partial(block_kernel, plan, len(blocks), n_dp, n...  26.4 us
    ppermute x18, starting transfers between devices, ring_send(): return lax.ppermute(value, 'expert', forward if step > 0 else backward)  19.9 us
    ppermute x18, waiting for transfers between devices, ring_send(): return lax.ppermute(value, 'expert', forward if step > 0 else backward)  17.1 us
    ppermute x6, waiting for transfers between devices, shift(): lax.ppermute(value, 'dp', [(i, (i + step) % n_dp) for i in range(n_dp)])  14.7 us
    pallas_call x2, Pallas kernels, weight_product(): pl.pallas_call(functools.partial(weight_kernel, len(blocks), len(scaleds)...  12.2 us
    unnamed x24, local copies, waits for them, and re-layouts  8.26 us
    ppermute x6, starting transfers between devices, shift(): lax.ppermute(value, 'dp', [(i, (i + step) % n_dp) for i in range(n_dp)])  7.91 us
  transfers between devices with their start and end apart: 29, of which 13 were waited for; matrix products, arithmetic and copies ran while one was open for 5% of the time, Pallas kernels for 35%

profile of v11, /device:TPU:0, one launch (start us, length us, event | category | flops | bytes accessed | tf_op | source)
XLA Modules:
  0.0 116.7 jit_solution(5908001491299711187)
XLA Ops:
  0.6 0.5 collective-permute-start.6
  1.2 1.0 copy-done.4
  2.1 0.7 copy-done.7
  2.8 0.7 copy-done.9
  3.5 0.5 pack.1
  4.0 2.6 %collective-permute-start.1 = (bf16[48,2176]{1,0:T(8,128)(2,1)S(1)}, bf16[48,2176]{1,0:T(8,128)(2,1)S(1)}, u32[]{:S(2)}, u32[]{:S(2)}) collective-permute-start(bf16[48,2176]{1,0:T(8,128)(2,1)S(1)} %get-tuple-element.67), channel_id=1, source_target_pairs={{0,16},{16,0},{1,17},{17,1},{2,18},{18,2},{3,19},{19,3},{4,20},{20... | collective-permute-start | bytes 626696 | tf_op jit(solution)/shard_map/ppermute | solution.py:435
  6.6 1.5 %collective-permute-start.3 = (bf16[1,48,2176]{2,1,0:T(8,128)(2,1)S(1)}, bf16[1,48,2176]{2,1,0:T(8,128)(2,1)S(1)}, u32[]{:S(2)}, u32[]{:S(2)}) collective-permute-start(bf16[1,48,2176]{2,1,0:T(8,128)(2,1)S(1)} %bitcast.32), channel_id=1, source_target_pairs={{0,2},{1,3},{4,0},{5,1},{8,4},{9,5},{12,8},{13,9},{14,12},{15,13},... | collective-permute-start | bytes 626696 | tf_op jit(solution)/shard_map/ppermute | solution.py:438
  8.1 0.5 collective-permute-start
  8.6 3.8 %collective-permute-done.1 = bf16[48,2176]{1,0:T(8,128)(2,1)S(1)} collective-permute-done((bf16[48,2176]{1,0:T(8,128)(2,1)S(1)}, bf16[48,2176]{1,0:T(8,128)(2,1)S(1)}, u32[]{:S(2)}, u32[]{:S(2)}) %collective-permute-start.1) | collective-permute-done | bytes 208928 | tf_op jit(solution)/shard_map/ppermute | solution.py:435
  12.4 1.8 %collective-permute-start.4 = (bf16[1,48,2176]{2,1,0:T(8,128)(2,1)S(1)}, bf16[1,48,2176]{2,1,0:T(8,128)(2,1)S(1)}, u32[]{:S(2)}, u32[]{:S(2)}) collective-permute-start(bf16[1,48,2176]{2,1,0:T(8,128)(2,1)S(1)} %bitcast.37), channel_id=1, source_target_pairs={{0,2},{1,3},{4,0},{5,1},{8,4},{9,5},{12,8},{13,9},{14,12},{15,13},... | collective-permute-start | bytes 626696 | tf_op jit(solution)/shard_map/ppermute | solution.py:438
  14.2 1.3 %collective-permute-start.2 = (bf16[1,48,2176]{2,1,0:T(8,128)(2,1)S(1)}, bf16[1,48,2176]{2,1,0:T(8,128)(2,1)S(1)}, u32[]{:S(2)}, u32[]{:S(2)}) collective-permute-start(bf16[1,48,2176]{2,1,0:T(8,128)(2,1)S(1)} %bitcast.38), channel_id=1, source_target_pairs={{0,4},{1,5},{4,8},{5,9},{8,12},{9,13},{12,14},{13,15},{14,10},{15,... | collective-permute-start | bytes 626696 | tf_op jit(solution)/shard_map/ppermute | solution.py:438
  15.4 0.7 copy-done.5
  16.1 0.7 collective-permute-start.9
  16.8 0.7 constant_dynamic-update-slice_fusion.3
  17.6 0.7 constant_dynamic-update-slice_fusion.1
  18.3 1.1 collective-permute-done.4
  19.4 0.7 constant_dynamic-update-slice_fusion.2.refs_3_.refs_5_.refs_2_
  20.1 1.6 %collective-permute-start.8 = (bf16[2,48,2176]{2,1,0:T(8,128)(2,1)}, bf16[2,48,2176]{2,1,0:T(8,128)(2,1)}, u32[]{:S(2)}, u32[]{:S(2)}) collective-permute-start(bf16[2,48,2176]{2,1,0:T(8,128)(2,1)} %constant_dynamic-update-slice_fusion.2.refs_3_.refs_5_.refs_2_), channel_id=1, source_target_pairs={{0,2},{1,3},{4,0},{5,1},{8,4},{9,5},{12,8},{13,9},{14,12},{15,13},... | collective-permute-start | bytes 1253384 | tf_op jit(solution)/shard_map/ppermute | solution.py:438
  21.6 0.7 constant_dynamic-update-slice_fusion.refs_2_.refs_4_.refs_1_
  22.3 0.5 collective-permute-start.7
  22.8 0.7 dynamic-slice_bitcast_fusion.refs_0_
  23.5 1.9 %copy-done = bf16[1,768,2048]{2,1,0:T(8,128)(2,1)S(1)} copy-done((bf16[1,768,2048]{2,1,0:T(8,128)(2,1)S(1)}, bf16[1,768,2048]{2,1,0:T(8,128)(2,1)}, u32[]{:S(2)}) %copy-start) | copy-done | bytes 3145752
  25.4 1.2 copy-done.2
  26.6 5.7 %block_product.4 = (bf16[48,2176]{1,0:T(8,128)(2,1)S(1)}, bf16[48,2176]{1,0:T(8,128)(2,1)S(1)}, bf16[48,2176]{1,0:T(8,128)(2,1)S(1)}, bf16[2,144,768]{2,1,0:T(8,...) custom-call(s32[10]{0:T(128)S(1)} %dynamic-slice_bitcast_fusion.refs_0_, ...), custom_call_target="tpu_custom_call" | custom-call | flops 1811939328 | bytes 7987200 | tf_op jit(solution)/shard_map/block_product/pallas_call | solution.py:290
  32.3 0.5 collective-permute-done.7.refs_1_.refs_3_
  32.7 4.4 %collective-permute-done.9.refs_8_.refs_5_ = bf16[576,768]{1,0:T(8,128)(2,1)} collective-permute-done((bf16[576,768]{1,0:T(8,128)(2,1)}, bf16[576,768]{1,0:T(8,128)(2,1)}, u32[]{:S(2)}, u32[]{:S(2)}) %collective-permute-start.9) | collective-permute-done | bytes 884768 | tf_op jit(solution)/shard_map/ppermute | solution.py:435
  37.1 0.8 collective-permute-start.12
  37.9 1.2 %collective-permute-start.11 = (bf16[2,48,2176]{2,1,0:T(8,128)(2,1)}, bf16[2,48,2176]{2,1,0:T(8,128)(2,1)S(1)}, u32[]{:S(2)}, u32[]{:S(2)}) collective-permute-start(bf16[2,48,2176]{2,1,0:T(8,128)(2,1)} %collective-permute-done.7.refs_1_.refs_3_), channel_id=1, source_target_pairs={{0,4},{1,5},{4,8},{5,9},{8,12},{9,13},{12,14},{13,15},{14,10},{15,... | collective-permute-start | bytes 1253384 | tf_op jit(solution)/shard_map/ppermute | solution.py:438
  39.1 0.6 collective-permute-done.10.refs_9_.refs_6_
  39.7 8.4 %block_product.5 = (bf16[48,2176]{1,0:T(8,128)(2,1)S(1)}, bf16[48,2176]{1,0:T(8,128)(2,1)S(1)}, bf16[48,2176]{1,0:T(8,128)(2,1)S(1)}, bf16[48,2176]{1,0:T(8,128)...) custom-call(s32[10]{0:T(128)S(1)} %dynamic-slice_bitcast_fusion.refs, ...), custom_call_target="tpu_custom_call" | custom-call | flops 4227858432 | bytes 10248192 | tf_op jit(solution)/shard_map/block_product/pallas_call | solution.py:290
  48.1 1.2 %collective-permute-done.12.refs_2_.refs_7_ = bf16[2,48,2176]{2,1,0:T(8,128)(2,1)S(1)} collective-permute-done((bf16[2,48,2176]{2,1,0:T(8,128)(2,1)}, bf16[2,48,2176]{2,1,0:T(8,128)(2,1)S(1)}, u32[]{:S(2)}, u32[]{:S(2)}) %collective-permute-start.12) | collective-permute-done | bytes 417824 | tf_op jit(solution)/shard_map/ppermute | solution.py:438
  49.4 0.9 collective-permute-start.14
  50.3 1.5 %collective-permute-start.13 = (bf16[1,48,2176]{2,1,0:T(8,128)(2,1)S(1)}, bf16[1,48,2176]{2,1,0:T(8,128)(2,1)S(1)}, u32[]{:S(2)}, u32[]{:S(2)}) collective-permute-start(bf16[1,48,2176]{2,1,0:T(8,128)(2,1)S(1)} %slice.6), channel_id=1, source_target_pairs={{0,4},{1,5},{4,8},{5,9},{8,12},{9,13},{12,14},{13,15},{14,10},{15,... | collective-permute-start | bytes 626696 | tf_op jit(solution)/shard_map/ppermute | solution.py:438
  51.7 0.8 collective-permute-start.18
  52.5 6.4 %block_product.6 = (bf16[48,2176]{1,0:T(8,128)(2,1)S(1)}, bf16[48,2176]{1,0:T(8,128)(2,1)S(1)}, bf16[48,2176]{1,0:T(8,128)(2,1)S(1)}, bf16[48,2176]{1,0:T(8,128)...) custom-call(s32[10]{0:T(128)S(1)} %dynamic-slice_bitcast_fusion.refs, ...), custom_call_target="tpu_custom_call" | custom-call | flops 2415919104 | bytes 8552448 | tf_op jit(solution)/shard_map/block_product/pallas_call | solution.py:290
  58.9 5.9 %block_product.7 = (bf16[48,2176]{1,0:T(8,128)(2,1)S(1)}, bf16[48,2176]{1,0:T(8,128)(2,1)S(1)}, bf16[2,48,768]{2,1,0:T(8,128)(2,1)S(1)}, bf16[2,48,768]{2,1,0:T(...) custom-call(s32[10]{0:T(128)S(1)} %dynamic-slice_bitcast_fusion.refs, ...), custom_call_target="tpu_custom_call" | custom-call | flops 1207959552 | bytes 7421952 | tf_op jit(solution)/shard_map/block_product/pallas_call | solution.py:290
  64.8 1.6 %collective-permute-start.17 = (bf16[1,48,2176]{2,1,0:T(8,128)(2,1)S(1)}, bf16[1,48,2176]{2,1,0:T(8,128)(2,1)S(1)}, u32[]{:S(2)}, u32[]{:S(2)}) collective-permute-start(bf16[1,48,2176]{2,1,0:T(8,128)(2,1)S(1)} %bitcast.45), channel_id=1, source_target_pairs={{0,2},{1,3},{4,0},{5,1},{8,4},{9,5},{12,8},{13,9},{14,12},{15,13},... | collective-permute-start | bytes 626696 | tf_op jit(solution)/shard_map/ppermute | solution.py:438
  66.4 0.5 collective-permute-start.15
  66.9 1.2 %collective-permute-start.19 = (bf16[2,96,768]{2,1,0:T(8,128)(2,1)S(1)}, bf16[2,96,768]{2,1,0:T(8,128)(2,1)S(1)}, u32[]{:S(2)}, u32[]{:S(2)}) collective-permute-start(bf16[2,96,768]{2,1,0:T(8,128)(2,1)S(1)} %get-tuple-element.86), channel_id=1, source_target_pairs={{0,16},{16,0},{1,17},{17,1},{2,18},{18,2},{3,19},{19,3},{4,20},{20... | collective-permute-start | bytes 884744 | tf_op jit(solution)/shard_map/ppermute | solution.py:435
  68.2 2.7 %collective-permute-done.17.refs_2_ = bf16[1,48,2176]{2,1,0:T(8,128)(2,1)S(1)} collective-permute-done((bf16[1,48,2176]{2,1,0:T(8,128)(2,1)S(1)}, bf16[1,48,2176]{2,1,0:T(8,128)(2,1)S(1)}, u32[]{:S(2)}, u32[]{:S(2)}) %collective-permute-start.17) | collective-permute-done | bytes 208928 | tf_op jit(solution)/shard_map/ppermute | solution.py:438
  70.9 1.6 %collective-permute-start.22 = (bf16[2,48,2176]{2,1,0:T(8,128)(2,1)S(1)}, bf16[2,48,2176]{2,1,0:T(8,128)(2,1)S(1)}, u32[]{:S(2)}, u32[]{:S(2)}) collective-permute-start(bf16[2,48,2176]{2,1,0:T(8,128)(2,1)S(1)} %sums.8), channel_id=1, source_target_pairs={{0,2},{1,3},{4,0},{5,1},{8,4},{9,5},{12,8},{13,9},{14,12},{15,13},... | collective-permute-start | bytes 1253384 | tf_op jit(solution)/shard_map/ppermute | solution.py:438
  72.6 0.6 collective-permute-start.16
  73.1 1.2 %collective-permute-start.20 = (bf16[2,48,768]{2,1,0:T(8,128)(2,1)S(1)}, bf16[2,48,768]{2,1,0:T(8,128)(2,1)S(1)}, u32[]{:S(2)}, u32[]{:S(2)}) collective-permute-start(bf16[2,48,768]{2,1,0:T(8,128)(2,1)S(1)} %get-tuple-element.87), channel_id=1, source_target_pairs={{0,16},{16,0},{1,17},{17,1},{2,18},{18,2},{3,19},{19,3},{4,20},{20... | collective-permute-start | bytes 442376 | tf_op jit(solution)/shard_map/ppermute | solution.py:435
  74.4 2.6 %collective-permute-done.19.refs_13_ = bf16[2,96,768]{2,1,0:T(8,128)(2,1)S(1)} collective-permute-done((bf16[2,96,768]{2,1,0:T(8,128)(2,1)S(1)}, bf16[2,96,768]{2,1,0:T(8,128)(2,1)S(1)}, u32[]{:S(2)}, u32[]{:S(2)}) %collective-permute-start.19) | collective-permute-done | bytes 294944 | tf_op jit(solution)/shard_map/ppermute | solution.py:435
  77.0 1.8 %collective-permute-done.20.refs_14_ = bf16[2,48,768]{2,1,0:T(8,128)(2,1)S(1)} collective-permute-done((bf16[2,48,768]{2,1,0:T(8,128)(2,1)S(1)}, bf16[2,48,768]{2,1,0:T(8,128)(2,1)S(1)}, u32[]{:S(2)}, u32[]{:S(2)}) %collective-permute-start.20) | collective-permute-done | bytes 147488 | tf_op jit(solution)/shard_map/ppermute | solution.py:435
  78.8 5.4 %weight_product.2 = bf16[768,2048]{1,0:T(8,128)(2,1)S(1)} custom-call(bf16[1,48,2176]{2,1,0:T(8,128)(2,1)S(1)} %bitcast.35, bf16[2,48,2176]{2,1,0:T(8,128)(2,1)} %constant_dynamic-update-slice_fusion.refs_2_.refs_4_.refs_1_, bf16[2,48,2176]{2,1,0:T(8,128)(2,1)} %constant_dynamic-update-slice_fusion.2.refs_3_.refs_5_.refs_2_, ...), custom_call_target="tpu_custom_call" | custom-call | flops 2415919104 | bytes 10616832 | tf_op jit(solution)/shard_map/weight_product/pallas_call | solution.py:372
  84.2 0.1 sums.9
  84.3 1.1 collective-permute-start.23
  85.4 0.1 sums.7
  85.5 1.0 collective-permute-start.21
  86.6 1.3 %spread_product.1 = (bf16[576,768]{1,0:T(8,128)(2,1)S(1)}, bf16[576,768]{1,0:T(8,128)(2,1)S(1)}) custom-call(s32[144,2]{1,0:T(8,128)S(1)} %get-tuple-element.106.refs_0_, s32[96,2]{1,0:T(8,128)S(1)} %get-tuple-element.107.refs_1_, s32[96,2]{1,0:T(8,128)S(1)} %get-tuple-element.108.refs_2_, s32[48,2]{1,0:T(8,128)S(1)} %get-tuple-element.109.refs_3_, ...), custom_call_target="tpu_custom_call" | custom-call | flops 679477248 | bytes 3538944 | tf_op jit(solution)/shard_map/spread_product/pallas_call | solution.py:337
  88.0 8.5 %collective-permute-done.23.refs_2_ = bf16[2,48,2176]{2,1,0:T(8,128)(2,1)S(1)} collective-permute-done((bf16[2,48,2176]{2,1,0:T(8,128)(2,1)S(1)}, bf16[2,48,2176]{2,1,0:T(8,128)(2,1)S(1)}, u32[]{:S(2)}, u32[]{:S(2)}) %collective-permute-start.23) | collective-permute-done | bytes 417824 | tf_op jit(solution)/shard_map/ppermute | solution.py:438
  96.5 1.1 collective-permute-start.26
  97.6 0.1 sums.10
  97.7 1.0 collective-permute-start.25
  98.8 6.8 %weight_product.3 = f32[768,2048]{1,0:T(8,128)} custom-call(bf16[1,48,2176]{2,1,0:T(8,128)(2,1)S(1)} %bitcast.36, bf16[2,48,2176]{2,1,0:T(8,128)(2,1)} %constant_dynamic-update-slice_fusion.refs_2_.refs_4_.refs_1_, bf16[2,48,2176]{2,1,0:T(8,128)(2,1)} %constant_dynamic-update-slice_fusion.2.refs_3_.refs_5_.refs_2_, ...), custom_call_target="tpu_custom_call" | custom-call | flops 2415919104 | bytes 10616832 | tf_op jit(solution)/shard_map/weight_product/pallas_call | solution.py:372
  105.6 2.2 %collective-permute-done.26.refs_3_ = bf16[2,48,2176]{2,1,0:T(8,128)(2,1)S(1)} collective-permute-done((bf16[2,48,2176]{2,1,0:T(8,128)(2,1)S(1)}, bf16[2,48,2176]{2,1,0:T(8,128)(2,1)S(1)}, u32[]{:S(2)}, u32[]{:S(2)}) %collective-permute-start.26) | collective-permute-done | bytes 417824 | tf_op jit(solution)/shard_map/ppermute | solution.py:438
  107.8 0.9 collective-permute-done.25.refs_2_
  108.8 0.2 close.1
  108.9 1.3 %collective-permute-start.27 = (bf16[48,2176]{1,0:T(8,128)(2,1)S(1)}, bf16[48,2176]{1,0:T(8,128)(2,1)S(1)}, u32[]{:S(2)}, u32[]{:S(2)}) collective-permute-start(bf16[48,2176]{1,0:T(8,128)(2,1)S(1)} %get-tuple-element.124), channel_id=1, source_target_pairs={{0,16},{16,0},{1,17},{17,1},{2,18},{18,2},{3,19},{19,3},{4,20},{20... | collective-permute-start | bytes 626696 | tf_op jit(solution)/shard_map/ppermute | solution.py:435
  110.3 2.3 %add.8 = bf16[576,768]{1,0:T(8,128)(2,1)} add(bf16[576,768]{1,0:T(8,128)(2,1)S(1)} %get-tuple-element.118, bf16[576,768]{1,0:T(8,128)(2,1)} %collective-permute-done.28) | non-fusion elementwise | flops 442368 | bytes 2654208 | tf_op jit(solution)/shard_map/add | solution.py:555
  112.6 2.2 %collective-permute-done.27.refs_1_ = bf16[48,2176]{1,0:T(8,128)(2,1)S(1)} collective-permute-done((bf16[48,2176]{1,0:T(8,128)(2,1)S(1)}, bf16[48,2176]{1,0:T(8,128)(2,1)S(1)}, u32[]{:S(2)}, u32[]{:S(2)}) %collective-permute-start.27) | collective-permute-done | bytes 208928 | tf_op jit(solution)/shard_map/ppermute | solution.py:435
  114.8 1.3 %home.1 = (bf16[48,4096]{1,0:T(8,128)(2,1)}, f32[48,8]{1,0:T(8,128)S(1)}) custom-call(s32[1]{0:T(128)} %bitcast.where, s32[48,8]{1,0:T(8,128)S(1)} %copy.10.ids, bf16[48,2176]{1,0:T(8,128)(2,1)S(1)} %get-tuple-element.123.refs_0_, bf16[48,2176]{1,0:T(8,128)(2,1)S(1)} %collective-permute-done.27.refs_1_), custom_call_target="tpu_custom_call" | custom-call | tf_op jit(solution)/shard_map/home/pallas_call | solution.py:172
  116.1 0.7 copy.11
  (40 shorter events, 0.6 us)
Async XLA Ops:
  0.6 22.9 %collective-permute-start.6 = (bf16[768,2048]{1,0:T(8,128)(2,1)}, bf16[768,2048]{1,0:T(8,128)(2,1)S(1)}, u32[]{:S(2)}, u32[]{:S(2)}) collective-permute-start(bf16[768,2048]{1,0:T(8,128)(2,1)} %bitcast.21), channel_id=1, source_target_pairs={{0,1},{1,0},{2,3},{3,2},{4,5},{5,4},{6,7},{7,6},{8,9},{9,8},{10,11... | collective-permute-start | bytes 9437192 | tf_op jit(solution)/shard_map/ppermute | solution.py:441
  1.1 1.0 copy-start.4
  2.1 0.7 copy-start.7
  2.8 0.7 copy-start.9
  4.0 8.4 %collective-permute-start.1 = (bf16[48,2176]{1,0:T(8,128)(2,1)S(1)}, bf16[48,2176]{1,0:T(8,128)(2,1)S(1)}, u32[]{:S(2)}, u32[]{:S(2)}) collective-permute-start(bf16[48,2176]{1,0:T(8,128)(2,1)S(1)} %get-tuple-element.67), channel_id=1, source_target_pairs={{0,16},{16,0},{1,17},{17,1},{2,18},{18,2},{3,19},{19,3},{4,20},{20... | collective-permute-start | bytes 626696 | tf_op jit(solution)/shard_map/ppermute | solution.py:435
  6.6 7.6 %collective-permute-start.3 = (bf16[1,48,2176]{2,1,0:T(8,128)(2,1)S(1)}, bf16[1,48,2176]{2,1,0:T(8,128)(2,1)S(1)}, u32[]{:S(2)}, u32[]{:S(2)}) collective-permute-start(bf16[1,48,2176]{2,1,0:T(8,128)(2,1)S(1)} %bitcast.32), channel_id=1, source_target_pairs={{0,2},{1,3},{4,0},{5,1},{8,4},{9,5},{12,8},{13,9},{14,12},{15,13},... | collective-permute-start | bytes 626696 | tf_op jit(solution)/shard_map/ppermute | solution.py:438
  8.1 8.0 %collective-permute-start = (bf16[1,48,2176]{2,1,0:T(8,128)(2,1)S(1)}, bf16[1,48,2176]{2,1,0:T(8,128)(2,1)S(1)}, u32[]{:S(2)}, u32[]{:S(2)}) collective-permute-start(bf16[1,48,2176]{2,1,0:T(8,128)(2,1)S(1)} %bitcast.33), channel_id=1, source_target_pairs={{0,4},{1,5},{4,8},{5,9},{8,12},{9,13},{12,14},{13,15},{14,10},{15,... | collective-permute-start | bytes 626696 | tf_op jit(solution)/shard_map/ppermute | solution.py:438
  8.6 14.9 %collective-permute-start.5 = (bf16[576,768]{1,0:T(8,128)(2,1)}, bf16[576,768]{1,0:T(8,128)(2,1)}, u32[]{:S(2)}, u32[]{:S(2)}) collective-permute-start(bf16[576,768]{1,0:T(8,128)(2,1)} %bitcast.26), channel_id=1, source_target_pairs={{0,1},{1,0},{2,3},{3,2},{4,5},{5,4},{6,7},{7,6},{8,9},{9,8},{10,11... | collective-permute-start | bytes 2654216 | tf_op jit(solution)/shard_map/ppermute | solution.py:441
  12.4 7.0 %collective-permute-start.4 = (bf16[1,48,2176]{2,1,0:T(8,128)(2,1)S(1)}, bf16[1,48,2176]{2,1,0:T(8,128)(2,1)S(1)}, u32[]{:S(2)}, u32[]{:S(2)}) collective-permute-start(bf16[1,48,2176]{2,1,0:T(8,128)(2,1)S(1)} %bitcast.37), channel_id=1, source_target_pairs={{0,2},{1,3},{4,0},{5,1},{8,4},{9,5},{12,8},{13,9},{14,12},{15,13},... | collective-permute-start | bytes 626696 | tf_op jit(solution)/shard_map/ppermute | solution.py:438
  14.2 7.5 %collective-permute-start.2 = (bf16[1,48,2176]{2,1,0:T(8,128)(2,1)S(1)}, bf16[1,48,2176]{2,1,0:T(8,128)(2,1)S(1)}, u32[]{:S(2)}, u32[]{:S(2)}) collective-permute-start(bf16[1,48,2176]{2,1,0:T(8,128)(2,1)S(1)} %bitcast.38), channel_id=1, source_target_pairs={{0,4},{1,5},{4,8},{5,9},{8,12},{9,13},{12,14},{13,15},{14,10},{15,... | collective-permute-start | bytes 626696 | tf_op jit(solution)/shard_map/ppermute | solution.py:438
  15.4 0.7 copy-start.5
  16.1 21.0 %collective-permute-start.9 = (bf16[576,768]{1,0:T(8,128)(2,1)}, bf16[576,768]{1,0:T(8,128)(2,1)}, u32[]{:S(2)}, u32[]{:S(2)}) collective-permute-start(bf16[576,768]{1,0:T(8,128)(2,1)} %bitcast.27), channel_id=1, source_target_pairs={{0,16},{16,0},{1,17},{17,1},{2,18},{18,2},{3,19},{19,3},{4,20},{20... | collective-permute-start | bytes 2654216 | tf_op jit(solution)/shard_map/ppermute | solution.py:435
  20.1 12.2 %collective-permute-start.8 = (bf16[2,48,2176]{2,1,0:T(8,128)(2,1)}, bf16[2,48,2176]{2,1,0:T(8,128)(2,1)}, u32[]{:S(2)}, u32[]{:S(2)}) collective-permute-start(bf16[2,48,2176]{2,1,0:T(8,128)(2,1)} %constant_dynamic-update-slice_fusion.2.refs_3_.refs_5_.refs_2_), channel_id=1, source_target_pairs={{0,2},{1,3},{4,0},{5,1},{8,4},{9,5},{12,8},{13,9},{14,12},{15,13},... | collective-permute-start | bytes 1253384 | tf_op jit(solution)/shard_map/ppermute | solution.py:438
  22.3 10.4 %collective-permute-start.7 = (bf16[2,48,2176]{2,1,0:T(8,128)(2,1)}, bf16[2,48,2176]{2,1,0:T(8,128)(2,1)}, u32[]{:S(2)}, u32[]{:S(2)}) collective-permute-start(bf16[2,48,2176]{2,1,0:T(8,128)(2,1)} %constant_dynamic-update-slice_fusion.refs_2_.refs_4_.refs_1_), channel_id=1, source_target_pairs={{0,4},{1,5},{4,8},{5,9},{8,12},{9,13},{12,14},{13,15},{14,10},{15,... | collective-permute-start | bytes 1253384 | tf_op jit(solution)/shard_map/ppermute | solution.py:438
  23.5 1.9 %copy-start = (bf16[1,768,2048]{2,1,0:T(8,128)(2,1)S(1)}, bf16[1,768,2048]{2,1,0:T(8,128)(2,1)}, u32[]{:S(2)}) copy-start(bf16[1,768,2048]{2,1,0:T(8,128)(2,1)} %param.9) | copy-start | bytes 9437188
  25.4 1.2 copy-start.2
  26.5 13.2 %copy-start.1 = (bf16[1,768,2048]{2,1,0:T(8,128)(2,1)S(1)}, bf16[1,768,2048]{2,1,0:T(8,128)(2,1)}, u32[]{:S(2)}) copy-start(bf16[1,768,2048]{2,1,0:T(8,128)(2,1)} %param.9) | copy-start | bytes 9437188
  26.5 13.2 %copy-start.3 = (bf16[1,1,16,36,768]{4,2,3,1,0:T(8,128)(2,1)S(1)}, bf16[1,1,16,36,768]{4,2,3,1,0:T(8,128)(2,1)}, u32[]{:S(2)}) copy-start(bf16[1,1,16,36,768]{4,2,3,1,0:T(8,128)(2,1)} %param.8) | copy-start | bytes 2654212
  26.6 13.2 %copy-start.6 = (bf16[48,2176]{1,0:T(8,128)(2,1)S(1)}, bf16[48,2176]{1,0:T(8,128)(2,1)}, u32[]{:S(2)}) copy-start(bf16[48,2176]{1,0:T(8,128)(2,1)} %copy-done.5) | copy-start | bytes 626692
  37.1 2.6 %collective-permute-start.10 = (bf16[576,768]{1,0:T(8,128)(2,1)}, bf16[576,768]{1,0:T(8,128)(2,1)S(1)}, u32[]{:S(2)}, u32[]{:S(2)}) collective-permute-start(bf16[576,768]{1,0:T(8,128)(2,1)} %collective-permute-done.9.refs_8_.refs_5_), channel_id=1, source_target_pairs={{0,1},{1,0},{2,3},{3,2},{4,5},{5,4},{6,7},{7,6},{8,9},{9,8},{10,11... | collective-permute-start | bytes 2654216 | tf_op jit(solution)/shard_map/ppermute | solution.py:441
  37.1 12.3 %collective-permute-start.12 = (bf16[2,48,2176]{2,1,0:T(8,128)(2,1)}, bf16[2,48,2176]{2,1,0:T(8,128)(2,1)S(1)}, u32[]{:S(2)}, u32[]{:S(2)}) collective-permute-start(bf16[2,48,2176]{2,1,0:T(8,128)(2,1)} %collective-permute-done.8.refs_2_.refs_4_), channel_id=1, source_target_pairs={{0,2},{1,3},{4,0},{5,1},{8,4},{9,5},{12,8},{13,9},{14,12},{15,13},... | collective-permute-start | bytes 1253384 | tf_op jit(solution)/shard_map/ppermute | solution.py:438
  37.9 12.3 %collective-permute-start.11 = (bf16[2,48,2176]{2,1,0:T(8,128)(2,1)}, bf16[2,48,2176]{2,1,0:T(8,128)(2,1)S(1)}, u32[]{:S(2)}, u32[]{:S(2)}) collective-permute-start(bf16[2,48,2176]{2,1,0:T(8,128)(2,1)} %collective-permute-done.7.refs_1_.refs_3_), channel_id=1, source_target_pairs={{0,4},{1,5},{4,8},{5,9},{8,12},{9,13},{12,14},{13,15},{14,10},{15,... | collective-permute-start | bytes 1253384 | tf_op jit(solution)/shard_map/ppermute | solution.py:438
  49.4 9.5 %collective-permute-start.14 = (bf16[1,48,2176]{2,1,0:T(8,128)(2,1)S(1)}, bf16[1,48,2176]{2,1,0:T(8,128)(2,1)S(1)}, u32[]{:S(2)}, u32[]{:S(2)}) collective-permute-start(bf16[1,48,2176]{2,1,0:T(8,128)(2,1)S(1)} %slice.7), channel_id=1, source_target_pairs={{0,2},{1,3},{4,0},{5,1},{8,4},{9,5},{12,8},{13,9},{14,12},{15,13},... | collective-permute-start | bytes 626696 | tf_op jit(solution)/shard_map/ppermute | solution.py:438
  50.3 8.6 %collective-permute-start.13 = (bf16[1,48,2176]{2,1,0:T(8,128)(2,1)S(1)}, bf16[1,48,2176]{2,1,0:T(8,128)(2,1)S(1)}, u32[]{:S(2)}, u32[]{:S(2)}) collective-permute-start(bf16[1,48,2176]{2,1,0:T(8,128)(2,1)S(1)} %slice.6), channel_id=1, source_target_pairs={{0,4},{1,5},{4,8},{5,9},{8,12},{9,13},{12,14},{13,15},{14,10},{15,... | collective-permute-start | bytes 626696 | tf_op jit(solution)/shard_map/ppermute | solution.py:438
  51.7 27.0 %collective-permute-start.18 = (bf16[2,240,768]{2,1,0:T(8,128)(2,1)S(1)}, bf16[2,240,768]{2,1,0:T(8,128)(2,1)S(1)}, u32[]{:S(2)}, u32[]{:S(2)}) collective-permute-start(bf16[2,240,768]{2,1,0:T(8,128)(2,1)S(1)} %get-tuple-element.85), channel_id=1, source_target_pairs={{0,16},{16,0},{1,17},{17,1},{2,18},{18,2},{3,19},{19,3},{4,20},{20... | collective-permute-start | bytes 2211848 | tf_op jit(solution)/shard_map/ppermute | solution.py:435
  64.8 6.0 %collective-permute-start.17 = (bf16[1,48,2176]{2,1,0:T(8,128)(2,1)S(1)}, bf16[1,48,2176]{2,1,0:T(8,128)(2,1)S(1)}, u32[]{:S(2)}, u32[]{:S(2)}) collective-permute-start(bf16[1,48,2176]{2,1,0:T(8,128)(2,1)S(1)} %bitcast.45), channel_id=1, source_target_pairs={{0,2},{1,3},{4,0},{5,1},{8,4},{9,5},{12,8},{13,9},{14,12},{15,13},... | collective-permute-start | bytes 626696 | tf_op jit(solution)/shard_map/ppermute | solution.py:438
  66.4 6.1 %collective-permute-start.15 = (bf16[1,48,2176]{2,1,0:T(8,128)(2,1)S(1)}, bf16[1,48,2176]{2,1,0:T(8,128)(2,1)S(1)}, u32[]{:S(2)}, u32[]{:S(2)}) collective-permute-start(bf16[1,48,2176]{2,1,0:T(8,128)(2,1)S(1)} %bitcast.44), channel_id=1, source_target_pairs={{0,4},{1,5},{4,8},{5,9},{8,12},{9,13},{12,14},{13,15},{14,10},{15,... | collective-permute-start | bytes 626696 | tf_op jit(solution)/shard_map/ppermute | solution.py:438
  66.9 10.1 %collective-permute-start.19 = (bf16[2,96,768]{2,1,0:T(8,128)(2,1)S(1)}, bf16[2,96,768]{2,1,0:T(8,128)(2,1)S(1)}, u32[]{:S(2)}, u32[]{:S(2)}) collective-permute-start(bf16[2,96,768]{2,1,0:T(8,128)(2,1)S(1)} %get-tuple-element.86), channel_id=1, source_target_pairs={{0,16},{16,0},{1,17},{17,1},{2,18},{18,2},{3,19},{19,3},{4,20},{20... | collective-permute-start | bytes 884744 | tf_op jit(solution)/shard_map/ppermute | solution.py:435
  70.9 13.2 %collective-permute-start.22 = (bf16[2,48,2176]{2,1,0:T(8,128)(2,1)S(1)}, bf16[2,48,2176]{2,1,0:T(8,128)(2,1)S(1)}, u32[]{:S(2)}, u32[]{:S(2)}) collective-permute-start(bf16[2,48,2176]{2,1,0:T(8,128)(2,1)S(1)} %sums.8), channel_id=1, source_target_pairs={{0,2},{1,3},{4,0},{5,1},{8,4},{9,5},{12,8},{13,9},{14,12},{15,13},... | collective-permute-start | bytes 1253384 | tf_op jit(solution)/shard_map/ppermute | solution.py:438
  72.6 11.6 %collective-permute-start.16 = (bf16[2,48,2176]{2,1,0:T(8,128)(2,1)S(1)}, bf16[2,48,2176]{2,1,0:T(8,128)(2,1)S(1)}, u32[]{:S(2)}, u32[]{:S(2)}) collective-permute-start(bf16[2,48,2176]{2,1,0:T(8,128)(2,1)S(1)} %sums.6), channel_id=1, source_target_pairs={{0,4},{1,5},{4,8},{5,9},{8,12},{9,13},{12,14},{13,15},{14,10},{15,... | collective-permute-start | bytes 1253384 | tf_op jit(solution)/shard_map/ppermute | solution.py:438
  73.1 5.6 %collective-permute-start.20 = (bf16[2,48,768]{2,1,0:T(8,128)(2,1)S(1)}, bf16[2,48,768]{2,1,0:T(8,128)(2,1)S(1)}, u32[]{:S(2)}, u32[]{:S(2)}) collective-permute-start(bf16[2,48,768]{2,1,0:T(8,128)(2,1)S(1)} %get-tuple-element.87), channel_id=1, source_target_pairs={{0,16},{16,0},{1,17},{17,1},{2,18},{18,2},{3,19},{19,3},{4,20},{20... | collective-permute-start | bytes 442376 | tf_op jit(solution)/shard_map/ppermute | solution.py:435
  84.1 14.6 %collective-permute-start.24 = (bf16[768,2048]{1,0:T(8,128)(2,1)S(1)}, bf16[768,2048]{1,0:T(8,128)(2,1)S(1)}, u32[]{:S(2)}, u32[]{:S(2)}) collective-permute-start(bf16[768,2048]{1,0:T(8,128)(2,1)S(1)} %weight_product.2), channel_id=1, source_target_pairs={{0,1},{1,0},{2,3},{3,2},{4,5},{5,4},{6,7},{7,6},{8,9},{9,8},{10,11... | collective-permute-start | bytes 9437192 | tf_op jit(solution)/shard_map/ppermute | solution.py:441
  84.3 12.1 %collective-permute-start.23 = (bf16[2,48,2176]{2,1,0:T(8,128)(2,1)S(1)}, bf16[2,48,2176]{2,1,0:T(8,128)(2,1)S(1)}, u32[]{:S(2)}, u32[]{:S(2)}) collective-permute-start(bf16[2,48,2176]{2,1,0:T(8,128)(2,1)S(1)} %sums.9), channel_id=1, source_target_pairs={{0,2},{1,3},{4,0},{5,1},{8,4},{9,5},{12,8},{13,9},{14,12},{15,13},... | collective-permute-start | bytes 1253384 | tf_op jit(solution)/shard_map/ppermute | solution.py:438
  85.5 12.1 %collective-permute-start.21 = (bf16[2,48,2176]{2,1,0:T(8,128)(2,1)S(1)}, bf16[2,48,2176]{2,1,0:T(8,128)(2,1)S(1)}, u32[]{:S(2)}, u32[]{:S(2)}) collective-permute-start(bf16[2,48,2176]{2,1,0:T(8,128)(2,1)S(1)} %sums.7), channel_id=1, source_target_pairs={{0,4},{1,5},{4,8},{5,9},{8,12},{9,13},{12,14},{13,15},{14,10},{15,... | collective-permute-start | bytes 1253384 | tf_op jit(solution)/shard_map/ppermute | solution.py:438
  87.9 22.5 %collective-permute-start.28 = (bf16[576,768]{1,0:T(8,128)(2,1)S(1)}, bf16[576,768]{1,0:T(8,128)(2,1)}, u32[]{:S(2)}, u32[]{:S(2)}) collective-permute-start(bf16[576,768]{1,0:T(8,128)(2,1)S(1)} %get-tuple-element.127), channel_id=1, source_target_pairs={{0,1},{1,0},{2,3},{3,2},{4,5},{5,4},{6,7},{7,6},{8,9},{9,8},{10,11... | collective-permute-start | bytes 2654216 | tf_op jit(solution)/shard_map/ppermute | solution.py:441
  96.5 11.3 %collective-permute-start.26 = (bf16[2,48,2176]{2,1,0:T(8,128)(2,1)S(1)}, bf16[2,48,2176]{2,1,0:T(8,128)(2,1)S(1)}, u32[]{:S(2)}, u32[]{:S(2)}) collective-permute-start(bf16[2,48,2176]{2,1,0:T(8,128)(2,1)S(1)} %sums.11), channel_id=1, source_target_pairs={{0,2},{1,3},{4,0},{5,1},{8,4},{9,5},{12,8},{13,9},{14,12},{15,13},... | collective-permute-start | bytes 1253384 | tf_op jit(solution)/shard_map/ppermute | solution.py:438
  97.7 12.5 %copy-start.8 = (s32[48,8]{0,1:T(8,128)S(1)}, s32[48,8]{0,1:T(8,128)}, u32[]{:S(2)}) copy-start(s32[48,8]{0,1:T(8,128)} %param.6) | copy-start | bytes 4612
  97.7 11.0 %collective-permute-start.25 = (bf16[2,48,2176]{2,1,0:T(8,128)(2,1)S(1)}, bf16[2,48,2176]{2,1,0:T(8,128)(2,1)S(1)}, u32[]{:S(2)}, u32[]{:S(2)}) collective-permute-start(bf16[2,48,2176]{2,1,0:T(8,128)(2,1)S(1)} %sums.10), channel_id=1, source_target_pairs={{0,4},{1,5},{4,8},{5,9},{8,12},{9,13},{12,14},{13,15},{14,10},{15,... | collective-permute-start | bytes 1253384 | tf_op jit(solution)/shard_map/ppermute | solution.py:438
  108.9 5.9 %collective-permute-start.27 = (bf16[48,2176]{1,0:T(8,128)(2,1)S(1)}, bf16[48,2176]{1,0:T(8,128)(2,1)S(1)}, u32[]{:S(2)}, u32[]{:S(2)}) collective-permute-start(bf16[48,2176]{1,0:T(8,128)(2,1)S(1)} %get-tuple-element.124), channel_id=1, source_target_pairs={{0,16},{16,0},{1,17},{17,1},{2,18},{18,2},{3,19},{19,3},{4,20},{20... | collective-permute-start | bytes 626696 | tf_op jit(solution)/shard_map/ppermute | solution.py:435

commit v12 on v11

--- a/solution.py
+++ b/solution.py
@@ -485,41 +485,31 @@
                 if d == 0:
                     own_back.append(back[0])
                     facts.append(fact)
-                else:
-                    sent_back[d - 1].append(shift(back[d], -d))
+                    continue
+                sent_back[d - 1].append(shift(after(back[d], *blocks.get(half, ())), -d))
             return made[0]
 
-        both = lambda offs: [(off, d) for d in range(n_dp) for off in offs]
-        gate = ()
+        near = offsets[: 2 * min(2, half - 1) + 1]
         for step in range(1, half):
             if step == 1:
                 blocks[-1] = jnp.concatenate(halves[1], axis=0)
                 blocks[1] = jnp.concatenate(halves[-1], axis=0)
             else:
-                sent = blocks[1 - step], blocks[step - 1]
-                if gate:
-                    sent = after(sent[0], *gate), after(sent[1], *gate)
-                blocks[-step] = ring_send(sent[0], 1)
-                blocks[step] = ring_send(sent[1], -1)
-            if step == 1:
-                following = [(off, 0) for off in offsets[:3]]
-            elif step == 2:
-                following = [(off, d) for d in range(n_dp) for off in offsets[:5] if d > 0 or off not in offsets[:3]]
-            else:
-                following = both([-step, step])
-            if step == half - 1:
-                break
-            if step > 1:
-                gate = (ready,)
-            if step == 2:
-                for d in range(1, n_dp):
-                    value = hiddens[d][0]
-                    hiddens[d] = value, swap(after(value, blocks[-step], blocks[step], ready))
-            ready = work(following)
-        sent = after(blocks[1 - half], ready)[:per], after(blocks[half - 1], ready)[per:]
+                blocks[-step] = ring_send(blocks[1 - step], 1)
+                blocks[step] = ring_send(blocks[step - 1], -1)
+            if step == min(2, half - 1):
+                ready = work([(off, 0) for off in near])
+        arrived = blocks[1 - half], blocks[half - 1]
+        sent = after(arrived[0], ready)[:per], after(arrived[1], ready)[per:]
         blocks[half] = [ring_send(sent[0], 1), ring_send(sent[1], -1)]
-        ready = work(following)
-        work(both([half]), ready)
+        for d in range(1, n_dp):
+            value = hiddens[d][0]
+            hiddens[d] = value, swap(after(value, ready, *arrived))
+        later = [[(off, d) for off in near for d in range(1, n_dp)]]
+        later.append([(off, d) for off in offsets for d in range(n_dp) if off not in near])
+        for items in later:
+            for at in range(0, len(items), 12):
+                ready = work(sorted(items[at : at + 12], key=lambda item: item[1]), ready)
 
         carry = {}
 
@@ -542,9 +532,9 @@
         hop_on(half)
         second = hop_on(half - 1)
         other = weight_product(
-            [after(refs[0], *sending, *[value for sent in sent_back for value in sent])] + refs[1:], layout, scaleds, 1, jnp.bfloat16, width
+            [after(refs[0], *sending, *[sent[0] for sent in sent_back])] + refs[1:], layout, scaleds, 1, jnp.bfloat16, width
         )
-        swapped = swap(after(other, *second))
+        swapped = swap(after(other, *second, *[sent[-1] for sent in sent_back]))
         third = hop_on(half - 2, other)
         spread, spread_other = spread_product(
             [after(facts[0][0], *second)] + [fact[0] for fact in facts[1:]],

time: 117 us -> 116 us (level)
  waiting for transfers between devices: 32.4 us -> 38.1 us
  Pallas kernels: 42.3 us -> 38.5 us
  local copies, waits for them, and re-layouts: 10.4 us -> 7.93 us
    ppermute x18, waiting for transfers between devices: 17.1 us -> 27.3 us  [ring_send(): return lax.ppermute(value, 'expert', forward if step > 0 else backward)]
    pallas_call x4 -> x3, Pallas kernels: 26.4 us -> 22 us  [block_product(): pl.pallas_call(functools.partial(block_kernel, plan, len(blocks), n_dp, n...]
    ppermute x6 -> x5, waiting for transfers between devices: 14.7 us -> 10.4 us  [shift(): lax.ppermute(value, 'dp', [(i, (i + step) % n_dp) for i in range(n_dp)])]
    ppermute x6 -> x5, starting transfers between devices: 7.91 us -> 6.31 us  [shift(): lax.ppermute(value, 'dp', [(i, (i + step) % n_dp) for i in range(n_dp)])]
    unnamed x24 -> x30, local copies, waits for them, and re-layouts: 8.26 us -> 7.16 us
  transfers between devices with their start and end apart: 29 -> 28, of which waited for: 13 -> 12; matrix products, arithmetic and copies ran while one was open for 5% -> 3% of each run, Pallas kernels for 35% -> 32%
where the time goes in v12:
time: 116 us; the launch traced here: 115 us
  Pallas kernels  38.5 us (33%)
  waiting for transfers between devices  38.1 us (33%)
  starting transfers between devices  27.5 us (24%)
  local copies, waits for them, and re-layouts  7.93 us (7%)
  other arithmetic  2.29 us (2%)
    ppermute x18, waiting for transfers between devices, ring_send(): return lax.ppermute(value, 'expert', forward if step > 0 else backward)  27.3 us
    pallas_call x3, Pallas kernels, block_product(): pl.pallas_call(functools.partial(block_kernel, plan, len(blocks), n_dp, n...  22 us
    ppermute x18, starting transfers between devices, ring_send(): return lax.ppermute(value, 'expert', forward if step > 0 else backward)  20.6 us
    pallas_call x2, Pallas kernels, weight_product(): pl.pallas_call(functools.partial(weight_kernel, len(blocks), len(scaleds)...  11.8 us
    ppermute x5, waiting for transfers between devices, shift(): lax.ppermute(value, 'dp', [(i, (i + step) % n_dp) for i in range(n_dp)])  10.4 us
    unnamed x30, local copies, waits for them, and re-layouts  7.16 us
    ppermute x5, starting transfers between devices, shift(): lax.ppermute(value, 'dp', [(i, (i + step) % n_dp) for i in range(n_dp)])  6.31 us
  transfers between devices with their start and end apart: 28, of which 12 were waited for; matrix products, arithmetic and copies ran while one was open for 3% of the time, Pallas kernels for 32%

profile of v12, /device:TPU:0, one launch (start us, length us, event | category | flops | bytes accessed | tf_op | source)
XLA Modules:
  0.0 115.1 jit_solution(4407667291902861797)
XLA Ops:
  0.6 0.5 collective-permute-start.8
  1.2 1.0 copy-done
  2.1 0.7 copy-done.6
  2.8 0.7 copy-done.8
  3.5 0.5 pack.1
  4.0 0.0 copy-start.1
  4.0 2.6 %collective-permute-start.1 = (bf16[48,2176]{1,0:T(8,128)(2,1)S(1)}, bf16[48,2176]{1,0:T(8,128)(2,1)S(1)}, u32[]{:S(2)}, u32[]{:S(2)}) collective-permute-start(bf16[48,2176]{1,0:T(8,128)(2,1)S(1)} %get-tuple-element.58), channel_id=1, source_target_pairs={{0,16},{16,0},{1,17},{17,1},{2,18},{18,2},{3,19},{19,3},{4,20},{20... | collective-permute-start | bytes 626696 | tf_op jit(solution)/shard_map/ppermute | solution.py:435
  6.6 1.5 %collective-permute-start.3 = (bf16[1,48,2176]{2,1,0:T(8,128)(2,1)S(1)}, bf16[1,48,2176]{2,1,0:T(8,128)(2,1)S(1)}, u32[]{:S(2)}, u32[]{:S(2)}) collective-permute-start(bf16[1,48,2176]{2,1,0:T(8,128)(2,1)S(1)} %bitcast.21), channel_id=1, source_target_pairs={{0,2},{1,3},{4,0},{5,1},{8,4},{9,5},{12,8},{13,9},{14,12},{15,13},... | collective-permute-start | bytes 626696 | tf_op jit(solution)/shard_map/ppermute | solution.py:438
  8.1 0.5 collective-permute-start
  8.6 3.8 %collective-permute-done.1 = bf16[48,2176]{1,0:T(8,128)(2,1)S(1)} collective-permute-done((bf16[48,2176]{1,0:T(8,128)(2,1)S(1)}, bf16[48,2176]{1,0:T(8,128)(2,1)S(1)}, u32[]{:S(2)}, u32[]{:S(2)}) %collective-permute-start.1) | collective-permute-done | bytes 208928 | tf_op jit(solution)/shard_map/ppermute | solution.py:435
  12.4 1.8 %collective-permute-start.4 = (bf16[1,48,2176]{2,1,0:T(8,128)(2,1)S(1)}, bf16[1,48,2176]{2,1,0:T(8,128)(2,1)S(1)}, u32[]{:S(2)}, u32[]{:S(2)}) collective-permute-start(bf16[1,48,2176]{2,1,0:T(8,128)(2,1)S(1)} %bitcast.26), channel_id=1, source_target_pairs={{0,2},{1,3},{4,0},{5,1},{8,4},{9,5},{12,8},{13,9},{14,12},{15,13},... | collective-permute-start | bytes 626696 | tf_op jit(solution)/shard_map/ppermute | solution.py:438
  14.2 1.3 %collective-permute-start.2 = (bf16[1,48,2176]{2,1,0:T(8,128)(2,1)S(1)}, bf16[1,48,2176]{2,1,0:T(8,128)(2,1)S(1)}, u32[]{:S(2)}, u32[]{:S(2)}) collective-permute-start(bf16[1,48,2176]{2,1,0:T(8,128)(2,1)S(1)} %bitcast.27), channel_id=1, source_target_pairs={{0,4},{1,5},{4,8},{5,9},{8,12},{9,13},{12,14},{13,15},{14,10},{15,... | collective-permute-start | bytes 626696 | tf_op jit(solution)/shard_map/ppermute | solution.py:438
  15.4 0.7 collective-permute-start.9
  16.2 3.2 %collective-permute-done.4 = bf16[1,48,2176]{2,1,0:T(8,128)(2,1)S(1)} collective-permute-done((bf16[1,48,2176]{2,1,0:T(8,128)(2,1)S(1)}, bf16[1,48,2176]{2,1,0:T(8,128)(2,1)S(1)}, u32[]{:S(2)}, u32[]{:S(2)}) %collective-permute-start.4) | collective-permute-done | bytes 208928 | tf_op jit(solution)/shard_map/ppermute | solution.py:438
  19.4 1.6 %collective-permute-start.6 = (bf16[2,48,2176]{2,1,0:T(8,128)(2,1)S(1)}, bf16[2,48,2176]{2,1,0:T(8,128)(2,1)S(1)}, u32[]{:S(2)}, u32[]{:S(2)}) collective-permute-start(bf16[2,48,2176]{2,1,0:T(8,128)(2,1)S(1)} %constant_dynamic-update-slice_fusion.2.refs_3_.refs_2_), channel_id=1, source_target_pairs={{0,2},{1,3},{4,0},{5,1},{8,4},{9,5},{12,8},{13,9},{14,12},{15,13},... | collective-permute-start | bytes 1253384 | tf_op jit(solution)/shard_map/ppermute | solution.py:438
  21.0 0.9 collective-permute-start.5
  22.0 8.1 %collective-permute-done.6.refs_5_.refs_4_ = bf16[2,48,2176]{2,1,0:T(8,128)(2,1)S(1)} collective-permute-done((bf16[2,48,2176]{2,1,0:T(8,128)(2,1)S(1)}, bf16[2,48,2176]{2,1,0:T(8,128)(2,1)S(1)}, u32[]{:S(2)}, u32[]{:S(2)}) %collective-permute-start.6) | collective-permute-done | bytes 417824 | tf_op jit(solution)/shard_map/ppermute | solution.py:438
  30.0 1.3 %collective-permute-start.11 = (bf16[2,48,2176]{2,1,0:T(8,128)(2,1)S(1)}, bf16[2,48,2176]{2,1,0:T(8,128)(2,1)S(1)}, u32[]{:S(2)}, u32[]{:S(2)}) collective-permute-start(bf16[2,48,2176]{2,1,0:T(8,128)(2,1)S(1)} %collective-permute-done.6.refs_5_.refs_4_), channel_id=1, source_target_pairs={{0,2},{1,3},{4,0},{5,1},{8,4},{9,5},{12,8},{13,9},{14,12},{15,13},... | collective-permute-start | bytes 1253384 | tf_op jit(solution)/shard_map/ppermute | solution.py:438
  31.4 0.7 collective-permute-start.10
  32.1 0.7 dynamic-slice_bitcast_fusion.refs_0_
  32.8 0.0 copy-start.9
  32.8 1.9 %copy-done.9 = bf16[1,768,2048]{2,1,0:T(8,128)(2,1)S(1)} copy-done((bf16[1,768,2048]{2,1,0:T(8,128)(2,1)S(1)}, bf16[1,768,2048]{2,1,0:T(8,128)(2,1)}, u32[]{:S(2)}) %copy-start.9) | copy-done | bytes 3145752
  34.7 1.2 %copy-done.11 = bf16[1,1,16,36,768]{4,2,3,1,0:T(8,128)(2,1)S(1)} copy-done((bf16[1,1,16,36,768]{4,2,3,1,0:T(8,128)(2,1)S(1)}, bf16[1,1,16,36,768]{4,2,3,1,0:T(8,128)(2,1)}, u32[]{:S(2)}) %copy-start.11) | copy-done | bytes 884760
  35.8 7.0 %block_product.3 = (bf16[48,2176]{1,0:T(8,128)(2,1)S(1)}, bf16[48,2176]{1,0:T(8,128)(2,1)S(1)}, bf16[48,2176]{1,0:T(8,128)(2,1)S(1)}, bf16[48,2176]{1,0:T(8,128)...) custom-call(s32[10]{0:T(128)S(1)} %dynamic-slice_bitcast_fusion.refs, ...), custom_call_target="tpu_custom_call" | custom-call | flops 3019898880 | bytes 9117696 | tf_op jit(solution)/shard_map/block_product/pallas_call | solution.py:290
  42.9 0.1 collective-permute-start.12
  43.0 1.4 %collective-permute-start.14 = (bf16[1,48,2176]{2,1,0:T(8,128)(2,1)S(1)}, bf16[1,48,2176]{2,1,0:T(8,128)(2,1)S(1)}, u32[]{:S(2)}, u32[]{:S(2)}) collective-permute-start(bf16[1,48,2176]{2,1,0:T(8,128)(2,1)S(1)} %slice.7), channel_id=1, source_target_pairs={{0,2},{1,3},{4,0},{5,1},{8,4},{9,5},{12,8},{13,9},{14,12},{15,13},... | collective-permute-start | bytes 626696 | tf_op jit(solution)/shard_map/ppermute | solution.py:438
  44.4 0.9 collective-permute-start.13
  45.3 0.3 collective-permute-done.12.refs_7_.refs_8_
  45.6 0.9 copy-done.4
  46.5 7.0 %block_product.4 = (bf16[48,2176]{1,0:T(8,128)(2,1)S(1)}, bf16[48,2176]{1,0:T(8,128)(2,1)S(1)}, bf16[48,2176]{1,0:T(8,128)(2,1)S(1)}, bf16[48,2176]{1,0:T(8,128)...) custom-call(s32[10]{0:T(128)S(1)} %dynamic-slice_bitcast_fusion.refs_0_,, ...), custom_call_target="tpu_custom_call" | custom-call | flops 3019898880 | bytes 9117696 | tf_op jit(solution)/shard_map/block_product/pallas_call | solution.py:290
  53.6 1.4 %collective-permute-start.18 = (bf16[2,240,768]{2,1,0:T(8,128)(2,1)S(1)}, bf16[2,240,768]{2,1,0:T(8,128)(2,1)S(1)}, u32[]{:S(2)}, u32[]{:S(2)}) collective-permute-start(bf16[2,240,768]{2,1,0:T(8,128)(2,1)S(1)} %get-tuple-element.76), channel_id=1, source_target_pairs={{0,16},{16,0},{1,17},{17,1},{2,18},{18,2},{3,19},{19,3},{4,20},{20... | collective-permute-start | bytes 2211848 | tf_op jit(solution)/shard_map/ppermute | solution.py:435
  54.9 8.1 %block_product.5 = (bf16[48,2176]{1,0:T(8,128)(2,1)S(1)}, bf16[48,2176]{1,0:T(8,128)(2,1)S(1)}, bf16[48,2176]{1,0:T(8,128)(2,1)S(1)}, bf16[48,2176]{1,0:T(8,128)...) custom-call(s32[10]{0:T(128)S(1)} %dynamic-slice_bitcast_fusion.refs, ...), custom_call_target="tpu_custom_call" | custom-call | flops 3623878656 | bytes 9682944 | tf_op jit(solution)/shard_map/block_product/pallas_call | solution.py:290
  63.0 1.6 %collective-permute-start.17 = (bf16[1,48,2176]{2,1,0:T(8,128)(2,1)S(1)}, bf16[1,48,2176]{2,1,0:T(8,128)(2,1)S(1)}, u32[]{:S(2)}, u32[]{:S(2)}) collective-permute-start(bf16[1,48,2176]{2,1,0:T(8,128)(2,1)S(1)} %bitcast.42), channel_id=1, source_target_pairs={{0,2},{1,3},{4,0},{5,1},{8,4},{9,5},{12,8},{13,9},{14,12},{15,13},... | collective-permute-start | bytes 626696 | tf_op jit(solution)/shard_map/ppermute | solution.py:438
  64.6 0.5 collective-permute-start.15
  65.1 0.7 collective-permute-start.22
  65.8 4.2 %collective-permute-done.17.refs_2_ = bf16[1,48,2176]{2,1,0:T(8,128)(2,1)S(1)} collective-permute-done((bf16[1,48,2176]{2,1,0:T(8,128)(2,1)S(1)}, bf16[1,48,2176]{2,1,0:T(8,128)(2,1)S(1)}, u32[]{:S(2)}, u32[]{:S(2)}) %collective-permute-start.17) | collective-permute-done | bytes 208928 | tf_op jit(solution)/shard_map/ppermute | solution.py:438
  70.0 0.1 sums.8
  70.1 1.6 %collective-permute-start.20 = (bf16[2,48,2176]{2,1,0:T(8,128)(2,1)S(1)}, bf16[2,48,2176]{2,1,0:T(8,128)(2,1)S(1)}, u32[]{:S(2)}, u32[]{:S(2)}) collective-permute-start(bf16[2,48,2176]{2,1,0:T(8,128)(2,1)S(1)} %sums.8), channel_id=1, source_target_pairs={{0,2},{1,3},{4,0},{5,1},{8,4},{9,5},{12,8},{13,9},{14,12},{15,13},... | collective-permute-start | bytes 1253384 | tf_op jit(solution)/shard_map/ppermute | solution.py:438
  71.6 0.1 sums.6
  71.7 0.6 collective-permute-start.16
  72.3 0.7 collective-permute-done.18.refs_6_
  73.0 5.3 %weight_product.2 = bf16[768,2048]{1,0:T(8,128)(2,1)S(1)} custom-call(bf16[1,48,2176]{2,1,0:T(8,128)(2,1)S(1)} %bitcast.24, bf16[2,48,2176]{2,1,0:T(8,128)(2,1)S(1)} %constant_dynamic-update-slice_fusion.refs_2_.refs_1_, bf16[2,48,2176]{2,1,0:T(8,128)(2,1)S(1)} %constant_dynamic-update-slice_fusion.2.refs_3_.refs_2_, ...), custom_call_target="tpu_custom_call" | custom-call | flops 2415919104 | bytes 10616832 | tf_op jit(solution)/shard_map/weight_product/pallas_call | solution.py:372
  78.3 3.4 %collective-permute-done.22.refs_7_ = bf16[2,144,768]{2,1,0:T(8,128)(2,1)S(1)} collective-permute-done((bf16[2,144,768]{2,1,0:T(8,128)(2,1)S(1)}, bf16[2,144,768]{2,1,0:T(8,128)(2,1)S(1)}, u32[]{:S(2)}, u32[]{:S(2)}) %collective-permute-start.22) | collective-permute-done | bytes 442400 | tf_op jit(solution)/shard_map/ppermute | solution.py:435
  81.6 0.4 collective-permute-done.16.refs_2_
  82.0 0.1 sums.9
  82.1 1.7 %collective-permute-start.21 = (bf16[2,48,2176]{2,1,0:T(8,128)(2,1)S(1)}, bf16[2,48,2176]{2,1,0:T(8,128)(2,1)S(1)}, u32[]{:S(2)}, u32[]{:S(2)}) collective-permute-start(bf16[2,48,2176]{2,1,0:T(8,128)(2,1)S(1)} %sums.9), channel_id=1, source_target_pairs={{0,2},{1,3},{4,0},{5,1},{8,4},{9,5},{12,8},{13,9},{14,12},{15,13},... | collective-permute-start | bytes 1253384 | tf_op jit(solution)/shard_map/ppermute | solution.py:438
  83.8 0.1 sums.7
  83.9 0.7 collective-permute-start.19
  84.6 2.2 %spread_product.1 = (bf16[576,768]{1,0:T(8,128)(2,1)S(1)}, bf16[576,768]{1,0:T(8,128)(2,1)}) custom-call(s32[240,2]{1,0:T(8,128)S(1)} %get-tuple-element.94.refs_0_, s32[144,2]{1,0:T(8,128)S(1)} %get-tuple-element.95.refs_1_, f32[240,2]{1,0:T(8,128)S(1)} %get-tuple-element.96.refs_2_, f32[144,2]{1,0:T(8,128)S(1)} %get-tuple-element.97.refs_3_, ...), custom_call_target="tpu_custom_call" | custom-call | flops 679477248 | bytes 3538944 | tf_op jit(solution)/shard_map/spread_product/pallas_call | solution.py:337
  86.8 7.4 %collective-permute-done.21.refs_2_ = bf16[2,48,2176]{2,1,0:T(8,128)(2,1)S(1)} collective-permute-done((bf16[2,48,2176]{2,1,0:T(8,128)(2,1)S(1)}, bf16[2,48,2176]{2,1,0:T(8,128)(2,1)S(1)}, u32[]{:S(2)}, u32[]{:S(2)}) %collective-permute-start.21) | collective-permute-done | bytes 417824 | tf_op jit(solution)/shard_map/ppermute | solution.py:438
  94.2 0.1 sums.11
  94.3 1.7 %collective-permute-start.25 = (bf16[2,48,2176]{2,1,0:T(8,128)(2,1)S(1)}, bf16[2,48,2176]{2,1,0:T(8,128)(2,1)S(1)}, u32[]{:S(2)}, u32[]{:S(2)}) collective-permute-start(bf16[2,48,2176]{2,1,0:T(8,128)(2,1)S(1)} %sums.11), channel_id=1, source_target_pairs={{0,2},{1,3},{4,0},{5,1},{8,4},{9,5},{12,8},{13,9},{14,12},{15,13},... | collective-permute-start | bytes 1253384 | tf_op jit(solution)/shard_map/ppermute | solution.py:438
  96.0 0.1 sums.10
  96.1 0.5 collective-permute-start.24
  96.6 6.5 %weight_product.3 = f32[768,2048]{1,0:T(8,128)} custom-call(bf16[1,48,2176]{2,1,0:T(8,128)(2,1)S(1)} %bitcast.25, bf16[2,48,2176]{2,1,0:T(8,128)(2,1)S(1)} %constant_dynamic-update-slice_fusion.refs_2_.refs_1_, bf16[2,48,2176]{2,1,0:T(8,128)(2,1)S(1)} %constant_dynamic-update-slice_fusion.2.refs_3_.refs_2_, ...), custom_call_target="tpu_custom_call" | custom-call | flops 2415919104 | bytes 10616832 | tf_op jit(solution)/shard_map/weight_product/pallas_call | solution.py:372
  103.1 2.6 %collective-permute-done.25.refs_3_ = bf16[2,48,2176]{2,1,0:T(8,128)(2,1)S(1)} collective-permute-done((bf16[2,48,2176]{2,1,0:T(8,128)(2,1)S(1)}, bf16[2,48,2176]{2,1,0:T(8,128)(2,1)S(1)}, u32[]{:S(2)}, u32[]{:S(2)}) %collective-permute-start.25) | collective-permute-done | bytes 417824 | tf_op jit(solution)/shard_map/ppermute | solution.py:438
  105.7 1.5 %collective-permute-done.24.refs_2_ = bf16[2,48,2176]{2,1,0:T(8,128)(2,1)S(1)} collective-permute-done((bf16[2,48,2176]{2,1,0:T(8,128)(2,1)S(1)}, bf16[2,48,2176]{2,1,0:T(8,128)(2,1)S(1)}, u32[]{:S(2)}, u32[]{:S(2)}) %collective-permute-start.24) | collective-permute-done | bytes 417824 | tf_op jit(solution)/shard_map/ppermute | solution.py:438
  107.2 0.2 close.1
  107.3 0.9 collective-permute-start.26
  108.2 0.1 copy.10.ids
  108.3 2.3 %add.8 = bf16[576,768]{1,0:T(8,128)(2,1)} add(bf16[576,768]{1,0:T(8,128)(2,1)S(1)} %get-tuple-element.100, bf16[576,768]{1,0:T(8,128)(2,1)} %collective-permute-done.27) | non-fusion elementwise | flops 442368 | bytes 2654208 | tf_op jit(solution)/shard_map/add | solution.py:545
  110.6 2.6 %collective-permute-done.26.refs_1_ = bf16[48,2176]{1,0:T(8,128)(2,1)S(1)} collective-permute-done((bf16[48,2176]{1,0:T(8,128)(2,1)S(1)}, bf16[48,2176]{1,0:T(8,128)(2,1)S(1)}, u32[]{:S(2)}, u32[]{:S(2)}) %collective-permute-start.26) | collective-permute-done | bytes 208928 | tf_op jit(solution)/shard_map/ppermute | solution.py:435
  113.2 1.3 %home.1 = (bf16[48,4096]{1,0:T(8,128)(2,1)}, f32[48,8]{1,0:T(8,128)S(1)}) custom-call(s32[1]{0:T(128)} %bitcast.where, s32[48,8]{1,0:T(8,128)S(1)} %copy.10.ids, bf16[48,2176]{1,0:T(8,128)(2,1)S(1)} %get-tuple-element.105.refs_0_, bf16[48,2176]{1,0:T(8,128)(2,1)S(1)} %collective-permute-done.26.refs_1_), custom_call_target="tpu_custom_call" | custom-call | tf_op jit(solution)/shard_map/home/pallas_call | solution.py:172
  114.5 0.7 copy.11
  (43 shorter events, 0.2 us)
Async XLA Ops:
  0.6 32.1 %collective-permute-start.8 = (bf16[768,2048]{1,0:T(8,128)(2,1)}, bf16[768,2048]{1,0:T(8,128)(2,1)}, u32[]{:S(2)}, u32[]{:S(2)}) collective-permute-start(bf16[768,2048]{1,0:T(8,128)(2,1)} %bitcast.33), channel_id=1, source_target_pairs={{0,1},{1,0},{2,3},{3,2},{4,5},{5,4},{6,7},{7,6},{8,9},{9,8},{10,11... | collective-permute-start | bytes 9437192 | tf_op jit(solution)/shard_map/ppermute | solution.py:441
  1.1 1.0 copy-start
  2.1 0.7 copy-start.6
  2.8 0.7 copy-start.8
  4.0 38.9 %copy-start.1 = (bf16[48,2176]{1,0:T(8,128)(2,1)}, bf16[48,2176]{1,0:T(8,128)(2,1)S(1)}, u32[]{:S(2)}) copy-start(bf16[48,2176]{1,0:T(8,128)(2,1)S(1)} %get-tuple-element.57) | copy-start | bytes 626692
  4.0 8.4 %collective-permute-start.1 = (bf16[48,2176]{1,0:T(8,128)(2,1)S(1)}, bf16[48,2176]{1,0:T(8,128)(2,1)S(1)}, u32[]{:S(2)}, u32[]{:S(2)}) collective-permute-start(bf16[48,2176]{1,0:T(8,128)(2,1)S(1)} %get-tuple-element.58), channel_id=1, source_target_pairs={{0,16},{16,0},{1,17},{17,1},{2,18},{18,2},{3,19},{19,3},{4,20},{20... | collective-permute-start | bytes 626696 | tf_op jit(solution)/shard_map/ppermute | solution.py:435
  6.6 7.6 %collective-permute-start.3 = (bf16[1,48,2176]{2,1,0:T(8,128)(2,1)S(1)}, bf16[1,48,2176]{2,1,0:T(8,128)(2,1)S(1)}, u32[]{:S(2)}, u32[]{:S(2)}) collective-permute-start(bf16[1,48,2176]{2,1,0:T(8,128)(2,1)S(1)} %bitcast.21), channel_id=1, source_target_pairs={{0,2},{1,3},{4,0},{5,1},{8,4},{9,5},{12,8},{13,9},{14,12},{15,13},... | collective-permute-start | bytes 626696 | tf_op jit(solution)/shard_map/ppermute | solution.py:438
  8.1 7.3 %collective-permute-start = (bf16[1,48,2176]{2,1,0:T(8,128)(2,1)S(1)}, bf16[1,48,2176]{2,1,0:T(8,128)(2,1)S(1)}, u32[]{:S(2)}, u32[]{:S(2)}) collective-permute-start(bf16[1,48,2176]{2,1,0:T(8,128)(2,1)S(1)} %bitcast.22), channel_id=1, source_target_pairs={{0,4},{1,5},{4,8},{5,9},{8,12},{9,13},{12,14},{13,15},{14,10},{15,... | collective-permute-start | bytes 626696 | tf_op jit(solution)/shard_map/ppermute | solution.py:438
  8.6 24.2 %collective-permute-start.7 = (bf16[576,768]{1,0:T(8,128)(2,1)}, bf16[576,768]{1,0:T(8,128)(2,1)}, u32[]{:S(2)}, u32[]{:S(2)}) collective-permute-start(bf16[576,768]{1,0:T(8,128)(2,1)} %bitcast.37), channel_id=1, source_target_pairs={{0,1},{1,0},{2,3},{3,2},{4,5},{5,4},{6,7},{7,6},{8,9},{9,8},{10,11... | collective-permute-start | bytes 2654216 | tf_op jit(solution)/shard_map/ppermute | solution.py:441
  12.4 30.5 %copy-start.3 = (bf16[48,2176]{1,0:T(8,128)(2,1)}, bf16[48,2176]{1,0:T(8,128)(2,1)S(1)}, u32[]{:S(2)}) copy-start(bf16[48,2176]{1,0:T(8,128)(2,1)S(1)} %collective-permute-done.1) | copy-start | bytes 626692
  12.4 7.0 %collective-permute-start.4 = (bf16[1,48,2176]{2,1,0:T(8,128)(2,1)S(1)}, bf16[1,48,2176]{2,1,0:T(8,128)(2,1)S(1)}, u32[]{:S(2)}, u32[]{:S(2)}) collective-permute-start(bf16[1,48,2176]{2,1,0:T(8,128)(2,1)S(1)} %bitcast.26), channel_id=1, source_target_pairs={{0,2},{1,3},{4,0},{5,1},{8,4},{9,5},{12,8},{13,9},{14,12},{15,13},... | collective-permute-start | bytes 626696 | tf_op jit(solution)/shard_map/ppermute | solution.py:438
  14.2 6.8 %collective-permute-start.2 = (bf16[1,48,2176]{2,1,0:T(8,128)(2,1)S(1)}, bf16[1,48,2176]{2,1,0:T(8,128)(2,1)S(1)}, u32[]{:S(2)}, u32[]{:S(2)}) collective-permute-start(bf16[1,48,2176]{2,1,0:T(8,128)(2,1)S(1)} %bitcast.27), channel_id=1, source_target_pairs={{0,4},{1,5},{4,8},{5,9},{8,12},{9,13},{12,14},{13,15},{14,10},{15,... | collective-permute-start | bytes 626696 | tf_op jit(solution)/shard_map/ppermute | solution.py:438
  15.4 27.4 %collective-permute-start.9 = (bf16[576,768]{1,0:T(8,128)(2,1)}, bf16[576,768]{1,0:T(8,128)(2,1)}, u32[]{:S(2)}, u32[]{:S(2)}) collective-permute-start(bf16[576,768]{1,0:T(8,128)(2,1)} %bitcast.38), channel_id=1, source_target_pairs={{0,16},{16,0},{1,17},{17,1},{2,18},{18,2},{3,19},{19,3},{4,20},{20... | collective-permute-start | bytes 2654216 | tf_op jit(solution)/shard_map/ppermute | solution.py:435
  19.4 10.6 %collective-permute-start.6 = (bf16[2,48,2176]{2,1,0:T(8,128)(2,1)S(1)}, bf16[2,48,2176]{2,1,0:T(8,128)(2,1)S(1)}, u32[]{:S(2)}, u32[]{:S(2)}) collective-permute-start(bf16[2,48,2176]{2,1,0:T(8,128)(2,1)S(1)} %constant_dynamic-update-slice_fusion.2.refs_3_.refs_2_), channel_id=1, source_target_pairs={{0,2},{1,3},{4,0},{5,1},{8,4},{9,5},{12,8},{13,9},{14,12},{15,13},... | collective-permute-start | bytes 1253384 | tf_op jit(solution)/shard_map/ppermute | solution.py:438
  21.0 10.3 %collective-permute-start.5 = (bf16[2,48,2176]{2,1,0:T(8,128)(2,1)S(1)}, bf16[2,48,2176]{2,1,0:T(8,128)(2,1)S(1)}, u32[]{:S(2)}, u32[]{:S(2)}) collective-permute-start(bf16[2,48,2176]{2,1,0:T(8,128)(2,1)S(1)} %constant_dynamic-update-slice_fusion.refs_2_.refs_1_), channel_id=1, source_target_pairs={{0,4},{1,5},{4,8},{5,9},{8,12},{9,13},{12,14},{13,15},{14,10},{15,... | collective-permute-start | bytes 1253384 | tf_op jit(solution)/shard_map/ppermute | solution.py:438
  30.0 12.8 %collective-permute-start.11 = (bf16[2,48,2176]{2,1,0:T(8,128)(2,1)S(1)}, bf16[2,48,2176]{2,1,0:T(8,128)(2,1)S(1)}, u32[]{:S(2)}, u32[]{:S(2)}) collective-permute-start(bf16[2,48,2176]{2,1,0:T(8,128)(2,1)S(1)} %collective-permute-done.6.refs_5_.refs_4_), channel_id=1, source_target_pairs={{0,2},{1,3},{4,0},{5,1},{8,4},{9,5},{12,8},{13,9},{14,12},{15,13},... | collective-permute-start | bytes 1253384 | tf_op jit(solution)/shard_map/ppermute | solution.py:438
  31.4 11.5 %collective-permute-start.10 = (bf16[2,48,2176]{2,1,0:T(8,128)(2,1)S(1)}, bf16[2,48,2176]{2,1,0:T(8,128)(2,1)S(1)}, u32[]{:S(2)}, u32[]{:S(2)}) collective-permute-start(bf16[2,48,2176]{2,1,0:T(8,128)(2,1)S(1)} %collective-permute-done.5.refs_4_.refs_3_), channel_id=1, source_target_pairs={{0,4},{1,5},{4,8},{5,9},{8,12},{9,13},{12,14},{13,15},{14,10},{15,... | collective-permute-start | bytes 1253384 | tf_op jit(solution)/shard_map/ppermute | solution.py:438
  32.8 1.9 %copy-start.9 = (bf16[1,768,2048]{2,1,0:T(8,128)(2,1)S(1)}, bf16[1,768,2048]{2,1,0:T(8,128)(2,1)}, u32[]{:S(2)}) copy-start(bf16[1,768,2048]{2,1,0:T(8,128)(2,1)} %param.9) | copy-start | bytes 9437188
  34.7 1.2 %copy-start.11 = (bf16[1,1,16,36,768]{4,2,3,1,0:T(8,128)(2,1)S(1)}, bf16[1,1,16,36,768]{4,2,3,1,0:T(8,128)(2,1)}, u32[]{:S(2)}) copy-start(bf16[1,1,16,36,768]{4,2,3,1,0:T(8,128)(2,1)} %param.8) | copy-start | bytes 2654212
  35.8 9.8 %copy-start.10 = (bf16[1,768,2048]{2,1,0:T(8,128)(2,1)S(1)}, bf16[1,768,2048]{2,1,0:T(8,128)(2,1)}, u32[]{:S(2)}) copy-start(bf16[1,768,2048]{2,1,0:T(8,128)(2,1)} %param.9) | copy-start | bytes 9437188
  42.9 2.7 %collective-permute-start.12 = (bf16[576,768]{1,0:T(8,128)(2,1)}, bf16[576,768]{1,0:T(8,128)(2,1)S(1)}, u32[]{:S(2)}, u32[]{:S(2)}) collective-permute-start(bf16[576,768]{1,0:T(8,128)(2,1)} %collective-permute-done.9.refs_6_.refs_7_), channel_id=1, source_target_pairs={{0,1},{1,0},{2,3},{3,2},{4,5},{5,4},{6,7},{7,6},{8,9},{9,8},{10,11... | collective-permute-start | bytes 2654216 | tf_op jit(solution)/shard_map/ppermute | solution.py:441
  43.0 10.5 %collective-permute-start.14 = (bf16[1,48,2176]{2,1,0:T(8,128)(2,1)S(1)}, bf16[1,48,2176]{2,1,0:T(8,128)(2,1)S(1)}, u32[]{:S(2)}, u32[]{:S(2)}) collective-permute-start(bf16[1,48,2176]{2,1,0:T(8,128)(2,1)S(1)} %slice.7), channel_id=1, source_target_pairs={{0,2},{1,3},{4,0},{5,1},{8,4},{9,5},{12,8},{13,9},{14,12},{15,13},... | collective-permute-start | bytes 626696 | tf_op jit(solution)/shard_map/ppermute | solution.py:438
  44.4 9.1 %collective-permute-start.13 = (bf16[1,48,2176]{2,1,0:T(8,128)(2,1)S(1)}, bf16[1,48,2176]{2,1,0:T(8,128)(2,1)S(1)}, u32[]{:S(2)}, u32[]{:S(2)}) collective-permute-start(bf16[1,48,2176]{2,1,0:T(8,128)(2,1)S(1)} %slice.6), channel_id=1, source_target_pairs={{0,4},{1,5},{4,8},{5,9},{8,12},{9,13},{12,14},{13,15},{14,10},{15,... | collective-permute-start | bytes 626696 | tf_op jit(solution)/shard_map/ppermute | solution.py:438
  45.6 0.9 copy-start.4
  46.5 8.4 %copy-start.12 = (bf16[1,1,16,36,768]{4,2,3,1,0:T(8,128)(2,1)S(1)}, bf16[1,1,16,36,768]{4,2,3,1,0:T(8,128)(2,1)}, u32[]{:S(2)}) copy-start(bf16[1,1,16,36,768]{4,2,3,1,0:T(8,128)(2,1)} %param.8) | copy-start | bytes 2654212
  53.5 19.4 %copy-start.2 = (bf16[48,2176]{1,0:T(8,128)(2,1)S(1)}, bf16[48,2176]{1,0:T(8,128)(2,1)}, u32[]{:S(2)}) copy-start(bf16[48,2176]{1,0:T(8,128)(2,1)} %copy-done.1) | copy-start | bytes 626692
  53.6 19.4 %copy-start.5 = (bf16[48,2176]{1,0:T(8,128)(2,1)S(1)}, bf16[48,2176]{1,0:T(8,128)(2,1)}, u32[]{:S(2)}) copy-start(bf16[48,2176]{1,0:T(8,128)(2,1)} %copy-done.3) | copy-start | bytes 626692
  53.6 19.4 %collective-permute-start.18 = (bf16[2,240,768]{2,1,0:T(8,128)(2,1)S(1)}, bf16[2,240,768]{2,1,0:T(8,128)(2,1)S(1)}, u32[]{:S(2)}, u32[]{:S(2)}) collective-permute-start(bf16[2,240,768]{2,1,0:T(8,128)(2,1)S(1)} %get-tuple-element.76), channel_id=1, source_target_pairs={{0,16},{16,0},{1,17},{17,1},{2,18},{18,2},{3,19},{19,3},{4,20},{20... | collective-permute-start | bytes 2211848 | tf_op jit(solution)/shard_map/ppermute | solution.py:435
  63.0 7.0 %collective-permute-start.17 = (bf16[1,48,2176]{2,1,0:T(8,128)(2,1)S(1)}, bf16[1,48,2176]{2,1,0:T(8,128)(2,1)S(1)}, u32[]{:S(2)}, u32[]{:S(2)}) collective-permute-start(bf16[1,48,2176]{2,1,0:T(8,128)(2,1)S(1)} %bitcast.42), channel_id=1, source_target_pairs={{0,2},{1,3},{4,0},{5,1},{8,4},{9,5},{12,8},{13,9},{14,12},{15,13},... | collective-permute-start | bytes 626696 | tf_op jit(solution)/shard_map/ppermute | solution.py:438
  64.6 7.1 %collective-permute-start.15 = (bf16[1,48,2176]{2,1,0:T(8,128)(2,1)S(1)}, bf16[1,48,2176]{2,1,0:T(8,128)(2,1)S(1)}, u32[]{:S(2)}, u32[]{:S(2)}) collective-permute-start(bf16[1,48,2176]{2,1,0:T(8,128)(2,1)S(1)} %bitcast.41), channel_id=1, source_target_pairs={{0,4},{1,5},{4,8},{5,9},{8,12},{9,13},{12,14},{13,15},{14,10},{15,... | collective-permute-start | bytes 626696 | tf_op jit(solution)/shard_map/ppermute | solution.py:438
  65.1 16.5 %collective-permute-start.22 = (bf16[2,144,768]{2,1,0:T(8,128)(2,1)S(1)}, bf16[2,144,768]{2,1,0:T(8,128)(2,1)S(1)}, u32[]{:S(2)}, u32[]{:S(2)}) collective-permute-start(bf16[2,144,768]{2,1,0:T(8,128)(2,1)S(1)} %get-tuple-element.88), channel_id=1, source_target_pairs={{0,16},{16,0},{1,17},{17,1},{2,18},{18,2},{3,19},{19,3},{4,20},{20... | collective-permute-start | bytes 1327112 | tf_op jit(solution)/shard_map/ppermute | solution.py:435
  70.1 11.6 %collective-permute-start.20 = (bf16[2,48,2176]{2,1,0:T(8,128)(2,1)S(1)}, bf16[2,48,2176]{2,1,0:T(8,128)(2,1)S(1)}, u32[]{:S(2)}, u32[]{:S(2)}) collective-permute-start(bf16[2,48,2176]{2,1,0:T(8,128)(2,1)S(1)} %sums.8), channel_id=1, source_target_pairs={{0,2},{1,3},{4,0},{5,1},{8,4},{9,5},{12,8},{13,9},{14,12},{15,13},... | collective-permute-start | bytes 1253384 | tf_op jit(solution)/shard_map/ppermute | solution.py:438
  71.7 10.3 %collective-permute-start.16 = (bf16[2,48,2176]{2,1,0:T(8,128)(2,1)S(1)}, bf16[2,48,2176]{2,1,0:T(8,128)(2,1)S(1)}, u32[]{:S(2)}, u32[]{:S(2)}) collective-permute-start(bf16[2,48,2176]{2,1,0:T(8,128)(2,1)S(1)} %sums.6), channel_id=1, source_target_pairs={{0,4},{1,5},{4,8},{5,9},{8,12},{9,13},{12,14},{13,15},{14,10},{15,... | collective-permute-start | bytes 1253384 | tf_op jit(solution)/shard_map/ppermute | solution.py:438
  82.0 14.6 %collective-permute-start.23 = (bf16[768,2048]{1,0:T(8,128)(2,1)S(1)}, bf16[768,2048]{1,0:T(8,128)(2,1)S(1)}, u32[]{:S(2)}, u32[]{:S(2)}) collective-permute-start(bf16[768,2048]{1,0:T(8,128)(2,1)S(1)} %weight_product.2), channel_id=1, source_target_pairs={{0,1},{1,0},{2,3},{3,2},{4,5},{5,4},{6,7},{7,6},{8,9},{9,8},{10,11... | collective-permute-start | bytes 9437192 | tf_op jit(solution)/shard_map/ppermute | solution.py:441
  82.1 12.1 %collective-permute-start.21 = (bf16[2,48,2176]{2,1,0:T(8,128)(2,1)S(1)}, bf16[2,48,2176]{2,1,0:T(8,128)(2,1)S(1)}, u32[]{:S(2)}, u32[]{:S(2)}) collective-permute-start(bf16[2,48,2176]{2,1,0:T(8,128)(2,1)S(1)} %sums.9), channel_id=1, source_target_pairs={{0,2},{1,3},{4,0},{5,1},{8,4},{9,5},{12,8},{13,9},{14,12},{15,13},... | collective-permute-start | bytes 1253384 | tf_op jit(solution)/shard_map/ppermute | solution.py:438
  83.9 12.1 %collective-permute-start.19 = (bf16[2,48,2176]{2,1,0:T(8,128)(2,1)S(1)}, bf16[2,48,2176]{2,1,0:T(8,128)(2,1)S(1)}, u32[]{:S(2)}, u32[]{:S(2)}) collective-permute-start(bf16[2,48,2176]{2,1,0:T(8,128)(2,1)S(1)} %sums.7), channel_id=1, source_target_pairs={{0,4},{1,5},{4,8},{5,9},{8,12},{9,13},{12,14},{13,15},{14,10},{15,... | collective-permute-start | bytes 1253384 | tf_op jit(solution)/shard_map/ppermute | solution.py:438
  86.8 21.5 %collective-permute-start.27 = (bf16[576,768]{1,0:T(8,128)(2,1)}, bf16[576,768]{1,0:T(8,128)(2,1)}, u32[]{:S(2)}, u32[]{:S(2)}) collective-permute-start(bf16[576,768]{1,0:T(8,128)(2,1)} %get-tuple-element.109), channel_id=1, source_target_pairs={{0,1},{1,0},{2,3},{3,2},{4,5},{5,4},{6,7},{7,6},{8,9},{9,8},{10,11... | collective-permute-start | bytes 2654216 | tf_op jit(solution)/shard_map/ppermute | solution.py:441
  94.3 11.3 %collective-permute-start.25 = (bf16[2,48,2176]{2,1,0:T(8,128)(2,1)S(1)}, bf16[2,48,2176]{2,1,0:T(8,128)(2,1)S(1)}, u32[]{:S(2)}, u32[]{:S(2)}) collective-permute-start(bf16[2,48,2176]{2,1,0:T(8,128)(2,1)S(1)} %sums.11), channel_id=1, source_target_pairs={{0,2},{1,3},{4,0},{5,1},{8,4},{9,5},{12,8},{13,9},{14,12},{15,13},... | collective-permute-start | bytes 1253384 | tf_op jit(solution)/shard_map/ppermute | solution.py:438
  96.1 12.1 %copy-start.7 = (s32[48,8]{0,1:T(8,128)S(1)}, s32[48,8]{0,1:T(8,128)}, u32[]{:S(2)}) copy-start(s32[48,8]{0,1:T(8,128)} %param.6) | copy-start | bytes 4612
  96.1 11.0 %collective-permute-start.24 = (bf16[2,48,2176]{2,1,0:T(8,128)(2,1)S(1)}, bf16[2,48,2176]{2,1,0:T(8,128)(2,1)S(1)}, u32[]{:S(2)}, u32[]{:S(2)}) collective-permute-start(bf16[2,48,2176]{2,1,0:T(8,128)(2,1)S(1)} %sums.10), channel_id=1, source_target_pairs={{0,4},{1,5},{4,8},{5,9},{8,12},{9,13},{12,14},{13,15},{14,10},{15,... | collective-permute-start | bytes 1253384 | tf_op jit(solution)/shard_map/ppermute | solution.py:438
  107.3 5.9 %collective-permute-start.26 = (bf16[48,2176]{1,0:T(8,128)(2,1)S(1)}, bf16[48,2176]{1,0:T(8,128)(2,1)S(1)}, u32[]{:S(2)}, u32[]{:S(2)}) collective-permute-start(bf16[48,2176]{1,0:T(8,128)(2,1)S(1)} %get-tuple-element.106), channel_id=1, source_target_pairs={{0,16},{16,0},{1,17},{17,1},{2,18},{18,2},{3,19},{19,3},{4,20},{20... | collective-permute-start | bytes 626696 | tf_op jit(solution)/shard_map/ppermute | solution.py:435

commit v13 on v12

--- a/solution.py
+++ b/solution.py
@@ -152,7 +152,7 @@
 def home_kernel(n_ex, where, ids, *refs):
     pieces, (layer, prob) = refs[:-2], refs[-2:]
     n_dp = len(pieces)
-    tok, top = ids.shape
+    top, tok = ids.shape
     width = layer.shape[1] // n_dp
     inner = jnp.zeros((tok, n_ex), jnp.float32)
     for d, piece in enumerate(pieces):
@@ -160,14 +160,23 @@
         layer[:, pl.ds(pl.multiple_of(at, 128), width)] = piece[:, :width]
         more = piece[:, width:].astype(jnp.float32)
         inner = inner + more[:, :n_ex] + more[:, n_ex : 2 * n_ex]
-    lane = lax.broadcasted_iota(jnp.int32, (tok, n_ex), 1)
+    row = lax.broadcasted_iota(jnp.int32, (n_ex, n_ex), 0)
+    col = lax.broadcasted_iota(jnp.int32, (n_ex, n_ex), 1)
+    inner = lax.dot_general(
+        (row == col).astype(jnp.float32),
+        inner,
+        (((1,), (1,)), ((), ())),
+        precision=lax.Precision.HIGHEST,
+        preferred_element_type=jnp.float32,
+    )
+    row = lax.broadcasted_iota(jnp.int32, (n_ex, tok), 0)
     for k in range(top):
-        mine = lane == ids[:, k : k + 1]
-        prob[:, k : k + 1] = jnp.sum(jnp.where(mine, inner, 0.0), axis=1, keepdims=True)
+        mine = row == ids[k : k + 1, :]
+        prob[k : k + 1, :] = jnp.sum(jnp.where(mine, inner, 0.0), axis=0, keepdims=True)
 
 
 def home(where, ids, pieces, width, n_ex):
-    tok, top = ids.shape
+    top, tok = ids.shape
     vmem = pl.BlockSpec(memory_space=pltpu.VMEM)
     return pl.pallas_call(
         functools.partial(home_kernel, n_ex),
@@ -175,7 +184,7 @@
         out_specs=[vmem] * 2,
         out_shape=[
             jax.ShapeDtypeStruct((tok, len(pieces) * width), jnp.bfloat16),
-            jax.ShapeDtypeStruct((tok, top), jnp.float32),
+            jax.ShapeDtypeStruct((top, tok), jnp.float32),
         ],
         compiler_params=kernel_memory(tok),
         name="home",
@@ -446,6 +455,7 @@
         seeds = [packed[0]] + [shift(packed[d], d) for d in range(1, n_dp)]
         blocks = {0: [jnp.stack(seeds[:per]), jnp.stack(seeds[per:])]}
         halves = {step: [ring_send(value, step) for value in blocks[0]] for step in (1, -1)}
+        halves[1][1] = after(halves[1][1], meta)
 
         sibling_weight = swap(weight)
         hidden = expert_hidden[0, 0].transpose(1, 0, 2).reshape(slots, ff)
@@ -551,8 +561,8 @@
         )
         totals = close([after(parts[0, 0], weight_grad)] + [parts[0, d] for d in range(1, n_dp)], carry[1], carry[-1])
         pieces = [totals[0]] + [shift(totals[d], -d) for d in range(1, n_dp)]
-        layer_out, prob_grad = home(where, expert_ids, pieces, width, n_ex)
-        return (layer_out, prob_grad, hidden_grad, weight_grad[None])
+        layer_out, prob_grad = home(where, expert_ids.T, pieces, width, n_ex)
+        return (layer_out, prob_grad.T, hidden_grad, weight_grad[None])
 
     return shards
 

time: 116 us -> 112 us (0.966)
  Pallas kernels: 38.5 us -> 36.1 us
  waiting for transfers between devices: 38.1 us -> 40.2 us
  local copies, waits for them, and re-layouts: 7.93 us -> 6.24 us
    unnamed x30 -> x18, local copies, waits for them, and re-layouts: 7.16 us -> 5.47 us
    ppermute x18, waiting for transfers between devices: 27.3 us -> 29 us  [ring_send(): return lax.ppermute(value, 'expert', forward if step > 0 else backward)]
  transfers between devices with their start and end apart: 28 -> 28, of which waited for: 12 -> 13; matrix products, arithmetic and copies ran while one was open for 3% -> 2% of each run, Pallas kernels for 32% -> 32%
where the time goes in v13:
time: 112 us
  waiting for transfers between devices  40.2 us (36%)
  Pallas kernels  36.1 us (32%)
  starting transfers between devices  27 us (24%)
  local copies, waits for them, and re-layouts  6.24 us (6%)
  other arithmetic  1.15 us (1%)
    ppermute x18, waiting for transfers between devices, ring_send(): return lax.ppermute(value, 'expert', forward if step > 0 else backward)  29 us
    pallas_call x3, Pallas kernels, block_product(): pl.pallas_call(functools.partial(block_kernel, plan, len(blocks), n_dp, n...  21 us
    ppermute x18, starting transfers between devices, ring_send(): return lax.ppermute(value, 'expert', forward if step > 0 else backward)  19.9 us
    pallas_call x2, Pallas kernels, weight_product(): pl.pallas_call(functools.partial(weight_kernel, len(blocks), len(scaleds)...  11.7 us
    ppermute x5, waiting for transfers between devices, shift(): lax.ppermute(value, 'dp', [(i, (i + step) % n_dp) for i in range(n_dp)])  11 us
    ppermute x5, starting transfers between devices, shift(): lax.ppermute(value, 'dp', [(i, (i + step) % n_dp) for i in range(n_dp)])  6.39 us
    unnamed x18, local copies, waits for them, and re-layouts  5.47 us
  transfers between devices with their start and end apart: 28, of which 13 were waited for; matrix products, arithmetic and copies ran while one was open for 2% of the time, Pallas kernels for 32%

profile of v13, /device:TPU:0, one launch (start us, length us, event | category | flops | bytes accessed | tf_op | source)
XLA Modules:
  0.0 111.5 jit_solution(15567358436593113042)
XLA Ops:
  0.6 0.5 collective-permute-start.8
  1.2 1.0 copy-done
  2.1 0.7 copy-done.1
  2.8 0.7 copy-done.3
  3.5 0.5 pack.1
  4.0 2.6 %collective-permute-start.1 = (bf16[48,2176]{1,0:T(8,128)(2,1)S(1)}, bf16[48,2176]{1,0:T(8,128)(2,1)S(1)}, u32[]{:S(2)}, u32[]{:S(2)}) collective-permute-start(bf16[48,2176]{1,0:T(8,128)(2,1)S(1)} %get-tuple-element.59), channel_id=1, source_target_pairs={{0,16},{16,0},{1,17},{17,1},{2,18},{18,2},{3,19},{19,3},{4,20},{20... | collective-permute-start | bytes 626696 | tf_op jit(solution)/shard_map/ppermute | solution.py:444
  6.6 1.5 %collective-permute-start.3 = (bf16[1,48,2176]{2,1,0:T(8,128)(2,1)S(1)}, bf16[1,48,2176]{2,1,0:T(8,128)(2,1)S(1)}, u32[]{:S(2)}, u32[]{:S(2)}) collective-permute-start(bf16[1,48,2176]{2,1,0:T(8,128)(2,1)S(1)} %bitcast.22), channel_id=1, source_target_pairs={{0,2},{1,3},{4,0},{5,1},{8,4},{9,5},{12,8},{13,9},{14,12},{15,13},... | collective-permute-start | bytes 626696 | tf_op jit(solution)/shard_map/ppermute | solution.py:447
  8.1 0.5 collective-permute-start
  8.6 0.0 collective-permute-start.7
  8.6 0.7 dynamic-slice_bitcast_fusion.refs_0_
  9.3 3.1 %collective-permute-done.1 = bf16[48,2176]{1,0:T(8,128)(2,1)S(1)} collective-permute-done((bf16[48,2176]{1,0:T(8,128)(2,1)S(1)}, bf16[48,2176]{1,0:T(8,128)(2,1)S(1)}, u32[]{:S(2)}, u32[]{:S(2)}) %collective-permute-start.1) | collective-permute-done | bytes 208928 | tf_op jit(solution)/shard_map/ppermute | solution.py:444
  12.4 1.8 %collective-permute-start.4 = (bf16[1,48,2176]{2,1,0:T(8,128)(2,1)S(1)}, bf16[1,48,2176]{2,1,0:T(8,128)(2,1)S(1)}, u32[]{:S(2)}, u32[]{:S(2)}) collective-permute-start(bf16[1,48,2176]{2,1,0:T(8,128)(2,1)S(1)} %bitcast.27), channel_id=1, source_target_pairs={{0,2},{1,3},{4,0},{5,1},{8,4},{9,5},{12,8},{13,9},{14,12},{15,13},... | collective-permute-start | bytes 626696 | tf_op jit(solution)/shard_map/ppermute | solution.py:447
  14.2 1.3 %collective-permute-start.2 = (bf16[1,48,2176]{2,1,0:T(8,128)(2,1)S(1)}, bf16[1,48,2176]{2,1,0:T(8,128)(2,1)S(1)}, u32[]{:S(2)}, u32[]{:S(2)}) collective-permute-start(bf16[1,48,2176]{2,1,0:T(8,128)(2,1)S(1)} %bitcast.28), channel_id=1, source_target_pairs={{0,4},{1,5},{4,8},{5,9},{8,12},{9,13},{12,14},{13,15},{14,10},{15,... | collective-permute-start | bytes 626696 | tf_op jit(solution)/shard_map/ppermute | solution.py:447
  15.4 0.7 collective-permute-start.9
  16.2 4.4 %collective-permute-done.2 = bf16[1,48,2176]{2,1,0:T(8,128)(2,1)S(1)} collective-permute-done((bf16[1,48,2176]{2,1,0:T(8,128)(2,1)S(1)}, bf16[1,48,2176]{2,1,0:T(8,128)(2,1)S(1)}, u32[]{:S(2)}, u32[]{:S(2)}) %collective-permute-start.2) | collective-permute-done | bytes 208928 | tf_op jit(solution)/shard_map/ppermute | solution.py:447
  20.7 0.0 collective-permute-done.4
  20.7 1.6 %collective-permute-start.6 = (bf16[2,48,2176]{2,1,0:T(8,128)(2,1)S(1)}, bf16[2,48,2176]{2,1,0:T(8,128)(2,1)S(1)}, u32[]{:S(2)}, u32[]{:S(2)}) collective-permute-start(bf16[2,48,2176]{2,1,0:T(8,128)(2,1)S(1)} %constant_dynamic-update-slice_fusion.2.refs_3_.refs_2_), channel_id=1, source_target_pairs={{0,2},{1,3},{4,0},{5,1},{8,4},{9,5},{12,8},{13,9},{14,12},{15,13},... | collective-permute-start | bytes 1253384 | tf_op jit(solution)/shard_map/ppermute | solution.py:447
  22.3 0.5 collective-permute-start.5
  22.8 7.9 %collective-permute-done.6.refs_5_.refs_4_ = bf16[2,48,2176]{2,1,0:T(8,128)(2,1)S(1)} collective-permute-done((bf16[2,48,2176]{2,1,0:T(8,128)(2,1)S(1)}, bf16[2,48,2176]{2,1,0:T(8,128)(2,1)S(1)}, u32[]{:S(2)}, u32[]{:S(2)}) %collective-permute-start.6) | collective-permute-done | bytes 417824 | tf_op jit(solution)/shard_map/ppermute | solution.py:447
  30.8 1.6 %collective-permute-start.11 = (bf16[2,48,2176]{2,1,0:T(8,128)(2,1)S(1)}, bf16[2,48,2176]{2,1,0:T(8,128)(2,1)S(1)}, u32[]{:S(2)}, u32[]{:S(2)}) collective-permute-start(bf16[2,48,2176]{2,1,0:T(8,128)(2,1)S(1)} %collective-permute-done.6.refs_5_.refs_4_), channel_id=1, source_target_pairs={{0,2},{1,3},{4,0},{5,1},{8,4},{9,5},{12,8},{13,9},{14,12},{15,13},... | collective-permute-start | bytes 1253384 | tf_op jit(solution)/shard_map/ppermute | solution.py:447
  32.4 0.5 collective-permute-start.10
  32.8 1.9 %copy-done.4 = bf16[1,768,2048]{2,1,0:T(8,128)(2,1)S(1)} copy-done((bf16[1,768,2048]{2,1,0:T(8,128)(2,1)S(1)}, bf16[1,768,2048]{2,1,0:T(8,128)(2,1)}, u32[]{:S(2)}) %copy-start.4) | copy-done | bytes 3145752
  34.7 1.2 %copy-done.6 = bf16[1,1,16,36,768]{4,2,3,1,0:T(8,128)(2,1)S(1)} copy-done((bf16[1,1,16,36,768]{4,2,3,1,0:T(8,128)(2,1)S(1)}, bf16[1,1,16,36,768]{4,2,3,1,0:T(8,128)(2,1)}, u32[]{:S(2)}) %copy-start.6) | copy-done | bytes 884760
  35.9 6.7 %block_product.3 = (bf16[48,2176]{1,0:T(8,128)(2,1)S(1)}, bf16[48,2176]{1,0:T(8,128)(2,1)S(1)}, bf16[48,2176]{1,0:T(8,128)(2,1)S(1)}, bf16[48,2176]{1,0:T(8,128)...) custom-call(s32[10]{0:T(128)S(1)} %dynamic-slice_bitcast_fusion.refs, ...), custom_call_target="tpu_custom_call" | custom-call | flops 3019898880 | bytes 9117696 | tf_op jit(solution)/shard_map/block_product/pallas_call | solution.py:299
  42.7 0.1 collective-permute-start.12
  42.8 0.0 copy-start.7
  42.8 1.6 %collective-permute-start.14 = (bf16[1,48,2176]{2,1,0:T(8,128)(2,1)S(1)}, bf16[1,48,2176]{2,1,0:T(8,128)(2,1)S(1)}, u32[]{:S(2)}, u32[]{:S(2)}) collective-permute-start(bf16[1,48,2176]{2,1,0:T(8,128)(2,1)S(1)} %slice.7), channel_id=1, source_target_pairs={{0,2},{1,3},{4,0},{5,1},{8,4},{9,5},{12,8},{13,9},{14,12},{15,13},... | collective-permute-start | bytes 626696 | tf_op jit(solution)/shard_map/ppermute | solution.py:447
  44.4 0.5 collective-permute-start.13
  44.9 0.3 collective-permute-done.12.refs_7_.refs_8_
  45.2 6.7 %block_product.4 = (bf16[48,2176]{1,0:T(8,128)(2,1)S(1)}, bf16[48,2176]{1,0:T(8,128)(2,1)S(1)}, bf16[48,2176]{1,0:T(8,128)(2,1)S(1)}, bf16[48,2176]{1,0:T(8,128)...) custom-call(s32[10]{0:T(128)S(1)} %dynamic-slice_bitcast_fusion.refs_0_,, ...), custom_call_target="tpu_custom_call" | custom-call | flops 3019898880 | bytes 9117696 | tf_op jit(solution)/shard_map/block_product/pallas_call | solution.py:299
  51.9 1.6 %collective-permute-start.18 = (bf16[2,240,768]{2,1,0:T(8,128)(2,1)S(1)}, bf16[2,240,768]{2,1,0:T(8,128)(2,1)S(1)}, u32[]{:S(2)}, u32[]{:S(2)}) collective-permute-start(bf16[2,240,768]{2,1,0:T(8,128)(2,1)S(1)} %get-tuple-element.78), channel_id=1, source_target_pairs={{0,16},{16,0},{1,17},{17,1},{2,18},{18,2},{3,19},{19,3},{4,20},{20... | collective-permute-start | bytes 2211848 | tf_op jit(solution)/shard_map/ppermute | solution.py:444
  53.4 7.6 %block_product.5 = (bf16[48,2176]{1,0:T(8,128)(2,1)S(1)}, bf16[48,2176]{1,0:T(8,128)(2,1)S(1)}, bf16[48,2176]{1,0:T(8,128)(2,1)S(1)}, bf16[48,2176]{1,0:T(8,128)...) custom-call(s32[10]{0:T(128)S(1)} %dynamic-slice_bitcast_fusion.refs, ...), custom_call_target="tpu_custom_call" | custom-call | flops 3623878656 | bytes 9682944 | tf_op jit(solution)/shard_map/block_product/pallas_call | solution.py:299
  61.1 0.7 collective-permute-start.15
  61.8 1.4 %collective-permute-start.17 = (bf16[1,48,2176]{2,1,0:T(8,128)(2,1)S(1)}, bf16[1,48,2176]{2,1,0:T(8,128)(2,1)S(1)}, u32[]{:S(2)}, u32[]{:S(2)}) collective-permute-start(bf16[1,48,2176]{2,1,0:T(8,128)(2,1)S(1)} %bitcast.43), channel_id=1, source_target_pairs={{0,2},{1,3},{4,0},{5,1},{8,4},{9,5},{12,8},{13,9},{14,12},{15,13},... | collective-permute-start | bytes 626696 | tf_op jit(solution)/shard_map/ppermute | solution.py:447
  63.1 0.5 collective-permute-start.22
  63.6 4.4 %collective-permute-done.15.refs_2_ = bf16[1,48,2176]{2,1,0:T(8,128)(2,1)S(1)} collective-permute-done((bf16[1,48,2176]{2,1,0:T(8,128)(2,1)S(1)}, bf16[1,48,2176]{2,1,0:T(8,128)(2,1)S(1)}, u32[]{:S(2)}, u32[]{:S(2)}) %collective-permute-start.15) | collective-permute-done | bytes 208928 | tf_op jit(solution)/shard_map/ppermute | solution.py:447
  68.0 0.1 sums.6
  68.1 0.3 collective-permute-done.17.refs_2_
  68.4 0.1 sums.8
  68.4 1.4 %collective-permute-start.20 = (bf16[2,48,2176]{2,1,0:T(8,128)(2,1)S(1)}, bf16[2,48,2176]{2,1,0:T(8,128)(2,1)S(1)}, u32[]{:S(2)}, u32[]{:S(2)}) collective-permute-start(bf16[2,48,2176]{2,1,0:T(8,128)(2,1)S(1)} %sums.8), channel_id=1, source_target_pairs={{0,2},{1,3},{4,0},{5,1},{8,4},{9,5},{12,8},{13,9},{14,12},{15,13},... | collective-permute-start | bytes 1253384 | tf_op jit(solution)/shard_map/ppermute | solution.py:447
  69.9 0.6 collective-permute-start.16
  70.5 0.7 collective-permute-done.18.refs_6_
  71.3 5.2 %weight_product.2 = bf16[768,2048]{1,0:T(8,128)(2,1)S(1)} custom-call(bf16[1,48,2176]{2,1,0:T(8,128)(2,1)S(1)} %bitcast.25, bf16[2,48,2176]{2,1,0:T(8,128)(2,1)S(1)} %constant_dynamic-update-slice_fusion.refs_2_.refs_1_, bf16[2,48,2176]{2,1,0:T(8,128)(2,1)S(1)} %constant_dynamic-update-slice_fusion.2.refs_3_.refs_2_, ...), custom_call_target="tpu_custom_call" | custom-call | flops 2415919104 | bytes 10616832 | tf_op jit(solution)/shard_map/weight_product/pallas_call | solution.py:381
  76.5 3.4 %collective-permute-done.22.refs_7_ = bf16[2,144,768]{2,1,0:T(8,128)(2,1)S(1)} collective-permute-done((bf16[2,144,768]{2,1,0:T(8,128)(2,1)S(1)}, bf16[2,144,768]{2,1,0:T(8,128)(2,1)S(1)}, u32[]{:S(2)}, u32[]{:S(2)}) %collective-permute-start.22) | collective-permute-done | bytes 442400 | tf_op jit(solution)/shard_map/ppermute | solution.py:444
  79.9 0.1 collective-permute-done.16.refs_2_
  80.0 0.1 sums.7
  80.1 1.2 %collective-permute-start.19 = (bf16[2,48,2176]{2,1,0:T(8,128)(2,1)S(1)}, bf16[2,48,2176]{2,1,0:T(8,128)(2,1)S(1)}, u32[]{:S(2)}, u32[]{:S(2)}) collective-permute-start(bf16[2,48,2176]{2,1,0:T(8,128)(2,1)S(1)} %sums.7), channel_id=1, source_target_pairs={{0,4},{1,5},{4,8},{5,9},{8,12},{9,13},{12,14},{13,15},{14,10},{15,... | collective-permute-start | bytes 1253384 | tf_op jit(solution)/shard_map/ppermute | solution.py:447
  81.3 0.1 sums.9
  81.4 1.2 %collective-permute-start.21 = (bf16[2,48,2176]{2,1,0:T(8,128)(2,1)S(1)}, bf16[2,48,2176]{2,1,0:T(8,128)(2,1)S(1)}, u32[]{:S(2)}, u32[]{:S(2)}) collective-permute-start(bf16[2,48,2176]{2,1,0:T(8,128)(2,1)S(1)} %sums.9), channel_id=1, source_target_pairs={{0,2},{1,3},{4,0},{5,1},{8,4},{9,5},{12,8},{13,9},{14,12},{15,13},... | collective-permute-start | bytes 1253384 | tf_op jit(solution)/shard_map/ppermute | solution.py:447
  82.6 1.3 %spread_product.1 = (bf16[576,768]{1,0:T(8,128)(2,1)S(1)}, bf16[576,768]{1,0:T(8,128)(2,1)S(1)}) custom-call(s32[240,2]{1,0:T(8,128)S(1)} %get-tuple-element.96.refs_0_, s32[144,2]{1,0:T(8,128)S(1)} %get-tuple-element.97.refs_1_, f32[240,2]{1,0:T(8,128)S(1)} %get-tuple-element.98.refs_2_, f32[144,2]{1,0:T(8,128)S(1)} %get-tuple-element.99.refs_3_, ...), custom_call_target="tpu_custom_call" | custom-call | flops 679477248 | bytes 3538944 | tf_op jit(solution)/shard_map/spread_product/pallas_call | solution.py:346
  83.9 0.1 collective-permute-start.27
  84.0 8.3 %collective-permute-done.19.refs_2_ = bf16[2,48,2176]{2,1,0:T(8,128)(2,1)S(1)} collective-permute-done((bf16[2,48,2176]{2,1,0:T(8,128)(2,1)S(1)}, bf16[2,48,2176]{2,1,0:T(8,128)(2,1)S(1)}, u32[]{:S(2)}, u32[]{:S(2)}) %collective-permute-start.19) | collective-permute-done | bytes 417824 | tf_op jit(solution)/shard_map/ppermute | solution.py:447
  92.2 0.1 sums.10
  92.3 1.2 %collective-permute-start.24 = (bf16[2,48,2176]{2,1,0:T(8,128)(2,1)S(1)}, bf16[2,48,2176]{2,1,0:T(8,128)(2,1)S(1)}, u32[]{:S(2)}, u32[]{:S(2)}) collective-permute-start(bf16[2,48,2176]{2,1,0:T(8,128)(2,1)S(1)} %sums.10), channel_id=1, source_target_pairs={{0,4},{1,5},{4,8},{5,9},{8,12},{9,13},{12,14},{13,15},{14,10},{15,... | collective-permute-start | bytes 1253384 | tf_op jit(solution)/shard_map/ppermute | solution.py:447
  93.5 0.1 sums.11
  93.6 1.0 collective-permute-start.25
  94.6 6.5 %weight_product.3 = f32[768,2048]{1,0:T(8,128)} custom-call(bf16[1,48,2176]{2,1,0:T(8,128)(2,1)S(1)} %bitcast.26, bf16[2,48,2176]{2,1,0:T(8,128)(2,1)S(1)} %constant_dynamic-update-slice_fusion.refs_2_.refs_1_, bf16[2,48,2176]{2,1,0:T(8,128)(2,1)S(1)} %constant_dynamic-update-slice_fusion.2.refs_3_.refs_2_, ...), custom_call_target="tpu_custom_call" | custom-call | flops 2415919104 | bytes 10616832 | tf_op jit(solution)/shard_map/weight_product/pallas_call | solution.py:381
  101.0 2.6 %collective-permute-done.24.refs_2_ = bf16[2,48,2176]{2,1,0:T(8,128)(2,1)S(1)} collective-permute-done((bf16[2,48,2176]{2,1,0:T(8,128)(2,1)S(1)}, bf16[2,48,2176]{2,1,0:T(8,128)(2,1)S(1)}, u32[]{:S(2)}, u32[]{:S(2)}) %collective-permute-start.24) | collective-permute-done | bytes 417824 | tf_op jit(solution)/shard_map/ppermute | solution.py:447
  103.6 1.0 collective-permute-done.25.refs_3_
  104.6 0.2 close.1
  104.8 1.0 collective-permute-start.26
  105.8 1.1 %add.8 = bf16[576,768]{1,0:T(8,128)(2,1)} add(bf16[576,768]{1,0:T(8,128)(2,1)S(1)} %get-tuple-element.102, bf16[576,768]{1,0:T(8,128)(2,1)S(1)} %collective-permute-done.27) | non-fusion elementwise | flops 442368 | bytes 2654208 | tf_op jit(solution)/shard_map/add | solution.py:555
  107.0 3.7 %collective-permute-done.26.refs_1_ = bf16[48,2176]{1,0:T(8,128)(2,1)S(1)} collective-permute-done((bf16[48,2176]{1,0:T(8,128)(2,1)S(1)}, bf16[48,2176]{1,0:T(8,128)(2,1)S(1)}, u32[]{:S(2)}, u32[]{:S(2)}) %collective-permute-start.26) | collective-permute-done | bytes 208928 | tf_op jit(solution)/shard_map/ppermute | solution.py:444
  110.7 0.9 home.1
  (31 shorter events, 0.2 us)
Async XLA Ops:
  0.6 32.2 %collective-permute-start.8 = (bf16[768,2048]{1,0:T(8,128)(2,1)}, bf16[768,2048]{1,0:T(8,128)(2,1)}, u32[]{:S(2)}, u32[]{:S(2)}) collective-permute-start(bf16[768,2048]{1,0:T(8,128)(2,1)} %bitcast.35), channel_id=1, source_target_pairs={{0,1},{1,0},{2,3},{3,2},{4,5},{5,4},{6,7},{7,6},{8,9},{9,8},{10,11... | collective-permute-start | bytes 9437192 | tf_op jit(solution)/shard_map/ppermute | solution.py:450
  1.1 1.0 copy-start
  2.1 0.7 copy-start.1
  2.8 0.7 copy-start.3
  4.0 8.4 %collective-permute-start.1 = (bf16[48,2176]{1,0:T(8,128)(2,1)S(1)}, bf16[48,2176]{1,0:T(8,128)(2,1)S(1)}, u32[]{:S(2)}, u32[]{:S(2)}) collective-permute-start(bf16[48,2176]{1,0:T(8,128)(2,1)S(1)} %get-tuple-element.59), channel_id=1, source_target_pairs={{0,16},{16,0},{1,17},{17,1},{2,18},{18,2},{3,19},{19,3},{4,20},{20... | collective-permute-start | bytes 626696 | tf_op jit(solution)/shard_map/ppermute | solution.py:444
  6.6 7.6 %collective-permute-start.3 = (bf16[1,48,2176]{2,1,0:T(8,128)(2,1)S(1)}, bf16[1,48,2176]{2,1,0:T(8,128)(2,1)S(1)}, u32[]{:S(2)}, u32[]{:S(2)}) collective-permute-start(bf16[1,48,2176]{2,1,0:T(8,128)(2,1)S(1)} %bitcast.22), channel_id=1, source_target_pairs={{0,2},{1,3},{4,0},{5,1},{8,4},{9,5},{12,8},{13,9},{14,12},{15,13},... | collective-permute-start | bytes 626696 | tf_op jit(solution)/shard_map/ppermute | solution.py:447
  8.1 7.3 %collective-permute-start = (bf16[1,48,2176]{2,1,0:T(8,128)(2,1)S(1)}, bf16[1,48,2176]{2,1,0:T(8,128)(2,1)S(1)}, u32[]{:S(2)}, u32[]{:S(2)}) collective-permute-start(bf16[1,48,2176]{2,1,0:T(8,128)(2,1)S(1)} %bitcast.23), channel_id=1, source_target_pairs={{0,4},{1,5},{4,8},{5,9},{8,12},{9,13},{12,14},{13,15},{14,10},{15,... | collective-permute-start | bytes 626696 | tf_op jit(solution)/shard_map/ppermute | solution.py:447
  8.6 24.2 %collective-permute-start.7 = (bf16[576,768]{1,0:T(8,128)(2,1)}, bf16[576,768]{1,0:T(8,128)(2,1)S(1)}, u32[]{:S(2)}, u32[]{:S(2)}) collective-permute-start(bf16[576,768]{1,0:T(8,128)(2,1)} %bitcast.39), channel_id=1, source_target_pairs={{0,1},{1,0},{2,3},{3,2},{4,5},{5,4},{6,7},{7,6},{8,9},{9,8},{10,11... | collective-permute-start | bytes 2654216 | tf_op jit(solution)/shard_map/ppermute | solution.py:450
  12.4 8.3 %collective-permute-start.4 = (bf16[1,48,2176]{2,1,0:T(8,128)(2,1)S(1)}, bf16[1,48,2176]{2,1,0:T(8,128)(2,1)S(1)}, u32[]{:S(2)}, u32[]{:S(2)}) collective-permute-start(bf16[1,48,2176]{2,1,0:T(8,128)(2,1)S(1)} %bitcast.27), channel_id=1, source_target_pairs={{0,2},{1,3},{4,0},{5,1},{8,4},{9,5},{12,8},{13,9},{14,12},{15,13},... | collective-permute-start | bytes 626696 | tf_op jit(solution)/shard_map/ppermute | solution.py:447
  14.2 6.5 %collective-permute-start.2 = (bf16[1,48,2176]{2,1,0:T(8,128)(2,1)S(1)}, bf16[1,48,2176]{2,1,0:T(8,128)(2,1)S(1)}, u32[]{:S(2)}, u32[]{:S(2)}) collective-permute-start(bf16[1,48,2176]{2,1,0:T(8,128)(2,1)S(1)} %bitcast.28), channel_id=1, source_target_pairs={{0,4},{1,5},{4,8},{5,9},{8,12},{9,13},{12,14},{13,15},{14,10},{15,... | collective-permute-start | bytes 626696 | tf_op jit(solution)/shard_map/ppermute | solution.py:447
  15.4 27.2 %collective-permute-start.9 = (bf16[576,768]{1,0:T(8,128)(2,1)}, bf16[576,768]{1,0:T(8,128)(2,1)S(1)}, u32[]{:S(2)}, u32[]{:S(2)}) collective-permute-start(bf16[576,768]{1,0:T(8,128)(2,1)} %bitcast.40), channel_id=1, source_target_pairs={{0,16},{16,0},{1,17},{17,1},{2,18},{18,2},{3,19},{19,3},{4,20},{20... | collective-permute-start | bytes 2654216 | tf_op jit(solution)/shard_map/ppermute | solution.py:444
  20.7 10.1 %collective-permute-start.6 = (bf16[2,48,2176]{2,1,0:T(8,128)(2,1)S(1)}, bf16[2,48,2176]{2,1,0:T(8,128)(2,1)S(1)}, u32[]{:S(2)}, u32[]{:S(2)}) collective-permute-start(bf16[2,48,2176]{2,1,0:T(8,128)(2,1)S(1)} %constant_dynamic-update-slice_fusion.2.refs_3_.refs_2_), channel_id=1, source_target_pairs={{0,2},{1,3},{4,0},{5,1},{8,4},{9,5},{12,8},{13,9},{14,12},{15,13},... | collective-permute-start | bytes 1253384 | tf_op jit(solution)/shard_map/ppermute | solution.py:447
  22.3 10.0 %collective-permute-start.5 = (bf16[2,48,2176]{2,1,0:T(8,128)(2,1)S(1)}, bf16[2,48,2176]{2,1,0:T(8,128)(2,1)S(1)}, u32[]{:S(2)}, u32[]{:S(2)}) collective-permute-start(bf16[2,48,2176]{2,1,0:T(8,128)(2,1)S(1)} %constant_dynamic-update-slice_fusion.refs_2_.refs_1_), channel_id=1, source_target_pairs={{0,4},{1,5},{4,8},{5,9},{8,12},{9,13},{12,14},{13,15},{14,10},{15,... | collective-permute-start | bytes 1253384 | tf_op jit(solution)/shard_map/ppermute | solution.py:447
  30.8 11.9 %collective-permute-start.11 = (bf16[2,48,2176]{2,1,0:T(8,128)(2,1)S(1)}, bf16[2,48,2176]{2,1,0:T(8,128)(2,1)S(1)}, u32[]{:S(2)}, u32[]{:S(2)}) collective-permute-start(bf16[2,48,2176]{2,1,0:T(8,128)(2,1)S(1)} %collective-permute-done.6.refs_5_.refs_4_), channel_id=1, source_target_pairs={{0,2},{1,3},{4,0},{5,1},{8,4},{9,5},{12,8},{13,9},{14,12},{15,13},... | collective-permute-start | bytes 1253384 | tf_op jit(solution)/shard_map/ppermute | solution.py:447
  32.4 10.3 %collective-permute-start.10 = (bf16[2,48,2176]{2,1,0:T(8,128)(2,1)S(1)}, bf16[2,48,2176]{2,1,0:T(8,128)(2,1)S(1)}, u32[]{:S(2)}, u32[]{:S(2)}) collective-permute-start(bf16[2,48,2176]{2,1,0:T(8,128)(2,1)S(1)} %collective-permute-done.5.refs_4_.refs_3_), channel_id=1, source_target_pairs={{0,4},{1,5},{4,8},{5,9},{8,12},{9,13},{12,14},{13,15},{14,10},{15,... | collective-permute-start | bytes 1253384 | tf_op jit(solution)/shard_map/ppermute | solution.py:447
  32.8 1.9 %copy-start.4 = (bf16[1,768,2048]{2,1,0:T(8,128)(2,1)S(1)}, bf16[1,768,2048]{2,1,0:T(8,128)(2,1)}, u32[]{:S(2)}) copy-start(bf16[1,768,2048]{2,1,0:T(8,128)(2,1)} %param.9) | copy-start | bytes 9437188
  34.7 1.2 %copy-start.6 = (bf16[1,1,16,36,768]{4,2,3,1,0:T(8,128)(2,1)S(1)}, bf16[1,1,16,36,768]{4,2,3,1,0:T(8,128)(2,1)}, u32[]{:S(2)}) copy-start(bf16[1,1,16,36,768]{4,2,3,1,0:T(8,128)(2,1)} %param.8) | copy-start | bytes 2654212
  35.9 9.3 %copy-start.5 = (bf16[1,768,2048]{2,1,0:T(8,128)(2,1)S(1)}, bf16[1,768,2048]{2,1,0:T(8,128)(2,1)}, u32[]{:S(2)}) copy-start(bf16[1,768,2048]{2,1,0:T(8,128)(2,1)} %param.9) | copy-start | bytes 9437188
  42.7 2.5 %collective-permute-start.12 = (bf16[576,768]{1,0:T(8,128)(2,1)S(1)}, bf16[576,768]{1,0:T(8,128)(2,1)S(1)}, u32[]{:S(2)}, u32[]{:S(2)}) collective-permute-start(bf16[576,768]{1,0:T(8,128)(2,1)S(1)} %collective-permute-done.9.refs_6_.refs_7_), channel_id=1, source_target_pairs={{0,1},{1,0},{2,3},{3,2},{4,5},{5,4},{6,7},{7,6},{8,9},{9,8},{10,11... | collective-permute-start | bytes 2654216 | tf_op jit(solution)/shard_map/ppermute | solution.py:450
  42.8 10.6 %copy-start.7 = (bf16[1,1,16,36,768]{4,2,3,1,0:T(8,128)(2,1)S(1)}, bf16[1,1,16,36,768]{4,2,3,1,0:T(8,128)(2,1)}, u32[]{:S(2)}) copy-start(bf16[1,1,16,36,768]{4,2,3,1,0:T(8,128)(2,1)} %param.8) | copy-start | bytes 2654212
  42.8 9.0 %collective-permute-start.14 = (bf16[1,48,2176]{2,1,0:T(8,128)(2,1)S(1)}, bf16[1,48,2176]{2,1,0:T(8,128)(2,1)S(1)}, u32[]{:S(2)}, u32[]{:S(2)}) collective-permute-start(bf16[1,48,2176]{2,1,0:T(8,128)(2,1)S(1)} %slice.7), channel_id=1, source_target_pairs={{0,2},{1,3},{4,0},{5,1},{8,4},{9,5},{12,8},{13,9},{14,12},{15,13},... | collective-permute-start | bytes 626696 | tf_op jit(solution)/shard_map/ppermute | solution.py:447
  44.4 7.4 %collective-permute-start.13 = (bf16[1,48,2176]{2,1,0:T(8,128)(2,1)S(1)}, bf16[1,48,2176]{2,1,0:T(8,128)(2,1)S(1)}, u32[]{:S(2)}, u32[]{:S(2)}) collective-permute-start(bf16[1,48,2176]{2,1,0:T(8,128)(2,1)S(1)} %slice.6), channel_id=1, source_target_pairs={{0,4},{1,5},{4,8},{5,9},{8,12},{9,13},{12,14},{13,15},{14,10},{15,... | collective-permute-start | bytes 626696 | tf_op jit(solution)/shard_map/ppermute | solution.py:447
  51.9 19.4 %collective-permute-start.18 = (bf16[2,240,768]{2,1,0:T(8,128)(2,1)S(1)}, bf16[2,240,768]{2,1,0:T(8,128)(2,1)S(1)}, u32[]{:S(2)}, u32[]{:S(2)}) collective-permute-start(bf16[2,240,768]{2,1,0:T(8,128)(2,1)S(1)} %get-tuple-element.78), channel_id=1, source_target_pairs={{0,16},{16,0},{1,17},{17,1},{2,18},{18,2},{3,19},{19,3},{4,20},{20... | collective-permute-start | bytes 2211848 | tf_op jit(solution)/shard_map/ppermute | solution.py:444
  61.1 6.9 %collective-permute-start.15 = (bf16[1,48,2176]{2,1,0:T(8,128)(2,1)S(1)}, bf16[1,48,2176]{2,1,0:T(8,128)(2,1)S(1)}, u32[]{:S(2)}, u32[]{:S(2)}) collective-permute-start(bf16[1,48,2176]{2,1,0:T(8,128)(2,1)S(1)} %bitcast.44), channel_id=1, source_target_pairs={{0,4},{1,5},{4,8},{5,9},{8,12},{9,13},{12,14},{13,15},{14,10},{15,... | collective-permute-start | bytes 626696 | tf_op jit(solution)/shard_map/ppermute | solution.py:447
  61.8 6.6 %collective-permute-start.17 = (bf16[1,48,2176]{2,1,0:T(8,128)(2,1)S(1)}, bf16[1,48,2176]{2,1,0:T(8,128)(2,1)S(1)}, u32[]{:S(2)}, u32[]{:S(2)}) collective-permute-start(bf16[1,48,2176]{2,1,0:T(8,128)(2,1)S(1)} %bitcast.43), channel_id=1, source_target_pairs={{0,2},{1,3},{4,0},{5,1},{8,4},{9,5},{12,8},{13,9},{14,12},{15,13},... | collective-permute-start | bytes 626696 | tf_op jit(solution)/shard_map/ppermute | solution.py:447
  63.1 16.8 %collective-permute-start.22 = (bf16[2,144,768]{2,1,0:T(8,128)(2,1)S(1)}, bf16[2,144,768]{2,1,0:T(8,128)(2,1)S(1)}, u32[]{:S(2)}, u32[]{:S(2)}) collective-permute-start(bf16[2,144,768]{2,1,0:T(8,128)(2,1)S(1)} %get-tuple-element.90), channel_id=1, source_target_pairs={{0,16},{16,0},{1,17},{17,1},{2,18},{18,2},{3,19},{19,3},{4,20},{20... | collective-permute-start | bytes 1327112 | tf_op jit(solution)/shard_map/ppermute | solution.py:444
  68.4 11.5 %collective-permute-start.20 = (bf16[2,48,2176]{2,1,0:T(8,128)(2,1)S(1)}, bf16[2,48,2176]{2,1,0:T(8,128)(2,1)S(1)}, u32[]{:S(2)}, u32[]{:S(2)}) collective-permute-start(bf16[2,48,2176]{2,1,0:T(8,128)(2,1)S(1)} %sums.8), channel_id=1, source_target_pairs={{0,2},{1,3},{4,0},{5,1},{8,4},{9,5},{12,8},{13,9},{14,12},{15,13},... | collective-permute-start | bytes 1253384 | tf_op jit(solution)/shard_map/ppermute | solution.py:447
  69.9 10.1 %collective-permute-start.16 = (bf16[2,48,2176]{2,1,0:T(8,128)(2,1)S(1)}, bf16[2,48,2176]{2,1,0:T(8,128)(2,1)S(1)}, u32[]{:S(2)}, u32[]{:S(2)}) collective-permute-start(bf16[2,48,2176]{2,1,0:T(8,128)(2,1)S(1)} %sums.6), channel_id=1, source_target_pairs={{0,4},{1,5},{4,8},{5,9},{8,12},{9,13},{12,14},{13,15},{14,10},{15,... | collective-permute-start | bytes 1253384 | tf_op jit(solution)/shard_map/ppermute | solution.py:447
  80.0 14.6 %collective-permute-start.23 = (bf16[768,2048]{1,0:T(8,128)(2,1)S(1)}, bf16[768,2048]{1,0:T(8,128)(2,1)S(1)}, u32[]{:S(2)}, u32[]{:S(2)}) collective-permute-start(bf16[768,2048]{1,0:T(8,128)(2,1)S(1)} %weight_product.2), channel_id=1, source_target_pairs={{0,1},{1,0},{2,3},{3,2},{4,5},{5,4},{6,7},{7,6},{8,9},{9,8},{10,11... | collective-permute-start | bytes 9437192 | tf_op jit(solution)/shard_map/ppermute | solution.py:450
  80.1 12.1 %collective-permute-start.19 = (bf16[2,48,2176]{2,1,0:T(8,128)(2,1)S(1)}, bf16[2,48,2176]{2,1,0:T(8,128)(2,1)S(1)}, u32[]{:S(2)}, u32[]{:S(2)}) collective-permute-start(bf16[2,48,2176]{2,1,0:T(8,128)(2,1)S(1)} %sums.7), channel_id=1, source_target_pairs={{0,4},{1,5},{4,8},{5,9},{8,12},{9,13},{12,14},{13,15},{14,10},{15,... | collective-permute-start | bytes 1253384 | tf_op jit(solution)/shard_map/ppermute | solution.py:447
  81.4 12.1 %collective-permute-start.21 = (bf16[2,48,2176]{2,1,0:T(8,128)(2,1)S(1)}, bf16[2,48,2176]{2,1,0:T(8,128)(2,1)S(1)}, u32[]{:S(2)}, u32[]{:S(2)}) collective-permute-start(bf16[2,48,2176]{2,1,0:T(8,128)(2,1)S(1)} %sums.9), channel_id=1, source_target_pairs={{0,2},{1,3},{4,0},{5,1},{8,4},{9,5},{12,8},{13,9},{14,12},{15,13},... | collective-permute-start | bytes 1253384 | tf_op jit(solution)/shard_map/ppermute | solution.py:447
  83.9 21.9 %collective-permute-start.27 = (bf16[576,768]{1,0:T(8,128)(2,1)S(1)}, bf16[576,768]{1,0:T(8,128)(2,1)S(1)}, u32[]{:S(2)}, u32[]{:S(2)}) collective-permute-start(bf16[576,768]{1,0:T(8,128)(2,1)S(1)} %get-tuple-element.111), channel_id=1, source_target_pairs={{0,1},{1,0},{2,3},{3,2},{4,5},{5,4},{6,7},{7,6},{8,9},{9,8},{10,11... | collective-permute-start | bytes 2654216 | tf_op jit(solution)/shard_map/ppermute | solution.py:450
  92.3 11.3 %collective-permute-start.24 = (bf16[2,48,2176]{2,1,0:T(8,128)(2,1)S(1)}, bf16[2,48,2176]{2,1,0:T(8,128)(2,1)S(1)}, u32[]{:S(2)}, u32[]{:S(2)}) collective-permute-start(bf16[2,48,2176]{2,1,0:T(8,128)(2,1)S(1)} %sums.10), channel_id=1, source_target_pairs={{0,4},{1,5},{4,8},{5,9},{8,12},{9,13},{12,14},{13,15},{14,10},{15,... | collective-permute-start | bytes 1253384 | tf_op jit(solution)/shard_map/ppermute | solution.py:447
  93.6 11.0 %collective-permute-start.25 = (bf16[2,48,2176]{2,1,0:T(8,128)(2,1)S(1)}, bf16[2,48,2176]{2,1,0:T(8,128)(2,1)S(1)}, u32[]{:S(2)}, u32[]{:S(2)}) collective-permute-start(bf16[2,48,2176]{2,1,0:T(8,128)(2,1)S(1)} %sums.11), channel_id=1, source_target_pairs={{0,2},{1,3},{4,0},{5,1},{8,4},{9,5},{12,8},{13,9},{14,12},{15,13},... | collective-permute-start | bytes 1253384 | tf_op jit(solution)/shard_map/ppermute | solution.py:447
  101.0 9.6 %copy-start.2 = (s32[48,8]{0,1:T(8,128)S(1)}, s32[48,8]{0,1:T(8,128)}, u32[]{:S(2)}) copy-start(s32[48,8]{0,1:T(8,128)} %param.6) | copy-start | bytes 4612
  104.8 5.9 %collective-permute-start.26 = (bf16[48,2176]{1,0:T(8,128)(2,1)S(1)}, bf16[48,2176]{1,0:T(8,128)(2,1)S(1)}, u32[]{:S(2)}, u32[]{:S(2)}) collective-permute-start(bf16[48,2176]{1,0:T(8,128)(2,1)S(1)} %get-tuple-element.108), channel_id=1, source_target_pairs={{0,16},{16,0},{1,17},{17,1},{2,18},{18,2},{3,19},{19,3},{4,20},{20... | collective-permute-start | bytes 626696 | tf_op jit(solution)/shard_map/ppermute | solution.py:444

commit v14 on v13

--- a/solution.py
+++ b/solution.py
@@ -102,22 +102,22 @@
 def sum_kernel(starts, n_out, *refs):
     outs = refs[-n_out:]
     at = 0
-    for out, (n_rows, arrives) in zip(outs, starts):
-        carry = refs[at + n_rows] if arrives else None
+    for out, (n_rows, first, last, base) in zip(outs, starts):
+        carry = refs[at + n_rows]
         for i in range(n_rows):
             value = refs[at + i][...]
-            if carry is not None and arrives[0] <= i < arrives[1]:
-                value = value.astype(jnp.float32) + carry[i - arrives[0]].astype(jnp.float32)
+            if first <= i < last:
+                value = value.astype(jnp.float32) + carry[i - first + base].astype(jnp.float32)
             out[i] = value.astype(jnp.bfloat16)
-        at += n_rows + (1 if arrives else 0)
+        at += n_rows + 1
 
 
 def sums(jobs):
     tok, full = jobs[0][0][0].shape
     flat, starts, shapes = [], [], []
-    for parts, carry, first, last in jobs:
+    for parts, carry, first, last, base in jobs:
         flat += list(parts) + [carry]
-        starts.append((len(parts), (first, last)))
+        starts.append((len(parts), first, last, base))
         shapes.append(jax.ShapeDtypeStruct((len(parts), tok, full), jnp.bfloat16))
     vmem = pl.BlockSpec(memory_space=pltpu.VMEM)
     return pl.pallas_call(
@@ -530,8 +530,8 @@
                 values.append(jnp.stack([parts[half, d] for d in every[per:]]))
             else:
                 first, last = ((0, per), (per, n_dp)) if hop == half - 1 else ((0, n_dp), (0, n_dp))
-                values = sums([([parts[hop, d] for d in every], carry[1], *first)])
-                values += sums([([parts[-hop, d] for d in every], carry[-1], *last)])
+                values = sums([([parts[hop, d] for d in every], carry[1], *first, 0)])
+                values += sums([([parts[-hop, d] for d in every], carry[-1], *last, 0)])
             values = [after(value, *done) for value in values]
             carry[1] = ring_send(values[0], 1)
             carry[-1] = ring_send(values[1], -1)
@@ -546,22 +546,31 @@
         )
         swapped = swap(after(other, *second, *[sent[-1] for sent in sent_back]))
         third = hop_on(half - 2, other)
+        weight_grad = weight_product(
+            [after(refs[0], *sending)] + refs[1:], layout, scaleds, 0, jnp.float32, width, swapped
+        )
         spread, spread_other = spread_product(
-            [after(facts[0][0], *second)] + [fact[0] for fact in facts[1:]],
+            [after(facts[0][0], *second, weight_grad)] + [fact[0] for fact in facts[1:]],
             [fact[1] for fact in facts],
             [own_back] + sent_back,
             slots,
         )
-        hidden_grad = spread + swap(spread_other)
+        hidden_grad = spread + swap(after(spread_other, *third))
         hidden_grad = hidden_grad.reshape(cap, n_ex, ff).transpose(1, 0, 2)[None, None]
-        for hop in range(half - 3, 0, -1):
+        for hop in range(half - 3, 1, -1):
             hop_on(hop, spread)
-        weight_grad = weight_product(
-            [after(refs[0], *third)] + refs[1:], layout, scaleds, 0, jnp.float32, width, swapped
-        )
-        totals = close([after(parts[0, 0], weight_grad)] + [parts[0, d] for d in range(1, n_dp)], carry[1], carry[-1])
-        pieces = [totals[0]] + [shift(totals[d], -d) for d in range(1, n_dp)]
-        layer_out, prob_grad = home(where, expert_ids.T, pieces, width, n_ex)
+
+        groups = [range(per, n_dp), range(per)]
+        ends = {}
+        for direction in (1, -1):
+            jobs = [([parts[direction, d] for d in g], carry[direction], 0, len(g), g[0]) for g in groups]
+            ends[direction] = [ring_send(after(value, spread), direction) for value in sums(jobs)]
+        pieces = {}
+        for i, group in enumerate(groups):
+            totals = close([parts[0, d] for d in group], ends[1][i], ends[-1][i])
+            for d, total in zip(group, totals):
+                pieces[d] = total if d == 0 else shift(total, -d)
+        layer_out, prob_grad = home(where, after(expert_ids.T, hidden_grad), [pieces[d] for d in range(n_dp)], width, n_ex)
         return (layer_out, prob_grad.T, hidden_grad, weight_grad[None])
 
     return shards

time: 112 us -> 110 us (0.982)
  waiting for transfers between devices: 40.2 us -> 36.7 us
  starting transfers between devices: 27 us -> 28.9 us
    ppermute x18 -> x20, waiting for transfers between devices: 29 us -> 24.8 us  [ring_send(): return lax.ppermute(value, 'expert', forward if step > 0 else backward)]
    ppermute x5, waiting for transfers between devices: 0.28 us -> 3.65 us  [swap(): return lax.ppermute(value, 'expert', sibling)]
    ppermute x5, waiting for transfers between devices: 11 us -> 8.24 us  [shift(): lax.ppermute(value, 'dp', [(i, (i + step) % n_dp) for i in range(n_dp)])]
    ppermute x18 -> x20, starting transfers between devices: 19.9 us -> 21.6 us  [ring_send(): return lax.ppermute(value, 'expert', forward if step > 0 else backward)]
  transfers between devices with their start and end apart: 28 -> 30, of which waited for: 13 -> 15; matrix products, arithmetic and copies ran while one was open for 2% -> 2% of each run, Pallas kernels for 32% -> 32%
where the time goes in v14:
time: 110 us
  waiting for transfers between devices  36.7 us (33%)
  Pallas kernels  36.1 us (33%)
  starting transfers between devices  28.9 us (26%)
  local copies, waits for them, and re-layouts  6.24 us (6%)
  other arithmetic  1.12 us (1%)
    ppermute x20, waiting for transfers between devices, ring_send(): return lax.ppermute(value, 'expert', forward if step > 0 else backward)  24.8 us
    ppermute x20, starting transfers between devices, ring_send(): return lax.ppermute(value, 'expert', forward if step > 0 else backward)  21.6 us
    pallas_call x3, Pallas kernels, block_product(): pl.pallas_call(functools.partial(block_kernel, plan, len(blocks), n_dp, n...  21.1 us
    pallas_call x2, Pallas kernels, weight_product(): pl.pallas_call(functools.partial(weight_kernel, len(blocks), len(scaleds)...  11.7 us
    ppermute x5, waiting for transfers between devices, shift(): lax.ppermute(value, 'dp', [(i, (i + step) % n_dp) for i in range(n_dp)])  8.24 us
    ppermute x5, starting transfers between devices, shift(): lax.ppermute(value, 'dp', [(i, (i + step) % n_dp) for i in range(n_dp)])  6.44 us
    unnamed x18, local copies, waits for them, and re-layouts  5.47 us
    ppermute x5, waiting for transfers between devices, swap(): return lax.ppermute(value, 'expert', sibling)  3.65 us
  transfers between devices with their start and end apart: 30, of which 15 were waited for; matrix products, arithmetic and copies ran while one was open for 2% of the time, Pallas kernels for 32%

profile of v14, /device:TPU:0, one launch (start us, length us, event | category | flops | bytes accessed | tf_op | source)
XLA Modules:
  0.0 109.9 jit_solution(665306472694192710)
XLA Ops:
  0.6 0.5 collective-permute-start.8
  1.2 1.0 copy-done
  2.1 0.7 copy-done.1
  2.8 0.7 copy-done.3
  3.5 0.5 pack.1
  4.0 2.6 %collective-permute-start.1 = (bf16[48,2176]{1,0:T(8,128)(2,1)S(1)}, bf16[48,2176]{1,0:T(8,128)(2,1)S(1)}, u32[]{:S(2)}, u32[]{:S(2)}) collective-permute-start(bf16[48,2176]{1,0:T(8,128)(2,1)S(1)} %get-tuple-element.64), channel_id=1, source_target_pairs={{0,16},{16,0},{1,17},{17,1},{2,18},{18,2},{3,19},{19,3},{4,20},{20... | collective-permute-start | bytes 626696 | tf_op jit(solution)/shard_map/ppermute | solution.py:444
  6.6 1.5 %collective-permute-start.3 = (bf16[1,48,2176]{2,1,0:T(8,128)(2,1)S(1)}, bf16[1,48,2176]{2,1,0:T(8,128)(2,1)S(1)}, u32[]{:S(2)}, u32[]{:S(2)}) collective-permute-start(bf16[1,48,2176]{2,1,0:T(8,128)(2,1)S(1)} %bitcast.22), channel_id=1, source_target_pairs={{0,2},{1,3},{4,0},{5,1},{8,4},{9,5},{12,8},{13,9},{14,12},{15,13},... | collective-permute-start | bytes 626696 | tf_op jit(solution)/shard_map/ppermute | solution.py:447
  8.1 0.5 collective-permute-start
  8.6 0.7 dynamic-slice_bitcast_fusion.refs_0_
  9.3 3.1 %collective-permute-done.1 = bf16[48,2176]{1,0:T(8,128)(2,1)S(1)} collective-permute-done((bf16[48,2176]{1,0:T(8,128)(2,1)S(1)}, bf16[48,2176]{1,0:T(8,128)(2,1)S(1)}, u32[]{:S(2)}, u32[]{:S(2)}) %collective-permute-start.1) | collective-permute-done | bytes 208928 | tf_op jit(solution)/shard_map/ppermute | solution.py:444
  12.4 1.8 %collective-permute-start.4 = (bf16[1,48,2176]{2,1,0:T(8,128)(2,1)S(1)}, bf16[1,48,2176]{2,1,0:T(8,128)(2,1)S(1)}, u32[]{:S(2)}, u32[]{:S(2)}) collective-permute-start(bf16[1,48,2176]{2,1,0:T(8,128)(2,1)S(1)} %bitcast.27), channel_id=1, source_target_pairs={{0,2},{1,3},{4,0},{5,1},{8,4},{9,5},{12,8},{13,9},{14,12},{15,13},... | collective-permute-start | bytes 626696 | tf_op jit(solution)/shard_map/ppermute | solution.py:447
  14.2 1.3 %collective-permute-start.2 = (bf16[1,48,2176]{2,1,0:T(8,128)(2,1)S(1)}, bf16[1,48,2176]{2,1,0:T(8,128)(2,1)S(1)}, u32[]{:S(2)}, u32[]{:S(2)}) collective-permute-start(bf16[1,48,2176]{2,1,0:T(8,128)(2,1)S(1)} %bitcast.28), channel_id=1, source_target_pairs={{0,4},{1,5},{4,8},{5,9},{8,12},{9,13},{12,14},{13,15},{14,10},{15,... | collective-permute-start | bytes 626696 | tf_op jit(solution)/shard_map/ppermute | solution.py:447
  15.4 0.7 collective-permute-start.10
  16.2 4.4 %collective-permute-done.2 = bf16[1,48,2176]{2,1,0:T(8,128)(2,1)S(1)} collective-permute-done((bf16[1,48,2176]{2,1,0:T(8,128)(2,1)S(1)}, bf16[1,48,2176]{2,1,0:T(8,128)(2,1)S(1)}, u32[]{:S(2)}, u32[]{:S(2)}) %collective-permute-start.2) | collective-permute-done | bytes 208928 | tf_op jit(solution)/shard_map/ppermute | solution.py:447
  20.7 1.6 %collective-permute-start.6 = (bf16[2,48,2176]{2,1,0:T(8,128)(2,1)S(1)}, bf16[2,48,2176]{2,1,0:T(8,128)(2,1)S(1)}, u32[]{:S(2)}, u32[]{:S(2)}) collective-permute-start(bf16[2,48,2176]{2,1,0:T(8,128)(2,1)S(1)} %constant_dynamic-update-slice_fusion.2.refs_3_.refs_2_), channel_id=1, source_target_pairs={{0,2},{1,3},{4,0},{5,1},{8,4},{9,5},{12,8},{13,9},{14,12},{15,13},... | collective-permute-start | bytes 1253384 | tf_op jit(solution)/shard_map/ppermute | solution.py:447
  22.3 0.5 collective-permute-start.5
  22.8 7.9 %collective-permute-done.6.refs_5_.refs_4_ = bf16[2,48,2176]{2,1,0:T(8,128)(2,1)S(1)} collective-permute-done((bf16[2,48,2176]{2,1,0:T(8,128)(2,1)S(1)}, bf16[2,48,2176]{2,1,0:T(8,128)(2,1)S(1)}, u32[]{:S(2)}, u32[]{:S(2)}) %collective-permute-start.6) | collective-permute-done | bytes 417824 | tf_op jit(solution)/shard_map/ppermute | solution.py:447
  30.8 1.6 %collective-permute-start.11 = (bf16[2,48,2176]{2,1,0:T(8,128)(2,1)S(1)}, bf16[2,48,2176]{2,1,0:T(8,128)(2,1)S(1)}, u32[]{:S(2)}, u32[]{:S(2)}) collective-permute-start(bf16[2,48,2176]{2,1,0:T(8,128)(2,1)S(1)} %collective-permute-done.6.refs_5_.refs_4_), channel_id=1, source_target_pairs={{0,2},{1,3},{4,0},{5,1},{8,4},{9,5},{12,8},{13,9},{14,12},{15,13},... | collective-permute-start | bytes 1253384 | tf_op jit(solution)/shard_map/ppermute | solution.py:447
  32.4 0.5 collective-permute-start.9
  32.8 1.9 %copy-done.4 = bf16[1,768,2048]{2,1,0:T(8,128)(2,1)S(1)} copy-done((bf16[1,768,2048]{2,1,0:T(8,128)(2,1)S(1)}, bf16[1,768,2048]{2,1,0:T(8,128)(2,1)}, u32[]{:S(2)}) %copy-start.4) | copy-done | bytes 3145752
  34.7 1.2 %copy-done.6 = bf16[1,1,16,36,768]{4,2,3,1,0:T(8,128)(2,1)S(1)} copy-done((bf16[1,1,16,36,768]{4,2,3,1,0:T(8,128)(2,1)S(1)}, bf16[1,1,16,36,768]{4,2,3,1,0:T(8,128)(2,1)}, u32[]{:S(2)}) %copy-start.6) | copy-done | bytes 884760
  35.9 6.7 %block_product.3 = (bf16[48,2176]{1,0:T(8,128)(2,1)S(1)}, bf16[48,2176]{1,0:T(8,128)(2,1)S(1)}, bf16[48,2176]{1,0:T(8,128)(2,1)S(1)}, bf16[48,2176]{1,0:T(8,128)...) custom-call(s32[10]{0:T(128)S(1)} %dynamic-slice_bitcast_fusion.refs, ...), custom_call_target="tpu_custom_call" | custom-call | flops 3019898880 | bytes 9117696 | tf_op jit(solution)/shard_map/block_product/pallas_call | solution.py:299
  42.8 1.6 %collective-permute-start.14 = (bf16[1,48,2176]{2,1,0:T(8,128)(2,1)S(1)}, bf16[1,48,2176]{2,1,0:T(8,128)(2,1)S(1)}, u32[]{:S(2)}, u32[]{:S(2)}) collective-permute-start(bf16[1,48,2176]{2,1,0:T(8,128)(2,1)S(1)} %slice.7), channel_id=1, source_target_pairs={{0,2},{1,3},{4,0},{5,1},{8,4},{9,5},{12,8},{13,9},{14,12},{15,13},... | collective-permute-start | bytes 626696 | tf_op jit(solution)/shard_map/ppermute | solution.py:447
  44.4 0.5 collective-permute-start.13
  44.9 0.3 collective-permute-done.12.refs_7_.refs_8_
  45.2 6.7 %block_product.4 = (bf16[48,2176]{1,0:T(8,128)(2,1)S(1)}, bf16[48,2176]{1,0:T(8,128)(2,1)S(1)}, bf16[48,2176]{1,0:T(8,128)(2,1)S(1)}, bf16[48,2176]{1,0:T(8,128)...) custom-call(s32[10]{0:T(128)S(1)} %dynamic-slice_bitcast_fusion.refs_0_,, ...), custom_call_target="tpu_custom_call" | custom-call | flops 3019898880 | bytes 9117696 | tf_op jit(solution)/shard_map/block_product/pallas_call | solution.py:299
  51.9 1.6 %collective-permute-start.19 = (bf16[2,240,768]{2,1,0:T(8,128)(2,1)S(1)}, bf16[2,240,768]{2,1,0:T(8,128)(2,1)S(1)}, u32[]{:S(2)}, u32[]{:S(2)}) collective-permute-start(bf16[2,240,768]{2,1,0:T(8,128)(2,1)S(1)} %get-tuple-element.84), channel_id=1, source_target_pairs={{0,16},{16,0},{1,17},{17,1},{2,18},{18,2},{3,19},{19,3},{4,20},{20... | collective-permute-start | bytes 2211848 | tf_op jit(solution)/shard_map/ppermute | solution.py:444
  53.4 7.6 %block_product.5 = (bf16[48,2176]{1,0:T(8,128)(2,1)S(1)}, bf16[48,2176]{1,0:T(8,128)(2,1)S(1)}, bf16[48,2176]{1,0:T(8,128)(2,1)S(1)}, bf16[48,2176]{1,0:T(8,128)...) custom-call(s32[10]{0:T(128)S(1)} %dynamic-slice_bitcast_fusion.refs, ...), custom_call_target="tpu_custom_call" | custom-call | flops 3623878656 | bytes 9682944 | tf_op jit(solution)/shard_map/block_product/pallas_call | solution.py:299
  61.1 0.7 collective-permute-start.15
  61.8 1.4 %collective-permute-start.17 = (bf16[1,48,2176]{2,1,0:T(8,128)(2,1)S(1)}, bf16[1,48,2176]{2,1,0:T(8,128)(2,1)S(1)}, u32[]{:S(2)}, u32[]{:S(2)}) collective-permute-start(bf16[1,48,2176]{2,1,0:T(8,128)(2,1)S(1)} %bitcast.43), channel_id=1, source_target_pairs={{0,2},{1,3},{4,0},{5,1},{8,4},{9,5},{12,8},{13,9},{14,12},{15,13},... | collective-permute-start | bytes 626696 | tf_op jit(solution)/shard_map/ppermute | solution.py:447
  63.1 0.6 collective-permute-start.20
  63.7 4.3 %collective-permute-done.15.refs_2_ = bf16[1,48,2176]{2,1,0:T(8,128)(2,1)S(1)} collective-permute-done((bf16[1,48,2176]{2,1,0:T(8,128)(2,1)S(1)}, bf16[1,48,2176]{2,1,0:T(8,128)(2,1)S(1)}, u32[]{:S(2)}, u32[]{:S(2)}) %collective-permute-start.15) | collective-permute-done | bytes 208928 | tf_op jit(solution)/shard_map/ppermute | solution.py:447
  68.1 0.3 collective-permute-done.17.refs_2_
  68.4 0.1 sums.7
  68.5 1.4 %collective-permute-start.18 = (bf16[2,48,2176]{2,1,0:T(8,128)(2,1)S(1)}, bf16[2,48,2176]{2,1,0:T(8,128)(2,1)S(1)}, u32[]{:S(2)}, u32[]{:S(2)}) collective-permute-start(bf16[2,48,2176]{2,1,0:T(8,128)(2,1)S(1)} %sums.7), channel_id=1, source_target_pairs={{0,2},{1,3},{4,0},{5,1},{8,4},{9,5},{12,8},{13,9},{14,12},{15,13},... | collective-permute-start | bytes 1253384 | tf_op jit(solution)/shard_map/ppermute | solution.py:447
  69.9 0.6 collective-permute-start.16
  70.5 0.7 collective-permute-done.19.refs_6_
  71.3 5.2 %weight_product.2 = bf16[768,2048]{1,0:T(8,128)(2,1)S(1)} custom-call(bf16[1,48,2176]{2,1,0:T(8,128)(2,1)S(1)} %bitcast.25, bf16[2,48,2176]{2,1,0:T(8,128)(2,1)S(1)} %constant_dynamic-update-slice_fusion.refs_2_.refs_1_, bf16[2,48,2176]{2,1,0:T(8,128)(2,1)S(1)} %constant_dynamic-update-slice_fusion.2.refs_3_.refs_2_, ...), custom_call_target="tpu_custom_call" | custom-call | flops 2415919104 | bytes 10616832 | tf_op jit(solution)/shard_map/weight_product/pallas_call | solution.py:381
  76.5 3.4 %collective-permute-done.20.refs_7_ = bf16[2,144,768]{2,1,0:T(8,128)(2,1)S(1)} collective-permute-done((bf16[2,144,768]{2,1,0:T(8,128)(2,1)S(1)}, bf16[2,144,768]{2,1,0:T(8,128)(2,1)S(1)}, u32[]{:S(2)}, u32[]{:S(2)}) %collective-permute-start.20) | collective-permute-done | bytes 442400 | tf_op jit(solution)/shard_map/ppermute | solution.py:444
  79.9 0.1 collective-permute-done.16.refs_2_
  80.0 0.1 sums.9
  80.1 0.1 sums.8
  80.2 1.2 %collective-permute-start.22 = (bf16[2,48,2176]{2,1,0:T(8,128)(2,1)S(1)}, bf16[2,48,2176]{2,1,0:T(8,128)(2,1)S(1)}, u32[]{:S(2)}, u32[]{:S(2)}) collective-permute-start(bf16[2,48,2176]{2,1,0:T(8,128)(2,1)S(1)} %sums.8), channel_id=1, source_target_pairs={{0,4},{1,5},{4,8},{5,9},{8,12},{9,13},{12,14},{13,15},{14,10},{15,... | collective-permute-start | bytes 1253384 | tf_op jit(solution)/shard_map/ppermute | solution.py:447
  81.4 0.9 collective-permute-start.23
  82.3 3.4 %collective-permute-done.21.refs_14_ = bf16[768,2048]{1,0:T(8,128)(2,1)S(1)} collective-permute-done((bf16[768,2048]{1,0:T(8,128)(2,1)S(1)}, bf16[768,2048]{1,0:T(8,128)(2,1)S(1)}, u32[]{:S(2)}, u32[]{:S(2)}) %collective-permute-start.21) | collective-permute-done | bytes 3145760 | tf_op jit(solution)/shard_map/ppermute | solution.py:450
  85.7 6.5 %weight_product.3 = f32[768,2048]{1,0:T(8,128)} custom-call(bf16[1,48,2176]{2,1,0:T(8,128)(2,1)S(1)} %bitcast.26, bf16[2,48,2176]{2,1,0:T(8,128)(2,1)S(1)} %constant_dynamic-update-slice_fusion.refs_2_.refs_1_, bf16[2,48,2176]{2,1,0:T(8,128)(2,1)S(1)} %constant_dynamic-update-slice_fusion.2.refs_3_.refs_2_, ...), custom_call_target="tpu_custom_call" | custom-call | flops 2415919104 | bytes 10616832 | tf_op jit(solution)/shard_map/weight_product/pallas_call | solution.py:381
  92.1 1.3 %spread_product.1 = (bf16[576,768]{1,0:T(8,128)(2,1)S(1)}, bf16[576,768]{1,0:T(8,128)(2,1)S(1)}) custom-call(s32[240,2]{1,0:T(8,128)S(1)} %get-tuple-element.98.refs_0_, s32[144,2]{1,0:T(8,128)S(1)} %get-tuple-element.99.refs_1_, f32[240,2]{1,0:T(8,128)S(1)} %get-tuple-element.100.refs_2_, f32[144,2]{1,0:T(8,128)S(1)} %get-tuple-element.101.refs_3_, ...), custom_call_target="tpu_custom_call" | custom-call | flops 679477248 | bytes 3538944 | tf_op jit(solution)/shard_map/spread_product/pallas_call | solution.py:346
  93.5 0.2 collective-permute-start.24
  93.7 0.1 sums.10
  93.8 0.1 sums.11
  93.9 1.1 %collective-permute-start.27 = (bf16[1,48,2176]{2,1,0:T(8,128)(2,1)S(1)}, bf16[1,48,2176]{2,1,0:T(8,128)(2,1)S(1)}, u32[]{:S(2)}, u32[]{:S(2)}) collective-permute-start(bf16[1,48,2176]{2,1,0:T(8,128)(2,1)S(1)} %get-tuple-element.117), channel_id=1, source_target_pairs={{0,4},{1,5},{4,8},{5,9},{8,12},{9,13},{12,14},{13,15},{14,10},{15,... | collective-permute-start | bytes 626696 | tf_op jit(solution)/shard_map/ppermute | solution.py:447
  95.0 0.9 collective-permute-start.28
  96.0 1.1 collective-permute-start.25
  97.1 0.9 collective-permute-start.26
  98.0 3.9 %collective-permute-done.27.refs_1_ = bf16[1,48,2176]{2,1,0:T(8,128)(2,1)S(1)} collective-permute-done((bf16[1,48,2176]{2,1,0:T(8,128)(2,1)S(1)}, bf16[1,48,2176]{2,1,0:T(8,128)(2,1)S(1)}, u32[]{:S(2)}, u32[]{:S(2)}) %collective-permute-start.27) | collective-permute-done | bytes 208928 | tf_op jit(solution)/shard_map/ppermute | solution.py:447
  101.9 1.1 %collective-permute-done.28.refs_2_ = bf16[1,48,2176]{2,1,0:T(8,128)(2,1)S(1)} collective-permute-done((bf16[1,48,2176]{2,1,0:T(8,128)(2,1)S(1)}, bf16[1,48,2176]{2,1,0:T(8,128)(2,1)S(1)}, u32[]{:S(2)}, u32[]{:S(2)}) %collective-permute-start.28) | collective-permute-done | bytes 208928 | tf_op jit(solution)/shard_map/ppermute | solution.py:447
  103.0 0.1 close.3
  103.1 1.0 collective-permute-start.29
  104.2 1.7 %collective-permute-done.25.refs_1_ = bf16[1,48,2176]{2,1,0:T(8,128)(2,1)S(1)} collective-permute-done((bf16[1,48,2176]{2,1,0:T(8,128)(2,1)S(1)}, bf16[1,48,2176]{2,1,0:T(8,128)(2,1)S(1)}, u32[]{:S(2)}, u32[]{:S(2)}) %collective-permute-start.25) | collective-permute-done | bytes 208928 | tf_op jit(solution)/shard_map/ppermute | solution.py:447
  105.9 0.9 collective-permute-done.26.refs_2_
  106.8 0.1 close.2.refs_0_
  106.9 1.1 %add.8 = bf16[576,768]{1,0:T(8,128)(2,1)} add(bf16[576,768]{1,0:T(8,128)(2,1)S(1)} %get-tuple-element.104, bf16[576,768]{1,0:T(8,128)(2,1)S(1)} %collective-permute-done.24) | non-fusion elementwise | flops 442368 | bytes 2654208 | tf_op jit(solution)/shard_map/add | solution.py:558
  108.0 1.0 collective-permute-done.29.refs_1_
  109.0 0.9 home.1
  (36 shorter events, 0.3 us)
Async XLA Ops:
  0.6 32.2 %collective-permute-start.8 = (bf16[768,2048]{1,0:T(8,128)(2,1)}, bf16[768,2048]{1,0:T(8,128)(2,1)}, u32[]{:S(2)}, u32[]{:S(2)}) collective-permute-start(bf16[768,2048]{1,0:T(8,128)(2,1)} %bitcast.35), channel_id=1, source_target_pairs={{0,1},{1,0},{2,3},{3,2},{4,5},{5,4},{6,7},{7,6},{8,9},{9,8},{10,11... | collective-permute-start | bytes 9437192 | tf_op jit(solution)/shard_map/ppermute | solution.py:450
  1.1 1.0 copy-start
  2.1 0.7 copy-start.1
  2.8 0.7 copy-start.3
  4.0 8.4 %collective-permute-start.1 = (bf16[48,2176]{1,0:T(8,128)(2,1)S(1)}, bf16[48,2176]{1,0:T(8,128)(2,1)S(1)}, u32[]{:S(2)}, u32[]{:S(2)}) collective-permute-start(bf16[48,2176]{1,0:T(8,128)(2,1)S(1)} %get-tuple-element.64), channel_id=1, source_target_pairs={{0,16},{16,0},{1,17},{17,1},{2,18},{18,2},{3,19},{19,3},{4,20},{20... | collective-permute-start | bytes 626696 | tf_op jit(solution)/shard_map/ppermute | solution.py:444
  6.6 7.6 %collective-permute-start.3 = (bf16[1,48,2176]{2,1,0:T(8,128)(2,1)S(1)}, bf16[1,48,2176]{2,1,0:T(8,128)(2,1)S(1)}, u32[]{:S(2)}, u32[]{:S(2)}) collective-permute-start(bf16[1,48,2176]{2,1,0:T(8,128)(2,1)S(1)} %bitcast.22), channel_id=1, source_target_pairs={{0,2},{1,3},{4,0},{5,1},{8,4},{9,5},{12,8},{13,9},{14,12},{15,13},... | collective-permute-start | bytes 626696 | tf_op jit(solution)/shard_map/ppermute | solution.py:447
  8.1 7.3 %collective-permute-start = (bf16[1,48,2176]{2,1,0:T(8,128)(2,1)S(1)}, bf16[1,48,2176]{2,1,0:T(8,128)(2,1)S(1)}, u32[]{:S(2)}, u32[]{:S(2)}) collective-permute-start(bf16[1,48,2176]{2,1,0:T(8,128)(2,1)S(1)} %bitcast.23), channel_id=1, source_target_pairs={{0,4},{1,5},{4,8},{5,9},{8,12},{9,13},{12,14},{13,15},{14,10},{15,... | collective-permute-start | bytes 626696 | tf_op jit(solution)/shard_map/ppermute | solution.py:447
  8.6 24.2 %collective-permute-start.7 = (bf16[576,768]{1,0:T(8,128)(2,1)}, bf16[576,768]{1,0:T(8,128)(2,1)S(1)}, u32[]{:S(2)}, u32[]{:S(2)}) collective-permute-start(bf16[576,768]{1,0:T(8,128)(2,1)} %bitcast.39), channel_id=1, source_target_pairs={{0,1},{1,0},{2,3},{3,2},{4,5},{5,4},{6,7},{7,6},{8,9},{9,8},{10,11... | collective-permute-start | bytes 2654216 | tf_op jit(solution)/shard_map/ppermute | solution.py:450
  12.4 8.3 %collective-permute-start.4 = (bf16[1,48,2176]{2,1,0:T(8,128)(2,1)S(1)}, bf16[1,48,2176]{2,1,0:T(8,128)(2,1)S(1)}, u32[]{:S(2)}, u32[]{:S(2)}) collective-permute-start(bf16[1,48,2176]{2,1,0:T(8,128)(2,1)S(1)} %bitcast.27), channel_id=1, source_target_pairs={{0,2},{1,3},{4,0},{5,1},{8,4},{9,5},{12,8},{13,9},{14,12},{15,13},... | collective-permute-start | bytes 626696 | tf_op jit(solution)/shard_map/ppermute | solution.py:447
  14.2 6.5 %collective-permute-start.2 = (bf16[1,48,2176]{2,1,0:T(8,128)(2,1)S(1)}, bf16[1,48,2176]{2,1,0:T(8,128)(2,1)S(1)}, u32[]{:S(2)}, u32[]{:S(2)}) collective-permute-start(bf16[1,48,2176]{2,1,0:T(8,128)(2,1)S(1)} %bitcast.28), channel_id=1, source_target_pairs={{0,4},{1,5},{4,8},{5,9},{8,12},{9,13},{12,14},{13,15},{14,10},{15,... | collective-permute-start | bytes 626696 | tf_op jit(solution)/shard_map/ppermute | solution.py:447
  15.4 27.2 %collective-permute-start.10 = (bf16[576,768]{1,0:T(8,128)(2,1)}, bf16[576,768]{1,0:T(8,128)(2,1)S(1)}, u32[]{:S(2)}, u32[]{:S(2)}) collective-permute-start(bf16[576,768]{1,0:T(8,128)(2,1)} %bitcast.40), channel_id=1, source_target_pairs={{0,16},{16,0},{1,17},{17,1},{2,18},{18,2},{3,19},{19,3},{4,20},{20... | collective-permute-start | bytes 2654216 | tf_op jit(solution)/shard_map/ppermute | solution.py:444
  20.7 10.1 %collective-permute-start.6 = (bf16[2,48,2176]{2,1,0:T(8,128)(2,1)S(1)}, bf16[2,48,2176]{2,1,0:T(8,128)(2,1)S(1)}, u32[]{:S(2)}, u32[]{:S(2)}) collective-permute-start(bf16[2,48,2176]{2,1,0:T(8,128)(2,1)S(1)} %constant_dynamic-update-slice_fusion.2.refs_3_.refs_2_), channel_id=1, source_target_pairs={{0,2},{1,3},{4,0},{5,1},{8,4},{9,5},{12,8},{13,9},{14,12},{15,13},... | collective-permute-start | bytes 1253384 | tf_op jit(solution)/shard_map/ppermute | solution.py:447
  22.3 10.0 %collective-permute-start.5 = (bf16[2,48,2176]{2,1,0:T(8,128)(2,1)S(1)}, bf16[2,48,2176]{2,1,0:T(8,128)(2,1)S(1)}, u32[]{:S(2)}, u32[]{:S(2)}) collective-permute-start(bf16[2,48,2176]{2,1,0:T(8,128)(2,1)S(1)} %constant_dynamic-update-slice_fusion.refs_2_.refs_1_), channel_id=1, source_target_pairs={{0,4},{1,5},{4,8},{5,9},{8,12},{9,13},{12,14},{13,15},{14,10},{15,... | collective-permute-start | bytes 1253384 | tf_op jit(solution)/shard_map/ppermute | solution.py:447
  30.8 11.9 %collective-permute-start.11 = (bf16[2,48,2176]{2,1,0:T(8,128)(2,1)S(1)}, bf16[2,48,2176]{2,1,0:T(8,128)(2,1)S(1)}, u32[]{:S(2)}, u32[]{:S(2)}) collective-permute-start(bf16[2,48,2176]{2,1,0:T(8,128)(2,1)S(1)} %collective-permute-done.6.refs_5_.refs_4_), channel_id=1, source_target_pairs={{0,2},{1,3},{4,0},{5,1},{8,4},{9,5},{12,8},{13,9},{14,12},{15,13},... | collective-permute-start | bytes 1253384 | tf_op jit(solution)/shard_map/ppermute | solution.py:447
  32.4 10.3 %collective-permute-start.9 = (bf16[2,48,2176]{2,1,0:T(8,128)(2,1)S(1)}, bf16[2,48,2176]{2,1,0:T(8,128)(2,1)S(1)}, u32[]{:S(2)}, u32[]{:S(2)}) collective-permute-start(bf16[2,48,2176]{2,1,0:T(8,128)(2,1)S(1)} %collective-permute-done.5.refs_4_.refs_3_), channel_id=1, source_target_pairs={{0,4},{1,5},{4,8},{5,9},{8,12},{9,13},{12,14},{13,15},{14,10},{15,... | collective-permute-start | bytes 1253384 | tf_op jit(solution)/shard_map/ppermute | solution.py:447
  32.8 1.9 %copy-start.4 = (bf16[1,768,2048]{2,1,0:T(8,128)(2,1)S(1)}, bf16[1,768,2048]{2,1,0:T(8,128)(2,1)}, u32[]{:S(2)}) copy-start(bf16[1,768,2048]{2,1,0:T(8,128)(2,1)} %param.9) | copy-start | bytes 9437188
  34.7 1.2 %copy-start.6 = (bf16[1,1,16,36,768]{4,2,3,1,0:T(8,128)(2,1)S(1)}, bf16[1,1,16,36,768]{4,2,3,1,0:T(8,128)(2,1)}, u32[]{:S(2)}) copy-start(bf16[1,1,16,36,768]{4,2,3,1,0:T(8,128)(2,1)} %param.8) | copy-start | bytes 2654212
  35.9 9.3 %copy-start.5 = (bf16[1,768,2048]{2,1,0:T(8,128)(2,1)S(1)}, bf16[1,768,2048]{2,1,0:T(8,128)(2,1)}, u32[]{:S(2)}) copy-start(bf16[1,768,2048]{2,1,0:T(8,128)(2,1)} %param.9) | copy-start | bytes 9437188
  42.7 2.5 %collective-permute-start.12 = (bf16[576,768]{1,0:T(8,128)(2,1)S(1)}, bf16[576,768]{1,0:T(8,128)(2,1)S(1)}, u32[]{:S(2)}, u32[]{:S(2)}) collective-permute-start(bf16[576,768]{1,0:T(8,128)(2,1)S(1)} %collective-permute-done.10.refs_6_.refs_7_), channel_id=1, source_target_pairs={{0,1},{1,0},{2,3},{3,2},{4,5},{5,4},{6,7},{7,6},{8,9},{9,8},{10,11... | collective-permute-start | bytes 2654216 | tf_op jit(solution)/shard_map/ppermute | solution.py:450
  42.8 10.6 %copy-start.7 = (bf16[1,1,16,36,768]{4,2,3,1,0:T(8,128)(2,1)S(1)}, bf16[1,1,16,36,768]{4,2,3,1,0:T(8,128)(2,1)}, u32[]{:S(2)}) copy-start(bf16[1,1,16,36,768]{4,2,3,1,0:T(8,128)(2,1)} %param.8) | copy-start | bytes 2654212
  42.8 9.0 %collective-permute-start.14 = (bf16[1,48,2176]{2,1,0:T(8,128)(2,1)S(1)}, bf16[1,48,2176]{2,1,0:T(8,128)(2,1)S(1)}, u32[]{:S(2)}, u32[]{:S(2)}) collective-permute-start(bf16[1,48,2176]{2,1,0:T(8,128)(2,1)S(1)} %slice.7), channel_id=1, source_target_pairs={{0,2},{1,3},{4,0},{5,1},{8,4},{9,5},{12,8},{13,9},{14,12},{15,13},... | collective-permute-start | bytes 626696 | tf_op jit(solution)/shard_map/ppermute | solution.py:447
  44.4 7.4 %collective-permute-start.13 = (bf16[1,48,2176]{2,1,0:T(8,128)(2,1)S(1)}, bf16[1,48,2176]{2,1,0:T(8,128)(2,1)S(1)}, u32[]{:S(2)}, u32[]{:S(2)}) collective-permute-start(bf16[1,48,2176]{2,1,0:T(8,128)(2,1)S(1)} %slice.6), channel_id=1, source_target_pairs={{0,4},{1,5},{4,8},{5,9},{8,12},{9,13},{12,14},{13,15},{14,10},{15,... | collective-permute-start | bytes 626696 | tf_op jit(solution)/shard_map/ppermute | solution.py:447
  51.9 19.4 %collective-permute-start.19 = (bf16[2,240,768]{2,1,0:T(8,128)(2,1)S(1)}, bf16[2,240,768]{2,1,0:T(8,128)(2,1)S(1)}, u32[]{:S(2)}, u32[]{:S(2)}) collective-permute-start(bf16[2,240,768]{2,1,0:T(8,128)(2,1)S(1)} %get-tuple-element.84), channel_id=1, source_target_pairs={{0,16},{16,0},{1,17},{17,1},{2,18},{18,2},{3,19},{19,3},{4,20},{20... | collective-permute-start | bytes 2211848 | tf_op jit(solution)/shard_map/ppermute | solution.py:444
  61.1 7.0 %collective-permute-start.15 = (bf16[1,48,2176]{2,1,0:T(8,128)(2,1)S(1)}, bf16[1,48,2176]{2,1,0:T(8,128)(2,1)S(1)}, u32[]{:S(2)}, u32[]{:S(2)}) collective-permute-start(bf16[1,48,2176]{2,1,0:T(8,128)(2,1)S(1)} %bitcast.44), channel_id=1, source_target_pairs={{0,4},{1,5},{4,8},{5,9},{8,12},{9,13},{12,14},{13,15},{14,10},{15,... | collective-permute-start | bytes 626696 | tf_op jit(solution)/shard_map/ppermute | solution.py:447
  61.8 6.6 %collective-permute-start.17 = (bf16[1,48,2176]{2,1,0:T(8,128)(2,1)S(1)}, bf16[1,48,2176]{2,1,0:T(8,128)(2,1)S(1)}, u32[]{:S(2)}, u32[]{:S(2)}) collective-permute-start(bf16[1,48,2176]{2,1,0:T(8,128)(2,1)S(1)} %bitcast.43), channel_id=1, source_target_pairs={{0,2},{1,3},{4,0},{5,1},{8,4},{9,5},{12,8},{13,9},{14,12},{15,13},... | collective-permute-start | bytes 626696 | tf_op jit(solution)/shard_map/ppermute | solution.py:447
  63.1 16.8 %collective-permute-start.20 = (bf16[2,144,768]{2,1,0:T(8,128)(2,1)S(1)}, bf16[2,144,768]{2,1,0:T(8,128)(2,1)S(1)}, u32[]{:S(2)}, u32[]{:S(2)}) collective-permute-start(bf16[2,144,768]{2,1,0:T(8,128)(2,1)S(1)} %get-tuple-element.96), channel_id=1, source_target_pairs={{0,16},{16,0},{1,17},{17,1},{2,18},{18,2},{3,19},{19,3},{4,20},{20... | collective-permute-start | bytes 1327112 | tf_op jit(solution)/shard_map/ppermute | solution.py:444
  68.5 11.5 %collective-permute-start.18 = (bf16[2,48,2176]{2,1,0:T(8,128)(2,1)S(1)}, bf16[2,48,2176]{2,1,0:T(8,128)(2,1)S(1)}, u32[]{:S(2)}, u32[]{:S(2)}) collective-permute-start(bf16[2,48,2176]{2,1,0:T(8,128)(2,1)S(1)} %sums.7), channel_id=1, source_target_pairs={{0,2},{1,3},{4,0},{5,1},{8,4},{9,5},{12,8},{13,9},{14,12},{15,13},... | collective-permute-start | bytes 1253384 | tf_op jit(solution)/shard_map/ppermute | solution.py:447
  69.9 10.1 %collective-permute-start.16 = (bf16[2,48,2176]{2,1,0:T(8,128)(2,1)S(1)}, bf16[2,48,2176]{2,1,0:T(8,128)(2,1)S(1)}, u32[]{:S(2)}, u32[]{:S(2)}) collective-permute-start(bf16[2,48,2176]{2,1,0:T(8,128)(2,1)S(1)} %sums.6), channel_id=1, source_target_pairs={{0,4},{1,5},{4,8},{5,9},{8,12},{9,13},{12,14},{13,15},{14,10},{15,... | collective-permute-start | bytes 1253384 | tf_op jit(solution)/shard_map/ppermute | solution.py:447
  80.0 5.7 %collective-permute-start.21 = (bf16[768,2048]{1,0:T(8,128)(2,1)S(1)}, bf16[768,2048]{1,0:T(8,128)(2,1)S(1)}, u32[]{:S(2)}, u32[]{:S(2)}) collective-permute-start(bf16[768,2048]{1,0:T(8,128)(2,1)S(1)} %weight_product.2), channel_id=1, source_target_pairs={{0,1},{1,0},{2,3},{3,2},{4,5},{5,4},{6,7},{7,6},{8,9},{9,8},{10,11... | collective-permute-start | bytes 9437192 | tf_op jit(solution)/shard_map/ppermute | solution.py:450
  80.2 13.2 %collective-permute-start.22 = (bf16[2,48,2176]{2,1,0:T(8,128)(2,1)S(1)}, bf16[2,48,2176]{2,1,0:T(8,128)(2,1)S(1)}, u32[]{:S(2)}, u32[]{:S(2)}) collective-permute-start(bf16[2,48,2176]{2,1,0:T(8,128)(2,1)S(1)} %sums.8), channel_id=1, source_target_pairs={{0,4},{1,5},{4,8},{5,9},{8,12},{9,13},{12,14},{13,15},{14,10},{15,... | collective-permute-start | bytes 1253384 | tf_op jit(solution)/shard_map/ppermute | solution.py:447
  81.4 12.1 %collective-permute-start.23 = (bf16[2,48,2176]{2,1,0:T(8,128)(2,1)S(1)}, bf16[2,48,2176]{2,1,0:T(8,128)(2,1)S(1)}, u32[]{:S(2)}, u32[]{:S(2)}) collective-permute-start(bf16[2,48,2176]{2,1,0:T(8,128)(2,1)S(1)} %sums.9), channel_id=1, source_target_pairs={{0,2},{1,3},{4,0},{5,1},{8,4},{9,5},{12,8},{13,9},{14,12},{15,13},... | collective-permute-start | bytes 1253384 | tf_op jit(solution)/shard_map/ppermute | solution.py:447
  93.5 13.4 %collective-permute-start.24 = (bf16[576,768]{1,0:T(8,128)(2,1)S(1)}, bf16[576,768]{1,0:T(8,128)(2,1)S(1)}, u32[]{:S(2)}, u32[]{:S(2)}) collective-permute-start(bf16[576,768]{1,0:T(8,128)(2,1)S(1)} %get-tuple-element.106), channel_id=1, source_target_pairs={{0,1},{1,0},{2,3},{3,2},{4,5},{5,4},{6,7},{7,6},{8,9},{9,8},{10,11... | collective-permute-start | bytes 2654216 | tf_op jit(solution)/shard_map/ppermute | solution.py:450
  93.7 15.3 %copy-start.2 = (s32[48,8]{0,1:T(8,128)S(1)}, s32[48,8]{0,1:T(8,128)}, u32[]{:S(2)}) copy-start(s32[48,8]{0,1:T(8,128)} %param.6) | copy-start | bytes 4612
  93.9 8.0 %collective-permute-start.27 = (bf16[1,48,2176]{2,1,0:T(8,128)(2,1)S(1)}, bf16[1,48,2176]{2,1,0:T(8,128)(2,1)S(1)}, u32[]{:S(2)}, u32[]{:S(2)}) collective-permute-start(bf16[1,48,2176]{2,1,0:T(8,128)(2,1)S(1)} %get-tuple-element.117), channel_id=1, source_target_pairs={{0,4},{1,5},{4,8},{5,9},{8,12},{9,13},{12,14},{13,15},{14,10},{15,... | collective-permute-start | bytes 626696 | tf_op jit(solution)/shard_map/ppermute | solution.py:447
  95.0 8.0 %collective-permute-start.28 = (bf16[1,48,2176]{2,1,0:T(8,128)(2,1)S(1)}, bf16[1,48,2176]{2,1,0:T(8,128)(2,1)S(1)}, u32[]{:S(2)}, u32[]{:S(2)}) collective-permute-start(bf16[1,48,2176]{2,1,0:T(8,128)(2,1)S(1)} %get-tuple-element.119), channel_id=1, source_target_pairs={{0,2},{1,3},{4,0},{5,1},{8,4},{9,5},{12,8},{13,9},{14,12},{15,13},... | collective-permute-start | bytes 626696 | tf_op jit(solution)/shard_map/ppermute | solution.py:447
  96.0 9.9 %collective-permute-start.25 = (bf16[1,48,2176]{2,1,0:T(8,128)(2,1)S(1)}, bf16[1,48,2176]{2,1,0:T(8,128)(2,1)S(1)}, u32[]{:S(2)}, u32[]{:S(2)}) collective-permute-start(bf16[1,48,2176]{2,1,0:T(8,128)(2,1)S(1)} %get-tuple-element.111), channel_id=1, source_target_pairs={{0,4},{1,5},{4,8},{5,9},{8,12},{9,13},{12,14},{13,15},{14,10},{15,... | collective-permute-start | bytes 626696 | tf_op jit(solution)/shard_map/ppermute | solution.py:447
  97.1 9.7 %collective-permute-start.26 = (bf16[1,48,2176]{2,1,0:T(8,128)(2,1)S(1)}, bf16[1,48,2176]{2,1,0:T(8,128)(2,1)S(1)}, u32[]{:S(2)}, u32[]{:S(2)}) collective-permute-start(bf16[1,48,2176]{2,1,0:T(8,128)(2,1)S(1)} %get-tuple-element.115), channel_id=1, source_target_pairs={{0,2},{1,3},{4,0},{5,1},{8,4},{9,5},{12,8},{13,9},{14,12},{15,13},... | collective-permute-start | bytes 626696 | tf_op jit(solution)/shard_map/ppermute | solution.py:447
  103.1 5.9 %collective-permute-start.29 = (bf16[48,2176]{1,0:T(8,128)(2,1)S(1)}, bf16[48,2176]{1,0:T(8,128)(2,1)S(1)}, u32[]{:S(2)}, u32[]{:S(2)}) collective-permute-start(bf16[48,2176]{1,0:T(8,128)(2,1)S(1)} %close.3), channel_id=1, source_target_pairs={{0,16},{16,0},{1,17},{17,1},{2,18},{18,2},{3,19},{19,3},{4,20},{20... | collective-permute-start | bytes 626696 | tf_op jit(solution)/shard_map/ppermute | solution.py:444

commit v15 on v14

--- a/solution.py
+++ b/solution.py
@@ -546,16 +546,16 @@
         )
         swapped = swap(after(other, *second, *[sent[-1] for sent in sent_back]))
         third = hop_on(half - 2, other)
-        weight_grad = weight_product(
-            [after(refs[0], *sending)] + refs[1:], layout, scaleds, 0, jnp.float32, width, swapped
-        )
         spread, spread_other = spread_product(
-            [after(facts[0][0], *second, weight_grad)] + [fact[0] for fact in facts[1:]],
+            [after(facts[0][0], *second, *sending)] + [fact[0] for fact in facts[1:]],
             [fact[1] for fact in facts],
             [own_back] + sent_back,
             slots,
         )
-        hidden_grad = spread + swap(after(spread_other, *third))
+        weight_grad = weight_product(
+            [after(refs[0], spread)] + refs[1:], layout, scaleds, 0, jnp.float32, width, swapped
+        )
+        hidden_grad = spread + swap(after(spread_other, *third, weight_grad))
         hidden_grad = hidden_grad.reshape(cap, n_ex, ff).transpose(1, 0, 2)[None, None]
         for hop in range(half - 3, 1, -1):
             hop_on(hop, spread)
@@ -564,7 +564,7 @@
         ends = {}
         for direction in (1, -1):
             jobs = [([parts[direction, d] for d in g], carry[direction], 0, len(g), g[0]) for g in groups]
-            ends[direction] = [ring_send(after(value, spread), direction) for value in sums(jobs)]
+            ends[direction] = [ring_send(after(value, weight_grad), direction) for value in sums(jobs)]
         pieces = {}
         for i, group in enumerate(groups):
             totals = close([parts[0, d] for d in group], ends[1][i], ends[-1][i])

time: 110 us -> 110 us (level)
    ppermute x20, waiting for transfers between devices: 24.8 us -> 26.4 us  [ring_send(): return lax.ppermute(value, 'expert', forward if step > 0 else backward)]
    ppermute x5, waiting for transfers between devices: 3.65 us -> 2.33 us  [swap(): return lax.ppermute(value, 'expert', sibling)]
  transfers between devices with their start and end apart: 30 -> 30, of which waited for: 15 -> 17; matrix products, arithmetic and copies ran while one was open for 2% -> 2% of each run, Pallas kernels for 32% -> 32%
where the time goes in v15:
time: 110 us
  waiting for transfers between devices  36.9 us (34%)
  Pallas kernels  36.1 us (33%)
  starting transfers between devices  28.6 us (26%)
  local copies, waits for them, and re-layouts  6.24 us (6%)
  other arithmetic  1.12 us (1%)
    ppermute x20, waiting for transfers between devices, ring_send(): return lax.ppermute(value, 'expert', forward if step > 0 else backward)  26.4 us
    ppermute x20, starting transfers between devices, ring_send(): return lax.ppermute(value, 'expert', forward if step > 0 else backward)  21.6 us
    pallas_call x3, Pallas kernels, block_product(): pl.pallas_call(functools.partial(block_kernel, plan, len(blocks), n_dp, n...  21 us
    pallas_call x2, Pallas kernels, weight_product(): pl.pallas_call(functools.partial(weight_kernel, len(blocks), len(scaleds)...  11.7 us
    ppermute x5, waiting for transfers between devices, shift(): lax.ppermute(value, 'dp', [(i, (i + step) % n_dp) for i in range(n_dp)])  8.21 us
    ppermute x5, starting transfers between devices, shift(): lax.ppermute(value, 'dp', [(i, (i + step) % n_dp) for i in range(n_dp)])  6.39 us
    unnamed x18, local copies, waits for them, and re-layouts  5.47 us
    ppermute x5, waiting for transfers between devices, swap(): return lax.ppermute(value, 'expert', sibling)  2.33 us
  transfers between devices with their start and end apart: 30, of which 17 were waited for; matrix products, arithmetic and copies ran while one was open for 2% of the time, Pallas kernels for 32%

profile of v15, /device:TPU:0, one launch (start us, length us, event | category | flops | bytes accessed | tf_op | source)
XLA Modules:
  0.0 109.9 jit_solution(11316860928423580222)
XLA Ops:
  0.6 0.5 collective-permute-start.8
  1.2 1.0 copy-done
  2.1 0.7 copy-done.1
  2.8 0.7 copy-done.3
  3.5 0.5 pack.1
  4.0 2.6 %collective-permute-start.1 = (bf16[48,2176]{1,0:T(8,128)(2,1)S(1)}, bf16[48,2176]{1,0:T(8,128)(2,1)S(1)}, u32[]{:S(2)}, u32[]{:S(2)}) collective-permute-start(bf16[48,2176]{1,0:T(8,128)(2,1)S(1)} %get-tuple-element.64), channel_id=1, source_target_pairs={{0,16},{16,0},{1,17},{17,1},{2,18},{18,2},{3,19},{19,3},{4,20},{20... | collective-permute-start | bytes 626696 | tf_op jit(solution)/shard_map/ppermute | solution.py:444
  6.6 1.5 %collective-permute-start.3 = (bf16[1,48,2176]{2,1,0:T(8,128)(2,1)S(1)}, bf16[1,48,2176]{2,1,0:T(8,128)(2,1)S(1)}, u32[]{:S(2)}, u32[]{:S(2)}) collective-permute-start(bf16[1,48,2176]{2,1,0:T(8,128)(2,1)S(1)} %bitcast.22), channel_id=1, source_target_pairs={{0,2},{1,3},{4,0},{5,1},{8,4},{9,5},{12,8},{13,9},{14,12},{15,13},... | collective-permute-start | bytes 626696 | tf_op jit(solution)/shard_map/ppermute | solution.py:447
  8.1 0.5 collective-permute-start
  8.6 0.7 dynamic-slice_bitcast_fusion.refs_0_
  9.3 3.1 %collective-permute-done.1 = bf16[48,2176]{1,0:T(8,128)(2,1)S(1)} collective-permute-done((bf16[48,2176]{1,0:T(8,128)(2,1)S(1)}, bf16[48,2176]{1,0:T(8,128)(2,1)S(1)}, u32[]{:S(2)}, u32[]{:S(2)}) %collective-permute-start.1) | collective-permute-done | bytes 208928 | tf_op jit(solution)/shard_map/ppermute | solution.py:444
  12.4 1.8 %collective-permute-start.4 = (bf16[1,48,2176]{2,1,0:T(8,128)(2,1)S(1)}, bf16[1,48,2176]{2,1,0:T(8,128)(2,1)S(1)}, u32[]{:S(2)}, u32[]{:S(2)}) collective-permute-start(bf16[1,48,2176]{2,1,0:T(8,128)(2,1)S(1)} %bitcast.27), channel_id=1, source_target_pairs={{0,2},{1,3},{4,0},{5,1},{8,4},{9,5},{12,8},{13,9},{14,12},{15,13},... | collective-permute-start | bytes 626696 | tf_op jit(solution)/shard_map/ppermute | solution.py:447
  14.2 1.3 %collective-permute-start.2 = (bf16[1,48,2176]{2,1,0:T(8,128)(2,1)S(1)}, bf16[1,48,2176]{2,1,0:T(8,128)(2,1)S(1)}, u32[]{:S(2)}, u32[]{:S(2)}) collective-permute-start(bf16[1,48,2176]{2,1,0:T(8,128)(2,1)S(1)} %bitcast.28), channel_id=1, source_target_pairs={{0,4},{1,5},{4,8},{5,9},{8,12},{9,13},{12,14},{13,15},{14,10},{15,... | collective-permute-start | bytes 626696 | tf_op jit(solution)/shard_map/ppermute | solution.py:447
  15.4 0.7 collective-permute-start.10
  16.2 4.4 %collective-permute-done.2 = bf16[1,48,2176]{2,1,0:T(8,128)(2,1)S(1)} collective-permute-done((bf16[1,48,2176]{2,1,0:T(8,128)(2,1)S(1)}, bf16[1,48,2176]{2,1,0:T(8,128)(2,1)S(1)}, u32[]{:S(2)}, u32[]{:S(2)}) %collective-permute-start.2) | collective-permute-done | bytes 208928 | tf_op jit(solution)/shard_map/ppermute | solution.py:447
  20.7 1.6 %collective-permute-start.6 = (bf16[2,48,2176]{2,1,0:T(8,128)(2,1)S(1)}, bf16[2,48,2176]{2,1,0:T(8,128)(2,1)S(1)}, u32[]{:S(2)}, u32[]{:S(2)}) collective-permute-start(bf16[2,48,2176]{2,1,0:T(8,128)(2,1)S(1)} %constant_dynamic-update-slice_fusion.2.refs_3_.refs_2_), channel_id=1, source_target_pairs={{0,2},{1,3},{4,0},{5,1},{8,4},{9,5},{12,8},{13,9},{14,12},{15,13},... | collective-permute-start | bytes 1253384 | tf_op jit(solution)/shard_map/ppermute | solution.py:447
  22.3 0.5 collective-permute-start.5
  22.8 7.9 %collective-permute-done.6.refs_5_.refs_4_ = bf16[2,48,2176]{2,1,0:T(8,128)(2,1)S(1)} collective-permute-done((bf16[2,48,2176]{2,1,0:T(8,128)(2,1)S(1)}, bf16[2,48,2176]{2,1,0:T(8,128)(2,1)S(1)}, u32[]{:S(2)}, u32[]{:S(2)}) %collective-permute-start.6) | collective-permute-done | bytes 417824 | tf_op jit(solution)/shard_map/ppermute | solution.py:447
  30.8 1.6 %collective-permute-start.11 = (bf16[2,48,2176]{2,1,0:T(8,128)(2,1)S(1)}, bf16[2,48,2176]{2,1,0:T(8,128)(2,1)S(1)}, u32[]{:S(2)}, u32[]{:S(2)}) collective-permute-start(bf16[2,48,2176]{2,1,0:T(8,128)(2,1)S(1)} %collective-permute-done.6.refs_5_.refs_4_), channel_id=1, source_target_pairs={{0,2},{1,3},{4,0},{5,1},{8,4},{9,5},{12,8},{13,9},{14,12},{15,13},... | collective-permute-start | bytes 1253384 | tf_op jit(solution)/shard_map/ppermute | solution.py:447
  32.4 0.5 collective-permute-start.9
  32.8 1.9 %copy-done.4 = bf16[1,768,2048]{2,1,0:T(8,128)(2,1)S(1)} copy-done((bf16[1,768,2048]{2,1,0:T(8,128)(2,1)S(1)}, bf16[1,768,2048]{2,1,0:T(8,128)(2,1)}, u32[]{:S(2)}) %copy-start.4) | copy-done | bytes 3145752
  34.7 1.2 %copy-done.6 = bf16[1,1,16,36,768]{4,2,3,1,0:T(8,128)(2,1)S(1)} copy-done((bf16[1,1,16,36,768]{4,2,3,1,0:T(8,128)(2,1)S(1)}, bf16[1,1,16,36,768]{4,2,3,1,0:T(8,128)(2,1)}, u32[]{:S(2)}) %copy-start.6) | copy-done | bytes 884760
  35.9 6.7 %block_product.3 = (bf16[48,2176]{1,0:T(8,128)(2,1)S(1)}, bf16[48,2176]{1,0:T(8,128)(2,1)S(1)}, bf16[48,2176]{1,0:T(8,128)(2,1)S(1)}, bf16[48,2176]{1,0:T(8,128)...) custom-call(s32[10]{0:T(128)S(1)} %dynamic-slice_bitcast_fusion.refs, ...), custom_call_target="tpu_custom_call" | custom-call | flops 3019898880 | bytes 9117696 | tf_op jit(solution)/shard_map/block_product/pallas_call | solution.py:299
  42.8 1.6 %collective-permute-start.14 = (bf16[1,48,2176]{2,1,0:T(8,128)(2,1)S(1)}, bf16[1,48,2176]{2,1,0:T(8,128)(2,1)S(1)}, u32[]{:S(2)}, u32[]{:S(2)}) collective-permute-start(bf16[1,48,2176]{2,1,0:T(8,128)(2,1)S(1)} %slice.7), channel_id=1, source_target_pairs={{0,2},{1,3},{4,0},{5,1},{8,4},{9,5},{12,8},{13,9},{14,12},{15,13},... | collective-permute-start | bytes 626696 | tf_op jit(solution)/shard_map/ppermute | solution.py:447
  44.4 0.5 collective-permute-start.13
  44.9 0.3 collective-permute-done.12.refs_7_.refs_8_
  45.2 6.7 %block_product.4 = (bf16[48,2176]{1,0:T(8,128)(2,1)S(1)}, bf16[48,2176]{1,0:T(8,128)(2,1)S(1)}, bf16[48,2176]{1,0:T(8,128)(2,1)S(1)}, bf16[48,2176]{1,0:T(8,128)...) custom-call(s32[10]{0:T(128)S(1)} %dynamic-slice_bitcast_fusion.refs_0_,, ...), custom_call_target="tpu_custom_call" | custom-call | flops 3019898880 | bytes 9117696 | tf_op jit(solution)/shard_map/block_product/pallas_call | solution.py:299
  51.9 1.6 %collective-permute-start.19 = (bf16[2,240,768]{2,1,0:T(8,128)(2,1)S(1)}, bf16[2,240,768]{2,1,0:T(8,128)(2,1)S(1)}, u32[]{:S(2)}, u32[]{:S(2)}) collective-permute-start(bf16[2,240,768]{2,1,0:T(8,128)(2,1)S(1)} %get-tuple-element.84), channel_id=1, source_target_pairs={{0,16},{16,0},{1,17},{17,1},{2,18},{18,2},{3,19},{19,3},{4,20},{20... | collective-permute-start | bytes 2211848 | tf_op jit(solution)/shard_map/ppermute | solution.py:444
  53.4 7.6 %block_product.5 = (bf16[48,2176]{1,0:T(8,128)(2,1)S(1)}, bf16[48,2176]{1,0:T(8,128)(2,1)S(1)}, bf16[48,2176]{1,0:T(8,128)(2,1)S(1)}, bf16[48,2176]{1,0:T(8,128)...) custom-call(s32[10]{0:T(128)S(1)} %dynamic-slice_bitcast_fusion.refs, ...), custom_call_target="tpu_custom_call" | custom-call | flops 3623878656 | bytes 9682944 | tf_op jit(solution)/shard_map/block_product/pallas_call | solution.py:299
  61.1 0.7 collective-permute-start.15
  61.8 1.4 %collective-permute-start.17 = (bf16[1,48,2176]{2,1,0:T(8,128)(2,1)S(1)}, bf16[1,48,2176]{2,1,0:T(8,128)(2,1)S(1)}, u32[]{:S(2)}, u32[]{:S(2)}) collective-permute-start(bf16[1,48,2176]{2,1,0:T(8,128)(2,1)S(1)} %bitcast.43), channel_id=1, source_target_pairs={{0,2},{1,3},{4,0},{5,1},{8,4},{9,5},{12,8},{13,9},{14,12},{15,13},... | collective-permute-start | bytes 626696 | tf_op jit(solution)/shard_map/ppermute | solution.py:447
  63.1 0.5 collective-permute-start.20
  63.6 4.4 %collective-permute-done.15.refs_2_ = bf16[1,48,2176]{2,1,0:T(8,128)(2,1)S(1)} collective-permute-done((bf16[1,48,2176]{2,1,0:T(8,128)(2,1)S(1)}, bf16[1,48,2176]{2,1,0:T(8,128)(2,1)S(1)}, u32[]{:S(2)}, u32[]{:S(2)}) %collective-permute-start.15) | collective-permute-done | bytes 208928 | tf_op jit(solution)/shard_map/ppermute | solution.py:447
  68.1 0.3 collective-permute-done.17.refs_2_
  68.4 0.1 sums.7
  68.4 1.4 %collective-permute-start.18 = (bf16[2,48,2176]{2,1,0:T(8,128)(2,1)S(1)}, bf16[2,48,2176]{2,1,0:T(8,128)(2,1)S(1)}, u32[]{:S(2)}, u32[]{:S(2)}) collective-permute-start(bf16[2,48,2176]{2,1,0:T(8,128)(2,1)S(1)} %sums.7), channel_id=1, source_target_pairs={{0,2},{1,3},{4,0},{5,1},{8,4},{9,5},{12,8},{13,9},{14,12},{15,13},... | collective-permute-start | bytes 1253384 | tf_op jit(solution)/shard_map/ppermute | solution.py:447
  69.9 0.6 collective-permute-start.16
  70.5 0.7 collective-permute-done.19.refs_6_
  71.3 5.2 %weight_product.2 = bf16[768,2048]{1,0:T(8,128)(2,1)S(1)} custom-call(bf16[1,48,2176]{2,1,0:T(8,128)(2,1)S(1)} %bitcast.25, bf16[2,48,2176]{2,1,0:T(8,128)(2,1)S(1)} %constant_dynamic-update-slice_fusion.refs_2_.refs_1_, bf16[2,48,2176]{2,1,0:T(8,128)(2,1)S(1)} %constant_dynamic-update-slice_fusion.2.refs_3_.refs_2_, ...), custom_call_target="tpu_custom_call" | custom-call | flops 2415919104 | bytes 10616832 | tf_op jit(solution)/shard_map/weight_product/pallas_call | solution.py:381
  76.5 3.4 %collective-permute-done.20.refs_7_ = bf16[2,144,768]{2,1,0:T(8,128)(2,1)S(1)} collective-permute-done((bf16[2,144,768]{2,1,0:T(8,128)(2,1)S(1)}, bf16[2,144,768]{2,1,0:T(8,128)(2,1)S(1)}, u32[]{:S(2)}, u32[]{:S(2)}) %collective-permute-start.20) | collective-permute-done | bytes 442400 | tf_op jit(solution)/shard_map/ppermute | solution.py:444
  80.0 0.1 sums.9
  80.1 0.1 sums.8
  80.2 1.2 %collective-permute-start.21 = (bf16[2,48,2176]{2,1,0:T(8,128)(2,1)S(1)}, bf16[2,48,2176]{2,1,0:T(8,128)(2,1)S(1)}, u32[]{:S(2)}, u32[]{:S(2)}) collective-permute-start(bf16[2,48,2176]{2,1,0:T(8,128)(2,1)S(1)} %sums.8), channel_id=1, source_target_pairs={{0,4},{1,5},{4,8},{5,9},{8,12},{9,13},{12,14},{13,15},{14,10},{15,... | collective-permute-start | bytes 1253384 | tf_op jit(solution)/shard_map/ppermute | solution.py:447
  81.4 0.9 collective-permute-start.22
  82.3 1.3 %spread_product.1 = (bf16[576,768]{1,0:T(8,128)(2,1)S(1)}, bf16[576,768]{1,0:T(8,128)(2,1)S(1)}) custom-call(s32[240,2]{1,0:T(8,128)S(1)} %get-tuple-element.94.refs_0_, s32[144,2]{1,0:T(8,128)S(1)} %get-tuple-element.95.refs_1_, f32[240,2]{1,0:T(8,128)S(1)} %get-tuple-element.96.refs_2_, f32[144,2]{1,0:T(8,128)S(1)} %get-tuple-element.97.refs_3_, ...), custom_call_target="tpu_custom_call" | custom-call | flops 679477248 | bytes 3538944 | tf_op jit(solution)/shard_map/spread_product/pallas_call | solution.py:346
  83.6 2.0 %collective-permute-done.23.refs_14_ = bf16[768,2048]{1,0:T(8,128)(2,1)S(1)} collective-permute-done((bf16[768,2048]{1,0:T(8,128)(2,1)S(1)}, bf16[768,2048]{1,0:T(8,128)(2,1)S(1)}, u32[]{:S(2)}, u32[]{:S(2)}) %collective-permute-start.23) | collective-permute-done | bytes 3145760 | tf_op jit(solution)/shard_map/ppermute | solution.py:450
  85.7 6.4 %weight_product.3 = f32[768,2048]{1,0:T(8,128)} custom-call(bf16[1,48,2176]{2,1,0:T(8,128)(2,1)S(1)} %bitcast.26, bf16[2,48,2176]{2,1,0:T(8,128)(2,1)S(1)} %constant_dynamic-update-slice_fusion.refs_2_.refs_1_, bf16[2,48,2176]{2,1,0:T(8,128)(2,1)S(1)} %constant_dynamic-update-slice_fusion.2.refs_3_.refs_2_, ...), custom_call_target="tpu_custom_call" | custom-call | flops 2415919104 | bytes 10616832 | tf_op jit(solution)/shard_map/weight_product/pallas_call | solution.py:381
  92.1 0.2 collective-permute-done.21.refs_1_.refs_3_
  92.3 0.8 collective-permute-done.22.refs_1_.refs_3_
  93.2 0.1 sums.10
  93.3 0.1 sums.11
  93.4 1.6 %collective-permute-start.27 = (bf16[1,48,2176]{2,1,0:T(8,128)(2,1)S(1)}, bf16[1,48,2176]{2,1,0:T(8,128)(2,1)S(1)}, u32[]{:S(2)}, u32[]{:S(2)}) collective-permute-start(bf16[1,48,2176]{2,1,0:T(8,128)(2,1)S(1)} %get-tuple-element.117), channel_id=1, source_target_pairs={{0,4},{1,5},{4,8},{5,9},{8,12},{9,13},{12,14},{13,15},{14,10},{15,... | collective-permute-start | bytes 626696 | tf_op jit(solution)/shard_map/ppermute | solution.py:447
  95.0 0.4 collective-permute-start.28
  95.5 1.6 %collective-permute-start.25 = (bf16[1,48,2176]{2,1,0:T(8,128)(2,1)S(1)}, bf16[1,48,2176]{2,1,0:T(8,128)(2,1)S(1)}, u32[]{:S(2)}, u32[]{:S(2)}) collective-permute-start(bf16[1,48,2176]{2,1,0:T(8,128)(2,1)S(1)} %get-tuple-element.111), channel_id=1, source_target_pairs={{0,4},{1,5},{4,8},{5,9},{8,12},{9,13},{12,14},{13,15},{14,10},{15,... | collective-permute-start | bytes 626696 | tf_op jit(solution)/shard_map/ppermute | solution.py:447
  97.0 0.4 collective-permute-start.26
  97.5 3.9 %collective-permute-done.27.refs_1_ = bf16[1,48,2176]{2,1,0:T(8,128)(2,1)S(1)} collective-permute-done((bf16[1,48,2176]{2,1,0:T(8,128)(2,1)S(1)}, bf16[1,48,2176]{2,1,0:T(8,128)(2,1)S(1)}, u32[]{:S(2)}, u32[]{:S(2)}) %collective-permute-start.27) | collective-permute-done | bytes 208928 | tf_op jit(solution)/shard_map/ppermute | solution.py:447
  101.4 1.6 %collective-permute-done.28.refs_2_ = bf16[1,48,2176]{2,1,0:T(8,128)(2,1)S(1)} collective-permute-done((bf16[1,48,2176]{2,1,0:T(8,128)(2,1)S(1)}, bf16[1,48,2176]{2,1,0:T(8,128)(2,1)S(1)}, u32[]{:S(2)}, u32[]{:S(2)}) %collective-permute-start.28) | collective-permute-done | bytes 208928 | tf_op jit(solution)/shard_map/ppermute | solution.py:447
  103.0 0.1 close.3
  103.1 1.0 collective-permute-start.29
  104.1 1.4 %collective-permute-done.25.refs_1_ = bf16[1,48,2176]{2,1,0:T(8,128)(2,1)S(1)} collective-permute-done((bf16[1,48,2176]{2,1,0:T(8,128)(2,1)S(1)}, bf16[1,48,2176]{2,1,0:T(8,128)(2,1)S(1)}, u32[]{:S(2)}, u32[]{:S(2)}) %collective-permute-start.25) | collective-permute-done | bytes 208928 | tf_op jit(solution)/shard_map/ppermute | solution.py:447
  105.5 1.3 %collective-permute-done.26.refs_2_ = bf16[1,48,2176]{2,1,0:T(8,128)(2,1)S(1)} collective-permute-done((bf16[1,48,2176]{2,1,0:T(8,128)(2,1)S(1)}, bf16[1,48,2176]{2,1,0:T(8,128)(2,1)S(1)}, u32[]{:S(2)}, u32[]{:S(2)}) %collective-permute-start.26) | collective-permute-done | bytes 208928 | tf_op jit(solution)/shard_map/ppermute | solution.py:447
  106.8 0.1 close.2.refs_0_
  106.9 1.1 %add.8 = bf16[576,768]{1,0:T(8,128)(2,1)} add(bf16[576,768]{1,0:T(8,128)(2,1)S(1)} %get-tuple-element.102, bf16[576,768]{1,0:T(8,128)(2,1)S(1)} %collective-permute-done.24) | non-fusion elementwise | flops 442368 | bytes 2654208 | tf_op jit(solution)/shard_map/add | solution.py:558
  108.0 1.0 collective-permute-done.29.refs_1_
  109.0 0.9 home.1
  (36 shorter events, 0.4 us)
Async XLA Ops:
  0.6 32.2 %collective-permute-start.8 = (bf16[768,2048]{1,0:T(8,128)(2,1)}, bf16[768,2048]{1,0:T(8,128)(2,1)}, u32[]{:S(2)}, u32[]{:S(2)}) collective-permute-start(bf16[768,2048]{1,0:T(8,128)(2,1)} %bitcast.35), channel_id=1, source_target_pairs={{0,1},{1,0},{2,3},{3,2},{4,5},{5,4},{6,7},{7,6},{8,9},{9,8},{10,11... | collective-permute-start | bytes 9437192 | tf_op jit(solution)/shard_map/ppermute | solution.py:450
  1.1 1.0 copy-start
  2.1 0.7 copy-start.1
  2.8 0.7 copy-start.3
  4.0 8.4 %collective-permute-start.1 = (bf16[48,2176]{1,0:T(8,128)(2,1)S(1)}, bf16[48,2176]{1,0:T(8,128)(2,1)S(1)}, u32[]{:S(2)}, u32[]{:S(2)}) collective-permute-start(bf16[48,2176]{1,0:T(8,128)(2,1)S(1)} %get-tuple-element.64), channel_id=1, source_target_pairs={{0,16},{16,0},{1,17},{17,1},{2,18},{18,2},{3,19},{19,3},{4,20},{20... | collective-permute-start | bytes 626696 | tf_op jit(solution)/shard_map/ppermute | solution.py:444
  6.6 7.6 %collective-permute-start.3 = (bf16[1,48,2176]{2,1,0:T(8,128)(2,1)S(1)}, bf16[1,48,2176]{2,1,0:T(8,128)(2,1)S(1)}, u32[]{:S(2)}, u32[]{:S(2)}) collective-permute-start(bf16[1,48,2176]{2,1,0:T(8,128)(2,1)S(1)} %bitcast.22), channel_id=1, source_target_pairs={{0,2},{1,3},{4,0},{5,1},{8,4},{9,5},{12,8},{13,9},{14,12},{15,13},... | collective-permute-start | bytes 626696 | tf_op jit(solution)/shard_map/ppermute | solution.py:447
  8.1 7.3 %collective-permute-start = (bf16[1,48,2176]{2,1,0:T(8,128)(2,1)S(1)}, bf16[1,48,2176]{2,1,0:T(8,128)(2,1)S(1)}, u32[]{:S(2)}, u32[]{:S(2)}) collective-permute-start(bf16[1,48,2176]{2,1,0:T(8,128)(2,1)S(1)} %bitcast.23), channel_id=1, source_target_pairs={{0,4},{1,5},{4,8},{5,9},{8,12},{9,13},{12,14},{13,15},{14,10},{15,... | collective-permute-start | bytes 626696 | tf_op jit(solution)/shard_map/ppermute | solution.py:447
  8.6 24.2 %collective-permute-start.7 = (bf16[576,768]{1,0:T(8,128)(2,1)}, bf16[576,768]{1,0:T(8,128)(2,1)S(1)}, u32[]{:S(2)}, u32[]{:S(2)}) collective-permute-start(bf16[576,768]{1,0:T(8,128)(2,1)} %bitcast.39), channel_id=1, source_target_pairs={{0,1},{1,0},{2,3},{3,2},{4,5},{5,4},{6,7},{7,6},{8,9},{9,8},{10,11... | collective-permute-start | bytes 2654216 | tf_op jit(solution)/shard_map/ppermute | solution.py:450
  12.4 8.3 %collective-permute-start.4 = (bf16[1,48,2176]{2,1,0:T(8,128)(2,1)S(1)}, bf16[1,48,2176]{2,1,0:T(8,128)(2,1)S(1)}, u32[]{:S(2)}, u32[]{:S(2)}) collective-permute-start(bf16[1,48,2176]{2,1,0:T(8,128)(2,1)S(1)} %bitcast.27), channel_id=1, source_target_pairs={{0,2},{1,3},{4,0},{5,1},{8,4},{9,5},{12,8},{13,9},{14,12},{15,13},... | collective-permute-start | bytes 626696 | tf_op jit(solution)/shard_map/ppermute | solution.py:447
  14.2 6.5 %collective-permute-start.2 = (bf16[1,48,2176]{2,1,0:T(8,128)(2,1)S(1)}, bf16[1,48,2176]{2,1,0:T(8,128)(2,1)S(1)}, u32[]{:S(2)}, u32[]{:S(2)}) collective-permute-start(bf16[1,48,2176]{2,1,0:T(8,128)(2,1)S(1)} %bitcast.28), channel_id=1, source_target_pairs={{0,4},{1,5},{4,8},{5,9},{8,12},{9,13},{12,14},{13,15},{14,10},{15,... | collective-permute-start | bytes 626696 | tf_op jit(solution)/shard_map/ppermute | solution.py:447
  15.4 27.2 %collective-permute-start.10 = (bf16[576,768]{1,0:T(8,128)(2,1)}, bf16[576,768]{1,0:T(8,128)(2,1)S(1)}, u32[]{:S(2)}, u32[]{:S(2)}) collective-permute-start(bf16[576,768]{1,0:T(8,128)(2,1)} %bitcast.40), channel_id=1, source_target_pairs={{0,16},{16,0},{1,17},{17,1},{2,18},{18,2},{3,19},{19,3},{4,20},{20... | collective-permute-start | bytes 2654216 | tf_op jit(solution)/shard_map/ppermute | solution.py:444
  20.7 10.1 %collective-permute-start.6 = (bf16[2,48,2176]{2,1,0:T(8,128)(2,1)S(1)}, bf16[2,48,2176]{2,1,0:T(8,128)(2,1)S(1)}, u32[]{:S(2)}, u32[]{:S(2)}) collective-permute-start(bf16[2,48,2176]{2,1,0:T(8,128)(2,1)S(1)} %constant_dynamic-update-slice_fusion.2.refs_3_.refs_2_), channel_id=1, source_target_pairs={{0,2},{1,3},{4,0},{5,1},{8,4},{9,5},{12,8},{13,9},{14,12},{15,13},... | collective-permute-start | bytes 1253384 | tf_op jit(solution)/shard_map/ppermute | solution.py:447
  22.3 10.0 %collective-permute-start.5 = (bf16[2,48,2176]{2,1,0:T(8,128)(2,1)S(1)}, bf16[2,48,2176]{2,1,0:T(8,128)(2,1)S(1)}, u32[]{:S(2)}, u32[]{:S(2)}) collective-permute-start(bf16[2,48,2176]{2,1,0:T(8,128)(2,1)S(1)} %constant_dynamic-update-slice_fusion.refs_2_.refs_1_), channel_id=1, source_target_pairs={{0,4},{1,5},{4,8},{5,9},{8,12},{9,13},{12,14},{13,15},{14,10},{15,... | collective-permute-start | bytes 1253384 | tf_op jit(solution)/shard_map/ppermute | solution.py:447
  30.8 11.9 %collective-permute-start.11 = (bf16[2,48,2176]{2,1,0:T(8,128)(2,1)S(1)}, bf16[2,48,2176]{2,1,0:T(8,128)(2,1)S(1)}, u32[]{:S(2)}, u32[]{:S(2)}) collective-permute-start(bf16[2,48,2176]{2,1,0:T(8,128)(2,1)S(1)} %collective-permute-done.6.refs_5_.refs_4_), channel_id=1, source_target_pairs={{0,2},{1,3},{4,0},{5,1},{8,4},{9,5},{12,8},{13,9},{14,12},{15,13},... | collective-permute-start | bytes 1253384 | tf_op jit(solution)/shard_map/ppermute | solution.py:447
  32.4 10.3 %collective-permute-start.9 = (bf16[2,48,2176]{2,1,0:T(8,128)(2,1)S(1)}, bf16[2,48,2176]{2,1,0:T(8,128)(2,1)S(1)}, u32[]{:S(2)}, u32[]{:S(2)}) collective-permute-start(bf16[2,48,2176]{2,1,0:T(8,128)(2,1)S(1)} %collective-permute-done.5.refs_4_.refs_3_), channel_id=1, source_target_pairs={{0,4},{1,5},{4,8},{5,9},{8,12},{9,13},{12,14},{13,15},{14,10},{15,... | collective-permute-start | bytes 1253384 | tf_op jit(solution)/shard_map/ppermute | solution.py:447
  32.8 1.9 %copy-start.4 = (bf16[1,768,2048]{2,1,0:T(8,128)(2,1)S(1)}, bf16[1,768,2048]{2,1,0:T(8,128)(2,1)}, u32[]{:S(2)}) copy-start(bf16[1,768,2048]{2,1,0:T(8,128)(2,1)} %param.9) | copy-start | bytes 9437188
  34.7 1.2 %copy-start.6 = (bf16[1,1,16,36,768]{4,2,3,1,0:T(8,128)(2,1)S(1)}, bf16[1,1,16,36,768]{4,2,3,1,0:T(8,128)(2,1)}, u32[]{:S(2)}) copy-start(bf16[1,1,16,36,768]{4,2,3,1,0:T(8,128)(2,1)} %param.8) | copy-start | bytes 2654212
  35.9 9.3 %copy-start.5 = (bf16[1,768,2048]{2,1,0:T(8,128)(2,1)S(1)}, bf16[1,768,2048]{2,1,0:T(8,128)(2,1)}, u32[]{:S(2)}) copy-start(bf16[1,768,2048]{2,1,0:T(8,128)(2,1)} %param.9) | copy-start | bytes 9437188
  42.7 2.5 %collective-permute-start.12 = (bf16[576,768]{1,0:T(8,128)(2,1)S(1)}, bf16[576,768]{1,0:T(8,128)(2,1)S(1)}, u32[]{:S(2)}, u32[]{:S(2)}) collective-permute-start(bf16[576,768]{1,0:T(8,128)(2,1)S(1)} %collective-permute-done.10.refs_6_.refs_7_), channel_id=1, source_target_pairs={{0,1},{1,0},{2,3},{3,2},{4,5},{5,4},{6,7},{7,6},{8,9},{9,8},{10,11... | collective-permute-start | bytes 2654216 | tf_op jit(solution)/shard_map/ppermute | solution.py:450
  42.8 10.6 %copy-start.7 = (bf16[1,1,16,36,768]{4,2,3,1,0:T(8,128)(2,1)S(1)}, bf16[1,1,16,36,768]{4,2,3,1,0:T(8,128)(2,1)}, u32[]{:S(2)}) copy-start(bf16[1,1,16,36,768]{4,2,3,1,0:T(8,128)(2,1)} %param.8) | copy-start | bytes 2654212
  42.8 9.0 %collective-permute-start.14 = (bf16[1,48,2176]{2,1,0:T(8,128)(2,1)S(1)}, bf16[1,48,2176]{2,1,0:T(8,128)(2,1)S(1)}, u32[]{:S(2)}, u32[]{:S(2)}) collective-permute-start(bf16[1,48,2176]{2,1,0:T(8,128)(2,1)S(1)} %slice.7), channel_id=1, source_target_pairs={{0,2},{1,3},{4,0},{5,1},{8,4},{9,5},{12,8},{13,9},{14,12},{15,13},... | collective-permute-start | bytes 626696 | tf_op jit(solution)/shard_map/ppermute | solution.py:447
  44.4 7.4 %collective-permute-start.13 = (bf16[1,48,2176]{2,1,0:T(8,128)(2,1)S(1)}, bf16[1,48,2176]{2,1,0:T(8,128)(2,1)S(1)}, u32[]{:S(2)}, u32[]{:S(2)}) collective-permute-start(bf16[1,48,2176]{2,1,0:T(8,128)(2,1)S(1)} %slice.6), channel_id=1, source_target_pairs={{0,4},{1,5},{4,8},{5,9},{8,12},{9,13},{12,14},{13,15},{14,10},{15,... | collective-permute-start | bytes 626696 | tf_op jit(solution)/shard_map/ppermute | solution.py:447
  51.9 19.4 %collective-permute-start.19 = (bf16[2,240,768]{2,1,0:T(8,128)(2,1)S(1)}, bf16[2,240,768]{2,1,0:T(8,128)(2,1)S(1)}, u32[]{:S(2)}, u32[]{:S(2)}) collective-permute-start(bf16[2,240,768]{2,1,0:T(8,128)(2,1)S(1)} %get-tuple-element.84), channel_id=1, source_target_pairs={{0,16},{16,0},{1,17},{17,1},{2,18},{18,2},{3,19},{19,3},{4,20},{20... | collective-permute-start | bytes 2211848 | tf_op jit(solution)/shard_map/ppermute | solution.py:444
  61.1 6.9 %collective-permute-start.15 = (bf16[1,48,2176]{2,1,0:T(8,128)(2,1)S(1)}, bf16[1,48,2176]{2,1,0:T(8,128)(2,1)S(1)}, u32[]{:S(2)}, u32[]{:S(2)}) collective-permute-start(bf16[1,48,2176]{2,1,0:T(8,128)(2,1)S(1)} %bitcast.44), channel_id=1, source_target_pairs={{0,4},{1,5},{4,8},{5,9},{8,12},{9,13},{12,14},{13,15},{14,10},{15,... | collective-permute-start | bytes 626696 | tf_op jit(solution)/shard_map/ppermute | solution.py:447
  61.8 6.6 %collective-permute-start.17 = (bf16[1,48,2176]{2,1,0:T(8,128)(2,1)S(1)}, bf16[1,48,2176]{2,1,0:T(8,128)(2,1)S(1)}, u32[]{:S(2)}, u32[]{:S(2)}) collective-permute-start(bf16[1,48,2176]{2,1,0:T(8,128)(2,1)S(1)} %bitcast.43), channel_id=1, source_target_pairs={{0,2},{1,3},{4,0},{5,1},{8,4},{9,5},{12,8},{13,9},{14,12},{15,13},... | collective-permute-start | bytes 626696 | tf_op jit(solution)/shard_map/ppermute | solution.py:447
  63.1 16.8 %collective-permute-start.20 = (bf16[2,144,768]{2,1,0:T(8,128)(2,1)S(1)}, bf16[2,144,768]{2,1,0:T(8,128)(2,1)S(1)}, u32[]{:S(2)}, u32[]{:S(2)}) collective-permute-start(bf16[2,144,768]{2,1,0:T(8,128)(2,1)S(1)} %get-tuple-element.101), channel_id=1, source_target_pairs={{0,16},{16,0},{1,17},{17,1},{2,18},{18,2},{3,19},{19,3},{4,20},{20... | collective-permute-start | bytes 1327112 | tf_op jit(solution)/shard_map/ppermute | solution.py:444
  68.4 11.5 %collective-permute-start.18 = (bf16[2,48,2176]{2,1,0:T(8,128)(2,1)S(1)}, bf16[2,48,2176]{2,1,0:T(8,128)(2,1)S(1)}, u32[]{:S(2)}, u32[]{:S(2)}) collective-permute-start(bf16[2,48,2176]{2,1,0:T(8,128)(2,1)S(1)} %sums.7), channel_id=1, source_target_pairs={{0,2},{1,3},{4,0},{5,1},{8,4},{9,5},{12,8},{13,9},{14,12},{15,13},... | collective-permute-start | bytes 1253384 | tf_op jit(solution)/shard_map/ppermute | solution.py:447
  69.9 10.1 %collective-permute-start.16 = (bf16[2,48,2176]{2,1,0:T(8,128)(2,1)S(1)}, bf16[2,48,2176]{2,1,0:T(8,128)(2,1)S(1)}, u32[]{:S(2)}, u32[]{:S(2)}) collective-permute-start(bf16[2,48,2176]{2,1,0:T(8,128)(2,1)S(1)} %sums.6), channel_id=1, source_target_pairs={{0,4},{1,5},{4,8},{5,9},{8,12},{9,13},{12,14},{13,15},{14,10},{15,... | collective-permute-start | bytes 1253384 | tf_op jit(solution)/shard_map/ppermute | solution.py:447
  80.0 5.7 %collective-permute-start.23 = (bf16[768,2048]{1,0:T(8,128)(2,1)S(1)}, bf16[768,2048]{1,0:T(8,128)(2,1)S(1)}, u32[]{:S(2)}, u32[]{:S(2)}) collective-permute-start(bf16[768,2048]{1,0:T(8,128)(2,1)S(1)} %weight_product.2), channel_id=1, source_target_pairs={{0,1},{1,0},{2,3},{3,2},{4,5},{5,4},{6,7},{7,6},{8,9},{9,8},{10,11... | collective-permute-start | bytes 9437192 | tf_op jit(solution)/shard_map/ppermute | solution.py:450
  80.2 12.1 %collective-permute-start.21 = (bf16[2,48,2176]{2,1,0:T(8,128)(2,1)S(1)}, bf16[2,48,2176]{2,1,0:T(8,128)(2,1)S(1)}, u32[]{:S(2)}, u32[]{:S(2)}) collective-permute-start(bf16[2,48,2176]{2,1,0:T(8,128)(2,1)S(1)} %sums.8), channel_id=1, source_target_pairs={{0,4},{1,5},{4,8},{5,9},{8,12},{9,13},{12,14},{13,15},{14,10},{15,... | collective-permute-start | bytes 1253384 | tf_op jit(solution)/shard_map/ppermute | solution.py:447
  81.4 11.8 %collective-permute-start.22 = (bf16[2,48,2176]{2,1,0:T(8,128)(2,1)S(1)}, bf16[2,48,2176]{2,1,0:T(8,128)(2,1)S(1)}, u32[]{:S(2)}, u32[]{:S(2)}) collective-permute-start(bf16[2,48,2176]{2,1,0:T(8,128)(2,1)S(1)} %sums.9), channel_id=1, source_target_pairs={{0,2},{1,3},{4,0},{5,1},{8,4},{9,5},{12,8},{13,9},{14,12},{15,13},... | collective-permute-start | bytes 1253384 | tf_op jit(solution)/shard_map/ppermute | solution.py:447
  93.2 13.7 %collective-permute-start.24 = (bf16[576,768]{1,0:T(8,128)(2,1)S(1)}, bf16[576,768]{1,0:T(8,128)(2,1)S(1)}, u32[]{:S(2)}, u32[]{:S(2)}) collective-permute-start(bf16[576,768]{1,0:T(8,128)(2,1)S(1)} %get-tuple-element.106), channel_id=1, source_target_pairs={{0,1},{1,0},{2,3},{3,2},{4,5},{5,4},{6,7},{7,6},{8,9},{9,8},{10,11... | collective-permute-start | bytes 2654216 | tf_op jit(solution)/shard_map/ppermute | solution.py:450
  93.2 15.8 %copy-start.2 = (s32[48,8]{0,1:T(8,128)S(1)}, s32[48,8]{0,1:T(8,128)}, u32[]{:S(2)}) copy-start(s32[48,8]{0,1:T(8,128)} %param.6) | copy-start | bytes 4612
  93.4 8.0 %collective-permute-start.27 = (bf16[1,48,2176]{2,1,0:T(8,128)(2,1)S(1)}, bf16[1,48,2176]{2,1,0:T(8,128)(2,1)S(1)}, u32[]{:S(2)}, u32[]{:S(2)}) collective-permute-start(bf16[1,48,2176]{2,1,0:T(8,128)(2,1)S(1)} %get-tuple-element.117), channel_id=1, source_target_pairs={{0,4},{1,5},{4,8},{5,9},{8,12},{9,13},{12,14},{13,15},{14,10},{15,... | collective-permute-start | bytes 626696 | tf_op jit(solution)/shard_map/ppermute | solution.py:447
  95.0 8.0 %collective-permute-start.28 = (bf16[1,48,2176]{2,1,0:T(8,128)(2,1)S(1)}, bf16[1,48,2176]{2,1,0:T(8,128)(2,1)S(1)}, u32[]{:S(2)}, u32[]{:S(2)}) collective-permute-start(bf16[1,48,2176]{2,1,0:T(8,128)(2,1)S(1)} %get-tuple-element.119), channel_id=1, source_target_pairs={{0,2},{1,3},{4,0},{5,1},{8,4},{9,5},{12,8},{13,9},{14,12},{15,13},... | collective-permute-start | bytes 626696 | tf_op jit(solution)/shard_map/ppermute | solution.py:447
  95.5 10.0 %collective-permute-start.25 = (bf16[1,48,2176]{2,1,0:T(8,128)(2,1)S(1)}, bf16[1,48,2176]{2,1,0:T(8,128)(2,1)S(1)}, u32[]{:S(2)}, u32[]{:S(2)}) collective-permute-start(bf16[1,48,2176]{2,1,0:T(8,128)(2,1)S(1)} %get-tuple-element.111), channel_id=1, source_target_pairs={{0,4},{1,5},{4,8},{5,9},{8,12},{9,13},{12,14},{13,15},{14,10},{15,... | collective-permute-start | bytes 626696 | tf_op jit(solution)/shard_map/ppermute | solution.py:447
  97.0 9.7 %collective-permute-start.26 = (bf16[1,48,2176]{2,1,0:T(8,128)(2,1)S(1)}, bf16[1,48,2176]{2,1,0:T(8,128)(2,1)S(1)}, u32[]{:S(2)}, u32[]{:S(2)}) collective-permute-start(bf16[1,48,2176]{2,1,0:T(8,128)(2,1)S(1)} %get-tuple-element.115), channel_id=1, source_target_pairs={{0,2},{1,3},{4,0},{5,1},{8,4},{9,5},{12,8},{13,9},{14,12},{15,13},... | collective-permute-start | bytes 626696 | tf_op jit(solution)/shard_map/ppermute | solution.py:447
  103.1 5.9 %collective-permute-start.29 = (bf16[48,2176]{1,0:T(8,128)(2,1)S(1)}, bf16[48,2176]{1,0:T(8,128)(2,1)S(1)}, u32[]{:S(2)}, u32[]{:S(2)}) collective-permute-start(bf16[48,2176]{1,0:T(8,128)(2,1)S(1)} %close.3), channel_id=1, source_target_pairs={{0,16},{16,0},{1,17},{17,1},{2,18},{18,2},{3,19},{19,3},{4,20},{20... | collective-permute-start | bytes 626696 | tf_op jit(solution)/shard_map/ppermute | solution.py:444
